TPU v7x, 32 devices: a whole 2x2x4 slice. The times are simulated.
32 devices in a mesh: dp: 8 (over z, x), tensor: 4 (over y, core).
Axes of the slice: x: 2, y: 2, z: 4, core: 2. Of those that a mesh axis runs over, the one named last changes fastest.
Arguments:
- queries: bfloat16 [256, 32, 128], P('dp'), may hold values from -5 to 5
- new_keys: bfloat16 [256, 2, 128], P('dp'), may hold values from -5 to 5
- new_values: bfloat16 [256, 2, 128], P('dp'), may hold values from -5 to 5
- key_cache: bfloat16 [256, 2, 128, 128], P('dp', None, 'tensor'), may hold values from -160 to 160
- value_cache: bfloat16 [256, 2, 128, 128], P('dp', None, 'tensor'), may hold values from -5 to 5
- lengths: int32 [256], P('dp'), may hold values from 2 to 128, as said below
- residual_in: bfloat16 [256, 4096], P(('dp', 'tensor')), may hold values from -24 to 24
- query_gain: float32 [128], replicated, may hold values from 0.1 to 1.9
- key_gain: float32 [128], replicated, may hold values from 0.1 to 1.9
- out_proj: bfloat16 [4096, 4096], P('tensor'), may hold values from -0.09375 to 0.09375
- norm_gain: float32 [4096], replicated, may hold values from 0.1 to 1.9
- expert_ids: int32 [256, 8], P(('dp', 'tensor')), may hold values from 0 to 31, all different within a row; in each aligned block of 8 rows (0 to 7, 8 to 15, ...) at most 3 rows name the same one
- gate_weights: float32 [256, 8], P(('dp', 'tensor')), may hold values from 0.05 to 1
- expert_gate: bfloat16 [32, 4096, 768], P(('dp', 'tensor')), may hold values from -0.09375 to 0.09375
- expert_up: bfloat16 [32, 4096, 768], P(('dp', 'tensor')), may hold values from -0.09375 to 0.09375
- expert_down: bfloat16 [32, 768, 4096], P(('dp', 'tensor')), may hold values from -0.21875 to 0.21875
Outputs:
- mixed: bfloat16 [256, 4096], P(('dp', 'tensor'))
Inputs may be any that keep to these rules, and one draw needn't show every extreme that they name: `expert_ids`: rows are taken in aligned blocks of 8; within a block no expert is named by more than 3 rows, a bound that some block reaches. `lengths`: each group of 32 rows has a row with 128 positions in use.
All inputs are finite; a program needn't handle non-finite values.
Results may differ from a plain program's by a relative error of at most 0.013.
Values may be sent and summed in bfloat16 or wider, within the bound.
No kernel may reach another device: no remote copies, remote signals or barrier semaphores. Data moves between devices by JAX's collectives and lax.ppermute only.
A program may use at most 128 MiB of HBM per device.

v0:
```python
import jax
import jax.numpy as jnp
from jax import lax
from jax.sharding import PartitionSpec as P

CAP = 3


def rms_scale(values, gain):
    mean_sq = jnp.mean(values * values, axis=-1, keepdims=True)
    return values * lax.rsqrt(mean_sq + 1e-06) * gain


def expert_rows(block, expert_gate, expert_up, expert_down):
    width = block.shape[-1]
    flat_rows = block.reshape(-1, width)
    gate_val = jnp.dot(flat_rows, expert_gate[0], preferred_element_type=jnp.float32)
    up_val = jnp.dot(flat_rows, expert_up[0], preferred_element_type=jnp.float32)
    activation = (jax.nn.silu(gate_val) * up_val).astype(jnp.bfloat16)
    result = jnp.dot(activation, expert_down[0], preferred_element_type=jnp.float32).astype(
        jnp.bfloat16
    )
    return result.reshape(block.shape)


def shards(
    queries,
    new_keys,
    new_values,
    key_cache,
    value_cache,
    lengths,
    residual_in,
    query_gain,
    key_gain,
    out_proj,
    norm_gain,
    expert_ids,
    gate_weights,
    expert_gate,
    expert_up,
    expert_down,
):
    tensor_pos = lax.axis_index("tensor")
    tensor_count = lax.axis_size("tensor")
    dp_count = lax.axis_size("dp")
    row_total, head_total, head_dim = queries.shape
    kv_total = key_cache.shape[1]
    cache_local = key_cache.shape[2]
    group_size = head_total // kv_total
    query_norm = rms_scale(queries.astype(jnp.float32), query_gain).astype(jnp.bfloat16)
    key_norm = rms_scale(new_keys.astype(jnp.float32), key_gain).astype(jnp.bfloat16)
    grouped = query_norm.reshape(row_total, kv_total, group_size, head_dim)
    scaling = head_dim ** (-0.5)
    cache_scores = (
        jnp.einsum("rgqd,rgpd->rgqp", grouped, key_cache, preferred_element_type=jnp.float32)
        * scaling
    )
    new_score = (
        jnp.einsum("rgqd,rgd->rgq", grouped, key_norm, preferred_element_type=jnp.float32) * scaling
    )
    positions = tensor_pos * cache_local + jnp.arange(cache_local, dtype=jnp.int32)
    included = (positions[None, :] < lengths[:, None])[:, None, None, :]
    local_top = jnp.maximum(jnp.max(jnp.where(included, cache_scores, -1e30), axis=-1), new_score)
    score_top = lax.pmax(local_top, "tensor")
    cache_weights = jnp.where(included, jnp.exp(cache_scores - score_top[..., None]), 0.0).astype(
        jnp.bfloat16
    )
    new_weight = jnp.exp(new_score - score_top).astype(jnp.bfloat16)
    own_new = (tensor_pos == 0).astype(jnp.float32) * new_weight.astype(jnp.float32)
    numerator = jnp.einsum(
        "rgqp,rgpd->rgqd", cache_weights, value_cache, preferred_element_type=jnp.float32
    )
    numerator = numerator + own_new[..., None] * new_values.astype(jnp.float32)[:, :, None, :]
    weight_sum = jnp.sum(cache_weights.astype(jnp.float32), axis=-1) + own_new
    numer_own, denom_own = (
        lax.psum_scatter(
            numerator.reshape(row_total, head_total * head_dim).astype(jnp.bfloat16),
            "tensor",
            scatter_dimension=1,
            tiled=True,
        ).astype(jnp.float32),
        lax.psum_scatter(
            weight_sum.reshape(row_total, head_total).astype(jnp.bfloat16),
            "tensor",
            scatter_dimension=1,
            tiled=True,
        ).astype(jnp.float32),
    )
    heads_own = denom_own.shape[1]
    attn_own = (
        (numer_own.reshape(row_total, heads_own, head_dim) / denom_own[..., None])
        .reshape(row_total, heads_own * head_dim)
        .astype(jnp.bfloat16)
    )
    share_rows = residual_in.shape[0]
    partial_sum = jnp.dot(attn_own, out_proj, preferred_element_type=jnp.float32)
    whole_sum = lax.psum(partial_sum.astype(jnp.bfloat16), "tensor").astype(jnp.float32)
    proj_rows = lax.dynamic_slice_in_dim(whole_sum, tensor_pos * share_rows, share_rows, 0)
    hidden = residual_in.astype(jnp.float32) + proj_rows
    normed = rms_scale(hidden, norm_gain).astype(jnp.bfloat16)
    expert_total = expert_gate.shape[0] * dp_count * tensor_count
    capacity = CAP
    top_count = expert_ids.shape[1]
    flat_ids = expert_ids.reshape(-1)
    onehot = (flat_ids[:, None] == jnp.arange(expert_total, dtype=jnp.int32)[None, :]).astype(
        jnp.int32
    )
    earlier = jnp.cumsum(onehot, axis=0) - onehot
    slot_index = jnp.sum(earlier * onehot, axis=1)
    target = flat_ids * capacity + slot_index
    slot_ids = jnp.arange(expert_total * capacity, dtype=jnp.int32)
    placed = target[:, None] == slot_ids[None, :]
    dispatch_map = jnp.sum(
        placed.reshape(share_rows, top_count, -1).astype(jnp.int32), axis=1
    ).astype(jnp.bfloat16)
    outgoing = jnp.einsum(
        "ts,td->sd", dispatch_map, normed, preferred_element_type=jnp.float32
    ).astype(jnp.bfloat16)
    outgoing = outgoing.reshape(expert_total, capacity, -1)
    route_weights = (gate_weights / jnp.sum(gate_weights, axis=1, keepdims=True)).astype(
        jnp.bfloat16
    )
    combine_map = jnp.sum(
        jnp.where(placed, route_weights.reshape(-1)[:, None], jnp.zeros((), jnp.bfloat16)).reshape(
            share_rows, top_count, -1
        ),
        axis=1,
    )
    computed = expert_rows(
        lax.all_to_all(outgoing, ("dp", "tensor"), split_axis=0, concat_axis=0, tiled=True),
        expert_gate,
        expert_up,
        expert_down,
    )
    returned = lax.all_to_all(computed, ("dp", "tensor"), split_axis=0, concat_axis=0, tiled=True)
    moe_sum = jnp.dot(
        combine_map,
        returned.reshape(expert_total * capacity, -1),
        preferred_element_type=jnp.float32,
    )
    return (hidden + moe_sum).astype(jnp.bfloat16)


def solution(mesh):
    return jax.shard_map(
        shards,
        mesh=mesh,
        in_specs=(
            P("dp", None, None),
            P("dp", None, None),
            P("dp", None, None),
            P("dp", None, "tensor", None),
            P("dp", None, "tensor", None),
            P("dp"),
            P(("dp", "tensor"), None),
            P(),
            P(),
            P("tensor", None),
            P(),
            P(("dp", "tensor"), None),
            P(("dp", "tensor"), None),
            P(("dp", "tensor"), None, None),
            P(("dp", "tensor"), None, None),
            P(("dp", "tensor"), None, None),
        ),
        out_specs=P(("dp", "tensor"), None),
        check_vma=False,
    )
```

profile of v0, /device:TPU:0, one launch (start us, length us, event | category | flops | bytes accessed | tf_op | source)
XLA Modules:
  0.0 172.6 jit_solution(9146977614020217383)
XLA Ops:
  6.6 1.2 fusion.19
  7.8 0.8 fusion.33
  8.6 0.7 convert_element_type.98
  9.4 0.8 fusion.41
  10.2 1.2 fusion.21
  11.7 0.7 broadcast_compare_fusion
  12.4 1.5 select_reduce_fusion
  14.1 12.7 %pmax.7 = f32[32,2,16]{0,2,1:T(8,128)S(1)} all-reduce(f32[32,2,16]{0,2,1:T(8,128)S(1)} %fusion.42), channel_id=1, replica_groups=mesh['dp'=8,'tensor'=4] {'tensor'}, use_global_device_ids=true, to_apply=%region_3.4 | all-reduce | flops 1024 | bytes 8192 | tf_op jit(solution)/shard_map/pmax | solution.py:65
  27.8 0.8 copy.47
  30.5 5.9 %all-reduce = bf16[32,32]{0,1:T(8,128)(2,1)S(1)} all-reduce(bf16[32,32]{0,1:T(8,128)(2,1)S(1)} %bitcast.56), channel_id=3, replica_groups=mesh['dp'=8,'tensor'=4] {'tensor'}, use_global_device_ids=true, to_apply=%region_6.7.clone | all-reduce | flops 1024 | bytes 4096
  36.5 12.6 %reduce-scatter.2.cloned.1.call-done = bf16[32,1024]{1,0:T(8,128)(2,1)} async-done(((bf16[32,4096]{1,0:T(8,128)(2,1)}), bf16[32,1024]{1,0:T(8,128)(2,1)}) %reduce-scatter.2.cloned.1.call-update) | async-done | bytes 65552 | tf_op jit(solution)/shard_map/reduce_scatter | solution.py:77
  49.3 5.7 %convolution_convert_fusion.1 = bf16[32,4096]{1,0:T(8,128)(2,1)} fusion(bf16[1024,4096]{1,0:T(8,128)(2,1)} %param.25, f32[4,8,8,128]{3,2,1,0:T(8,128)S(1)} %bitcast.54, bf16[32,1024]{1,0:T(8,128)(2,1)} %reduce-scatter.2.cloned.1.call-done), kind=kOutput, calls=%fused_computation.8 | convolution fusion | flops 268664832 | bytes 8847360 | tf_op jit(solution)/shard_map/dot_general | solution.py:97
  55.0 32.0 %all-reduce.3.cloned.1.call-done = bf16[32,4096]{1,0:T(8,128)(2,1)} async-done(((bf16[32,4096]{1,0:T(8,128)(2,1)}), bf16[32,4096]{1,0:T(8,128)(2,1)}) %all-reduce.3.cloned.1.call-update) | async-done | bytes 262160 | tf_op jit(solution)/shard_map/psum | solution.py:98
  87.1 1.0 multiply_reduce_fusion
  88.1 1.3 convolution_convert_fusion
  89.8 30.6 %all_to_all.10 = bf16[32,3,4096]{2,1,0:T(4,128)(2,1)S(1)} all-to-all(bf16[32,3,4096]{2,1,0:T(4,128)(2,1)S(1)} %reshape.116), channel_id=1, replica_groups=mesh['dp'=8,'tensor'=4] {'dp','tensor'}, dimensions={0} | all-to-all | bytes 1572864 | tf_op jit(solution)/shard_map/all_to_all | solution.py:131
  120.5 0.7 reshape.117
  121.2 3.9 %fusion.4 = f32[96,768]{1,0:T(8,128)S(1)} fusion(bf16[96,4096]{1,0:T(8,128)(2,1)S(1)} %reshape.117, bf16[1,4096,768]{2,1,0:T(8,128)(2,1)} %param.29), kind=kOutput, calls=%fused_computation.4 | convolution fusion | flops 603979776 | bytes 7372800 | tf_op jit(solution)/shard_map/dot_general | solution.py:17
  125.1 7.1 %fusion.6 = bf16[96,4096]{1,0:T(8,128)(2,1)S(1)} fusion(bf16[1,768,4096]{2,1,0:T(8,128)(2,1)} %param.31, bf16[96,4096]{1,0:T(8,128)(2,1)S(1)} %reshape.117, bf16[1,4096,768]{2,1,0:T(8,128)(2,1)} %param.30, f32[96,768]{1,0:T(8,128)S(1)} %fusion.4), kind=kOutput, calls=%fused_computation.6 | convolution fusion | flops 1208795136 | bytes 14450688 | tf_op jit(solution)/shard_map/dot_general | solution.py:20
  132.3 1.3 reshape.118
  133.6 3.6 %all-to-all-start.1 = ((bf16[32,3,4096]{2,1,0:T(4,128)(2,1)}), bf16[32,3,4096]{2,1,0:T(4,128)(2,1)S(1)}, u32[]{:S(2)}, u32[]{:S(2)}) async-start(bf16[32,3,4096]{2,1,0:T(4,128)(2,1)} %reshape.118), calls=%async_computation.2 | async-start | bytes 2097152 | tf_op jit(solution)/shard_map/all_to_all | solution.py:136
  137.5 25.9 %all-to-all-done.1 = bf16[32,3,4096]{2,1,0:T(4,128)(2,1)S(1)} async-done(((bf16[32,3,4096]{2,1,0:T(4,128)(2,1)}), bf16[32,3,4096]{2,1,0:T(4,128)(2,1)S(1)}, u32[]{:S(2)}, u32[]{:S(2)}) %all-to-all-start.1) | async-done | bytes 786464 | tf_op jit(solution)/shard_map/all_to_all | solution.py:136
  163.4 0.7 reshape.119
  164.1 1.7 fusion.9
  (45 shorter events, 3.8 us)
Async XLA Ops:
  6.5 20.9 %copy-start = (bf16[32,2,32,128]{3,2,1,0:T(8,128)(2,1)S(1)}, bf16[32,2,32,128]{3,2,1,0:T(8,128)(2,1)}, u32[]{:S(2)}) copy-start(bf16[32,2,32,128]{3,2,1,0:T(8,128)(2,1)} %param.20) | copy-start | bytes 1572868
  6.5 22.7 %copy-start.5 = (u32[32]{0:T(128)S(1)}, u32[32]{0:T(128)}, u32[]{:S(2)}) copy-start(u32[32]{0:T(128)} %constant.51) | copy-start | bytes 388
  6.5 22.2 %copy-start.3 = (s32[8,8]{1,0:T(8,128)S(1)}, s32[8,8]{1,0:T(8,128)}, u32[]{:S(2)}) copy-start(s32[8,8]{1,0:T(8,128)} %param.27) | copy-start | bytes 772
  6.5 42.6 %reduce-scatter.2.cloned.1.call-start = ((), (), s32[]{:S(2)}) async-start(), calls=%async_computation.3 | async-start | bytes 327680 | tf_op jit(solution)/shard_map/reduce_scatter | solution.py:77
  28.7 58.4 %all-reduce.3.cloned.1.call-start = ((), (), s32[]{:S(2)}) async-start(), calls=%async_computation.4 | async-start | bytes 524288 | tf_op jit(solution)/shard_map/psum | solution.py:98
  49.2 37.8 %copy-start.1 = (bf16[8,4096]{1,0:T(8,128)(2,1)S(1)}, bf16[8,4096]{1,0:T(8,128)(2,1)}, u32[]{:S(2)}) copy-start(bf16[8,4096]{1,0:T(8,128)(2,1)} %param.22) | copy-start | bytes 196612
  49.2 38.8 %copy-start.2 = (f32[4096]{0:T(1024)S(1)}, f32[4096]{0:T(1024)}, u32[]{:S(2)}) copy-start(f32[4096]{0:T(1024)} %param.26) | copy-start | bytes 49156
  125.1 12.1 %copy-start.4 = (f32[8,8]{1,0:T(8,128)S(1)}, f32[8,8]{1,0:T(8,128)}, u32[]{:S(2)}) copy-start(f32[8,8]{1,0:T(8,128)} %param.28) | copy-start | bytes 772
  133.6 29.9 %all-to-all-start.1 = ((bf16[32,3,4096]{2,1,0:T(4,128)(2,1)}), bf16[32,3,4096]{2,1,0:T(4,128)(2,1)S(1)}, u32[]{:S(2)}, u32[]{:S(2)}) async-start(bf16[32,3,4096]{2,1,0:T(4,128)(2,1)} %reshape.118), calls=%async_computation.2 | async-start | bytes 2097152 | tf_op jit(solution)/shard_map/all_to_all | solution.py:136
Sparse Core Ops, SparseCore 0:
  28.8 20.3 reduce-scatter.1
  55.1 31.9 all-reduce.2
where the time goes:
time: 173 us
  waiting for transfers between devices  70.6 us (41%)
  blocking collectives  49.2 us (28%)
  matrix products  21.8 us (13%)
  between operations  14.3 us (8%)
  other arithmetic  7.72 us (4%)
  local copies, waits for them, and re-layouts  5.31 us (3%)
  starting transfers between devices  3.66 us (2%)
    psum x1, waiting for transfers between devices, shards(): lax.psum(partial_sum.astype(jnp.bfloat16), 'tensor').astype(jnp.float32)  32 us
    all_to_all x1, blocking collectives, shards(): lax.all_to_all(outgoing, ('dp', 'tensor'), split_axis=0, concat_axis=0, t...  30.6 us
    all_to_all x1, waiting for transfers between devices, shards(): lax.all_to_all(computed, ('dp', 'tensor'), split_axis=0, concat_axis=0, t...  25.9 us
    pmax x1, blocking collectives, shards(): score_top = lax.pmax(local_top, 'tensor')  12.7 us
    reduce_scatter x1, waiting for transfers between devices, shards(): lax.psum_scatter(numerator.reshape(row_total, head_total * head_dim).asty...  12.6 us
    dot_general x1, matrix products, expert_rows(): jnp.dot(activation, expert_down[0], preferred_element_type=jnp.float32)  7.15 us
    unnamed x1, blocking collectives  5.9 us
    dot_general x1, matrix products, shards(): jnp.dot(attn_own, out_proj, preferred_element_type=jnp.float32)  5.67 us
  transfers between devices with their start and end apart: 3, of which 3 were waited for; matrix products, arithmetic and copies ran while one was open for 1% of the time, Pallas kernels for 0%

commit v1 on v0

v1 whole, which is shorter than its diff:
```python
import jax
import jax.numpy as jnp
from jax import lax
from jax.sharding import PartitionSpec as P

BF = jnp.bfloat16
F32 = jnp.float32


def rms_scale(values, gain):
    mean_sq = jnp.mean(values * values, axis=-1, keepdims=True)
    return values * lax.rsqrt(mean_sq + 1e-06) * gain


def swap(x, axis, size, flip):
    return lax.ppermute(x, axis, [(i, i ^ flip) for i in range(size)])


class Plan:
    def __init__(self, dp, tensor):
        zlen = min(4, dp)
        xlen = dp // zlen
        ylen = tensor // 2
        self.axes = {
            "z": ("dp", dp, xlen, zlen),
            "x": ("dp", dp, 1, xlen),
            "y": ("tensor", tensor, 2, ylen),
            "c": ("tensor", tensor, 1, 2),
        }

    def length(self, name):
        return self.axes[name][3]

    def swap(self, x, name, j):
        axis, size, step, _ = self.axes[name]
        return swap(x, axis, size, j * step)


NAMES = "zxyc"


def gather(plan, x, order):
    for name in order:
        dim = NAMES.index(name)
        x = jnp.concatenate(
            [x] + [plan.swap(x, name, j) for j in range(1, plan.length(name))], axis=dim
        )
    return x


def reduce_slots(plan, x, order):
    for name in order:
        dim = NAMES.index(name)
        parts = [lax.slice_in_dim(x, j, j + 1, axis=dim) for j in range(plan.length(name))]
        total = parts[0].astype(F32)
        for j in range(1, plan.length(name)):
            total = total + plan.swap(parts[j].astype(BF), name, j).astype(F32)
        x = total
    return x


def shards(
    queries,
    new_keys,
    new_values,
    key_cache,
    value_cache,
    lengths,
    residual_in,
    query_gain,
    key_gain,
    out_proj,
    norm_gain,
    expert_ids,
    gate_weights,
    expert_gate,
    expert_up,
    expert_down,
):
    tensor_pos = lax.axis_index("tensor")
    dp_pos = lax.axis_index("dp")
    tensor = lax.axis_size("tensor")
    dp = lax.axis_size("dp")
    plan = Plan(dp, tensor)
    rows, heads, hd = queries.shape
    kvh = key_cache.shape[1]
    cache_local = key_cache.shape[2]
    share = residual_in.shape[0]
    width = residual_in.shape[1]
    expert_total = dp * tensor

    query_norm = rms_scale(queries.astype(F32), query_gain).astype(BF)
    key_norm = rms_scale(new_keys.astype(F32), key_gain).astype(BF)
    grouped = query_norm.reshape(rows, kvh, heads // kvh, hd)
    scaling = hd ** (-0.5)
    scores = jnp.einsum("rgqd,rgpd->rgqp", grouped, key_cache, preferred_element_type=F32) * scaling
    new_score = jnp.einsum("rgqd,rgd->rgq", grouped, key_norm, preferred_element_type=F32) * scaling
    positions = tensor_pos * cache_local + jnp.arange(cache_local, dtype=jnp.int32)
    included = (positions[None, :] < lengths[:, None])[:, None, None, :]
    top = jnp.maximum(jnp.max(jnp.where(included, scores, -1e30), axis=-1), new_score)
    top = top.astype(BF).astype(F32)
    weights = jnp.where(included, jnp.exp(scores - top[..., None]), 0.0).astype(BF)
    new_weight = jnp.exp(new_score - top).astype(BF).astype(F32)
    own_new = (tensor_pos == 0).astype(F32) * new_weight
    numer = jnp.einsum("rgqp,rgpd->rgqd", weights, value_cache, preferred_element_type=F32)
    numer = numer + own_new[..., None] * new_values.astype(F32)[:, :, None, :]
    denom = jnp.sum(weights.astype(F32), axis=-1) + own_new

    heads_own = heads // tensor
    numer = numer.reshape(rows, heads, hd).astype(BF)
    denom = denom.reshape(rows, heads)
    denom_hi = denom.astype(BF)
    denom_lo = (denom - denom_hi.astype(F32)).astype(BF)
    side = jnp.stack([top.reshape(rows, heads).astype(BF), denom_hi, denom_lo], axis=1)

    def for_device(j):
        first = (tensor_pos ^ j) * heads_own
        body = lax.dynamic_slice_in_dim(numer, first, heads_own, 1).reshape(rows, heads_own * hd)
        extra = lax.dynamic_slice_in_dim(side, first, heads_own, 2).reshape(rows, 3 * heads_own)
        extra = jnp.pad(extra, ((0, 0), (0, 128 - 3 * heads_own)))
        return jnp.concatenate([body, extra], axis=1)

    got = [for_device(0)] + [
        swap(for_device(j), "tensor", tensor, j) for j in range(1, tensor)
    ]
    got = jnp.stack(got).astype(F32)
    body = got[:, :, : heads_own * hd].reshape(tensor, rows, heads_own, hd)
    extra = got[:, :, heads_own * hd : heads_own * (hd + 3)].reshape(tensor, rows, 3, heads_own)
    tops = extra[:, :, 0]
    factor = jnp.exp(tops - jnp.max(tops, axis=0, keepdims=True))
    denom_all = jnp.sum(factor * (extra[:, :, 1] + extra[:, :, 2]), axis=0)
    attn = jnp.sum(body * factor[..., None], axis=0) / denom_all[..., None]
    attn = attn.reshape(rows, heads_own * hd).astype(BF)

    attn = jnp.concatenate(
        [
            lax.dynamic_slice_in_dim(attn, (tensor_pos ^ j) * share, share, 0)
            for j in range(tensor)
        ]
    )
    partial = jnp.dot(attn, out_proj, preferred_element_type=F32)
    projected = partial[:share]
    sent = partial.astype(BF)
    for j in range(1, tensor):
        projected = projected + swap(
            sent[j * share : (j + 1) * share], "tensor", tensor, j
        ).astype(F32)
    hidden = residual_in.astype(F32) + projected
    normed = rms_scale(hidden, norm_gain).astype(BF)

    route = (gate_weights / jnp.sum(gate_weights, axis=1, keepdims=True)).astype(BF)
    named = expert_ids[:, :, None] == jnp.arange(expert_total, dtype=jnp.int32)
    table = jnp.sum(jnp.where(named, route[:, :, None], jnp.zeros((), BF)), axis=1)
    table = jnp.pad(table, ((0, 0), (0, -expert_total % 128)))

    third = (width // 3) // 128 * 128
    cuts = [0, third, 2 * third, width]
    pieces = [normed[:, cuts[i] : cuts[i + 1]] for i in range(3)]
    pieces[0] = jnp.concatenate([pieces[0], table], axis=1)
    orders = ["zxyc", "xyzc", "yzxc"]
    gathered = [
        gather(plan, piece.reshape(1, 1, 1, 1, *piece.shape), order)
        for piece, order in zip(pieces, orders)
    ]
    total_rows = expert_total * share
    flat = [g.reshape(total_rows, g.shape[-1]) for g in gathered]
    every = jnp.concatenate([flat[0][:, :third], flat[1], flat[2]], axis=1)
    own = dp_pos * tensor + tensor_pos
    tables = flat[0][:, third:].astype(F32)
    mine = jnp.sum(
        jnp.where(jnp.arange(tables.shape[1], dtype=jnp.int32) == own, tables, 0.0),
        axis=1,
        keepdims=True,
    )
    gate_val = jnp.dot(every, expert_gate[0], preferred_element_type=F32)
    up_val = jnp.dot(every, expert_up[0], preferred_element_type=F32)
    activation = (jax.nn.silu(gate_val) * up_val).astype(BF)
    result = jnp.dot(activation, expert_down[0], preferred_element_type=F32)
    result = jnp.where(mine == 0.0, 0.0, result * mine)
    result = result.reshape(*[plan.length(n) for n in NAMES], share, width)
    first = reduce_slots(plan, result, "c")
    outs = []
    for i, order in enumerate(["yxz", "zyx", "xzy"]):
        outs.append(reduce_slots(plan, first[..., cuts[i] : cuts[i + 1]], order))
    moe_sum = jnp.concatenate(outs, axis=-1).reshape(share, width)
    return (hidden + moe_sum).astype(BF)


def solution(mesh):
    return jax.shard_map(
        shards,
        mesh=mesh,
        in_specs=(
            P("dp", None, None),
            P("dp", None, None),
            P("dp", None, None),
            P("dp", None, "tensor", None),
            P("dp", None, "tensor", None),
            P("dp"),
            P(("dp", "tensor"), None),
            P(),
            P(),
            P("tensor", None),
            P(),
            P(("dp", "tensor"), None),
            P(("dp", "tensor"), None),
            P(("dp", "tensor"), None, None),
            P(("dp", "tensor"), None, None),
            P(("dp", "tensor"), None, None),
        ),
        out_specs=P(("dp", "tensor"), None),
        check_vma=False,
    )
```

time: 173 us -> 119 us (0.69)
  blocking collectives: 49.2 us -> 0 us
  starting transfers between devices: 3.66 us -> 43.7 us
  waiting for transfers between devices: 70.6 us -> 36.9 us
  between operations: 14.3 us -> 0.59 us
  other arithmetic: 7.72 us -> 10.5 us
    ppermute x0 -> x40, starting transfers between devices: none -> 43.7 us  [swap(): return lax.ppermute(x, axis, [(i, i ^ flip) for i in range(size)])]
    ppermute x0 -> x40, waiting for transfers between devices: none -> 36.9 us  [swap(): return lax.ppermute(x, axis, [(i, i ^ flip) for i in range(size)])]
    psum x1 -> x0, waiting for transfers between devices: 32 us -> none  [shards(): lax.psum(partial_sum.astype(jnp.bfloat16), 'tensor').astype(jnp.float32)]
    all_to_all x1 -> x0, blocking collectives: 30.6 us -> none  [shards(): lax.all_to_all(outgoing, ('dp', 'tensor'), split_axis=0, concat_axis=0, t...]
    all_to_all x1 -> x0, waiting for transfers between devices: 25.9 us -> none  [shards(): lax.all_to_all(computed, ('dp', 'tensor'), split_axis=0, concat_axis=0, t...]
    pmax x1 -> x0, blocking collectives: 12.7 us -> none  [shards(): score_top = lax.pmax(local_top, 'tensor')]
    reduce_scatter x1 -> x0, waiting for transfers between devices: 12.6 us -> none  [shards(): lax.psum_scatter(numerator.reshape(row_total, head_total * head_dim).asty...]
    unnamed x1 -> x0, blocking collectives: 5.9 us -> none
  transfers between devices with their start and end apart: 3 -> 40, of which waited for: 3 -> 21; matrix products, arithmetic and copies ran while one was open for 1% -> 1% of each run, Pallas kernels for 0% -> 0%
where the time goes in v1:
time: 119 us
  starting transfers between devices  43.7 us (37%)
  waiting for transfers between devices  36.9 us (31%)
  matrix products  23 us (19%)
  other arithmetic  10.5 us (9%)
  local copies, waits for them, and re-layouts  4.19 us (4%)
    ppermute x40, starting transfers between devices, swap(): return lax.ppermute(x, axis, [(i, i ^ flip) for i in range(size)])  43.7 us
    ppermute x40, waiting for transfers between devices, swap(): return lax.ppermute(x, axis, [(i, i ^ flip) for i in range(size)])  36.9 us
    dot_general x1, matrix products, shards(): result = jnp.dot(activation, expert_down[0], preferred_element_type=F32)  11.3 us
    dot_general x1, matrix products, shards(): partial = jnp.dot(attn, out_proj, preferred_element_type=F32)  4.97 us
    dot_general x1, matrix products, shards(): gate_val = jnp.dot(every, expert_gate[0], preferred_element_type=F32)  4.57 us
  transfers between devices with their start and end apart: 40, of which 21 were waited for; matrix products, arithmetic and copies ran while one was open for 1% of the time, Pallas kernels for 0%

profile of v1, /device:TPU:0, one launch (start us, length us, event | category | flops | bytes accessed | tf_op | source)
XLA Modules:
  0.0 119.0 jit_solution(1916911643724188067)
XLA Ops:
  9.6 2.6 %collective-permute-start.1 = (bf16[32,1152]{1,0:T(8,128)(2,1)S(1)}, bf16[32,1152]{1,0:T(8,128)(2,1)S(1)}, u32[]{:S(2)}, u32[]{:S(2)}) collective-permute-start(bf16[32,1152]{1,0:T(8,128)(2,1)S(1)} %fusion.43), channel_id=1, source_target_pairs={{0,2},{1,3},{2,0},{3,1},{4,6},{5,7},{6,4},{7,5},{8,10},{9,11},{10,... | collective-permute-start | bytes 221192 | tf_op jit(solution)/shard_map/ppermute | solution.py:16
  12.9 2.2 %collective-permute-done.1 = bf16[32,1152]{1,0:T(8,128)(2,1)S(1)} collective-permute-done((bf16[32,1152]{1,0:T(8,128)(2,1)S(1)}, bf16[32,1152]{1,0:T(8,128)(2,1)S(1)}, u32[]{:S(2)}, u32[]{:S(2)}) %collective-permute-start.1) | collective-permute-done | bytes 73760 | tf_op jit(solution)/shard_map/ppermute | solution.py:16
  18.6 5.0 %fusion.87 = (bf16[32,4096]{1,0:T(8,128)(2,1)S(1)}, f32[32,4096]{1,0:T(8,128)S(1)}) fusion(bf16[1024,4096]{1,0:T(8,128)(2,1)} %param.25, bf16[8,1024]{1,0:T(8,128)(2,1)S(1)} %copy.88, bf16[8,1024]{1,0:T(8,128)(2,1)S(1)} %copy.87, bf16[8,1024]{1,0:T(8,128)(2,1)S(1)} %copy.86, bf16[8,1024]{1,0:T(8,128)(2,1)S(1)} %copy.85), kind=kOutput, calls=%fused_computation.159 | convolution fusion | flops 268828672 | bytes 9240576 | tf_op jit(solution)/shard_map/dot_general | solution.py:141
  25.8 1.9 %collective-permute-done.5 = bf16[8,4096]{1,0:T(8,128)(2,1)S(1)} collective-permute-done((bf16[8,4096]{1,0:T(8,128)(2,1)S(1)}, bf16[8,4096]{1,0:T(8,128)(2,1)S(1)}, u32[]{:S(2)}, u32[]{:S(2)}) %collective-permute-start.5) | collective-permute-done | bytes 65568 | tf_op jit(solution)/shard_map/ppermute | solution.py:16
  27.7 1.9 %collective-permute-done.4 = bf16[8,4096]{1,0:T(8,128)(2,1)S(1)} collective-permute-done((bf16[8,4096]{1,0:T(8,128)(2,1)S(1)}, bf16[8,4096]{1,0:T(8,128)(2,1)S(1)}, u32[]{:S(2)}, u32[]{:S(2)}) %collective-permute-start.4) | collective-permute-done | bytes 65568 | tf_op jit(solution)/shard_map/ppermute | solution.py:16
  31.5 3.6 %collective-permute-start.8 = (bf16[1,1,1,1,8,1408]{5,4,3,2,1,0:T(8,128)(2,1)S(1)}, bf16[1,1,1,1,8,1408]{5,4,3,2,1,0:T(8,128)(2,1)S(1)}, u32[]{:S(2)}, u32[]{:S(2)}) collective-permute-start(bf16[1,1,1,1,8,1408]{5,4,3,2,1,0:T(8,128)(2,1)S(1)} %fusion.63), channel_id=1, source_target_pairs={{0,24},{4,28},{8,16},{12,20},{16,8},{20,12},{24,0},{28,4},{1,25},{... | collective-permute-start | bytes 67592 | tf_op jit(solution)/shard_map/ppermute | solution.py:16
  40.4 2.9 %collective-permute-start.21 = (bf16[1,1,2,1,8,1536]{5,4,3,2,1,0:T(8,128)(2,1)S(1)}, bf16[1,1,2,1,8,1536]{5,4,3,2,1,0:T(8,128)(2,1)S(1)}, u32[]{:S(2)}, u32[]{:S(2)}) collective-permute-start(bf16[1,1,2,1,8,1536]{5,4,3,2,1,0:T(8,128)(2,1)S(1)} %pad_maximum_fusion.16), channel_id=1, source_target_pairs={{0,24},{4,28},{8,16},{12,20},{16,8},{20,12},{24,0},{28,4},{1,25},{... | collective-permute-start | bytes 147464 | tf_op jit(solution)/shard_map/ppermute | solution.py:16
  44.9 2.9 %collective-permute-start.16 = (bf16[1,2,2,1,8,1280]{5,4,3,2,1,0:T(8,128)(2,1)S(1)}, bf16[1,2,2,1,8,1280]{5,4,3,2,1,0:T(8,128)(2,1)S(1)}, u32[]{:S(2)}, u32[]{:S(2)}) collective-permute-start(bf16[1,2,2,1,8,1280]{5,4,3,2,1,0:T(8,128)(2,1)S(1)} %pad_maximum_fusion.15), channel_id=1, source_target_pairs={{0,24},{4,28},{8,16},{12,20},{16,8},{20,12},{24,0},{28,4},{1,25},{... | collective-permute-start | bytes 245768 | tf_op jit(solution)/shard_map/ppermute | solution.py:16
  47.8 2.0 %collective-permute-done.20 = bf16[1,1,2,1,8,1536]{5,4,3,2,1,0:T(8,128)(2,1)S(1)} collective-permute-done((bf16[1,1,2,1,8,1536]{5,4,3,2,1,0:T(8,128)(2,1)S(1)}, bf16[1,1,2,1,8,1536]{5,4,3,2,1,0:T(8,128)(2,1)S(1)}, u32[]{:S(2)}, u32[]{:S(2)}) %collective-permute-start.20) | collective-permute-done | bytes 49184 | tf_op jit(solution)/shard_map/ppermute | solution.py:16
  54.7 2.2 %collective-permute-done.10 = bf16[4,2,1,1,8,1408]{5,4,3,2,1,0:T(8,128)(2,1)S(1)} collective-permute-done((bf16[4,2,1,1,8,1408]{5,4,3,2,1,0:T(8,128)(2,1)S(1)}, bf16[4,2,1,1,8,1408]{5,4,3,2,1,0:T(8,128)(2,1)S(1)}, u32[]{:S(2)}, u32[]{:S(2)}) %collective-permute-start.10) | collective-permute-done | bytes 180256 | tf_op jit(solution)/shard_map/ppermute | solution.py:16
  59.3 4.6 %fusion.4 = f32[256,768]{1,0:T(8,128)S(1)} fusion(bf16[1,4096,768]{2,1,0:T(8,128)(2,1)} %param.29, bf16[256,1536]{1,0:T(8,128)(2,1)S(1)} %bitcast.118, bf16[256,1280]{1,0:T(8,128)(2,1)S(1)} %bitcast.120, bf16[256,1280]{1,0:T(8,128)(2,1)S(1)} %slice.198), kind=kOutput, calls=%fused_computation.4 | convolution fusion | flops 1616904192 | bytes 9175040 | tf_op jit(solution)/shard_map/dot_general | solution.py:175
  63.9 11.3 %fusion.9 = f32[256,4096]{1,0:T(8,128)} fusion(bf16[1,768,4096]{2,1,0:T(8,128)(2,1)} %param.31, f32[256]{0:T(256)S(1)} %select_reduce_fusion.1, pred[256]{0:T(512)(128)(4,1)S(1)} %broadcast_compare_fusion.1, bf16[1,4096,768]{2,1,0:T(8,128)(2,1)} %param.30, bf16[256,1536]{1,0:T(8,128)(2,1)S(1)} %bitcast.119, bf16[256,1280]{1,0:T(8,128)(2,1)S(1)} %bitcast.121, ...), kind=kOutput, calls=%fused_computation.7 | convolution fusion | flops 3230793728 | bytes 19662080 | tf_op jit(solution)/shard_map/dot_general | solution.py:178
  77.2 2.5 %collective-permute-done.24 = bf16[4,2,2,1,8,4096]{5,4,3,2,1,0:T(8,128)(2,1)S(1)} collective-permute-done((bf16[4,2,2,1,8,4096]{5,4,3,2,1,0:T(8,128)(2,1)S(1)}, bf16[4,2,2,1,8,4096]{5,4,3,2,1,0:T(8,128)(2,1)S(1)}, u32[]{:S(2)}, u32[]{:S(2)}) %collective-permute-start.24) | collective-permute-done | bytes 1048608 | tf_op jit(solution)/shard_map/ppermute | solution.py:16
  79.7 1.9 %fusion.79 = (bf16[4,2,2,1,8,4096]{5,4,3,2,1,0:T(8,128)(2,1)S(1)}, f32[4,2,2,1,8,4096]{5,4,3,2,1,0:T(8,128)S(1)}) fusion(bf16[4,2,2,1,8,4096]{5,4,3,2,1,0:T(8,128)(2,1)S(1)} %collective-permute-done.24, f32[4,2,2,2,8,4096]{5,4,3,2,1,0:T(8,128)} %bitcast.115), kind=kLoop, calls=%fused_computation.153 | loop fusion | flops 1572864 | bytes 6291456 | tf_op jit(solution)/shard_map/convert.15
  81.7 2.1 %collective-permute-start.30 = (bf16[1,2,2,1,8,1280]{5,4,3,2,1,0:T(8,128)(2,1)S(1)}, bf16[1,2,2,1,8,1280]{5,4,3,2,1,0:T(8,128)(2,1)S(1)}, u32[]{:S(2)}, u32[]{:S(2)}) collective-permute-start(bf16[1,2,2,1,8,1280]{5,4,3,2,1,0:T(8,128)(2,1)S(1)} %get-tuple-element.19), channel_id=1, source_target_pairs={{0,8},{4,12},{8,0},{12,4},{16,24},{20,28},{24,16},{28,20},{1,9},{5... | collective-permute-start | bytes 245768 | tf_op jit(solution)/shard_map/ppermute | solution.py:16
  83.8 1.9 %collective-permute-start.32 = (bf16[1,2,2,1,8,1280]{5,4,3,2,1,0:T(8,128)(2,1)S(1)}, bf16[1,2,2,1,8,1280]{5,4,3,2,1,0:T(8,128)(2,1)S(1)}, u32[]{:S(2)}, u32[]{:S(2)}) collective-permute-start(bf16[1,2,2,1,8,1280]{5,4,3,2,1,0:T(8,128)(2,1)S(1)} %get-tuple-element.20), channel_id=1, source_target_pairs={{0,24},{4,28},{8,16},{12,20},{16,8},{20,12},{24,0},{28,4},{1,25},{... | collective-permute-start | bytes 245768 | tf_op jit(solution)/shard_map/ppermute | solution.py:16
  86.5 4.4 %collective-permute-done.32 = bf16[1,2,2,1,8,1280]{5,4,3,2,1,0:T(8,128)(2,1)S(1)} collective-permute-done((bf16[1,2,2,1,8,1280]{5,4,3,2,1,0:T(8,128)(2,1)S(1)}, bf16[1,2,2,1,8,1280]{5,4,3,2,1,0:T(8,128)(2,1)S(1)}, u32[]{:S(2)}, u32[]{:S(2)}) %collective-permute-start.32) | collective-permute-done | bytes 81952 | tf_op jit(solution)/shard_map/ppermute | solution.py:16
  90.9 2.5 %collective-permute-done.31 = bf16[1,2,2,1,8,1280]{5,4,3,2,1,0:T(8,128)(2,1)S(1)} collective-permute-done((bf16[1,2,2,1,8,1280]{5,4,3,2,1,0:T(8,128)(2,1)S(1)}, bf16[1,2,2,1,8,1280]{5,4,3,2,1,0:T(8,128)(2,1)S(1)}, u32[]{:S(2)}, u32[]{:S(2)}) %collective-permute-start.31) | collective-permute-done | bytes 81952 | tf_op jit(solution)/shard_map/ppermute | solution.py:16
  95.1 2.4 %collective-permute-done.33 = bf16[1,2,1,1,8,1280]{5,4,3,2,1,0:T(8,128)(2,1)S(1)} collective-permute-done((bf16[1,2,1,1,8,1280]{5,4,3,2,1,0:T(8,128)(2,1)S(1)}, bf16[1,2,1,1,8,1280]{5,4,3,2,1,0:T(8,128)(2,1)S(1)}, u32[]{:S(2)}, u32[]{:S(2)}) %collective-permute-start.33) | collective-permute-done | bytes 40992 | tf_op jit(solution)/shard_map/ppermute | solution.py:16
  101.5 2.8 %collective-permute-done.25 = bf16[4,2,1,1,8,1280]{5,4,3,2,1,0:T(8,128)(2,1)S(1)} collective-permute-done((bf16[4,2,1,1,8,1280]{5,4,3,2,1,0:T(8,128)(2,1)S(1)}, bf16[4,2,1,1,8,1280]{5,4,3,2,1,0:T(8,128)(2,1)S(1)}, u32[]{:S(2)}, u32[]{:S(2)}) %collective-permute-start.25) | collective-permute-done | bytes 163872 | tf_op jit(solution)/shard_map/ppermute | solution.py:16
  105.2 1.8 %collective-permute-done.35 = bf16[4,1,2,1,8,1536]{5,4,3,2,1,0:T(8,128)(2,1)S(1)} collective-permute-done((bf16[4,1,2,1,8,1536]{5,4,3,2,1,0:T(8,128)(2,1)S(1)}, bf16[4,1,2,1,8,1536]{5,4,3,2,1,0:T(8,128)(2,1)S(1)}, u32[]{:S(2)}, u32[]{:S(2)}) %collective-permute-start.35) | collective-permute-done | bytes 196640 | tf_op jit(solution)/shard_map/ppermute | solution.py:16
  107.2 1.9 %collective-permute-start.38 = (bf16[1,1,2,1,8,1536]{5,4,3,2,1,0:T(8,128)(2,1)S(1)}, bf16[1,1,2,1,8,1536]{5,4,3,2,1,0:T(8,128)(2,1)S(1)}, u32[]{:S(2)}, u32[]{:S(2)}) collective-permute-start(bf16[1,1,2,1,8,1536]{5,4,3,2,1,0:T(8,128)(2,1)S(1)} %get-tuple-element.34), channel_id=1, source_target_pairs={{0,24},{4,28},{8,16},{12,20},{16,8},{20,12},{24,0},{28,4},{1,25},{... | collective-permute-start | bytes 147464 | tf_op jit(solution)/shard_map/ppermute | solution.py:16
  111.8 1.9 %collective-permute-start.29 = (bf16[1,1,1,1,8,1280]{5,4,3,2,1,0:T(8,128)(2,1)S(1)}, bf16[1,1,1,1,8,1280]{5,4,3,2,1,0:T(8,128)(2,1)S(1)}, u32[]{:S(2)}, u32[]{:S(2)}) collective-permute-start(bf16[1,1,1,1,8,1280]{5,4,3,2,1,0:T(8,128)(2,1)S(1)} %get-tuple-element.37), channel_id=1, source_target_pairs={{0,24},{4,28},{8,16},{12,20},{16,8},{20,12},{24,0},{28,4},{1,25},{... | collective-permute-start | bytes 61448 | tf_op jit(solution)/shard_map/ppermute | solution.py:16
  115.4 1.9 %collective-permute-done.29 = bf16[1,1,1,1,8,1280]{5,4,3,2,1,0:T(8,128)(2,1)S(1)} collective-permute-done((bf16[1,1,1,1,8,1280]{5,4,3,2,1,0:T(8,128)(2,1)S(1)}, bf16[1,1,1,1,8,1280]{5,4,3,2,1,0:T(8,128)(2,1)S(1)}, u32[]{:S(2)}, u32[]{:S(2)}) %collective-permute-start.29) | collective-permute-done | bytes 20512 | tf_op jit(solution)/shard_map/ppermute | solution.py:16
  (165 shorter events, 47.2 us)
Async XLA Ops:
  9.6 5.5 %collective-permute-start.1 = (bf16[32,1152]{1,0:T(8,128)(2,1)S(1)}, bf16[32,1152]{1,0:T(8,128)(2,1)S(1)}, u32[]{:S(2)}, u32[]{:S(2)}) collective-permute-start(bf16[32,1152]{1,0:T(8,128)(2,1)S(1)} %fusion.43), channel_id=1, source_target_pairs={{0,2},{1,3},{2,0},{3,1},{4,6},{5,7},{6,4},{7,5},{8,10},{9,11},{10,... | collective-permute-start | bytes 221192 | tf_op jit(solution)/shard_map/ppermute | solution.py:16
  29.9 7.4 %collective-permute-start.12 = (bf16[1,1,1,1,8,1280]{5,4,3,2,1,0:T(8,128)(2,1)S(1)}, bf16[1,1,1,1,8,1280]{5,4,3,2,1,0:T(8,128)(2,1)S(1)}, u32[]{:S(2)}, u32[]{:S(2)}) collective-permute-start(bf16[1,1,1,1,8,1280]{5,4,3,2,1,0:T(8,128)(2,1)S(1)} %get-tuple-element.39), channel_id=1, source_target_pairs={{0,4},{4,0},{8,12},{12,8},{16,20},{20,16},{24,28},{28,24},{1,5},{5... | collective-permute-start | bytes 61448 | tf_op jit(solution)/shard_map/ppermute | solution.py:16
  31.5 6.5 %collective-permute-start.8 = (bf16[1,1,1,1,8,1408]{5,4,3,2,1,0:T(8,128)(2,1)S(1)}, bf16[1,1,1,1,8,1408]{5,4,3,2,1,0:T(8,128)(2,1)S(1)}, u32[]{:S(2)}, u32[]{:S(2)}) collective-permute-start(bf16[1,1,1,1,8,1408]{5,4,3,2,1,0:T(8,128)(2,1)S(1)} %fusion.63), channel_id=1, source_target_pairs={{0,24},{4,28},{8,16},{12,20},{16,8},{20,12},{24,0},{28,4},{1,25},{... | collective-permute-start | bytes 67592 | tf_op jit(solution)/shard_map/ppermute | solution.py:16
  35.1 4.7 %collective-permute-start.7 = (bf16[1,1,1,1,8,1408]{5,4,3,2,1,0:T(8,128)(2,1)S(1)}, bf16[1,1,1,1,8,1408]{5,4,3,2,1,0:T(8,128)(2,1)S(1)}, u32[]{:S(2)}, u32[]{:S(2)}) collective-permute-start(bf16[1,1,1,1,8,1408]{5,4,3,2,1,0:T(8,128)(2,1)S(1)} %fusion.63), channel_id=1, source_target_pairs={{0,16},{4,20},{8,24},{12,28},{16,0},{20,4},{24,8},{28,12},{1,17},{... | collective-permute-start | bytes 67592 | tf_op jit(solution)/shard_map/ppermute | solution.py:16
  37.3 7.5 %collective-permute-start.13 = (bf16[1,2,1,1,8,1280]{5,4,3,2,1,0:T(8,128)(2,1)S(1)}, bf16[1,2,1,1,8,1280]{5,4,3,2,1,0:T(8,128)(2,1)S(1)}, u32[]{:S(2)}, u32[]{:S(2)}) collective-permute-start(bf16[1,2,1,1,8,1280]{5,4,3,2,1,0:T(8,128)(2,1)S(1)} %pad_maximum_fusion.17), channel_id=1, source_target_pairs={{0,2},{1,3},{2,0},{3,1},{4,6},{5,7},{6,4},{7,5},{8,10},{9,11},{10,... | collective-permute-start | bytes 122888 | tf_op jit(solution)/shard_map/ppermute | solution.py:16
  39.8 11.5 %collective-permute-start.9 = (bf16[4,1,1,1,8,1408]{5,4,3,2,1,0:T(8,128)(2,1)S(1)}, bf16[4,1,1,1,8,1408]{5,4,3,2,1,0:T(8,128)(2,1)S(1)}, u32[]{:S(2)}, u32[]{:S(2)}) collective-permute-start(bf16[4,1,1,1,8,1408]{5,4,3,2,1,0:T(8,128)(2,1)S(1)} %pad_maximum_fusion.14), channel_id=1, source_target_pairs={{0,4},{4,0},{8,12},{12,8},{16,20},{20,16},{24,28},{28,24},{1,5},{5... | collective-permute-start | bytes 270344 | tf_op jit(solution)/shard_map/ppermute | solution.py:16
  40.4 7.4 %collective-permute-start.21 = (bf16[1,1,2,1,8,1536]{5,4,3,2,1,0:T(8,128)(2,1)S(1)}, bf16[1,1,2,1,8,1536]{5,4,3,2,1,0:T(8,128)(2,1)S(1)}, u32[]{:S(2)}, u32[]{:S(2)}) collective-permute-start(bf16[1,1,2,1,8,1536]{5,4,3,2,1,0:T(8,128)(2,1)S(1)} %pad_maximum_fusion.16), channel_id=1, source_target_pairs={{0,24},{4,28},{8,16},{12,20},{16,8},{20,12},{24,0},{28,4},{1,25},{... | collective-permute-start | bytes 147464 | tf_op jit(solution)/shard_map/ppermute | solution.py:16
  43.3 6.5 %collective-permute-start.20 = (bf16[1,1,2,1,8,1536]{5,4,3,2,1,0:T(8,128)(2,1)S(1)}, bf16[1,1,2,1,8,1536]{5,4,3,2,1,0:T(8,128)(2,1)S(1)}, u32[]{:S(2)}, u32[]{:S(2)}) collective-permute-start(bf16[1,1,2,1,8,1536]{5,4,3,2,1,0:T(8,128)(2,1)S(1)} %pad_maximum_fusion.16), channel_id=1, source_target_pairs={{0,16},{4,20},{8,24},{12,28},{16,0},{20,4},{24,8},{28,12},{1,17},{... | collective-permute-start | bytes 147464 | tf_op jit(solution)/shard_map/ppermute | solution.py:16
  43.3 6.9 %collective-permute-start.19 = (bf16[1,1,2,1,8,1536]{5,4,3,2,1,0:T(8,128)(2,1)S(1)}, bf16[1,1,2,1,8,1536]{5,4,3,2,1,0:T(8,128)(2,1)S(1)}, u32[]{:S(2)}, u32[]{:S(2)}) collective-permute-start(bf16[1,1,2,1,8,1536]{5,4,3,2,1,0:T(8,128)(2,1)S(1)} %pad_maximum_fusion.16), channel_id=1, source_target_pairs={{0,8},{4,12},{8,0},{12,4},{16,24},{20,28},{24,16},{28,20},{1,9},{5... | collective-permute-start | bytes 147464 | tf_op jit(solution)/shard_map/ppermute | solution.py:16
  44.9 8.0 %collective-permute-start.16 = (bf16[1,2,2,1,8,1280]{5,4,3,2,1,0:T(8,128)(2,1)S(1)}, bf16[1,2,2,1,8,1280]{5,4,3,2,1,0:T(8,128)(2,1)S(1)}, u32[]{:S(2)}, u32[]{:S(2)}) collective-permute-start(bf16[1,2,2,1,8,1280]{5,4,3,2,1,0:T(8,128)(2,1)S(1)} %pad_maximum_fusion.15), channel_id=1, source_target_pairs={{0,24},{4,28},{8,16},{12,20},{16,8},{20,12},{24,0},{28,4},{1,25},{... | collective-permute-start | bytes 245768 | tf_op jit(solution)/shard_map/ppermute | solution.py:16
  47.8 5.9 %collective-permute-start.15 = (bf16[1,2,2,1,8,1280]{5,4,3,2,1,0:T(8,128)(2,1)S(1)}, bf16[1,2,2,1,8,1280]{5,4,3,2,1,0:T(8,128)(2,1)S(1)}, u32[]{:S(2)}, u32[]{:S(2)}) collective-permute-start(bf16[1,2,2,1,8,1280]{5,4,3,2,1,0:T(8,128)(2,1)S(1)} %pad_maximum_fusion.15), channel_id=1, source_target_pairs={{0,16},{4,20},{8,24},{12,28},{16,0},{20,4},{24,8},{28,12},{1,17},{... | collective-permute-start | bytes 245768 | tf_op jit(solution)/shard_map/ppermute | solution.py:16
  49.8 4.7 %collective-permute-start.14 = (bf16[1,2,2,1,8,1280]{5,4,3,2,1,0:T(8,128)(2,1)S(1)}, bf16[1,2,2,1,8,1280]{5,4,3,2,1,0:T(8,128)(2,1)S(1)}, u32[]{:S(2)}, u32[]{:S(2)}) collective-permute-start(bf16[1,2,2,1,8,1280]{5,4,3,2,1,0:T(8,128)(2,1)S(1)} %pad_maximum_fusion.15), channel_id=1, source_target_pairs={{0,8},{4,12},{8,0},{12,4},{16,24},{20,28},{24,16},{28,20},{1,9},{5... | collective-permute-start | bytes 245768 | tf_op jit(solution)/shard_map/ppermute | solution.py:16
  50.3 6.8 %collective-permute-start.22 = (bf16[4,1,2,1,8,1536]{5,4,3,2,1,0:T(8,128)(2,1)S(1)}, bf16[4,1,2,1,8,1536]{5,4,3,2,1,0:T(8,128)(2,1)S(1)}, u32[]{:S(2)}, u32[]{:S(2)}) collective-permute-start(bf16[4,1,2,1,8,1536]{5,4,3,2,1,0:T(8,128)(2,1)S(1)} %pad_maximum_fusion.12), channel_id=1, source_target_pairs={{0,4},{4,0},{8,12},{12,8},{16,20},{20,16},{24,28},{28,24},{1,5},{5... | collective-permute-start | bytes 589832 | tf_op jit(solution)/shard_map/ppermute | solution.py:16
  51.3 5.6 %collective-permute-start.10 = (bf16[4,2,1,1,8,1408]{5,4,3,2,1,0:T(8,128)(2,1)S(1)}, bf16[4,2,1,1,8,1408]{5,4,3,2,1,0:T(8,128)(2,1)S(1)}, u32[]{:S(2)}, u32[]{:S(2)}) collective-permute-start(bf16[4,2,1,1,8,1408]{5,4,3,2,1,0:T(8,128)(2,1)S(1)} %pad_maximum_fusion.13), channel_id=1, source_target_pairs={{0,2},{1,3},{2,0},{3,1},{4,6},{5,7},{6,4},{7,5},{8,10},{9,11},{10,... | collective-permute-start | bytes 540680 | tf_op jit(solution)/shard_map/ppermute | solution.py:16
  81.7 4.8 %collective-permute-start.30 = (bf16[1,2,2,1,8,1280]{5,4,3,2,1,0:T(8,128)(2,1)S(1)}, bf16[1,2,2,1,8,1280]{5,4,3,2,1,0:T(8,128)(2,1)S(1)}, u32[]{:S(2)}, u32[]{:S(2)}) collective-permute-start(bf16[1,2,2,1,8,1280]{5,4,3,2,1,0:T(8,128)(2,1)S(1)} %get-tuple-element.19), channel_id=1, source_target_pairs={{0,8},{4,12},{8,0},{12,4},{16,24},{20,28},{24,16},{28,20},{1,9},{5... | collective-permute-start | bytes 245768 | tf_op jit(solution)/shard_map/ppermute | solution.py:16
  83.8 7.1 %collective-permute-start.32 = (bf16[1,2,2,1,8,1280]{5,4,3,2,1,0:T(8,128)(2,1)S(1)}, bf16[1,2,2,1,8,1280]{5,4,3,2,1,0:T(8,128)(2,1)S(1)}, u32[]{:S(2)}, u32[]{:S(2)}) collective-permute-start(bf16[1,2,2,1,8,1280]{5,4,3,2,1,0:T(8,128)(2,1)S(1)} %get-tuple-element.20), channel_id=1, source_target_pairs={{0,24},{4,28},{8,16},{12,20},{16,8},{20,12},{24,0},{28,4},{1,25},{... | collective-permute-start | bytes 245768 | tf_op jit(solution)/shard_map/ppermute | solution.py:16
  85.7 7.7 %collective-permute-start.31 = (bf16[1,2,2,1,8,1280]{5,4,3,2,1,0:T(8,128)(2,1)S(1)}, bf16[1,2,2,1,8,1280]{5,4,3,2,1,0:T(8,128)(2,1)S(1)}, u32[]{:S(2)}, u32[]{:S(2)}) collective-permute-start(bf16[1,2,2,1,8,1280]{5,4,3,2,1,0:T(8,128)(2,1)S(1)} %get-tuple-element.21), channel_id=1, source_target_pairs={{0,16},{4,20},{8,24},{12,28},{16,0},{20,4},{24,8},{28,12},{1,17},{... | collective-permute-start | bytes 245768 | tf_op jit(solution)/shard_map/ppermute | solution.py:16
  98.9 5.4 %collective-permute-start.25 = (bf16[4,2,1,1,8,1280]{5,4,3,2,1,0:T(8,128)(2,1)S(1)}, bf16[4,2,1,1,8,1280]{5,4,3,2,1,0:T(8,128)(2,1)S(1)}, u32[]{:S(2)}, u32[]{:S(2)}) collective-permute-start(bf16[4,2,1,1,8,1280]{5,4,3,2,1,0:T(8,128)(2,1)S(1)} %slice.204), channel_id=1, source_target_pairs={{0,2},{1,3},{2,0},{3,1},{4,6},{5,7},{6,4},{7,5},{8,10},{9,11},{10,... | collective-permute-start | bytes 491528 | tf_op jit(solution)/shard_map/ppermute | solution.py:16
  100.5 6.5 %collective-permute-start.35 = (bf16[4,1,2,1,8,1536]{5,4,3,2,1,0:T(8,128)(2,1)S(1)}, bf16[4,1,2,1,8,1536]{5,4,3,2,1,0:T(8,128)(2,1)S(1)}, u32[]{:S(2)}, u32[]{:S(2)}) collective-permute-start(bf16[4,1,2,1,8,1536]{5,4,3,2,1,0:T(8,128)(2,1)S(1)} %slice.220), channel_id=1, source_target_pairs={{0,4},{4,0},{8,12},{12,8},{16,20},{20,16},{24,28},{28,24},{1,5},{5... | collective-permute-start | bytes 589832 | tf_op jit(solution)/shard_map/ppermute | solution.py:16
  104.4 6.3 %collective-permute-start.26 = (bf16[4,1,1,1,8,1280]{5,4,3,2,1,0:T(8,128)(2,1)S(1)}, bf16[4,1,1,1,8,1280]{5,4,3,2,1,0:T(8,128)(2,1)S(1)}, u32[]{:S(2)}, u32[]{:S(2)}) collective-permute-start(bf16[4,1,1,1,8,1280]{5,4,3,2,1,0:T(8,128)(2,1)S(1)} %slice.279), channel_id=1, source_target_pairs={{0,4},{4,0},{8,12},{12,8},{16,20},{20,16},{24,28},{28,24},{1,5},{5... | collective-permute-start | bytes 245768 | tf_op jit(solution)/shard_map/ppermute | solution.py:16
  107.1 6.5 %collective-permute-start.36 = (bf16[1,1,2,1,8,1536]{5,4,3,2,1,0:T(8,128)(2,1)S(1)}, bf16[1,1,2,1,8,1536]{5,4,3,2,1,0:T(8,128)(2,1)S(1)}, u32[]{:S(2)}, u32[]{:S(2)}) collective-permute-start(bf16[1,1,2,1,8,1536]{5,4,3,2,1,0:T(8,128)(2,1)S(1)} %get-tuple-element.33), channel_id=1, source_target_pairs={{0,8},{4,12},{8,0},{12,4},{16,24},{20,28},{24,16},{28,20},{1,9},{5... | collective-permute-start | bytes 147464 | tf_op jit(solution)/shard_map/ppermute | solution.py:16
  107.2 7.1 %collective-permute-start.38 = (bf16[1,1,2,1,8,1536]{5,4,3,2,1,0:T(8,128)(2,1)S(1)}, bf16[1,1,2,1,8,1536]{5,4,3,2,1,0:T(8,128)(2,1)S(1)}, u32[]{:S(2)}, u32[]{:S(2)}) collective-permute-start(bf16[1,1,2,1,8,1536]{5,4,3,2,1,0:T(8,128)(2,1)S(1)} %get-tuple-element.34), channel_id=1, source_target_pairs={{0,24},{4,28},{8,16},{12,20},{16,8},{20,12},{24,0},{28,4},{1,25},{... | collective-permute-start | bytes 147464 | tf_op jit(solution)/shard_map/ppermute | solution.py:16
  109.1 5.2 %collective-permute-start.37 = (bf16[1,1,2,1,8,1536]{5,4,3,2,1,0:T(8,128)(2,1)S(1)}, bf16[1,1,2,1,8,1536]{5,4,3,2,1,0:T(8,128)(2,1)S(1)}, u32[]{:S(2)}, u32[]{:S(2)}) collective-permute-start(bf16[1,1,2,1,8,1536]{5,4,3,2,1,0:T(8,128)(2,1)S(1)} %get-tuple-element.35), channel_id=1, source_target_pairs={{0,16},{4,20},{8,24},{12,28},{16,0},{20,4},{24,8},{28,12},{1,17},{... | collective-permute-start | bytes 147464 | tf_op jit(solution)/shard_map/ppermute | solution.py:16
  111.8 5.6 %collective-permute-start.29 = (bf16[1,1,1,1,8,1280]{5,4,3,2,1,0:T(8,128)(2,1)S(1)}, bf16[1,1,1,1,8,1280]{5,4,3,2,1,0:T(8,128)(2,1)S(1)}, u32[]{:S(2)}, u32[]{:S(2)}) collective-permute-start(bf16[1,1,1,1,8,1280]{5,4,3,2,1,0:T(8,128)(2,1)S(1)} %get-tuple-element.37), channel_id=1, source_target_pairs={{0,24},{4,28},{8,16},{12,20},{16,8},{20,12},{24,0},{28,4},{1,25},{... | collective-permute-start | bytes 61448 | tf_op jit(solution)/shard_map/ppermute | solution.py:16
  (21 other events, 105.5 us)

commit v2 on v1

v2 whole, which is shorter than its diff:
```python
import functools

import jax
import jax.numpy as jnp
from jax import lax
from jax.experimental import pallas as pl
from jax.experimental.pallas import tpu as pltpu
from jax.sharding import PartitionSpec as P

BF = jnp.bfloat16
F32 = jnp.float32
I32 = jnp.int32
MIB = 1 << 20
LANES = 128


def rms_scale(values, gain):
    mean_sq = jnp.mean(values * values, axis=-1, keepdims=True)
    return values * lax.rsqrt(mean_sq + 1e-06) * gain


def matmul(a, b):
    return jnp.dot(a, b, preferred_element_type=F32)


def matmul_t(a, b):
    return lax.dot_general(a, b, (((1,), (1,)), ((), ())), preferred_element_type=F32)


def iota(shape, dim):
    return lax.broadcasted_iota(I32, shape, dim)


def attention_kernel(
    lengths, q_ref, nk_ref, nv_ref, k_ref, v_ref, qg_ref, kg_ref, out_ref, nk_scr, nv_scr, num, stat
):
    tensor_pos = lax.axis_index("tensor")
    rows, heads, hd = q_ref.shape
    kvh, cache = k_ref.shape[1], k_ref.shape[2]
    group = heads // kvh
    parts = out_ref.shape[0]
    heads_own = heads // parts
    step = 4
    many, cols = step * heads, step * kvh * cache
    scaling = hd ** (-0.5)
    query_gain, key_gain = qg_ref[...], kg_ref[...]
    for r in range(rows):
        nk_scr[r * kvh : (r + 1) * kvh, :] = rms_scale(nk_ref[r].astype(F32), key_gain)
        nv_scr[r * kvh : (r + 1) * kvh, :] = nv_ref[r].astype(F32)
    new_keys = nk_scr[...].astype(BF)
    new_values = nv_scr[...].astype(BF)
    own = jnp.where(tensor_pos == 0, 1.0, 0.0).astype(F32)

    row_group = iota((many, cols), 0) // group
    col = iota((many, cols), 1)
    same = row_group == col // cache
    col_row = iota((1, cols), 1) // (kvh * cache)
    col_pos = iota((1, cols), 1) % cache + tensor_pos * cache
    new_col = iota((many, rows * kvh), 1)
    new_row = iota((many, rows * kvh), 0) // group
    lane = iota((many, LANES), 1)

    for b in range(rows // step):
        first = b * step
        query = q_ref[first : first + step].reshape(many, hd).astype(F32)
        query = rms_scale(query, query_gain).astype(BF)
        keys = k_ref[first : first + step].reshape(cols, hd)
        values = v_ref[first : first + step].reshape(cols, hd)
        limit = jnp.zeros((1, cols), I32)
        for i in range(step):
            limit = jnp.where(col_row == i, lengths[first + i], limit)
        included = same & (col_pos < limit)
        scores = matmul_t(query, keys) * scaling
        new_here = new_col == new_row + first * kvh
        new_score = jnp.sum(
            jnp.where(new_here, matmul_t(query, new_keys) * scaling, 0.0), axis=1, keepdims=True
        )
        top = jnp.max(jnp.where(included, scores, -1e30), axis=1, keepdims=True)
        top = jnp.maximum(top, new_score).astype(BF).astype(F32)
        weights = jnp.where(included, jnp.exp(scores - top), 0.0).astype(BF)
        new_weight = jnp.exp(new_score - top).astype(BF).astype(F32) * own
        total = jnp.sum(weights.astype(F32), axis=1, keepdims=True) + new_weight
        new_weights = jnp.where(new_here, new_weight, 0.0).astype(BF)
        num[b * many : (b + 1) * many, :] = matmul(weights, values) + matmul(
            new_weights, new_values
        )
        stat[b * many : (b + 1) * many, :] = jnp.where(lane == 0, top, total)

    lane = iota((rows, LANES), 1)
    for t in range(parts):
        side = jnp.zeros((rows, LANES), F32)
        for h in range(heads_own):
            which = pl.ds(t * heads_own + h, rows, stride=heads)
            out_ref[t, :, h * hd : (h + 1) * hd] = num[which, :].astype(BF)
            stats = stat[which, :]
            top, total = stats[:, 0:1], stats[:, 1:2]
            high = total.astype(BF).astype(F32)
            side = jnp.where(lane == h, top, side)
            side = jnp.where(lane == heads_own + h, high, side)
            side = jnp.where(lane == 2 * heads_own + h, total - high, side)
        out_ref[t, :, heads_own * hd :] = side.astype(BF)


def attention(lengths, queries, new_keys, new_values, key_cache, value_cache, qg, kg, parts):
    rows, heads, hd = queries.shape
    kvh = key_cache.shape[1]
    vmem = pl.BlockSpec(memory_space=pltpu.VMEM)
    return pl.pallas_call(
        attention_kernel,
        out_shape=jax.ShapeDtypeStruct((parts, rows, heads // parts * hd + LANES), BF),
        in_specs=[pl.BlockSpec(memory_space=pltpu.SMEM)] + [vmem] * 7,
        out_specs=vmem,
        scratch_shapes=[
            pltpu.VMEM((rows * kvh, hd), F32),
            pltpu.VMEM((rows * kvh, hd), F32),
            pltpu.VMEM((rows * heads, hd), F32),
            pltpu.VMEM((rows * heads, LANES), F32),
        ],
        compiler_params=pltpu.CompilerParams(vmem_limit_bytes=24 * MIB),
        name="attention",
    )(
        lengths,
        queries,
        new_keys,
        new_values,
        key_cache,
        value_cache,
        qg.reshape(1, -1),
        kg.reshape(1, -1),
    )


def projection_kernel(chunks, got_ref, w_hbm, out_ref, w_scr, attn, sem):
    parts, rows, _ = got_ref.shape
    depth, width = w_hbm.shape
    hd = LANES
    heads_own = depth // hd
    size = width // chunks

    def copy(i):
        cols = pl.ds(i * size, size)
        return pltpu.make_async_copy(w_hbm.at[:, cols], w_scr.at[:, cols], sem.at[i])

    for i in range(chunks):
        copy(i).start()
    sides = [got_ref[t, :, depth:].astype(F32) for t in range(parts)]
    tops = [s[:, :heads_own] for s in sides]
    top = functools.reduce(jnp.maximum, tops)
    factors = [jnp.exp(t - top) for t in tops]
    totals = [
        f * (s[:, heads_own : 2 * heads_own] + s[:, 2 * heads_own : 3 * heads_own])
        for f, s in zip(factors, sides)
    ]
    total = functools.reduce(jnp.add, totals)
    factors = [f / total for f in factors]
    for h in range(heads_own):
        cols = slice(h * hd, (h + 1) * hd)
        terms = [
            got_ref[t, :, cols].astype(F32) * factors[t][:, h : h + 1] for t in range(parts)
        ]
        attn[:, cols] = functools.reduce(jnp.add, terms).astype(BF)
    for i in range(chunks):
        copy(i).wait()
        cols = slice(i * size, (i + 1) * size)
        out_ref[:, cols] = matmul(attn[...], w_scr[:, cols]).astype(BF)


def projection(got, out_proj):
    rows = got.shape[1]
    depth, width = out_proj.shape
    chunks = 8
    return pl.pallas_call(
        functools.partial(projection_kernel, chunks),
        out_shape=jax.ShapeDtypeStruct((rows, width), BF),
        in_specs=[pl.BlockSpec(memory_space=pltpu.VMEM), pl.BlockSpec(memory_space=pl.ANY)],
        out_specs=pl.BlockSpec(memory_space=pltpu.VMEM),
        scratch_shapes=[
            pltpu.VMEM((depth, width), BF),
            pltpu.VMEM((rows, depth), BF),
            pltpu.SemaphoreType.DMA((chunks,)),
        ],
        compiler_params=pltpu.CompilerParams(vmem_limit_bytes=24 * MIB),
        name="projection",
    )(got, out_proj)


def expert_kernel(
    c0, c1, gate_hbm, up_hbm, down_hbm, kept, sent, x, table, gate, up, down, act, sem, wsem
):
    own = lax.axis_index("dp") * lax.axis_size("tensor") + lax.axis_index("tensor")
    half = c0.shape[0]
    _, width, hidden = gate_hbm.shape
    fsize = 256
    fchunks = hidden // fsize
    dsize = 1024
    dchunks = width // dsize

    def rows_copies():
        copies = []
        for i, ref in enumerate((c0, c1)):
            rows = pl.ds(i * half, half)
            copies.append(
                pltpu.make_async_copy(ref.at[:, pl.ds(0, width)], x.at[rows], sem.at[2 * i])
            )
            copies.append(
                pltpu.make_async_copy(
                    ref.at[:, pl.ds(width, table.shape[1])], table.at[rows], sem.at[2 * i + 1]
                )
            )
        return copies

    def up_copies(i):
        cols = pl.ds(i * fsize, fsize)
        return [
            pltpu.make_async_copy(gate_hbm.at[0, :, cols], gate.at[:, cols], wsem.at[2 * i]),
            pltpu.make_async_copy(up_hbm.at[0, :, cols], up.at[:, cols], wsem.at[2 * i + 1]),
        ]

    def down_copy(i):
        cols = pl.ds(i * dsize, dsize)
        return pltpu.make_async_copy(
            down_hbm.at[0, :, cols], down.at[:, cols], wsem.at[2 * fchunks + i]
        )

    for c in rows_copies():
        c.start()
    for i in range(fchunks):
        for c in up_copies(i):
            c.start()
    for i in range(dchunks):
        down_copy(i).start()
    for c in rows_copies():
        c.wait()
    tables = table[...].astype(F32)
    weight = jnp.sum(jnp.where(iota(tables.shape, 1) == own, tables, 0.0), axis=1, keepdims=True)
    for i in range(fchunks):
        for c in up_copies(i):
            c.wait()
        cols = slice(i * fsize, (i + 1) * fsize)
        g = matmul(x[...], gate[:, cols])
        u = matmul(x[...], up[:, cols])
        act[:, cols] = (g / (1.0 + jnp.exp(-g)) * u).astype(BF)
    for i in range(dchunks):
        down_copy(i).wait()
        cols = slice(i * dsize, (i + 1) * dsize)
        result = matmul(act[...], down[:, cols])
        result = jnp.where(weight == 0.0, 0.0, result * weight).astype(BF)
        kept[:, cols] = result[:half]
        sent[:, cols] = result[half:]


def experts(c0, c1, expert_gate, expert_up, expert_down):
    half, whole_width = c0.shape
    _, width, hidden = expert_gate.shape
    out = jax.ShapeDtypeStruct((half, width), BF)
    any_space = pl.BlockSpec(memory_space=pl.ANY)
    vmem = pl.BlockSpec(memory_space=pltpu.VMEM)
    return pl.pallas_call(
        expert_kernel,
        out_shape=(out, out),
        in_specs=[any_space] * 5,
        out_specs=(vmem, vmem),
        scratch_shapes=[
            pltpu.VMEM((2 * half, width), BF),
            pltpu.VMEM((2 * half, whole_width - width), BF),
            pltpu.VMEM((width, hidden), BF),
            pltpu.VMEM((width, hidden), BF),
            pltpu.VMEM((hidden, width), BF),
            pltpu.VMEM((2 * half, hidden), BF),
            pltpu.SemaphoreType.DMA((4,)),
            pltpu.SemaphoreType.DMA((2 * hidden // 256 + width // 1024,)),
        ],
        compiler_params=pltpu.CompilerParams(vmem_limit_bytes=48 * MIB),
        name="experts",
    )(c0, c1, expert_gate, expert_up, expert_down)


class Plan:
    def __init__(self, dp, tensor):
        self.zlen = min(4, dp)
        xlen = dp // self.zlen
        self.axes = {
            "x": ("dp", dp, 1, xlen),
            "y": ("tensor", tensor, 2, tensor // 2),
            "c": ("tensor", tensor, 1, 2),
        }
        self.zgroups = [[z * xlen + x for z in range(self.zlen)] for x in range(xlen)]

    def length(self, name):
        return self.axes[name][3]

    def swap(self, value, name, j):
        axis, size, step, _ = self.axes[name]
        return lax.ppermute(value, axis, [(i, i ^ (j * step)) for i in range(size)])

    def trade_z(self, value):
        return lax.all_to_all(
            value, "dp", split_axis=0, concat_axis=0, axis_index_groups=self.zgroups, tiled=True
        )

    def gather(self, value, name, dim):
        return jnp.concatenate(
            [value] + [self.swap(value, name, j) for j in range(1, self.length(name))], axis=dim
        )

    def reduce(self, value, name, dim):
        parts = [lax.slice_in_dim(value, j, j + 1, axis=dim) for j in range(self.length(name))]
        total = parts[0].astype(F32)
        for j in range(1, self.length(name)):
            total = total + self.swap(parts[j].astype(BF), name, j).astype(F32)
        return total


def shards(
    queries,
    new_keys,
    new_values,
    key_cache,
    value_cache,
    lengths,
    residual_in,
    query_gain,
    key_gain,
    out_proj,
    norm_gain,
    expert_ids,
    gate_weights,
    expert_gate,
    expert_up,
    expert_down,
):
    tensor = lax.axis_size("tensor")
    dp = lax.axis_size("dp")
    plan = Plan(dp, tensor)
    share, width = residual_in.shape
    expert_total = dp * tensor
    zlen, xlen, ylen = plan.zlen, plan.length("x"), plan.length("y")

    route = (gate_weights / jnp.sum(gate_weights, axis=1, keepdims=True)).astype(BF)
    named = expert_ids[:, :, None] == jnp.arange(expert_total, dtype=I32)
    table = jnp.sum(jnp.where(named, route[:, :, None], jnp.zeros((), BF)), axis=1)
    table = jnp.pad(table, ((0, 0), (0, -expert_total % LANES)))

    local = attention(
        lengths, queries, new_keys, new_values, key_cache, value_cache, query_gain, key_gain, tensor
    )
    got = lax.all_to_all(local, "tensor", split_axis=0, concat_axis=0, tiled=True)
    partial = projection(got, out_proj)
    sums = lax.all_to_all(partial, "tensor", split_axis=0, concat_axis=0, tiled=True)
    projected = jnp.sum(sums.reshape(tensor, share, width).astype(F32), axis=0)
    hidden = residual_in.astype(F32) + projected
    normed = rms_scale(hidden, norm_gain).astype(BF)

    full = jnp.concatenate([normed, table], axis=1)
    every_z = plan.trade_z(jnp.broadcast_to(full, (zlen, *full.shape)))
    every_z = every_z.reshape(zlen, 1, 1, share, full.shape[1])
    middle = width // 2
    a = plan.gather(every_z[..., :middle], "x", 1)
    b = plan.gather(every_z[..., middle:], "y", 2)
    a = plan.gather(a, "y", 2)
    b = plan.gather(b, "x", 1)
    c0 = jnp.concatenate([a, b], axis=-1).reshape(zlen * xlen * ylen * share, full.shape[1])
    c1 = plan.swap(c0, "c", 1)

    kept, sent = experts(c0, c1, expert_gate, expert_up, expert_down)
    total = kept.astype(F32) + plan.swap(sent, "c", 1).astype(F32)
    total = total.reshape(zlen, xlen, ylen, share, width)
    a = plan.reduce(total[..., :middle], "y", 2)
    b = plan.reduce(total[..., middle:], "x", 1)
    a = plan.reduce(a, "x", 1)
    b = plan.reduce(b, "y", 2)
    total = jnp.concatenate([a.astype(BF), b.astype(BF)], axis=-1).reshape(zlen, share, width)
    moe_sum = jnp.sum(plan.trade_z(total).astype(F32), axis=0)
    return (hidden + moe_sum).astype(BF)


def solution(mesh):
    return jax.shard_map(
        shards,
        mesh=mesh,
        in_specs=(
            P("dp", None, None),
            P("dp", None, None),
            P("dp", None, None),
            P("dp", None, "tensor", None),
            P("dp", None, "tensor", None),
            P("dp"),
            P(("dp", "tensor"), None),
            P(),
            P(),
            P("tensor", None),
            P(),
            P(("dp", "tensor"), None),
            P(("dp", "tensor"), None),
            P(("dp", "tensor"), None, None),
            P(("dp", "tensor"), None, None),
            P(("dp", "tensor"), None, None),
        ),
        out_specs=P(("dp", "tensor"), None),
        check_vma=False,
    )
```

time: 119 us -> 109 us (0.916)
  starting transfers between devices: 43.7 us -> 19.4 us
  blocking collectives: 0 us -> 24.2 us
  matrix products: 23 us -> 0 us
  Pallas kernels: 0 us -> 18.5 us
  other arithmetic: 10.5 us -> 1.97 us
  local copies, waits for them, and re-layouts: 4.19 us -> 9.94 us
  waiting for transfers between devices: 36.9 us -> 34.4 us
    ppermute x40 -> x10, starting transfers between devices: 43.7 us -> 11.7 us  [swap(): return lax.ppermute(value, axis, [(i, i ^ j * step) for i in range(size)])]
    all_to_all x0 -> x2, blocking collectives: none -> 24.2 us  [trade_z(): lax.all_to_all(value, 'dp', split_axis=0, concat_axis=0, axis_index_group...]
    dot_general x6 -> x0, matrix products: 23 us -> none  [the longest x1 11.3 us: shards(): result = jnp.dot(activation, expert_down[0], preferred_element_type=F32)]
    pallas_call x0 -> x3, Pallas kernels: none -> 18.5 us  [the longest x1 8.65 us: experts(): pl.pallas_call(expert_kernel, out_shape=(out, out), in_specs=[any_space]...]
    ppermute x40 -> x10, waiting for transfers between devices: 36.9 us -> 22.3 us  [swap(): return lax.ppermute(value, axis, [(i, i ^ j * step) for i in range(size)])]
    all_to_all x0 -> x2, waiting for transfers between devices: none -> 12.1 us  [the longest x1 6.27 us: shards(): lax.all_to_all(local, 'tensor', split_axis=0, concat_axis=0, tiled=True)]
    unnamed x18 -> x26, local copies, waits for them, and re-layouts: 0.42 us -> 9.83 us
    all_to_all x0 -> x2, starting transfers between devices: none -> 7.65 us  [the longest x1 4.24 us: shards(): lax.all_to_all(local, 'tensor', split_axis=0, concat_axis=0, tiled=True)]
  transfers between devices with their start and end apart: 40 -> 12, of which waited for: 21 -> 10; matrix products, arithmetic and copies ran while one was open for 1% -> 1% of each run, Pallas kernels for 0% -> 0%
where the time goes in v2:
time: 109 us
  waiting for transfers between devices  34.4 us (32%)
  blocking collectives  24.2 us (22%)
  starting transfers between devices  19.4 us (18%)
  Pallas kernels  18.5 us (17%)
  local copies, waits for them, and re-layouts  9.94 us (9%)
  other arithmetic  1.97 us (2%)
    all_to_all x2, blocking collectives, trade_z(): lax.all_to_all(value, 'dp', split_axis=0, concat_axis=0, axis_index_group...  24.2 us
    ppermute x10, waiting for transfers between devices, swap(): return lax.ppermute(value, axis, [(i, i ^ j * step) for i in range(size)])  22.3 us
    ppermute x10, starting transfers between devices, swap(): return lax.ppermute(value, axis, [(i, i ^ j * step) for i in range(size)])  11.7 us
    unnamed x26, local copies, waits for them, and re-layouts  9.83 us
    pallas_call x1, Pallas kernels, experts(): pl.pallas_call(expert_kernel, out_shape=(out, out), in_specs=[any_space]...  8.65 us
    all_to_all x1, waiting for transfers between devices, shards(): lax.all_to_all(local, 'tensor', split_axis=0, concat_axis=0, tiled=True)  6.27 us
    all_to_all x1, waiting for transfers between devices, shards(): lax.all_to_all(partial, 'tensor', split_axis=0, concat_axis=0, tiled=True)  5.82 us
    pallas_call x1, Pallas kernels, projection(): pl.pallas_call(functools.partial(projection_kernel, chunks), out_shape=ja...  5.56 us
  transfers between devices with their start and end apart: 12, of which 10 were waited for; matrix products, arithmetic and copies ran while one was open for 1% of the time, Pallas kernels for 0%

profile of v2, /device:TPU:0, one launch (start us, length us, event | category | flops | bytes accessed | tf_op | source)
XLA Modules:
  0.0 108.5 jit_solution(846198179334138709)
XLA Ops:
  6.4 4.3 %attention.1 = bf16[4,32,1152]{2,1,0:T(8,128)(2,1)} custom-call(s32[32]{0:T(128)S(1)} %copy-done.6, bf16[32,32,128]{2,1,0:T(8,128)(2,1)S(1)} %copy-done.3, bf16[32,2,128]{2,1,0:T(2,128)(2,1)S(1)} %copy-done.4, bf16[32,2,128]{2,1,0:T(2,128)(2,1)S(1)} %copy-done.5, bf16[32,2,32,128]{3,2,1,0:T(8,128)(2,1)S(1)} %copy-done.1, ...), custom_call_target="tpu_custom_call" | custom-call | tf_op jit(solution)/shard_map/attention/pallas_call | solution.py:108
  10.7 4.2 %all-to-all-start = ((bf16[4,32,1152]{2,1,0:T(8,128)(2,1)}), bf16[4,32,1152]{2,1,0:T(8,128)(2,1)S(1)}, u32[]{:S(2)}, u32[]{:S(2)}) async-start(bf16[4,32,1152]{2,1,0:T(8,128)(2,1)} %attention.1), calls=%async_computation | async-start | bytes 589824 | tf_op jit(solution)/shard_map/all_to_all | solution.py:347
  15.1 6.3 %all-to-all-done.got_ref = bf16[4,32,1152]{2,1,0:T(8,128)(2,1)S(1)} async-done(((bf16[4,32,1152]{2,1,0:T(8,128)(2,1)}), bf16[4,32,1152]{2,1,0:T(8,128)(2,1)S(1)}, u32[]{:S(2)}, u32[]{:S(2)}) %all-to-all-start) | async-done | bytes 294944 | tf_op jit(solution)/shard_map/all_to_all | solution.py:347
  21.4 3.4 %copy-done = bf16[1024,4096]{1,0:T(8,128)(2,1)S(1)} copy-done((bf16[1024,4096]{1,0:T(8,128)(2,1)S(1)}, bf16[1024,4096]{1,0:T(8,128)(2,1)}, u32[]{:S(2)}) %copy-start) | copy-done | bytes 8388632
  24.8 5.6 %projection.1 = bf16[32,4096]{1,0:T(8,128)(2,1)} custom-call(bf16[4,32,1152]{2,1,0:T(8,128)(2,1)S(1)} %all-to-all-done.got_ref, bf16[1024,4096]{1,0:T(8,128)(2,1)S(1)} %copy-done), custom_call_target="tpu_custom_call" | custom-call | tf_op jit(solution)/shard_map/projection/pallas_call | solution.py:172
  30.3 3.4 %all-to-all-start.1 = ((bf16[4,8,4096]{2,1,0:T(8,128)(2,1)}), bf16[4,8,4096]{2,1,0:T(8,128)(2,1)S(1)}, u32[]{:S(2)}, u32[]{:S(2)}) async-start(bf16[4,8,4096]{2,1,0:T(8,128)(2,1)} %bitcast.2), calls=%async_computation.1 | async-start | bytes 524288 | tf_op jit(solution)/shard_map/all_to_all | solution.py:349
  33.9 5.8 %all-to-all-done.1 = bf16[4,8,4096]{2,1,0:T(8,128)(2,1)S(1)} async-done(((bf16[4,8,4096]{2,1,0:T(8,128)(2,1)}), bf16[4,8,4096]{2,1,0:T(8,128)(2,1)S(1)}, u32[]{:S(2)}, u32[]{:S(2)}) %all-to-all-start.1) | async-done | bytes 262176 | tf_op jit(solution)/shard_map/all_to_all | solution.py:349
  40.1 14.2 %all_to_all.24 = bf16[4,8,4224]{2,1,0:T(8,128)(2,1)S(1)} all-to-all(bf16[4,8,4224]{2,1,0:T(8,128)(2,1)S(1)} %broadcast_in_dim.23), channel_id=1, replica_groups={{0,8,16,24},{4,12,20,28},{1,9,17,25},{5,13,21,29},{2,10,18,26},{6,14,22..., dimensions={0} | all-to-all | bytes 540672 | tf_op jit(solution)/shard_map/all_to_all | solution.py:297
  55.0 1.6 %collective-permute-start = (bf16[4,1,1,8,2048]{4,3,2,1,0:T(8,128)(2,1)S(1)}, bf16[4,1,1,8,2048]{4,3,2,1,0:T(8,128)(2,1)S(1)}, u32[]{:S(2)}, u32[]{:S(2)}) collective-permute-start(bf16[4,1,1,8,2048]{4,3,2,1,0:T(8,128)(2,1)S(1)} %slice.50), channel_id=1, source_target_pairs={{0,4},{4,0},{8,12},{12,8},{16,20},{20,16},{24,28},{28,24},{1,5},{5... | collective-permute-start | bytes 393224 | tf_op jit(solution)/shard_map/ppermute | solution.py:294
  56.5 2.9 %collective-permute-done.2 = bf16[4,1,1,8,2176]{4,3,2,1,0:T(8,128)(2,1)S(1)} collective-permute-done((bf16[4,1,1,8,2176]{4,3,2,1,0:T(8,128)(2,1)S(1)}, bf16[4,1,1,8,2176]{4,3,2,1,0:T(8,128)(2,1)S(1)}, u32[]{:S(2)}, u32[]{:S(2)}) %collective-permute-start.2) | collective-permute-done | bytes 139296 | tf_op jit(solution)/shard_map/ppermute | solution.py:294
  59.4 1.8 %collective-permute-start.3 = (bf16[4,1,2,8,2176]{4,3,2,1,0:T(8,128)(2,1)S(1)}, bf16[4,1,2,8,2176]{4,3,2,1,0:T(8,128)(2,1)S(1)}, u32[]{:S(2)}, u32[]{:S(2)}) collective-permute-start(bf16[4,1,2,8,2176]{4,3,2,1,0:T(8,128)(2,1)S(1)} %pad_maximum_fusion), channel_id=1, source_target_pairs={{0,4},{4,0},{8,12},{12,8},{16,20},{20,16},{24,28},{28,24},{1,5},{5... | collective-permute-start | bytes 835592 | tf_op jit(solution)/shard_map/ppermute | solution.py:294
  61.4 1.4 %collective-permute-start.1 = (bf16[4,2,1,8,2048]{4,3,2,1,0:T(8,128)(2,1)S(1)}, bf16[4,2,1,8,2048]{4,3,2,1,0:T(8,128)(2,1)S(1)}, u32[]{:S(2)}, u32[]{:S(2)}) collective-permute-start(bf16[4,2,1,8,2048]{4,3,2,1,0:T(8,128)(2,1)S(1)} %pad_maximum_fusion.1), channel_id=1, source_target_pairs={{0,2},{1,3},{2,0},{3,1},{4,6},{5,7},{6,4},{7,5},{8,10},{9,11},{10,... | collective-permute-start | bytes 786440 | tf_op jit(solution)/shard_map/ppermute | solution.py:294
  62.8 5.0 %collective-permute-done.1 = bf16[4,2,1,8,2048]{4,3,2,1,0:T(8,128)(2,1)S(1)} collective-permute-done((bf16[4,2,1,8,2048]{4,3,2,1,0:T(8,128)(2,1)S(1)}, bf16[4,2,1,8,2048]{4,3,2,1,0:T(8,128)(2,1)S(1)}, u32[]{:S(2)}, u32[]{:S(2)}) %collective-permute-start.1) | collective-permute-done | bytes 262176 | tf_op jit(solution)/shard_map/ppermute | solution.py:294
  68.0 2.7 %collective-permute-done.4.c1 = bf16[128,4224]{1,0:T(8,128)(2,1)S(1)} collective-permute-done((bf16[128,4224]{1,0:T(8,128)(2,1)S(1)}, bf16[128,4224]{1,0:T(8,128)(2,1)S(1)}, u32[]{:S(2)}, u32[]{:S(2)}) %collective-permute-start.4) | collective-permute-done | bytes 1081376 | tf_op jit(solution)/shard_map/ppermute | solution.py:294
  70.7 8.7 %experts.1 = (bf16[128,4096]{1,0:T(8,128)(2,1)S(1)}, bf16[128,4096]{1,0:T(8,128)(2,1)S(1)}) custom-call(bf16[128,4224]{1,0:T(8,128)(2,1)S(1)} %bitcast.9, bf16[128,4224]{1,0:T(8,128)(2,1)S(1)} %collective-permute-done.4.c1, bf16[1,4096,768]{2,1,0:T(8,128)(2,1)} %gate_hbm.1, bf16[1,4096,768]{2,1,0:T(8,128)(2,1)} %up_hbm.1, bf16[1,768,4096]{2,1,0:T(8,128)(2,1)} %down_hbm.1), custom_call_target="tpu_custom_call" | custom-call | tf_op jit(solution)/shard_map/experts/pallas_call | solution.py:258
  79.6 2.5 %collective-permute-done.5 = bf16[128,4096]{1,0:T(8,128)(2,1)S(1)} collective-permute-done((bf16[128,4096]{1,0:T(8,128)(2,1)S(1)}, bf16[128,4096]{1,0:T(8,128)(2,1)S(1)}, u32[]{:S(2)}, u32[]{:S(2)}) %collective-permute-start.5) | collective-permute-done | bytes 1048608 | tf_op jit(solution)/shard_map/ppermute | solution.py:294
  82.5 1.4 %collective-permute-start.6 = (bf16[4,2,1,8,2048]{4,3,2,1,0:T(8,128)(2,1)S(1)}, bf16[4,2,1,8,2048]{4,3,2,1,0:T(8,128)(2,1)S(1)}, u32[]{:S(2)}, u32[]{:S(2)}) collective-permute-start(bf16[4,2,1,8,2048]{4,3,2,1,0:T(8,128)(2,1)S(1)} %slice.53), channel_id=1, source_target_pairs={{0,2},{1,3},{2,0},{3,1},{4,6},{5,7},{6,4},{7,5},{8,10},{9,11},{10,... | collective-permute-start | bytes 786440 | tf_op jit(solution)/shard_map/ppermute | solution.py:294
  84.0 1.6 %collective-permute-start.8 = (bf16[4,1,2,8,2048]{4,3,2,1,0:T(8,128)(2,1)S(1)}, bf16[4,1,2,8,2048]{4,3,2,1,0:T(8,128)(2,1)S(1)}, u32[]{:S(2)}, u32[]{:S(2)}) collective-permute-start(bf16[4,1,2,8,2048]{4,3,2,1,0:T(8,128)(2,1)S(1)} %slice.57), channel_id=1, source_target_pairs={{0,4},{4,0},{8,12},{12,8},{16,20},{20,16},{24,28},{28,24},{1,5},{5... | collective-permute-start | bytes 786440 | tf_op jit(solution)/shard_map/ppermute | solution.py:294
  85.5 5.4 %collective-permute-done.6 = bf16[4,2,1,8,2048]{4,3,2,1,0:T(8,128)(2,1)S(1)} collective-permute-done((bf16[4,2,1,8,2048]{4,3,2,1,0:T(8,128)(2,1)S(1)}, bf16[4,2,1,8,2048]{4,3,2,1,0:T(8,128)(2,1)S(1)}, u32[]{:S(2)}, u32[]{:S(2)}) %collective-permute-start.6) | collective-permute-done | bytes 262176 | tf_op jit(solution)/shard_map/ppermute | solution.py:294
  91.0 1.6 %collective-permute-start.7 = (bf16[4,1,1,8,2048]{4,3,2,1,0:T(8,128)(2,1)S(1)}, bf16[4,1,1,8,2048]{4,3,2,1,0:T(8,128)(2,1)S(1)}, u32[]{:S(2)}, u32[]{:S(2)}) collective-permute-start(bf16[4,1,1,8,2048]{4,3,2,1,0:T(8,128)(2,1)S(1)} %slice.71), channel_id=1, source_target_pairs={{0,4},{4,0},{8,12},{12,8},{16,20},{20,16},{24,28},{28,24},{1,5},{5... | collective-permute-start | bytes 393224 | tf_op jit(solution)/shard_map/ppermute | solution.py:294
  92.7 1.4 %collective-permute-start.9 = (bf16[4,1,1,8,2048]{4,3,2,1,0:T(8,128)(2,1)S(1)}, bf16[4,1,1,8,2048]{4,3,2,1,0:T(8,128)(2,1)S(1)}, u32[]{:S(2)}, u32[]{:S(2)}) collective-permute-start(bf16[4,1,1,8,2048]{4,3,2,1,0:T(8,128)(2,1)S(1)} %slice.70), channel_id=1, source_target_pairs={{0,2},{1,3},{2,0},{3,1},{4,6},{5,7},{6,4},{7,5},{8,10},{9,11},{10,... | collective-permute-start | bytes 393224 | tf_op jit(solution)/shard_map/ppermute | solution.py:294
  94.1 2.0 %collective-permute-done.7 = bf16[4,1,1,8,2048]{4,3,2,1,0:T(8,128)(2,1)S(1)} collective-permute-done((bf16[4,1,1,8,2048]{4,3,2,1,0:T(8,128)(2,1)S(1)}, bf16[4,1,1,8,2048]{4,3,2,1,0:T(8,128)(2,1)S(1)}, u32[]{:S(2)}, u32[]{:S(2)}) %collective-permute-start.7) | collective-permute-done | bytes 131104 | tf_op jit(solution)/shard_map/ppermute | solution.py:294
  96.1 1.6 %collective-permute-done.9 = bf16[4,1,1,8,2048]{4,3,2,1,0:T(8,128)(2,1)S(1)} collective-permute-done((bf16[4,1,1,8,2048]{4,3,2,1,0:T(8,128)(2,1)S(1)}, bf16[4,1,1,8,2048]{4,3,2,1,0:T(8,128)(2,1)S(1)}, u32[]{:S(2)}, u32[]{:S(2)}) %collective-permute-start.9) | collective-permute-done | bytes 131104 | tf_op jit(solution)/shard_map/ppermute | solution.py:294
  97.8 10.1 %all_to_all.25 = bf16[4,8,4096]{2,1,0:T(8,128)(2,1)S(1)} all-to-all(bf16[4,8,4096]{2,1,0:T(8,128)(2,1)S(1)} %maximum_bitcast_fusion), channel_id=1, replica_groups={{0,8,16,24},{4,12,20,28},{1,9,17,25},{5,13,21,29},{2,10,18,26},{6,14,22..., dimensions={0} | all-to-all | bytes 524288 | tf_op jit(solution)/shard_map/all_to_all | solution.py:297
  (58 shorter events, 9.6 us)
Async XLA Ops:
  0.0 1.0 copy-start.1
  1.0 1.0 copy-start.2
  2.1 0.9 copy-start.3
  3.0 0.7 copy-start.4
  3.8 0.7 copy-start.5
  4.5 0.7 copy-start.6
  5.1 0.7 copy-start.7
  6.4 8.5 %copy-start.11 = (f32[8,8]{1,0:T(8,128)S(1)}, f32[8,8]{1,0:T(8,128)}, u32[]{:S(2)}) copy-start(f32[8,8]{1,0:T(8,128)} %param.28) | copy-start | bytes 772
  10.7 10.6 %all-to-all-start = ((bf16[4,32,1152]{2,1,0:T(8,128)(2,1)}), bf16[4,32,1152]{2,1,0:T(8,128)(2,1)S(1)}, u32[]{:S(2)}, u32[]{:S(2)}) async-start(bf16[4,32,1152]{2,1,0:T(8,128)(2,1)} %attention.1), calls=%async_computation | async-start | bytes 589824 | tf_op jit(solution)/shard_map/all_to_all | solution.py:347
  21.4 3.4 %copy-start = (bf16[1024,4096]{1,0:T(8,128)(2,1)S(1)}, bf16[1024,4096]{1,0:T(8,128)(2,1)}, u32[]{:S(2)}) copy-start(bf16[1024,4096]{1,0:T(8,128)(2,1)} %w_hbm.1) | copy-start | bytes 25165828
  24.7 9.1 %copy-start.12 = (s32[8,8]{1,0:T(8,128)S(1)}, s32[8,8]{1,0:T(8,128)}, u32[]{:S(2)}) copy-start(s32[8,8]{1,0:T(8,128)} %param.27) | copy-start | bytes 772
  24.7 15.0 %copy-start.9 = (bf16[8,4096]{1,0:T(8,128)(2,1)S(1)}, bf16[8,4096]{1,0:T(8,128)(2,1)}, u32[]{:S(2)}) copy-start(bf16[8,4096]{1,0:T(8,128)(2,1)} %param.22) | copy-start | bytes 196612
  24.8 15.2 %copy-start.10 = (f32[4096]{0:T(1024)S(1)}, f32[4096]{0:T(1024)}, u32[]{:S(2)}) copy-start(f32[4096]{0:T(1024)} %param.26) | copy-start | bytes 49156
  30.3 9.4 %all-to-all-start.1 = ((bf16[4,8,4096]{2,1,0:T(8,128)(2,1)}), bf16[4,8,4096]{2,1,0:T(8,128)(2,1)S(1)}, u32[]{:S(2)}, u32[]{:S(2)}) async-start(bf16[4,8,4096]{2,1,0:T(8,128)(2,1)} %bitcast.2), calls=%async_computation.1 | async-start | bytes 524288 | tf_op jit(solution)/shard_map/all_to_all | solution.py:349
  54.3 5.1 %collective-permute-start.2 = (bf16[4,1,1,8,2176]{4,3,2,1,0:T(8,128)(2,1)S(1)}, bf16[4,1,1,8,2176]{4,3,2,1,0:T(8,128)(2,1)S(1)}, u32[]{:S(2)}, u32[]{:S(2)}) collective-permute-start(bf16[4,1,1,8,2176]{4,3,2,1,0:T(8,128)(2,1)S(1)} %slice.51), channel_id=1, source_target_pairs={{0,2},{1,3},{2,0},{3,1},{4,6},{5,7},{6,4},{7,5},{8,10},{9,11},{10,... | collective-permute-start | bytes 417800 | tf_op jit(solution)/shard_map/ppermute | solution.py:294
  55.0 6.4 %collective-permute-start = (bf16[4,1,1,8,2048]{4,3,2,1,0:T(8,128)(2,1)S(1)}, bf16[4,1,1,8,2048]{4,3,2,1,0:T(8,128)(2,1)S(1)}, u32[]{:S(2)}, u32[]{:S(2)}) collective-permute-start(bf16[4,1,1,8,2048]{4,3,2,1,0:T(8,128)(2,1)S(1)} %slice.50), channel_id=1, source_target_pairs={{0,4},{4,0},{8,12},{12,8},{16,20},{20,16},{24,28},{28,24},{1,5},{5... | collective-permute-start | bytes 393224 | tf_op jit(solution)/shard_map/ppermute | solution.py:294
  59.4 8.5 %collective-permute-start.3 = (bf16[4,1,2,8,2176]{4,3,2,1,0:T(8,128)(2,1)S(1)}, bf16[4,1,2,8,2176]{4,3,2,1,0:T(8,128)(2,1)S(1)}, u32[]{:S(2)}, u32[]{:S(2)}) collective-permute-start(bf16[4,1,2,8,2176]{4,3,2,1,0:T(8,128)(2,1)S(1)} %pad_maximum_fusion), channel_id=1, source_target_pairs={{0,4},{4,0},{8,12},{12,8},{16,20},{20,16},{24,28},{28,24},{1,5},{5... | collective-permute-start | bytes 835592 | tf_op jit(solution)/shard_map/ppermute | solution.py:294
  61.4 6.4 %collective-permute-start.1 = (bf16[4,2,1,8,2048]{4,3,2,1,0:T(8,128)(2,1)S(1)}, bf16[4,2,1,8,2048]{4,3,2,1,0:T(8,128)(2,1)S(1)}, u32[]{:S(2)}, u32[]{:S(2)}) collective-permute-start(bf16[4,2,1,8,2048]{4,3,2,1,0:T(8,128)(2,1)S(1)} %pad_maximum_fusion.1), channel_id=1, source_target_pairs={{0,2},{1,3},{2,0},{3,1},{4,6},{5,7},{6,4},{7,5},{8,10},{9,11},{10,... | collective-permute-start | bytes 786440 | tf_op jit(solution)/shard_map/ppermute | solution.py:294
  68.0 2.8 %collective-permute-start.4 = (bf16[128,4224]{1,0:T(8,128)(2,1)S(1)}, bf16[128,4224]{1,0:T(8,128)(2,1)S(1)}, u32[]{:S(2)}, u32[]{:S(2)}) collective-permute-start(bf16[128,4224]{1,0:T(8,128)(2,1)S(1)} %bitcast.8), channel_id=1, source_target_pairs={{0,1},{1,0},{2,3},{3,2},{4,5},{5,4},{6,7},{7,6},{8,9},{9,8},{10,11... | collective-permute-start | bytes 3244040 | tf_op jit(solution)/shard_map/ppermute | solution.py:294
  79.4 2.7 %collective-permute-start.5 = (bf16[128,4096]{1,0:T(8,128)(2,1)S(1)}, bf16[128,4096]{1,0:T(8,128)(2,1)S(1)}, u32[]{:S(2)}, u32[]{:S(2)}) collective-permute-start(bf16[128,4096]{1,0:T(8,128)(2,1)S(1)} %get-tuple-element.8), channel_id=1, source_target_pairs={{0,1},{1,0},{2,3},{3,2},{4,5},{5,4},{6,7},{7,6},{8,9},{9,8},{10,11... | collective-permute-start | bytes 3145736 | tf_op jit(solution)/shard_map/ppermute | solution.py:294
  82.5 8.4 %collective-permute-start.6 = (bf16[4,2,1,8,2048]{4,3,2,1,0:T(8,128)(2,1)S(1)}, bf16[4,2,1,8,2048]{4,3,2,1,0:T(8,128)(2,1)S(1)}, u32[]{:S(2)}, u32[]{:S(2)}) collective-permute-start(bf16[4,2,1,8,2048]{4,3,2,1,0:T(8,128)(2,1)S(1)} %slice.53), channel_id=1, source_target_pairs={{0,2},{1,3},{2,0},{3,1},{4,6},{5,7},{6,4},{7,5},{8,10},{9,11},{10,... | collective-permute-start | bytes 786440 | tf_op jit(solution)/shard_map/ppermute | solution.py:294
  84.0 8.6 %collective-permute-start.8 = (bf16[4,1,2,8,2048]{4,3,2,1,0:T(8,128)(2,1)S(1)}, bf16[4,1,2,8,2048]{4,3,2,1,0:T(8,128)(2,1)S(1)}, u32[]{:S(2)}, u32[]{:S(2)}) collective-permute-start(bf16[4,1,2,8,2048]{4,3,2,1,0:T(8,128)(2,1)S(1)} %slice.57), channel_id=1, source_target_pairs={{0,4},{4,0},{8,12},{12,8},{16,20},{20,16},{24,28},{28,24},{1,5},{5... | collective-permute-start | bytes 786440 | tf_op jit(solution)/shard_map/ppermute | solution.py:294
  91.0 5.0 %collective-permute-start.7 = (bf16[4,1,1,8,2048]{4,3,2,1,0:T(8,128)(2,1)S(1)}, bf16[4,1,1,8,2048]{4,3,2,1,0:T(8,128)(2,1)S(1)}, u32[]{:S(2)}, u32[]{:S(2)}) collective-permute-start(bf16[4,1,1,8,2048]{4,3,2,1,0:T(8,128)(2,1)S(1)} %slice.71), channel_id=1, source_target_pairs={{0,4},{4,0},{8,12},{12,8},{16,20},{20,16},{24,28},{28,24},{1,5},{5... | collective-permute-start | bytes 393224 | tf_op jit(solution)/shard_map/ppermute | solution.py:294
  92.7 5.0 %collective-permute-start.9 = (bf16[4,1,1,8,2048]{4,3,2,1,0:T(8,128)(2,1)S(1)}, bf16[4,1,1,8,2048]{4,3,2,1,0:T(8,128)(2,1)S(1)}, u32[]{:S(2)}, u32[]{:S(2)}) collective-permute-start(bf16[4,1,1,8,2048]{4,3,2,1,0:T(8,128)(2,1)S(1)} %slice.70), channel_id=1, source_target_pairs={{0,2},{1,3},{2,0},{3,1},{4,6},{5,7},{6,4},{7,5},{8,10},{9,11},{10,... | collective-permute-start | bytes 393224 | tf_op jit(solution)/shard_map/ppermute | solution.py:294
  (1 other events, 0.7 us)

commit v3 on v2

v3 whole, which is shorter than its diff:
```python
import functools

import jax
import jax.numpy as jnp
from jax import lax
from jax.experimental import pallas as pl
from jax.experimental.pallas import tpu as pltpu
from jax.sharding import PartitionSpec as P

BF = jnp.bfloat16
F32 = jnp.float32
I32 = jnp.int32
MIB = 1 << 20
LANES = 128


def rms_scale(values, gain):
    mean_sq = jnp.mean(values * values, axis=-1, keepdims=True)
    return values * lax.rsqrt(mean_sq + 1e-06) * gain


def matmul(a, b):
    return jnp.dot(a, b, preferred_element_type=F32)


def matmul_t(a, b):
    return lax.dot_general(a, b, (((1,), (1,)), ((), ())), preferred_element_type=F32)


def iota(shape, dim):
    return lax.broadcasted_iota(I32, shape, dim)


def in_hbm(value):
    return pltpu.with_memory_space_constraint(value, pltpu.HBM)


def attention_kernel(
    len_hbm,
    q_hbm,
    nk_hbm,
    nv_hbm,
    k_hbm,
    v_hbm,
    qg_hbm,
    kg_hbm,
    ids_hbm,
    gates_hbm,
    w0_hbm,
    w1_hbm,
    out_ref,
    table_ref,
    w0_ref,
    w1_ref,
    lengths,
    q_ref,
    nk_ref,
    nv_ref,
    k_ref,
    v_ref,
    qg_ref,
    kg_ref,
    ids_ref,
    gates_ref,
    nk_scr,
    nv_scr,
    num,
    tops,
    totals,
    sem,
):
    sources = (len_hbm, nk_hbm, nv_hbm, qg_hbm, kg_hbm, ids_hbm, gates_hbm, q_hbm, k_hbm, v_hbm)
    targets = (lengths, nk_ref, nv_ref, qg_ref, kg_ref, ids_ref, gates_ref, q_ref, k_ref, v_ref)
    copies = [
        pltpu.make_async_copy(a, b, sem.at[i]) for i, (a, b) in enumerate(zip(sources, targets))
    ]
    ahead = [
        pltpu.make_async_copy(w0_hbm, w0_ref, sem.at[10]),
        pltpu.make_async_copy(w1_hbm, w1_ref, sem.at[11]),
    ]
    for c in copies + ahead:
        c.start()
    tensor_pos = lax.axis_index("tensor")
    rows, heads, hd = q_ref.shape
    kvh, cache = k_ref.shape[1], k_ref.shape[2]
    group = heads // kvh
    parts = out_ref.shape[0]
    heads_own = heads // parts
    step = 4
    many, cols = step * heads, step * kvh * cache
    scaling = hd ** (-0.5)
    own = jnp.where(tensor_pos == 0, 1.0, 0.0).astype(F32)

    row_group = iota((many, cols), 0) // group
    col = iota((many, cols), 1)
    same = row_group == col // cache
    col_row = iota((1, cols), 1) // (kvh * cache)
    col_pos = iota((1, cols), 1) % cache + tensor_pos * cache
    new_col = iota((many, rows * kvh), 1)
    new_row = iota((many, rows * kvh), 0) // group

    for c in copies[:7]:
        c.wait()
    gates = gates_ref[...]
    route = (gates / jnp.sum(gates, axis=1, keepdims=True)).astype(BF).astype(F32)
    expert = iota(table_ref.shape, 1)
    table = jnp.zeros(table_ref.shape, F32)
    for k in range(gates.shape[1]):
        table = jnp.where(expert == ids_ref[:, k : k + 1], route[:, k : k + 1], table)
    table_ref[...] = table.astype(BF)
    for r in range(rows):
        nk_scr[r * kvh : (r + 1) * kvh, :] = nk_ref[r].astype(F32)
        nv_scr[r * kvh : (r + 1) * kvh, :] = nv_ref[r].astype(F32)
    query_gain = qg_ref[...]
    new_keys = rms_scale(nk_scr[...], kg_ref[...]).astype(BF)
    new_values = nv_scr[...].astype(BF)
    for c in copies[7:]:
        c.wait()

    for b in range(rows // step):
        first = b * step
        query = q_ref[first : first + step].reshape(many, hd).astype(F32)
        query = rms_scale(query, query_gain).astype(BF)
        keys = k_ref[first : first + step].reshape(cols, hd)
        values = v_ref[first : first + step].reshape(cols, hd)
        limit = jnp.zeros((1, cols), I32)
        for i in range(step):
            limit = jnp.where(col_row == i, lengths[first + i], limit)
        included = same & (col_pos < limit)
        scores = matmul_t(query, keys) * scaling
        new_here = new_col == new_row + first * kvh
        new_score = jnp.sum(
            jnp.where(new_here, matmul_t(query, new_keys) * scaling, 0.0), axis=1, keepdims=True
        )
        top = jnp.max(jnp.where(included, scores, -1e30), axis=1, keepdims=True)
        top = jnp.maximum(top, new_score).astype(BF).astype(F32)
        weights = jnp.where(included, jnp.exp(scores - top), 0.0).astype(BF)
        new_weight = jnp.exp(new_score - top).astype(BF).astype(F32) * own
        total = jnp.sum(weights.astype(F32), axis=1, keepdims=True) + new_weight
        new_weights = jnp.where(new_here, new_weight, 0.0).astype(BF)
        block = slice(b * many, (b + 1) * many)
        num[block, :] = matmul(weights, values) + matmul(new_weights, new_values)
        tops[block, :] = jnp.broadcast_to(top, (many, LANES))
        totals[block, :] = jnp.broadcast_to(total, (many, LANES))

    lane = iota((rows, LANES), 1)
    for t in range(parts):
        slot = tensor_pos ^ t
        side = jnp.zeros((rows, LANES), F32)
        for h in range(heads_own):
            which = pl.ds(t * heads_own + h, rows, stride=heads)
            out_ref[slot, :, h * hd : (h + 1) * hd] = num[which, :].astype(BF)
            total = totals[which, :]
            high = total.astype(BF).astype(F32)
            side = jnp.where(lane == h, tops[which, :], side)
            side = jnp.where(lane == heads_own + h, high, side)
            side = jnp.where(lane == 2 * heads_own + h, total - high, side)
        out_ref[slot, :, heads_own * hd :] = side.astype(BF)
    for c in ahead:
        c.wait()


def attention(
    lengths,
    queries,
    new_keys,
    new_values,
    key_cache,
    value_cache,
    qg,
    kg,
    expert_ids,
    gate_weights,
    parts,
    lanes,
    weights,
):
    rows, heads, hd = queries.shape
    kvh = key_cache.shape[1]
    args = (
        lengths,
        queries,
        new_keys,
        new_values,
        key_cache,
        value_cache,
        qg.reshape(1, -1),
        kg.reshape(1, -1),
        expert_ids,
        gate_weights,
    )
    return pl.pallas_call(
        attention_kernel,
        out_shape=(
            jax.ShapeDtypeStruct((parts, rows, heads // parts * hd + LANES), BF),
            jax.ShapeDtypeStruct((expert_ids.shape[0], lanes), BF),
            *[pltpu.VMEM(w.shape, w.dtype) for w in weights],
        ),
        in_specs=[pl.BlockSpec(memory_space=pltpu.HBM)] * 12,
        out_specs=(pl.BlockSpec(memory_space=pltpu.VMEM),) * 4,
        scratch_shapes=[pltpu.SMEM(args[0].shape, I32)]
        + [pltpu.VMEM(a.shape, a.dtype) for a in args[1:]]
        + [
            pltpu.VMEM((rows * kvh, hd), F32),
            pltpu.VMEM((rows * kvh, hd), F32),
            pltpu.VMEM((rows * heads, hd), F32),
            pltpu.VMEM((rows * heads, LANES), F32),
            pltpu.VMEM((rows * heads, LANES), F32),
            pltpu.SemaphoreType.DMA((12,)),
        ],
        compiler_params=pltpu.CompilerParams(vmem_limit_bytes=16 * MIB),
        name="attention",
    )(*[in_hbm(a) for a in (*args, *weights)])


def projection_kernel(parts, *refs):
    got = refs[:parts]
    w_ref, ahead_hbm, out_ref, ahead_ref, attn, sem = refs[parts:]
    ahead = pltpu.make_async_copy(ahead_hbm, ahead_ref, sem)
    ahead.start()
    tensor_pos = lax.axis_index("tensor")
    depth, width = w_ref.shape
    share = out_ref.shape[2]
    hd = LANES
    heads_own = depth // hd
    size = 512
    sides = [g[:, depth:].astype(F32) for g in got]
    tops = [s[:, :heads_own] for s in sides]
    top = functools.reduce(jnp.maximum, tops)
    factors = [jnp.exp(t - top) for t in tops]
    totals = [
        f * (s[:, heads_own : 2 * heads_own] + s[:, 2 * heads_own : 3 * heads_own])
        for f, s in zip(factors, sides)
    ]
    total = functools.reduce(jnp.add, totals)
    factors = [f / total for f in factors]
    for h in range(heads_own):
        cols = slice(h * hd, (h + 1) * hd)
        terms = [g[:, cols].astype(F32) * f[:, h : h + 1] for g, f in zip(got, factors)]
        attn[:, cols] = functools.reduce(jnp.add, terms).astype(BF)
    for i in range(width // size):
        cols = slice(i * size, (i + 1) * size)
        result = matmul(attn[...], w_ref[:, cols])
        for t in range(parts):
            slot = tensor_pos ^ t
            out_ref[slot & 1, slot >> 1, :, cols] = result[t * share : (t + 1) * share].astype(BF)
    ahead.wait()


def projection(got, out_proj, share, weight):
    parts = len(got)
    rows = got[0].shape[0]
    depth, width = out_proj.shape
    vmem = pl.BlockSpec(memory_space=pltpu.VMEM)
    return pl.pallas_call(
        functools.partial(projection_kernel, parts),
        out_shape=(
            jax.ShapeDtypeStruct((2, parts // 2, share, width), BF),
            pltpu.VMEM(weight.shape, weight.dtype),
        ),
        in_specs=[vmem] * (parts + 1) + [pl.BlockSpec(memory_space=pltpu.HBM)],
        out_specs=(vmem, vmem),
        scratch_shapes=[pltpu.VMEM((rows, depth), BF), pltpu.SemaphoreType.DMA],
        compiler_params=pltpu.CompilerParams(vmem_limit_bytes=12 * MIB),
        name="projection",
    )(*got, out_proj, in_hbm(weight))


def expert_kernel(xlen, ylen, *refs):
    count = 2 * (xlen + ylen)
    pieces = refs[:count]
    gate, up, down_hbm = refs[count : count + 3]
    outs = refs[count + 3 : 2 * count + 3]
    x, table, down, act, sem = refs[2 * count + 3 :]
    own = lax.axis_index("dp") * lax.axis_size("tensor") + lax.axis_index("tensor")
    block = x.shape[0] // (2 * xlen * ylen)
    _, width, hidden = gate.shape
    middle = width // 2
    fsize = 256
    dsize = 1024
    dchunks = width // dsize

    def down_copy(i):
        cols = pl.ds(i * dsize, dsize)
        return pltpu.make_async_copy(down_hbm.at[0, :, cols], down.at[:, cols], sem.at[i])

    halves = ([], [])
    for core in range(2):
        for iy in range(ylen):
            for ix in range(xlen):
                row = ((core * ylen + iy) * xlen + ix) * block
                first = core * (xlen + ylen)
                halves[0].append((first + iy, ix * block, row))
                halves[1].append((first + ylen + ix, iy * block, row))

    for i in range(dchunks):
        down_copy(i).start()
    for i, row, there in halves[0]:
        x[there : there + block, :middle] = pieces[i][row : row + block, :]
    for i, row, there in halves[1]:
        x[there : there + block, middle:] = pieces[i][row : row + block, :middle]
        table[there : there + block, :] = pieces[i][row : row + block, middle:]
    tables = table[...].astype(F32)
    weight = jnp.sum(jnp.where(iota(tables.shape, 1) == own, tables, 0.0), axis=1, keepdims=True)
    for i in range(hidden // fsize):
        cols = slice(i * fsize, (i + 1) * fsize)
        g = matmul(x[...], gate[0, :, cols])
        u = matmul(x[...], up[0, :, cols])
        act[:, cols] = (g / (1.0 + jnp.exp(-g)) * u).astype(BF)
    for i in range(dchunks):
        down_copy(i).wait()
        result = matmul(act[...], down[:, i * dsize : (i + 1) * dsize])
        result = jnp.where(weight == 0.0, 0.0, result * weight).astype(BF)
        half, start = divmod(i * dsize, middle)
        for k, row, there in halves[half]:
            outs[k][row : row + block, start : start + dsize] = result[there : there + block]


def experts(pieces, expert_gate, expert_up, expert_down, xlen, ylen):
    count = len(pieces)
    _, width, hidden = expert_gate.shape
    middle = width // 2
    vmem = pl.BlockSpec(memory_space=pltpu.VMEM)
    every = 2 * ylen * pieces[0].shape[0]
    lanes = pieces[-1].shape[1] - middle
    return pl.pallas_call(
        functools.partial(expert_kernel, xlen, ylen),
        out_shape=tuple(jax.ShapeDtypeStruct((p.shape[0], middle), BF) for p in pieces),
        in_specs=[vmem] * (count + 2) + [pl.BlockSpec(memory_space=pltpu.HBM)],
        out_specs=(vmem,) * count,
        scratch_shapes=[
            pltpu.VMEM((every, width), BF),
            pltpu.VMEM((every, lanes), BF),
            pltpu.VMEM((hidden, width), BF),
            pltpu.VMEM((every, hidden), BF),
            pltpu.SemaphoreType.DMA((width // 1024,)),
        ],
        compiler_params=pltpu.CompilerParams(vmem_limit_bytes=(16 + every // 32) * MIB),
        name="experts",
    )(*pieces, expert_gate, expert_up, in_hbm(expert_down))


class Plan:
    def __init__(self, dp, tensor):
        self.z = min(4, dp)
        self.x = dp // self.z
        self.y = tensor // 2
        self.count = dp * tensor
        self.flip = {"c": 1, "y": 2, "x": tensor, "z": tensor * self.x}
        self.length = {"c": 2, "y": self.y, "x": self.x, "z": self.z}

    def swap(self, value, name, j=1):
        flip = j * self.flip[name]
        return lax.ppermute(value, ("dp", "tensor"), [(i, i ^ flip) for i in range(self.count)])

    def gather(self, value, name):
        far_first = [self.swap(value, name, j) for j in reversed(range(1, self.length[name]))]
        return far_first[::-1]

    def reduce(self, values, name):
        far_first = [
            self.swap(values[j].astype(BF), name, j) for j in reversed(range(1, len(values)))
        ]
        return total_of([values[0]] + far_first)


def total_of(values):
    return functools.reduce(jnp.add, [v.astype(F32) for v in values])


def shards(
    queries,
    new_keys,
    new_values,
    key_cache,
    value_cache,
    lengths,
    residual_in,
    query_gain,
    key_gain,
    out_proj,
    norm_gain,
    expert_ids,
    gate_weights,
    expert_gate,
    expert_up,
    expert_down,
):
    tensor = lax.axis_size("tensor")
    dp = lax.axis_size("dp")
    plan = Plan(dp, tensor)
    share, width = residual_in.shape
    middle = width // 2
    lanes = -(-dp * tensor // LANES) * LANES

    local, table, out_proj, expert_gate = attention(
        lengths,
        queries,
        new_keys,
        new_values,
        key_cache,
        value_cache,
        query_gain,
        key_gain,
        expert_ids,
        gate_weights,
        tensor,
        lanes,
        (out_proj, expert_gate),
    )
    got = [plan.swap(local[j], "c", j) for j in reversed(range(1, tensor))]
    got = [local[0]] + got[::-1]
    partial, expert_up = projection(got, out_proj, share, expert_up)
    pair = total_of([partial[0], plan.swap(partial[1], "c")])
    projected = plan.reduce(list(pair), "y")
    hidden = residual_in.astype(F32) + projected
    normed = rms_scale(hidden, norm_gain).astype(BF)

    mine = jnp.concatenate([normed, table], axis=1)
    column = jnp.concatenate([mine] + plan.gather(mine, "z"))
    halves = (column[:, :middle], column[:, middle:])
    orders = ("xy", "yx")
    early = [
        jnp.concatenate([half] + plan.gather(half, order[0]))
        for half, order in zip(halves, orders)
    ]
    pieces = []
    for half, order in zip(early, orders):
        pieces += [half] + plan.gather(half, order[1])
    pieces = pieces + [plan.swap(piece, "c") for piece in pieces]

    results = experts(pieces, expert_gate, expert_up, expert_down, plan.x, plan.y)

    half = len(results) // 2
    sums = [total_of([results[i], plan.swap(results[half + i], "c")]) for i in range(half)]
    halves = (sums[: plan.y], sums[plan.y :])
    early = [plan.reduce(half, order[1]) for half, order in zip(halves, orders)]
    column = [
        plan.reduce(list(half.reshape(-1, plan.z * share, middle)), order[0])
        for half, order in zip(early, orders)
    ]
    column = jnp.concatenate(column, axis=1).reshape(plan.z, share, width)
    moe_sum = plan.reduce(list(column), "z")
    return (hidden + moe_sum).astype(BF)


def solution(mesh):
    return jax.shard_map(
        shards,
        mesh=mesh,
        in_specs=(
            P("dp", None, None),
            P("dp", None, None),
            P("dp", None, None),
            P("dp", None, "tensor", None),
            P("dp", None, "tensor", None),
            P("dp"),
            P(("dp", "tensor"), None),
            P(),
            P(),
            P("tensor", None),
            P(),
            P(("dp", "tensor"), None),
            P(("dp", "tensor"), None),
            P(("dp", "tensor"), None, None),
            P(("dp", "tensor"), None, None),
            P(("dp", "tensor"), None, None),
        ),
        out_specs=P(("dp", "tensor"), None),
        check_vma=False,
    )
```

time: 109 us -> 80.5 us (0.74)
  blocking collectives: 24.2 us -> 0 us
  local copies, waits for them, and re-layouts: 9.94 us -> 0.1 us
  starting transfers between devices: 19.4 us -> 24.8 us
  waiting for transfers between devices: 34.4 us -> 37.9 us
  Pallas kernels: 18.5 us -> 16.1 us
    all_to_all x2 -> x0, blocking collectives: 24.2 us -> none  [trade_z(): lax.all_to_all(value, 'dp', split_axis=0, concat_axis=0, axis_index_group...]
    ppermute x10 -> x27, waiting for transfers between devices: 22.3 us -> 37.9 us  [swap(): lax.ppermute(value, ('dp', 'tensor'), [(i, i ^ flip) for i in range(self....]
    ppermute x10 -> x27, starting transfers between devices: 11.7 us -> 24.8 us  [swap(): lax.ppermute(value, ('dp', 'tensor'), [(i, i ^ flip) for i in range(self....]
    all_to_all x2 -> x0, waiting for transfers between devices: 12.1 us -> none  [the longest x1 6.27 us: shards(): lax.all_to_all(local, 'tensor', split_axis=0, concat_axis=0, tiled=True)]
    unnamed x26 -> x4, local copies, waits for them, and re-layouts: 9.83 us -> 0.01 us
    all_to_all x2 -> x0, starting transfers between devices: 7.65 us -> none  [the longest x1 4.24 us: shards(): lax.all_to_all(local, 'tensor', split_axis=0, concat_axis=0, tiled=True)]
    pallas_call x3, Pallas kernels: 18.5 us -> 16.1 us  [the longest x1 7.05 us: experts(): pl.pallas_call(functools.partial(expert_kernel, xlen, ylen), out_shape=tu...]
  transfers between devices with their start and end apart: 12 -> 27, of which waited for: 10 -> 19; matrix products, arithmetic and copies ran while one was open for 1% -> 1% of each run, Pallas kernels for 0% -> 0%
where the time goes in v3:
time: 80.5 us; the launch traced here: 80.4 us
  waiting for transfers between devices  37.9 us (47%)
  starting transfers between devices  24.8 us (31%)
  Pallas kernels  16.1 us (20%)
  other arithmetic  1.42 us (2%)
    ppermute x27, waiting for transfers between devices, swap(): lax.ppermute(value, ('dp', 'tensor'), [(i, i ^ flip) for i in range(self....  37.9 us
    ppermute x27, starting transfers between devices, swap(): lax.ppermute(value, ('dp', 'tensor'), [(i, i ^ flip) for i in range(self....  24.8 us
    pallas_call x1, Pallas kernels, experts(): pl.pallas_call(functools.partial(expert_kernel, xlen, ylen), out_shape=tu...  7.05 us
    pallas_call x1, Pallas kernels, attention(): pl.pallas_call(attention_kernel, out_shape=(jax.ShapeDtypeStruct((parts,...  5.78 us
    pallas_call x1, Pallas kernels, projection(): pl.pallas_call(functools.partial(projection_kernel, parts), out_shape=(ja...  3.22 us
  transfers between devices with their start and end apart: 27, of which 19 were waited for; matrix products, arithmetic and copies ran while one was open for 1% of the time, Pallas kernels for 0%

profile of v3, /device:TPU:0, one launch (start us, length us, event | category | flops | bytes accessed | tf_op | source)
XLA Modules:
  0.0 80.4 jit_solution(2372380790665985764)
XLA Ops:
  0.0 5.8 %attention.1 = (bf16[4,32,1152]{2,1,0:T(8,128)(2,1)S(1)}, bf16[8,128]{1,0:T(8,128)(2,1)S(1)}, bf16[1024,4096]{1,0:T(8,128)(2,1)S(1)}, bf16[1,4096,768]{2,1,0:T(8,128)(2,1)S(1)}) custom-call(s32[32]{0:T(128)} %len_hbm.1, bf16[32,32,128]{2,1,0:T(8,128)(2,1)} %q_hbm.1, bf16[32,2,128]{2,1,0:T(2,128)(2,1)} %nk_hbm.1, bf16[32,2,128]{2,1,0:T(2,128)(2,1)} %nv_hbm.1, ...), custom_call_target="tpu_custom_call" | custom-call | tf_op jit(solution)/shard_map/attention/pallas_call | solution.py:192
  5.8 2.5 %collective-permute-start.2 = (bf16[32,1152]{1,0:T(8,128)(2,1)S(1)}, bf16[32,1152]{1,0:T(8,128)(2,1)S(1)}, u32[]{:S(2)}, u32[]{:S(2)}) collective-permute-start(bf16[32,1152]{1,0:T(8,128)(2,1)S(1)} %get-tuple-element.33), channel_id=1, source_target_pairs={{0,3},{1,2},{2,1},{3,0},{4,7},{5,6},{6,5},{7,4},{8,11},{9,10},{10,... | collective-permute-start | bytes 221192 | tf_op jit(solution)/shard_map/ppermute | solution.py:354
  9.0 2.0 %collective-permute-done.2.refs_3_ = bf16[32,1152]{1,0:T(8,128)(2,1)S(1)} collective-permute-done((bf16[32,1152]{1,0:T(8,128)(2,1)S(1)}, bf16[32,1152]{1,0:T(8,128)(2,1)S(1)}, u32[]{:S(2)}, u32[]{:S(2)}) %collective-permute-start.2) | collective-permute-done | bytes 73760 | tf_op jit(solution)/shard_map/ppermute | solution.py:354
  11.0 2.2 %collective-permute-done.1.refs_2_ = bf16[32,1152]{1,0:T(8,128)(2,1)S(1)} collective-permute-done((bf16[32,1152]{1,0:T(8,128)(2,1)S(1)}, bf16[32,1152]{1,0:T(8,128)(2,1)S(1)}, u32[]{:S(2)}, u32[]{:S(2)}) %collective-permute-start.1) | collective-permute-done | bytes 73760 | tf_op jit(solution)/shard_map/ppermute | solution.py:354
  13.2 3.2 %projection.1 = (bf16[2,2,8,4096]{3,2,1,0:T(8,128)(2,1)S(1)}, bf16[1,4096,768]{2,1,0:T(8,128)(2,1)S(1)}) custom-call(bf16[32,1152]{1,0:T(8,128)(2,1)S(1)} %get-tuple-element.36.refs_0_, bf16[32,1152]{1,0:T(8,128)(2,1)S(1)} %collective-permute-done.refs_1_, bf16[32,1152]{1,0:T(8,128)(2,1)S(1)} %collective-permute-done.1.refs_2_, ...), custom_call_target="tpu_custom_call" | custom-call | tf_op jit(solution)/shard_map/projection/pallas_call | solution.py:255
  17.9 1.9 %collective-permute-start.4 = (bf16[8,4096]{1,0:T(8,128)(2,1)S(1)}, bf16[8,4096]{1,0:T(8,128)(2,1)S(1)}, u32[]{:S(2)}, u32[]{:S(2)}) collective-permute-start(bf16[8,4096]{1,0:T(8,128)(2,1)S(1)} %fusion.9), channel_id=1, source_target_pairs={{0,2},{1,3},{2,0},{3,1},{4,6},{5,7},{6,4},{7,5},{8,10},{9,11},{10,... | collective-permute-start | bytes 196616 | tf_op jit(solution)/shard_map/ppermute | solution.py:354
  19.8 2.4 %collective-permute-done.4 = bf16[8,4096]{1,0:T(8,128)(2,1)S(1)} collective-permute-done((bf16[8,4096]{1,0:T(8,128)(2,1)S(1)}, bf16[8,4096]{1,0:T(8,128)(2,1)S(1)}, u32[]{:S(2)}, u32[]{:S(2)}) %collective-permute-start.4) | collective-permute-done | bytes 65568 | tf_op jit(solution)/shard_map/ppermute | solution.py:354
  22.5 4.0 %collective-permute-start.7 = (bf16[8,4224]{1,0:T(8,128)(2,1)S(1)}, bf16[8,4224]{1,0:T(8,128)(2,1)S(1)}, u32[]{:S(2)}, u32[]{:S(2)}) collective-permute-start(bf16[8,4224]{1,0:T(8,128)(2,1)S(1)} %pad_maximum_fusion.8), channel_id=1, source_target_pairs={{0,24},{1,25},{2,26},{3,27},{4,28},{5,29},{6,30},{7,31},{8,16},{9,... | collective-permute-start | bytes 202760 | tf_op jit(solution)/shard_map/ppermute | solution.py:354
  27.1 2.1 %collective-permute-done.7 = bf16[8,4224]{1,0:T(8,128)(2,1)S(1)} collective-permute-done((bf16[8,4224]{1,0:T(8,128)(2,1)S(1)}, bf16[8,4224]{1,0:T(8,128)(2,1)S(1)}, u32[]{:S(2)}, u32[]{:S(2)}) %collective-permute-start.7) | collective-permute-done | bytes 67616 | tf_op jit(solution)/shard_map/ppermute | solution.py:354
  29.2 2.6 %collective-permute-done.6 = bf16[8,4224]{1,0:T(8,128)(2,1)S(1)} collective-permute-done((bf16[8,4224]{1,0:T(8,128)(2,1)S(1)}, bf16[8,4224]{1,0:T(8,128)(2,1)S(1)}, u32[]{:S(2)}, u32[]{:S(2)}) %collective-permute-start.6) | collective-permute-done | bytes 67616 | tf_op jit(solution)/shard_map/ppermute | solution.py:354
  31.9 1.6 %collective-permute-start.10 = (bf16[32,2176]{1,0:T(8,128)(2,1)S(1)}, bf16[32,2176]{1,0:T(8,128)(2,1)S(1)}, u32[]{:S(2)}, u32[]{:S(2)}) collective-permute-start(bf16[32,2176]{1,0:T(8,128)(2,1)S(1)} %pad_maximum_fusion.3), channel_id=1, source_target_pairs={{0,2},{1,3},{2,0},{3,1},{4,6},{5,7},{6,4},{7,5},{8,10},{9,11},{10,... | collective-permute-start | bytes 417800 | tf_op jit(solution)/shard_map/ppermute | solution.py:354
  33.5 1.6 %collective-permute-start.8 = (bf16[32,2048]{1,0:T(8,128)(2,1)S(1)}, bf16[32,2048]{1,0:T(8,128)(2,1)S(1)}, u32[]{:S(2)}, u32[]{:S(2)}) collective-permute-start(bf16[32,2048]{1,0:T(8,128)(2,1)S(1)} %pad_maximum_fusion.7), channel_id=1, source_target_pairs={{0,4},{1,5},{2,6},{3,7},{4,0},{5,1},{6,2},{7,3},{8,12},{9,13},{10,... | collective-permute-start | bytes 393224 | tf_op jit(solution)/shard_map/ppermute | solution.py:354
  35.1 2.0 %collective-permute-done.10 = bf16[32,2176]{1,0:T(8,128)(2,1)S(1)} collective-permute-done((bf16[32,2176]{1,0:T(8,128)(2,1)S(1)}, bf16[32,2176]{1,0:T(8,128)(2,1)S(1)}, u32[]{:S(2)}, u32[]{:S(2)}) %collective-permute-start.10) | collective-permute-done | bytes 139296 | tf_op jit(solution)/shard_map/ppermute | solution.py:354
  37.0 1.6 %collective-permute-start.11 = (bf16[64,2176]{1,0:T(8,128)(2,1)S(1)}, bf16[64,2176]{1,0:T(8,128)(2,1)S(1)}, u32[]{:S(2)}, u32[]{:S(2)}) collective-permute-start(bf16[64,2176]{1,0:T(8,128)(2,1)S(1)} %pad_maximum_fusion.1.refs_2_), channel_id=1, source_target_pairs={{0,4},{1,5},{2,6},{3,7},{4,0},{5,1},{6,2},{7,3},{8,12},{9,13},{10,... | collective-permute-start | bytes 835592 | tf_op jit(solution)/shard_map/ppermute | solution.py:354
  40.2 4.3 %collective-permute-done.11.refs_3_ = bf16[64,2176]{1,0:T(8,128)(2,1)S(1)} collective-permute-done((bf16[64,2176]{1,0:T(8,128)(2,1)S(1)}, bf16[64,2176]{1,0:T(8,128)(2,1)S(1)}, u32[]{:S(2)}, u32[]{:S(2)}) %collective-permute-start.11) | collective-permute-done | bytes 278560 | tf_op jit(solution)/shard_map/ppermute | solution.py:354
  47.8 7.0 %experts.1 = (bf16[64,2048]{1,0:T(8,128)(2,1)S(1)}, bf16[64,2048]{1,0:T(8,128)(2,1)S(1)}, bf16[64,2048]{1,0:T(8,128)(2,1)S(1)}, bf16[64,2048]{1,0:T(8,128)(2,1)S...) custom-call(bf16[64,2048]{1,0:T(8,128)(2,1)S(1)} %pad_maximum_fusion, ...), custom_call_target="tpu_custom_call" | custom-call | tf_op jit(solution)/shard_map/experts/pallas_call | solution.py:326
  57.7 1.6 %collective-permute-start.22 = (bf16[64,2048]{1,0:T(8,128)(2,1)S(1)}, bf16[64,2048]{1,0:T(8,128)(2,1)S(1)}, u32[]{:S(2)}, u32[]{:S(2)}) collective-permute-start(bf16[64,2048]{1,0:T(8,128)(2,1)S(1)} %add_convert_fusion), channel_id=1, source_target_pairs={{0,4},{1,5},{2,6},{3,7},{4,0},{5,1},{6,2},{7,3},{8,12},{9,13},{10,... | collective-permute-start | bytes 786440 | tf_op jit(solution)/shard_map/ppermute | solution.py:354
  59.2 5.7 %collective-permute-done.18 = bf16[64,2048]{1,0:T(8,128)(2,1)S(1)} collective-permute-done((bf16[64,2048]{1,0:T(8,128)(2,1)S(1)}, bf16[64,2048]{1,0:T(8,128)(2,1)S(1)}, u32[]{:S(2)}, u32[]{:S(2)}) %collective-permute-start.18) | collective-permute-done | bytes 262176 | tf_op jit(solution)/shard_map/ppermute | solution.py:354
  65.1 1.6 %collective-permute-start.19 = (bf16[32,2048]{1,0:T(8,128)(2,1)S(1)}, bf16[32,2048]{1,0:T(8,128)(2,1)S(1)}, u32[]{:S(2)}, u32[]{:S(2)}) collective-permute-start(bf16[32,2048]{1,0:T(8,128)(2,1)S(1)} %unstack.100), channel_id=1, source_target_pairs={{0,4},{1,5},{2,6},{3,7},{4,0},{5,1},{6,2},{7,3},{8,12},{9,13},{10,... | collective-permute-start | bytes 393224 | tf_op jit(solution)/shard_map/ppermute | solution.py:354
  67.1 3.0 %collective-permute-done.19 = bf16[32,2048]{1,0:T(8,128)(2,1)S(1)} collective-permute-done((bf16[32,2048]{1,0:T(8,128)(2,1)S(1)}, bf16[32,2048]{1,0:T(8,128)(2,1)S(1)}, u32[]{:S(2)}, u32[]{:S(2)}) %collective-permute-start.19) | collective-permute-done | bytes 131104 | tf_op jit(solution)/shard_map/ppermute | solution.py:354
  70.1 1.7 %collective-permute-done.23 = bf16[32,2048]{1,0:T(8,128)(2,1)S(1)} collective-permute-done((bf16[32,2048]{1,0:T(8,128)(2,1)S(1)}, bf16[32,2048]{1,0:T(8,128)(2,1)S(1)}, u32[]{:S(2)}, u32[]{:S(2)}) %collective-permute-start.23) | collective-permute-done | bytes 131104 | tf_op jit(solution)/shard_map/ppermute | solution.py:354
  71.9 2.5 %collective-permute-start.24 = (bf16[8,4096]{1,0:T(8,128)(2,1)S(1)}, bf16[8,4096]{1,0:T(8,128)(2,1)S(1)}, u32[]{:S(2)}, u32[]{:S(2)}) collective-permute-start(bf16[8,4096]{1,0:T(8,128)(2,1)S(1)} %get-tuple-element.37), channel_id=1, source_target_pairs={{0,24},{1,25},{2,26},{3,27},{4,28},{5,29},{6,30},{7,31},{8,16},{9,... | collective-permute-start | bytes 196616 | tf_op jit(solution)/shard_map/ppermute | solution.py:354
  74.4 1.9 %collective-permute-start.25 = (bf16[8,4096]{1,0:T(8,128)(2,1)S(1)}, bf16[8,4096]{1,0:T(8,128)(2,1)S(1)}, u32[]{:S(2)}, u32[]{:S(2)}) collective-permute-start(bf16[8,4096]{1,0:T(8,128)(2,1)S(1)} %get-tuple-element.39), channel_id=1, source_target_pairs={{0,16},{1,17},{2,18},{3,19},{4,20},{5,21},{6,22},{7,23},{8,24},{9,... | collective-permute-start | bytes 196616 | tf_op jit(solution)/shard_map/ppermute | solution.py:354
  76.3 2.1 %collective-permute-done.24 = bf16[8,4096]{1,0:T(8,128)(2,1)S(1)} collective-permute-done((bf16[8,4096]{1,0:T(8,128)(2,1)S(1)}, bf16[8,4096]{1,0:T(8,128)(2,1)S(1)}, u32[]{:S(2)}, u32[]{:S(2)}) %collective-permute-start.24) | collective-permute-done | bytes 65568 | tf_op jit(solution)/shard_map/ppermute | solution.py:354
  (60 shorter events, 13.4 us)
Async XLA Ops:
  5.8 5.1 %collective-permute-start.2 = (bf16[32,1152]{1,0:T(8,128)(2,1)S(1)}, bf16[32,1152]{1,0:T(8,128)(2,1)S(1)}, u32[]{:S(2)}, u32[]{:S(2)}) collective-permute-start(bf16[32,1152]{1,0:T(8,128)(2,1)S(1)} %get-tuple-element.33), channel_id=1, source_target_pairs={{0,3},{1,2},{2,1},{3,0},{4,7},{5,6},{6,5},{7,4},{8,11},{9,10},{10,... | collective-permute-start | bytes 221192 | tf_op jit(solution)/shard_map/ppermute | solution.py:354
  8.3 4.8 %collective-permute-start.1 = (bf16[32,1152]{1,0:T(8,128)(2,1)S(1)}, bf16[32,1152]{1,0:T(8,128)(2,1)S(1)}, u32[]{:S(2)}, u32[]{:S(2)}) collective-permute-start(bf16[32,1152]{1,0:T(8,128)(2,1)S(1)} %get-tuple-element.34), channel_id=1, source_target_pairs={{0,2},{1,3},{2,0},{3,1},{4,6},{5,7},{6,4},{7,5},{8,10},{9,11},{10,... | collective-permute-start | bytes 221192 | tf_op jit(solution)/shard_map/ppermute | solution.py:354
  8.9 4.2 %collective-permute-start = (bf16[32,1152]{1,0:T(8,128)(2,1)S(1)}, bf16[32,1152]{1,0:T(8,128)(2,1)S(1)}, u32[]{:S(2)}, u32[]{:S(2)}) collective-permute-start(bf16[32,1152]{1,0:T(8,128)(2,1)S(1)} %get-tuple-element.35), channel_id=1, source_target_pairs={{0,1},{1,0},{2,3},{3,2},{4,5},{5,4},{6,7},{7,6},{8,9},{9,8},{10,11... | collective-permute-start | bytes 221192 | tf_op jit(solution)/shard_map/ppermute | solution.py:354
  17.9 4.3 %collective-permute-start.4 = (bf16[8,4096]{1,0:T(8,128)(2,1)S(1)}, bf16[8,4096]{1,0:T(8,128)(2,1)S(1)}, u32[]{:S(2)}, u32[]{:S(2)}) collective-permute-start(bf16[8,4096]{1,0:T(8,128)(2,1)S(1)} %fusion.9), channel_id=1, source_target_pairs={{0,2},{1,3},{2,0},{3,1},{4,6},{5,7},{6,4},{7,5},{8,10},{9,11},{10,... | collective-permute-start | bytes 196616 | tf_op jit(solution)/shard_map/ppermute | solution.py:354
  22.5 6.8 %collective-permute-start.7 = (bf16[8,4224]{1,0:T(8,128)(2,1)S(1)}, bf16[8,4224]{1,0:T(8,128)(2,1)S(1)}, u32[]{:S(2)}, u32[]{:S(2)}) collective-permute-start(bf16[8,4224]{1,0:T(8,128)(2,1)S(1)} %pad_maximum_fusion.8), channel_id=1, source_target_pairs={{0,24},{1,25},{2,26},{3,27},{4,28},{5,29},{6,30},{7,31},{8,16},{9,... | collective-permute-start | bytes 202760 | tf_op jit(solution)/shard_map/ppermute | solution.py:354
  26.5 5.4 %collective-permute-start.6 = (bf16[8,4224]{1,0:T(8,128)(2,1)S(1)}, bf16[8,4224]{1,0:T(8,128)(2,1)S(1)}, u32[]{:S(2)}, u32[]{:S(2)}) collective-permute-start(bf16[8,4224]{1,0:T(8,128)(2,1)S(1)} %pad_maximum_fusion.8), channel_id=1, source_target_pairs={{0,16},{1,17},{2,18},{3,19},{4,20},{5,21},{6,22},{7,23},{8,24},{9,... | collective-permute-start | bytes 202760 | tf_op jit(solution)/shard_map/ppermute | solution.py:354
  26.5 5.4 %collective-permute-start.5 = (bf16[8,4224]{1,0:T(8,128)(2,1)S(1)}, bf16[8,4224]{1,0:T(8,128)(2,1)S(1)}, u32[]{:S(2)}, u32[]{:S(2)}) collective-permute-start(bf16[8,4224]{1,0:T(8,128)(2,1)S(1)} %pad_maximum_fusion.8), channel_id=1, source_target_pairs={{0,8},{1,9},{2,10},{3,11},{4,12},{5,13},{6,14},{7,15},{8,0},{9,1},... | collective-permute-start | bytes 202760 | tf_op jit(solution)/shard_map/ppermute | solution.py:354
  31.9 5.1 %collective-permute-start.10 = (bf16[32,2176]{1,0:T(8,128)(2,1)S(1)}, bf16[32,2176]{1,0:T(8,128)(2,1)S(1)}, u32[]{:S(2)}, u32[]{:S(2)}) collective-permute-start(bf16[32,2176]{1,0:T(8,128)(2,1)S(1)} %pad_maximum_fusion.3), channel_id=1, source_target_pairs={{0,2},{1,3},{2,0},{3,1},{4,6},{5,7},{6,4},{7,5},{8,10},{9,11},{10,... | collective-permute-start | bytes 417800 | tf_op jit(solution)/shard_map/ppermute | solution.py:354
  33.5 6.3 %collective-permute-start.8 = (bf16[32,2048]{1,0:T(8,128)(2,1)S(1)}, bf16[32,2048]{1,0:T(8,128)(2,1)S(1)}, u32[]{:S(2)}, u32[]{:S(2)}) collective-permute-start(bf16[32,2048]{1,0:T(8,128)(2,1)S(1)} %pad_maximum_fusion.7), channel_id=1, source_target_pairs={{0,4},{1,5},{2,6},{3,7},{4,0},{5,1},{6,2},{7,3},{8,12},{9,13},{10,... | collective-permute-start | bytes 393224 | tf_op jit(solution)/shard_map/ppermute | solution.py:354
  37.0 7.5 %collective-permute-start.11 = (bf16[64,2176]{1,0:T(8,128)(2,1)S(1)}, bf16[64,2176]{1,0:T(8,128)(2,1)S(1)}, u32[]{:S(2)}, u32[]{:S(2)}) collective-permute-start(bf16[64,2176]{1,0:T(8,128)(2,1)S(1)} %pad_maximum_fusion.1.refs_2_), channel_id=1, source_target_pairs={{0,4},{1,5},{2,6},{3,7},{4,0},{5,1},{6,2},{7,3},{8,12},{9,13},{10,... | collective-permute-start | bytes 835592 | tf_op jit(solution)/shard_map/ppermute | solution.py:354
  39.8 6.4 %collective-permute-start.9 = (bf16[64,2048]{1,0:T(8,128)(2,1)S(1)}, bf16[64,2048]{1,0:T(8,128)(2,1)S(1)}, u32[]{:S(2)}, u32[]{:S(2)}) collective-permute-start(bf16[64,2048]{1,0:T(8,128)(2,1)S(1)} %pad_maximum_fusion.2.refs_0_), channel_id=1, source_target_pairs={{0,2},{1,3},{2,0},{3,1},{4,6},{5,7},{6,4},{7,5},{8,10},{9,11},{10,... | collective-permute-start | bytes 786440 | tf_op jit(solution)/shard_map/ppermute | solution.py:354
  40.2 6.2 %collective-permute-start.14 = (bf16[64,2176]{1,0:T(8,128)(2,1)S(1)}, bf16[64,2176]{1,0:T(8,128)(2,1)S(1)}, u32[]{:S(2)}, u32[]{:S(2)}) collective-permute-start(bf16[64,2176]{1,0:T(8,128)(2,1)S(1)} %pad_maximum_fusion.1.refs_2_), channel_id=1, source_target_pairs={{0,1},{1,0},{2,3},{3,2},{4,5},{5,4},{6,7},{7,6},{8,9},{9,8},{10,11... | collective-permute-start | bytes 835592 | tf_op jit(solution)/shard_map/ppermute | solution.py:354
  44.5 3.3 %collective-permute-start.15 = (bf16[64,2176]{1,0:T(8,128)(2,1)S(1)}, bf16[64,2176]{1,0:T(8,128)(2,1)S(1)}, u32[]{:S(2)}, u32[]{:S(2)}) collective-permute-start(bf16[64,2176]{1,0:T(8,128)(2,1)S(1)} %collective-permute-done.11.refs_3_), channel_id=1, source_target_pairs={{0,1},{1,0},{2,3},{3,2},{4,5},{5,4},{6,7},{7,6},{8,9},{9,8},{10,11... | collective-permute-start | bytes 835592 | tf_op jit(solution)/shard_map/ppermute | solution.py:354
  44.5 1.9 %collective-permute-start.12 = (bf16[64,2048]{1,0:T(8,128)(2,1)S(1)}, bf16[64,2048]{1,0:T(8,128)(2,1)S(1)}, u32[]{:S(2)}, u32[]{:S(2)}) collective-permute-start(bf16[64,2048]{1,0:T(8,128)(2,1)S(1)} %pad_maximum_fusion.2.refs_0_), channel_id=1, source_target_pairs={{0,1},{1,0},{2,3},{3,2},{4,5},{5,4},{6,7},{7,6},{8,9},{9,8},{10,11... | collective-permute-start | bytes 786440 | tf_op jit(solution)/shard_map/ppermute | solution.py:354
  55.1 4.2 %collective-permute-start.16 = (bf16[64,2048]{1,0:T(8,128)(2,1)S(1)}, bf16[64,2048]{1,0:T(8,128)(2,1)S(1)}, u32[]{:S(2)}, u32[]{:S(2)}) collective-permute-start(bf16[64,2048]{1,0:T(8,128)(2,1)S(1)} %get-tuple-element.26), channel_id=1, source_target_pairs={{0,1},{1,0},{2,3},{3,2},{4,5},{5,4},{6,7},{7,6},{8,9},{9,8},{10,11... | collective-permute-start | bytes 786440 | tf_op jit(solution)/shard_map/ppermute | solution.py:354
  55.4 11.2 %collective-permute-start.20 = (bf16[64,2048]{1,0:T(8,128)(2,1)S(1)}, bf16[64,2048]{1,0:T(8,128)(2,1)S(1)}, u32[]{:S(2)}, u32[]{:S(2)}) collective-permute-start(bf16[64,2048]{1,0:T(8,128)(2,1)S(1)} %get-tuple-element.30), channel_id=1, source_target_pairs={{0,1},{1,0},{2,3},{3,2},{4,5},{5,4},{6,7},{7,6},{8,9},{9,8},{10,11... | collective-permute-start | bytes 786440 | tf_op jit(solution)/shard_map/ppermute | solution.py:354
  55.6 2.0 %collective-permute-start.21 = (bf16[64,2048]{1,0:T(8,128)(2,1)S(1)}, bf16[64,2048]{1,0:T(8,128)(2,1)S(1)}, u32[]{:S(2)}, u32[]{:S(2)}) collective-permute-start(bf16[64,2048]{1,0:T(8,128)(2,1)S(1)} %get-tuple-element.32), channel_id=1, source_target_pairs={{0,1},{1,0},{2,3},{3,2},{4,5},{5,4},{6,7},{7,6},{8,9},{9,8},{10,11... | collective-permute-start | bytes 786440 | tf_op jit(solution)/shard_map/ppermute | solution.py:354
  56.5 8.4 %collective-permute-start.18 = (bf16[64,2048]{1,0:T(8,128)(2,1)S(1)}, bf16[64,2048]{1,0:T(8,128)(2,1)S(1)}, u32[]{:S(2)}, u32[]{:S(2)}) collective-permute-start(bf16[64,2048]{1,0:T(8,128)(2,1)S(1)} %add_convert_fusion.1), channel_id=1, source_target_pairs={{0,2},{1,3},{2,0},{3,1},{4,6},{5,7},{6,4},{7,5},{8,10},{9,11},{10,... | collective-permute-start | bytes 786440 | tf_op jit(solution)/shard_map/ppermute | solution.py:354
  57.7 9.0 %collective-permute-start.22 = (bf16[64,2048]{1,0:T(8,128)(2,1)S(1)}, bf16[64,2048]{1,0:T(8,128)(2,1)S(1)}, u32[]{:S(2)}, u32[]{:S(2)}) collective-permute-start(bf16[64,2048]{1,0:T(8,128)(2,1)S(1)} %add_convert_fusion), channel_id=1, source_target_pairs={{0,4},{1,5},{2,6},{3,7},{4,0},{5,1},{6,2},{7,3},{8,12},{9,13},{10,... | collective-permute-start | bytes 786440 | tf_op jit(solution)/shard_map/ppermute | solution.py:354
  65.1 5.0 %collective-permute-start.19 = (bf16[32,2048]{1,0:T(8,128)(2,1)S(1)}, bf16[32,2048]{1,0:T(8,128)(2,1)S(1)}, u32[]{:S(2)}, u32[]{:S(2)}) collective-permute-start(bf16[32,2048]{1,0:T(8,128)(2,1)S(1)} %unstack.100), channel_id=1, source_target_pairs={{0,4},{1,5},{2,6},{3,7},{4,0},{5,1},{6,2},{7,3},{8,12},{9,13},{10,... | collective-permute-start | bytes 393224 | tf_op jit(solution)/shard_map/ppermute | solution.py:354
  66.7 5.0 %collective-permute-start.23 = (bf16[32,2048]{1,0:T(8,128)(2,1)S(1)}, bf16[32,2048]{1,0:T(8,128)(2,1)S(1)}, u32[]{:S(2)}, u32[]{:S(2)}) collective-permute-start(bf16[32,2048]{1,0:T(8,128)(2,1)S(1)} %unstack.99), channel_id=1, source_target_pairs={{0,2},{1,3},{2,0},{3,1},{4,6},{5,7},{6,4},{7,5},{8,10},{9,11},{10,... | collective-permute-start | bytes 393224 | tf_op jit(solution)/shard_map/ppermute | solution.py:354
  71.9 6.6 %collective-permute-start.24 = (bf16[8,4096]{1,0:T(8,128)(2,1)S(1)}, bf16[8,4096]{1,0:T(8,128)(2,1)S(1)}, u32[]{:S(2)}, u32[]{:S(2)}) collective-permute-start(bf16[8,4096]{1,0:T(8,128)(2,1)S(1)} %get-tuple-element.37), channel_id=1, source_target_pairs={{0,24},{1,25},{2,26},{3,27},{4,28},{5,29},{6,30},{7,31},{8,16},{9,... | collective-permute-start | bytes 196616 | tf_op jit(solution)/shard_map/ppermute | solution.py:354
  74.3 5.3 %collective-permute-start.26 = (bf16[8,4096]{1,0:T(8,128)(2,1)S(1)}, bf16[8,4096]{1,0:T(8,128)(2,1)S(1)}, u32[]{:S(2)}, u32[]{:S(2)}) collective-permute-start(bf16[8,4096]{1,0:T(8,128)(2,1)S(1)} %get-tuple-element.38), channel_id=1, source_target_pairs={{0,8},{1,9},{2,10},{3,11},{4,12},{5,13},{6,14},{7,15},{8,0},{9,1},... | collective-permute-start | bytes 196616 | tf_op jit(solution)/shard_map/ppermute | solution.py:354
  74.4 5.3 %collective-permute-start.25 = (bf16[8,4096]{1,0:T(8,128)(2,1)S(1)}, bf16[8,4096]{1,0:T(8,128)(2,1)S(1)}, u32[]{:S(2)}, u32[]{:S(2)}) collective-permute-start(bf16[8,4096]{1,0:T(8,128)(2,1)S(1)} %get-tuple-element.39), channel_id=1, source_target_pairs={{0,16},{1,17},{2,18},{3,19},{4,20},{5,21},{6,22},{7,23},{8,24},{9,... | collective-permute-start | bytes 196616 | tf_op jit(solution)/shard_map/ppermute | solution.py:354
  (5 other events, 22.8 us)

commit v4 on v3

--- a/solution.py
+++ b/solution.py
@@ -12,6 +12,7 @@
 I32 = jnp.int32
 MIB = 1 << 20
 LANES = 128
+CAP = 3
 
 
 def rms_scale(values, gain):
@@ -266,102 +267,96 @@
     )(*got, out_proj, in_hbm(weight))
 
 
-def expert_kernel(xlen, ylen, *refs):
-    count = 2 * (xlen + ylen)
-    pieces = refs[:count]
-    gate, up, down_hbm = refs[count : count + 3]
-    outs = refs[count + 3 : 2 * count + 3]
-    x, table, down, act, sem = refs[2 * count + 3 :]
+def expert_kernel(slots, x_ref, gate, up, down_hbm, out_ref, down, xc, act, res, sem):
     own = lax.axis_index("dp") * lax.axis_size("tensor") + lax.axis_index("tensor")
-    block = x.shape[0] // (2 * xlen * ylen)
+    rows = x_ref.shape[0]
     _, width, hidden = gate.shape
-    middle = width // 2
+    padded = res.shape[0]
     fsize = 256
     dsize = 1024
-    dchunks = width // dsize
+    chunks = width // dsize
 
     def down_copy(i):
         cols = pl.ds(i * dsize, dsize)
         return pltpu.make_async_copy(down_hbm.at[0, :, cols], down.at[:, cols], sem.at[i])
 
-    halves = ([], [])
-    for core in range(2):
-        for iy in range(ylen):
-            for ix in range(xlen):
-                row = ((core * ylen + iy) * xlen + ix) * block
-                first = core * (xlen + ylen)
-                halves[0].append((first + iy, ix * block, row))
-                halves[1].append((first + ylen + ix, iy * block, row))
-
-    for i in range(dchunks):
+    for i in range(chunks):
         down_copy(i).start()
-    for i, row, there in halves[0]:
-        x[there : there + block, :middle] = pieces[i][row : row + block, :]
-    for i, row, there in halves[1]:
-        x[there : there + block, middle:] = pieces[i][row : row + block, :middle]
-        table[there : there + block, :] = pieces[i][row : row + block, middle:]
-    tables = table[...].astype(F32)
-    weight = jnp.sum(jnp.where(iota(tables.shape, 1) == own, tables, 0.0), axis=1, keepdims=True)
+    table = x_ref[:, width:]
+    pick = (iota((16, table.shape[1]), 1) == own).astype(F32).astype(BF)
+    named = matmul_t(pick, table) != 0.0
+    before = (iota((rows, rows), 0) < iota((rows, rows), 1)).astype(F32).astype(BF)
+    place = matmul(named.astype(F32).astype(BF), before)
+    place = jnp.where(named, place, -1.0)[:1]
+    take = (iota((slots, rows), 0).astype(F32) == place).astype(F32).astype(BF)
+    for i in range(chunks):
+        cols = slice(i * dsize, (i + 1) * dsize)
+        xc[:, cols] = matmul(take, x_ref[:, cols]).astype(BF)
+
+    lane = iota(table.shape, 1)
+    weight = jnp.sum(jnp.where(lane == own, table.astype(F32), 0.0), axis=1, keepdims=True)
+    named = jnp.broadcast_to((weight != 0.0).astype(F32), (rows, LANES)).astype(BF)
+    after = (iota((rows, rows), 1) < iota((rows, rows), 0)).astype(F32).astype(BF)
+    place = matmul(after, named)[:, :1]
+    spread = jnp.where(iota((rows, padded), 1).astype(F32) == place, weight, 0.0).astype(BF)
+    if padded > slots:
+        res[slots:, :] = jnp.zeros((padded - slots, dsize), BF)
+
     for i in range(hidden // fsize):
         cols = slice(i * fsize, (i + 1) * fsize)
-        g = matmul(x[...], gate[0, :, cols])
-        u = matmul(x[...], up[0, :, cols])
+        g = matmul(xc[...], gate[0, :, cols])
+        u = matmul(xc[...], up[0, :, cols])
         act[:, cols] = (g / (1.0 + jnp.exp(-g)) * u).astype(BF)
-    for i in range(dchunks):
+    for i in range(chunks):
         down_copy(i).wait()
-        result = matmul(act[...], down[:, i * dsize : (i + 1) * dsize])
-        result = jnp.where(weight == 0.0, 0.0, result * weight).astype(BF)
-        half, start = divmod(i * dsize, middle)
-        for k, row, there in halves[half]:
-            outs[k][row : row + block, start : start + dsize] = result[there : there + block]
-
-
-def experts(pieces, expert_gate, expert_up, expert_down, xlen, ylen):
-    count = len(pieces)
+        cols = slice(i * dsize, (i + 1) * dsize)
+        res[:slots, :] = matmul(act[...], down[:, cols]).astype(BF)
+        out_ref[:, cols] = matmul(spread, res[...]).astype(BF)
+
+
+def experts(x, expert_gate, expert_up, expert_down, share):
+    rows = x.shape[0]
     _, width, hidden = expert_gate.shape
-    middle = width // 2
+    slots = rows // share * CAP
     vmem = pl.BlockSpec(memory_space=pltpu.VMEM)
-    every = 2 * ylen * pieces[0].shape[0]
-    lanes = pieces[-1].shape[1] - middle
     return pl.pallas_call(
-        functools.partial(expert_kernel, xlen, ylen),
-        out_shape=tuple(jax.ShapeDtypeStruct((p.shape[0], middle), BF) for p in pieces),
-        in_specs=[vmem] * (count + 2) + [pl.BlockSpec(memory_space=pltpu.HBM)],
-        out_specs=(vmem,) * count,
+        functools.partial(expert_kernel, slots),
+        out_shape=jax.ShapeDtypeStruct((rows, width), BF),
+        in_specs=[vmem] * 3 + [pl.BlockSpec(memory_space=pltpu.HBM)],
+        out_specs=vmem,
         scratch_shapes=[
-            pltpu.VMEM((every, width), BF),
-            pltpu.VMEM((every, lanes), BF),
             pltpu.VMEM((hidden, width), BF),
-            pltpu.VMEM((every, hidden), BF),
+            pltpu.VMEM((slots, width), BF),
+            pltpu.VMEM((slots, hidden), BF),
+            pltpu.VMEM((-(-slots // LANES) * LANES, 1024), BF),
             pltpu.SemaphoreType.DMA((width // 1024,)),
         ],
-        compiler_params=pltpu.CompilerParams(vmem_limit_bytes=(16 + every // 32) * MIB),
+        compiler_params=pltpu.CompilerParams(vmem_limit_bytes=(16 + rows // 32) * MIB),
         name="experts",
-    )(*pieces, expert_gate, expert_up, in_hbm(expert_down))
+    )(x, expert_gate, expert_up, in_hbm(expert_down))
 
 
 class Plan:
     def __init__(self, dp, tensor):
-        self.z = min(4, dp)
-        self.x = dp // self.z
-        self.y = tensor // 2
+        self.zlen = min(4, dp)
+        xlen, ylen = dp // self.zlen, tensor // 2
         self.count = dp * tensor
-        self.flip = {"c": 1, "y": 2, "x": tensor, "z": tensor * self.x}
-        self.length = {"c": 2, "y": self.y, "x": self.x, "z": self.z}
-
-    def swap(self, value, name, j=1):
-        flip = j * self.flip[name]
+        self.core = 1
+        self.y = [2 * j for j in range(1, ylen)]
+        self.z = [tensor * xlen * j for j in range(1, self.zlen)]
+        self.plane = [
+            tensor * jx + 2 * jy for jx in range(xlen) for jy in range(ylen) if jx or jy
+        ]
+
+    def swap(self, value, flip):
         return lax.ppermute(value, ("dp", "tensor"), [(i, i ^ flip) for i in range(self.count)])
 
-    def gather(self, value, name):
-        far_first = [self.swap(value, name, j) for j in reversed(range(1, self.length[name]))]
-        return far_first[::-1]
-
-    def reduce(self, values, name):
-        far_first = [
-            self.swap(values[j].astype(BF), name, j) for j in reversed(range(1, len(values)))
-        ]
-        return total_of([values[0]] + far_first)
+    def swaps(self, values, flips):
+        pairs = list(zip(values, flips))[::-1]
+        return [self.swap(value.astype(BF), flip) for value, flip in pairs][::-1]
+
+    def spread(self, value, flips):
+        return self.swaps([value] * len(flips), flips)
 
 
 def total_of(values):
@@ -390,7 +385,6 @@
     dp = lax.axis_size("dp")
     plan = Plan(dp, tensor)
     share, width = residual_in.shape
-    middle = width // 2
     lanes = -(-dp * tensor // LANES) * LANES
 
     local, table, out_proj, expert_gate = attention(
@@ -408,39 +402,39 @@
         lanes,
         (out_proj, expert_gate),
     )
-    got = [plan.swap(local[j], "c", j) for j in reversed(range(1, tensor))]
-    got = [local[0]] + got[::-1]
+    got = [local[0]] + plan.swaps(list(local[1:]), list(range(1, tensor)))
     partial, expert_up = projection(got, out_proj, share, expert_up)
-    pair = total_of([partial[0], plan.swap(partial[1], "c")])
-    projected = plan.reduce(list(pair), "y")
+    pair = total_of([partial[0], plan.swap(partial[1], plan.core)])
+    projected = total_of([pair[0]] + plan.swaps(list(pair[1:]), plan.y))
     hidden = residual_in.astype(F32) + projected
     normed = rms_scale(hidden, norm_gain).astype(BF)
 
     mine = jnp.concatenate([normed, table], axis=1)
-    column = jnp.concatenate([mine] + plan.gather(mine, "z"))
-    halves = (column[:, :middle], column[:, middle:])
-    orders = ("xy", "yx")
-    early = [
-        jnp.concatenate([half] + plan.gather(half, order[0]))
-        for half, order in zip(halves, orders)
-    ]
-    pieces = []
-    for half, order in zip(early, orders):
-        pieces += [half] + plan.gather(half, order[1])
-    pieces = pieces + [plan.swap(piece, "c") for piece in pieces]
-
-    results = experts(pieces, expert_gate, expert_up, expert_down, plan.x, plan.y)
-
-    half = len(results) // 2
-    sums = [total_of([results[i], plan.swap(results[half + i], "c")]) for i in range(half)]
-    halves = (sums[: plan.y], sums[plan.y :])
-    early = [plan.reduce(half, order[1]) for half, order in zip(halves, orders)]
-    column = [
-        plan.reduce(list(half.reshape(-1, plan.z * share, middle)), order[0])
-        for half, order in zip(early, orders)
-    ]
-    column = jnp.concatenate(column, axis=1).reshape(plan.z, share, width)
-    moe_sum = plan.reduce(list(column), "z")
+    others = plan.spread(mine, plan.z)
+    near = plan.spread(mine, plan.plane)
+    far = plan.spread(jnp.concatenate(others), plan.plane)
+    pieces = [jnp.concatenate([mine] + others + near)] + far
+    x = jnp.concatenate(pieces + [plan.swap(piece, plan.core) for piece in pieces])
+
+    result = experts(x, expert_gate, expert_up, expert_down, share)
+
+    sizes = [piece.shape[0] for piece in pieces]
+    starts = [sum(sizes[:i]) for i in range(len(sizes) + 1)]
+    every = starts[-1]
+    sums = [
+        total_of(
+            [
+                result[starts[i] : starts[i + 1]],
+                plan.swap(result[every + starts[i] : every + starts[i + 1]], plan.core),
+            ]
+        )
+        for i in reversed(range(len(sizes)))
+    ][::-1]
+    blocks = sums[0].reshape(-1, share, width)
+    far = plan.swaps(sums[1:], plan.plane)
+    others = total_of([sums[0][share : plan.zlen * share]] + far).reshape(-1, share, width)
+    near = plan.swaps(list(blocks[plan.zlen :]), plan.plane)
+    moe_sum = total_of([blocks[0]] + near + plan.swaps(list(others), plan.z))
     return (hidden + moe_sum).astype(BF)
 
 

time: 80.5 us -> 78.5 us (0.975)
  waiting for transfers between devices: 37.9 us -> 33.2 us
  starting transfers between devices: 24.8 us -> 27.7 us
    ppermute x27 -> x31, waiting for transfers between devices: 37.9 us -> 33.2 us  [swap(): lax.ppermute(value, ('dp', 'tensor'), [(i, i ^ flip) for i in range(self....]
    ppermute x27 -> x31, starting transfers between devices: 24.8 us -> 27.7 us  [swap(): lax.ppermute(value, ('dp', 'tensor'), [(i, i ^ flip) for i in range(self....]
  transfers between devices with their start and end apart: 27 -> 31, of which waited for: 19 -> 17; matrix products, arithmetic and copies ran while one was open for 1% -> 1% of each run, Pallas kernels for 0% -> 0%
where the time goes in v4:
time: 78.5 us; the launch traced here: 78.4 us
  waiting for transfers between devices  33.2 us (42%)
  starting transfers between devices  27.7 us (35%)
  Pallas kernels  15.5 us (20%)
  other arithmetic  1.35 us (2%)
    ppermute x31, waiting for transfers between devices, swap(): lax.ppermute(value, ('dp', 'tensor'), [(i, i ^ flip) for i in range(self....  33.2 us
    ppermute x31, starting transfers between devices, swap(): lax.ppermute(value, ('dp', 'tensor'), [(i, i ^ flip) for i in range(self....  27.7 us
    pallas_call x1, Pallas kernels, experts(): pl.pallas_call(functools.partial(expert_kernel, slots), out_shape=jax.Sha...  6.48 us
    pallas_call x1, Pallas kernels, attention(): pl.pallas_call(attention_kernel, out_shape=(jax.ShapeDtypeStruct((parts,...  5.78 us
    pallas_call x1, Pallas kernels, projection(): pl.pallas_call(functools.partial(projection_kernel, parts), out_shape=(ja...  3.22 us
  transfers between devices with their start and end apart: 31, of which 17 were waited for; matrix products, arithmetic and copies ran while one was open for 1% of the time, Pallas kernels for 0%

profile of v4, /device:TPU:0, one launch (start us, length us, event | category | flops | bytes accessed | tf_op | source)
XLA Modules:
  0.0 78.4 jit_solution(16015528075683963754)
XLA Ops:
  0.0 5.8 %attention.1 = (bf16[4,32,1152]{2,1,0:T(8,128)(2,1)S(1)}, bf16[8,128]{1,0:T(8,128)(2,1)S(1)}, bf16[1024,4096]{1,0:T(8,128)(2,1)S(1)}, bf16[1,4096,768]{2,1,0:T(8,128)(2,1)S(1)}) custom-call(s32[32]{0:T(128)} %len_hbm.1, bf16[32,32,128]{2,1,0:T(8,128)(2,1)} %q_hbm.1, bf16[32,2,128]{2,1,0:T(2,128)(2,1)} %nk_hbm.1, bf16[32,2,128]{2,1,0:T(2,128)(2,1)} %nv_hbm.1, ...), custom_call_target="tpu_custom_call" | custom-call | tf_op jit(solution)/shard_map/attention/pallas_call | solution.py:193
  5.8 2.5 %collective-permute-start.2 = (bf16[32,1152]{1,0:T(8,128)(2,1)S(1)}, bf16[32,1152]{1,0:T(8,128)(2,1)S(1)}, u32[]{:S(2)}, u32[]{:S(2)}) collective-permute-start(bf16[32,1152]{1,0:T(8,128)(2,1)S(1)} %get-tuple-element.28), channel_id=1, source_target_pairs={{0,3},{1,2},{2,1},{3,0},{4,7},{5,6},{6,5},{7,4},{8,11},{9,10},{10,... | collective-permute-start | bytes 221192 | tf_op jit(solution)/shard_map/ppermute | solution.py:352
  9.0 2.0 %collective-permute-done.2.refs_3_ = bf16[32,1152]{1,0:T(8,128)(2,1)S(1)} collective-permute-done((bf16[32,1152]{1,0:T(8,128)(2,1)S(1)}, bf16[32,1152]{1,0:T(8,128)(2,1)S(1)}, u32[]{:S(2)}, u32[]{:S(2)}) %collective-permute-start.2) | collective-permute-done | bytes 73760 | tf_op jit(solution)/shard_map/ppermute | solution.py:352
  11.0 2.2 %collective-permute-done.1.refs_2_ = bf16[32,1152]{1,0:T(8,128)(2,1)S(1)} collective-permute-done((bf16[32,1152]{1,0:T(8,128)(2,1)S(1)}, bf16[32,1152]{1,0:T(8,128)(2,1)S(1)}, u32[]{:S(2)}, u32[]{:S(2)}) %collective-permute-start.1) | collective-permute-done | bytes 73760 | tf_op jit(solution)/shard_map/ppermute | solution.py:352
  13.2 3.2 %projection.1 = (bf16[2,2,8,4096]{3,2,1,0:T(8,128)(2,1)S(1)}, bf16[1,4096,768]{2,1,0:T(8,128)(2,1)S(1)}) custom-call(bf16[32,1152]{1,0:T(8,128)(2,1)S(1)} %get-tuple-element.31.refs_0_, bf16[32,1152]{1,0:T(8,128)(2,1)S(1)} %collective-permute-done.refs_1_, bf16[32,1152]{1,0:T(8,128)(2,1)S(1)} %collective-permute-done.1.refs_2_, ...), custom_call_target="tpu_custom_call" | custom-call | tf_op jit(solution)/shard_map/projection/pallas_call | solution.py:256
  16.5 1.3 %collective-permute-done.3 = bf16[2,8,4096]{2,1,0:T(8,128)(2,1)S(1)} collective-permute-done((bf16[2,8,4096]{2,1,0:T(8,128)(2,1)S(1)}, bf16[2,8,4096]{2,1,0:T(8,128)(2,1)S(1)}, u32[]{:S(2)}, u32[]{:S(2)}) %collective-permute-start.3) | collective-permute-done | bytes 131104 | tf_op jit(solution)/shard_map/ppermute | solution.py:352
  17.9 1.9 %collective-permute-start.4 = (bf16[8,4096]{1,0:T(8,128)(2,1)S(1)}, bf16[8,4096]{1,0:T(8,128)(2,1)S(1)}, u32[]{:S(2)}, u32[]{:S(2)}) collective-permute-start(bf16[8,4096]{1,0:T(8,128)(2,1)S(1)} %fusion.12), channel_id=1, source_target_pairs={{0,2},{1,3},{2,0},{3,1},{4,6},{5,7},{6,4},{7,5},{8,10},{9,11},{10,... | collective-permute-start | bytes 196616 | tf_op jit(solution)/shard_map/ppermute | solution.py:352
  19.8 2.4 %collective-permute-done.4 = bf16[8,4096]{1,0:T(8,128)(2,1)S(1)} collective-permute-done((bf16[8,4096]{1,0:T(8,128)(2,1)S(1)}, bf16[8,4096]{1,0:T(8,128)(2,1)S(1)}, u32[]{:S(2)}, u32[]{:S(2)}) %collective-permute-start.4) | collective-permute-done | bytes 65568 | tf_op jit(solution)/shard_map/ppermute | solution.py:352
  22.5 2.0 %collective-permute-start.5 = (bf16[8,4224]{1,0:T(8,128)(2,1)S(1)}, bf16[8,4224]{1,0:T(8,128)(2,1)S(1)}, u32[]{:S(2)}, u32[]{:S(2)}) collective-permute-start(bf16[8,4224]{1,0:T(8,128)(2,1)S(1)} %get-tuple-element.52), channel_id=1, source_target_pairs={{0,8},{1,9},{2,10},{3,11},{4,12},{5,13},{6,14},{7,15},{8,0},{9,1},... | collective-permute-start | bytes 202760 | tf_op jit(solution)/shard_map/ppermute | solution.py:352
  24.5 1.5 %collective-permute-start.9 = (bf16[8,4224]{1,0:T(8,128)(2,1)S(1)}, bf16[8,4224]{1,0:T(8,128)(2,1)S(1)}, u32[]{:S(2)}, u32[]{:S(2)}) collective-permute-start(bf16[8,4224]{1,0:T(8,128)(2,1)S(1)} %get-tuple-element.52), channel_id=1, source_target_pairs={{0,4},{1,5},{2,6},{3,7},{4,0},{5,1},{6,2},{7,3},{8,12},{9,13},{10,... | collective-permute-start | bytes 202760 | tf_op jit(solution)/shard_map/ppermute | solution.py:352
  26.0 1.5 %collective-permute-start.8 = (bf16[8,4224]{1,0:T(8,128)(2,1)S(1)}, bf16[8,4224]{1,0:T(8,128)(2,1)S(1)}, u32[]{:S(2)}, u32[]{:S(2)}) collective-permute-start(bf16[8,4224]{1,0:T(8,128)(2,1)S(1)} %get-tuple-element.52), channel_id=1, source_target_pairs={{0,2},{1,3},{2,0},{3,1},{4,6},{5,7},{6,4},{7,5},{8,10},{9,11},{10,... | collective-permute-start | bytes 202760 | tf_op jit(solution)/shard_map/ppermute | solution.py:352
  27.5 2.5 %collective-permute-start.7 = (bf16[8,4224]{1,0:T(8,128)(2,1)S(1)}, bf16[8,4224]{1,0:T(8,128)(2,1)S(1)}, u32[]{:S(2)}, u32[]{:S(2)}) collective-permute-start(bf16[8,4224]{1,0:T(8,128)(2,1)S(1)} %get-tuple-element.52), channel_id=1, source_target_pairs={{0,24},{1,25},{2,26},{3,27},{4,28},{5,29},{6,30},{7,31},{8,16},{9,... | collective-permute-start | bytes 202760 | tf_op jit(solution)/shard_map/ppermute | solution.py:352
  30.6 5.3 %collective-permute-done.6 = bf16[8,4224]{1,0:T(8,128)(2,1)S(1)} collective-permute-done((bf16[8,4224]{1,0:T(8,128)(2,1)S(1)}, bf16[8,4224]{1,0:T(8,128)(2,1)S(1)}, u32[]{:S(2)}, u32[]{:S(2)}) %collective-permute-start.6) | collective-permute-done | bytes 67616 | tf_op jit(solution)/shard_map/ppermute | solution.py:352
  36.5 1.5 %collective-permute-start.12 = (bf16[24,4224]{1,0:T(8,128)(2,1)S(1)}, bf16[24,4224]{1,0:T(8,128)(2,1)S(1)}, u32[]{:S(2)}, u32[]{:S(2)}) collective-permute-start(bf16[24,4224]{1,0:T(8,128)(2,1)S(1)} %get-tuple-element.43), channel_id=1, source_target_pairs={{0,4},{1,5},{2,6},{3,7},{4,0},{5,1},{6,2},{7,3},{8,12},{9,13},{10,... | collective-permute-start | bytes 608264 | tf_op jit(solution)/shard_map/ppermute | solution.py:352
  38.0 1.5 %collective-permute-start.11 = (bf16[24,4224]{1,0:T(8,128)(2,1)S(1)}, bf16[24,4224]{1,0:T(8,128)(2,1)S(1)}, u32[]{:S(2)}, u32[]{:S(2)}) collective-permute-start(bf16[24,4224]{1,0:T(8,128)(2,1)S(1)} %get-tuple-element.43), channel_id=1, source_target_pairs={{0,2},{1,3},{2,0},{3,1},{4,6},{5,7},{6,4},{7,5},{8,10},{9,11},{10,... | collective-permute-start | bytes 608264 | tf_op jit(solution)/shard_map/ppermute | solution.py:352
  39.6 4.4 %collective-permute-done.13 = bf16[24,4224]{1,0:T(8,128)(2,1)S(1)} collective-permute-done((bf16[24,4224]{1,0:T(8,128)(2,1)S(1)}, bf16[24,4224]{1,0:T(8,128)(2,1)S(1)}, u32[]{:S(2)}, u32[]{:S(2)}) %collective-permute-start.13) | collective-permute-done | bytes 202784 | tf_op jit(solution)/shard_map/ppermute | solution.py:352
  46.3 1.3 %collective-permute-done.15 = bf16[24,4224]{1,0:T(8,128)(2,1)S(1)} collective-permute-done((bf16[24,4224]{1,0:T(8,128)(2,1)S(1)}, bf16[24,4224]{1,0:T(8,128)(2,1)S(1)}, u32[]{:S(2)}, u32[]{:S(2)}) %collective-permute-start.15) | collective-permute-done | bytes 202784 | tf_op jit(solution)/shard_map/ppermute | solution.py:352
  47.7 6.5 %experts.1 = bf16[256,4096]{1,0:T(8,128)(2,1)S(1)} custom-call(bf16[256,4224]{1,0:T(8,128)(2,1)S(1)} %constant_dynamic-update-slice_fusion.10.x_ref, bf16[1,4096,768]{2,1,0:T(8,128)(2,1)S(1)} %get-tuple-element.15.gate, bf16[1,4096,768]{2,1,0:T(8,128)(2,1)S(1)} %get-tuple-element.16.up, bf16[1,768,4096]{2,1,0:T(8,128)(2,1)} %down_hbm.1), custom_call_target="tpu_custom_call" | custom-call | tf_op jit(solution)/shard_map/experts/pallas_call | solution.py:322
  58.5 1.5 %collective-permute-start.25 = (bf16[24,4096]{1,0:T(8,128)(2,1)S(1)}, bf16[24,4096]{1,0:T(8,128)(2,1)S(1)}, u32[]{:S(2)}, u32[]{:S(2)}) collective-permute-start(bf16[24,4096]{1,0:T(8,128)(2,1)S(1)} %get-tuple-element.21), channel_id=1, source_target_pairs={{0,4},{1,5},{2,6},{3,7},{4,0},{5,1},{6,2},{7,3},{8,12},{9,13},{10,... | collective-permute-start | bytes 589832 | tf_op jit(solution)/shard_map/ppermute | solution.py:352
  62.2 6.4 %collective-permute-done.23 = bf16[24,4096]{1,0:T(8,128)(2,1)S(1)} collective-permute-done((bf16[24,4096]{1,0:T(8,128)(2,1)S(1)}, bf16[24,4096]{1,0:T(8,128)(2,1)S(1)}, u32[]{:S(2)}, u32[]{:S(2)}) %collective-permute-start.23) | collective-permute-done | bytes 196640 | tf_op jit(solution)/shard_map/ppermute | solution.py:352
  69.9 1.3 %collective-permute-start.30 = (bf16[8,4096]{1,0:T(8,128)(2,1)S(1)}, bf16[8,4096]{1,0:T(8,128)(2,1)S(1)}, u32[]{:S(2)}, u32[]{:S(2)}) collective-permute-start(bf16[8,4096]{1,0:T(8,128)(2,1)S(1)} %get-tuple-element.33), channel_id=1, source_target_pairs={{0,24},{1,25},{2,26},{3,27},{4,28},{5,29},{6,30},{7,31},{8,16},{9,... | collective-permute-start | bytes 196616 | tf_op jit(solution)/shard_map/ppermute | solution.py:352
  71.2 2.1 %collective-permute-start.29 = (bf16[8,4096]{1,0:T(8,128)(2,1)S(1)}, bf16[8,4096]{1,0:T(8,128)(2,1)S(1)}, u32[]{:S(2)}, u32[]{:S(2)}) collective-permute-start(bf16[8,4096]{1,0:T(8,128)(2,1)S(1)} %get-tuple-element.34), channel_id=1, source_target_pairs={{0,16},{1,17},{2,18},{3,19},{4,20},{5,21},{6,22},{7,23},{8,24},{9,... | collective-permute-start | bytes 196616 | tf_op jit(solution)/shard_map/ppermute | solution.py:352
  73.4 1.5 %collective-permute-done.28 = bf16[8,4096]{1,0:T(8,128)(2,1)S(1)} collective-permute-done((bf16[8,4096]{1,0:T(8,128)(2,1)S(1)}, bf16[8,4096]{1,0:T(8,128)(2,1)S(1)}, u32[]{:S(2)}, u32[]{:S(2)}) %collective-permute-start.28) | collective-permute-done | bytes 65568 | tf_op jit(solution)/shard_map/ppermute | solution.py:352
  76.0 1.6 %collective-permute-done.29 = bf16[8,4096]{1,0:T(8,128)(2,1)S(1)} collective-permute-done((bf16[8,4096]{1,0:T(8,128)(2,1)S(1)}, bf16[8,4096]{1,0:T(8,128)(2,1)S(1)}, u32[]{:S(2)}, u32[]{:S(2)}) %collective-permute-start.29) | collective-permute-done | bytes 65568 | tf_op jit(solution)/shard_map/ppermute | solution.py:352
  (74 shorter events, 14.3 us)
Async XLA Ops:
  5.8 5.1 %collective-permute-start.2 = (bf16[32,1152]{1,0:T(8,128)(2,1)S(1)}, bf16[32,1152]{1,0:T(8,128)(2,1)S(1)}, u32[]{:S(2)}, u32[]{:S(2)}) collective-permute-start(bf16[32,1152]{1,0:T(8,128)(2,1)S(1)} %get-tuple-element.28), channel_id=1, source_target_pairs={{0,3},{1,2},{2,1},{3,0},{4,7},{5,6},{6,5},{7,4},{8,11},{9,10},{10,... | collective-permute-start | bytes 221192 | tf_op jit(solution)/shard_map/ppermute | solution.py:352
  8.3 4.8 %collective-permute-start.1 = (bf16[32,1152]{1,0:T(8,128)(2,1)S(1)}, bf16[32,1152]{1,0:T(8,128)(2,1)S(1)}, u32[]{:S(2)}, u32[]{:S(2)}) collective-permute-start(bf16[32,1152]{1,0:T(8,128)(2,1)S(1)} %get-tuple-element.29), channel_id=1, source_target_pairs={{0,2},{1,3},{2,0},{3,1},{4,6},{5,7},{6,4},{7,5},{8,10},{9,11},{10,... | collective-permute-start | bytes 221192 | tf_op jit(solution)/shard_map/ppermute | solution.py:352
  8.9 4.2 %collective-permute-start = (bf16[32,1152]{1,0:T(8,128)(2,1)S(1)}, bf16[32,1152]{1,0:T(8,128)(2,1)S(1)}, u32[]{:S(2)}, u32[]{:S(2)}) collective-permute-start(bf16[32,1152]{1,0:T(8,128)(2,1)S(1)} %get-tuple-element.30), channel_id=1, source_target_pairs={{0,1},{1,0},{2,3},{3,2},{4,5},{5,4},{6,7},{7,6},{8,9},{9,8},{10,11... | collective-permute-start | bytes 221192 | tf_op jit(solution)/shard_map/ppermute | solution.py:352
  17.9 4.3 %collective-permute-start.4 = (bf16[8,4096]{1,0:T(8,128)(2,1)S(1)}, bf16[8,4096]{1,0:T(8,128)(2,1)S(1)}, u32[]{:S(2)}, u32[]{:S(2)}) collective-permute-start(bf16[8,4096]{1,0:T(8,128)(2,1)S(1)} %fusion.12), channel_id=1, source_target_pairs={{0,2},{1,3},{2,0},{3,1},{4,6},{5,7},{6,4},{7,5},{8,10},{9,11},{10,... | collective-permute-start | bytes 196616 | tf_op jit(solution)/shard_map/ppermute | solution.py:352
  22.5 7.6 %collective-permute-start.5 = (bf16[8,4224]{1,0:T(8,128)(2,1)S(1)}, bf16[8,4224]{1,0:T(8,128)(2,1)S(1)}, u32[]{:S(2)}, u32[]{:S(2)}) collective-permute-start(bf16[8,4224]{1,0:T(8,128)(2,1)S(1)} %get-tuple-element.52), channel_id=1, source_target_pairs={{0,8},{1,9},{2,10},{3,11},{4,12},{5,13},{6,14},{7,15},{8,0},{9,1},... | collective-permute-start | bytes 202760 | tf_op jit(solution)/shard_map/ppermute | solution.py:352
  24.5 15.0 %collective-permute-start.9 = (bf16[8,4224]{1,0:T(8,128)(2,1)S(1)}, bf16[8,4224]{1,0:T(8,128)(2,1)S(1)}, u32[]{:S(2)}, u32[]{:S(2)}) collective-permute-start(bf16[8,4224]{1,0:T(8,128)(2,1)S(1)} %get-tuple-element.52), channel_id=1, source_target_pairs={{0,4},{1,5},{2,6},{3,7},{4,0},{5,1},{6,2},{7,3},{8,12},{9,13},{10,... | collective-permute-start | bytes 202760 | tf_op jit(solution)/shard_map/ppermute | solution.py:352
  26.0 12.0 %collective-permute-start.8 = (bf16[8,4224]{1,0:T(8,128)(2,1)S(1)}, bf16[8,4224]{1,0:T(8,128)(2,1)S(1)}, u32[]{:S(2)}, u32[]{:S(2)}) collective-permute-start(bf16[8,4224]{1,0:T(8,128)(2,1)S(1)} %get-tuple-element.52), channel_id=1, source_target_pairs={{0,2},{1,3},{2,0},{3,1},{4,6},{5,7},{6,4},{7,5},{8,10},{9,11},{10,... | collective-permute-start | bytes 202760 | tf_op jit(solution)/shard_map/ppermute | solution.py:352
  27.5 8.4 %collective-permute-start.7 = (bf16[8,4224]{1,0:T(8,128)(2,1)S(1)}, bf16[8,4224]{1,0:T(8,128)(2,1)S(1)}, u32[]{:S(2)}, u32[]{:S(2)}) collective-permute-start(bf16[8,4224]{1,0:T(8,128)(2,1)S(1)} %get-tuple-element.52), channel_id=1, source_target_pairs={{0,24},{1,25},{2,26},{3,27},{4,28},{5,29},{6,30},{7,31},{8,16},{9,... | collective-permute-start | bytes 202760 | tf_op jit(solution)/shard_map/ppermute | solution.py:352
  30.0 5.9 %collective-permute-start.6 = (bf16[8,4224]{1,0:T(8,128)(2,1)S(1)}, bf16[8,4224]{1,0:T(8,128)(2,1)S(1)}, u32[]{:S(2)}, u32[]{:S(2)}) collective-permute-start(bf16[8,4224]{1,0:T(8,128)(2,1)S(1)} %get-tuple-element.52), channel_id=1, source_target_pairs={{0,16},{1,17},{2,18},{3,19},{4,20},{5,21},{6,22},{7,23},{8,24},{9,... | collective-permute-start | bytes 202760 | tf_op jit(solution)/shard_map/ppermute | solution.py:352
  30.1 9.5 %collective-permute-start.10 = (bf16[8,4224]{1,0:T(8,128)(2,1)S(1)}, bf16[8,4224]{1,0:T(8,128)(2,1)S(1)}, u32[]{:S(2)}, u32[]{:S(2)}) collective-permute-start(bf16[8,4224]{1,0:T(8,128)(2,1)S(1)} %get-tuple-element.52), channel_id=1, source_target_pairs={{0,6},{1,7},{2,4},{3,5},{4,2},{5,3},{6,0},{7,1},{8,14},{9,15},{10,... | collective-permute-start | bytes 202760 | tf_op jit(solution)/shard_map/ppermute | solution.py:352
  35.9 8.2 %collective-permute-start.13 = (bf16[24,4224]{1,0:T(8,128)(2,1)S(1)}, bf16[24,4224]{1,0:T(8,128)(2,1)S(1)}, u32[]{:S(2)}, u32[]{:S(2)}) collective-permute-start(bf16[24,4224]{1,0:T(8,128)(2,1)S(1)} %get-tuple-element.43), channel_id=1, source_target_pairs={{0,6},{1,7},{2,4},{3,5},{4,2},{5,3},{6,0},{7,1},{8,14},{9,15},{10,... | collective-permute-start | bytes 608264 | tf_op jit(solution)/shard_map/ppermute | solution.py:352
  36.5 8.7 %collective-permute-start.12 = (bf16[24,4224]{1,0:T(8,128)(2,1)S(1)}, bf16[24,4224]{1,0:T(8,128)(2,1)S(1)}, u32[]{:S(2)}, u32[]{:S(2)}) collective-permute-start(bf16[24,4224]{1,0:T(8,128)(2,1)S(1)} %get-tuple-element.43), channel_id=1, source_target_pairs={{0,4},{1,5},{2,6},{3,7},{4,0},{5,1},{6,2},{7,3},{8,12},{9,13},{10,... | collective-permute-start | bytes 608264 | tf_op jit(solution)/shard_map/ppermute | solution.py:352
  38.0 8.2 %collective-permute-start.11 = (bf16[24,4224]{1,0:T(8,128)(2,1)S(1)}, bf16[24,4224]{1,0:T(8,128)(2,1)S(1)}, u32[]{:S(2)}, u32[]{:S(2)}) collective-permute-start(bf16[24,4224]{1,0:T(8,128)(2,1)S(1)} %get-tuple-element.43), channel_id=1, source_target_pairs={{0,2},{1,3},{2,0},{3,1},{4,6},{5,7},{6,4},{7,5},{8,10},{9,11},{10,... | collective-permute-start | bytes 608264 | tf_op jit(solution)/shard_map/ppermute | solution.py:352
  39.6 6.7 %collective-permute-start.14 = (bf16[56,4224]{1,0:T(8,128)(2,1)S(1)}, bf16[56,4224]{1,0:T(8,128)(2,1)S(1)}, u32[]{:S(2)}, u32[]{:S(2)}) collective-permute-start(bf16[56,4224]{1,0:T(8,128)(2,1)S(1)} %get-tuple-element.35), channel_id=1, source_target_pairs={{0,1},{1,0},{2,3},{3,2},{4,5},{5,4},{6,7},{7,6},{8,9},{9,8},{10,11... | collective-permute-start | bytes 1419272 | tf_op jit(solution)/shard_map/ppermute | solution.py:352
  55.0 5.0 %collective-permute-start.18 = (bf16[56,4096]{1,0:T(8,128)(2,1)S(1)}, bf16[56,4096]{1,0:T(8,128)(2,1)S(1)}, u32[]{:S(2)}, u32[]{:S(2)}) collective-permute-start(bf16[56,4096]{1,0:T(8,128)(2,1)S(1)} %slice.86), channel_id=1, source_target_pairs={{0,1},{1,0},{2,3},{3,2},{4,5},{5,4},{6,7},{7,6},{8,9},{9,8},{10,11... | collective-permute-start | bytes 1376264 | tf_op jit(solution)/shard_map/ppermute | solution.py:352
  56.4 12.1 %collective-permute-start.23 = (bf16[24,4096]{1,0:T(8,128)(2,1)S(1)}, bf16[24,4096]{1,0:T(8,128)(2,1)S(1)}, u32[]{:S(2)}, u32[]{:S(2)}) collective-permute-start(bf16[24,4096]{1,0:T(8,128)(2,1)S(1)} %get-tuple-element.19), channel_id=1, source_target_pairs={{0,2},{1,3},{2,0},{3,1},{4,6},{5,7},{6,4},{7,5},{8,10},{9,11},{10,... | collective-permute-start | bytes 589832 | tf_op jit(solution)/shard_map/ppermute | solution.py:352
  57.4 11.7 %collective-permute-start.27 = (bf16[24,4096]{1,0:T(8,128)(2,1)S(1)}, bf16[24,4096]{1,0:T(8,128)(2,1)S(1)}, u32[]{:S(2)}, u32[]{:S(2)}) collective-permute-start(bf16[24,4096]{1,0:T(8,128)(2,1)S(1)} %get-tuple-element.20), channel_id=1, source_target_pairs={{0,6},{1,7},{2,4},{3,5},{4,2},{5,3},{6,0},{7,1},{8,14},{9,15},{10,... | collective-permute-start | bytes 589832 | tf_op jit(solution)/shard_map/ppermute | solution.py:352
  58.5 11.2 %collective-permute-start.25 = (bf16[24,4096]{1,0:T(8,128)(2,1)S(1)}, bf16[24,4096]{1,0:T(8,128)(2,1)S(1)}, u32[]{:S(2)}, u32[]{:S(2)}) collective-permute-start(bf16[24,4096]{1,0:T(8,128)(2,1)S(1)} %get-tuple-element.21), channel_id=1, source_target_pairs={{0,4},{1,5},{2,6},{3,7},{4,0},{5,1},{6,2},{7,3},{8,12},{9,13},{10,... | collective-permute-start | bytes 589832 | tf_op jit(solution)/shard_map/ppermute | solution.py:352
  60.1 11.1 %collective-permute-start.19 = (bf16[8,4096]{1,0:T(8,128)(2,1)S(1)}, bf16[8,4096]{1,0:T(8,128)(2,1)S(1)}, u32[]{:S(2)}, u32[]{:S(2)}) collective-permute-start(bf16[8,4096]{1,0:T(8,128)(2,1)S(1)} %get-tuple-element.25), channel_id=1, source_target_pairs={{0,2},{1,3},{2,0},{3,1},{4,6},{5,7},{6,4},{7,5},{8,10},{9,11},{10,... | collective-permute-start | bytes 196616 | tf_op jit(solution)/shard_map/ppermute | solution.py:352
  61.1 12.3 %collective-permute-start.21 = (bf16[8,4096]{1,0:T(8,128)(2,1)S(1)}, bf16[8,4096]{1,0:T(8,128)(2,1)S(1)}, u32[]{:S(2)}, u32[]{:S(2)}) collective-permute-start(bf16[8,4096]{1,0:T(8,128)(2,1)S(1)} %get-tuple-element.26), channel_id=1, source_target_pairs={{0,6},{1,7},{2,4},{3,5},{4,2},{5,3},{6,0},{7,1},{8,14},{9,15},{10,... | collective-permute-start | bytes 196616 | tf_op jit(solution)/shard_map/ppermute | solution.py:352
  68.6 4.8 %collective-permute-start.20 = (bf16[8,4096]{1,0:T(8,128)(2,1)S(1)}, bf16[8,4096]{1,0:T(8,128)(2,1)S(1)}, u32[]{:S(2)}, u32[]{:S(2)}) collective-permute-start(bf16[8,4096]{1,0:T(8,128)(2,1)S(1)} %get-tuple-element.27), channel_id=1, source_target_pairs={{0,4},{1,5},{2,6},{3,7},{4,0},{5,1},{6,2},{7,3},{8,12},{9,13},{10,... | collective-permute-start | bytes 196616 | tf_op jit(solution)/shard_map/ppermute | solution.py:352
  69.8 5.1 %collective-permute-start.28 = (bf16[8,4096]{1,0:T(8,128)(2,1)S(1)}, bf16[8,4096]{1,0:T(8,128)(2,1)S(1)}, u32[]{:S(2)}, u32[]{:S(2)}) collective-permute-start(bf16[8,4096]{1,0:T(8,128)(2,1)S(1)} %get-tuple-element.32), channel_id=1, source_target_pairs={{0,8},{1,9},{2,10},{3,11},{4,12},{5,13},{6,14},{7,15},{8,0},{9,1},... | collective-permute-start | bytes 196616 | tf_op jit(solution)/shard_map/ppermute | solution.py:352
  69.9 6.2 %collective-permute-start.30 = (bf16[8,4096]{1,0:T(8,128)(2,1)S(1)}, bf16[8,4096]{1,0:T(8,128)(2,1)S(1)}, u32[]{:S(2)}, u32[]{:S(2)}) collective-permute-start(bf16[8,4096]{1,0:T(8,128)(2,1)S(1)} %get-tuple-element.33), channel_id=1, source_target_pairs={{0,24},{1,25},{2,26},{3,27},{4,28},{5,29},{6,30},{7,31},{8,16},{9,... | collective-permute-start | bytes 196616 | tf_op jit(solution)/shard_map/ppermute | solution.py:352
  71.2 6.5 %collective-permute-start.29 = (bf16[8,4096]{1,0:T(8,128)(2,1)S(1)}, bf16[8,4096]{1,0:T(8,128)(2,1)S(1)}, u32[]{:S(2)}, u32[]{:S(2)}) collective-permute-start(bf16[8,4096]{1,0:T(8,128)(2,1)S(1)} %get-tuple-element.34), channel_id=1, source_target_pairs={{0,16},{1,17},{2,18},{3,19},{4,20},{5,21},{6,22},{7,23},{8,24},{9,... | collective-permute-start | bytes 196616 | tf_op jit(solution)/shard_map/ppermute | solution.py:352
  (9 other events, 31.7 us)

commit v5 on v4

--- a/solution.py
+++ b/solution.py
@@ -47,12 +47,10 @@
     kg_hbm,
     ids_hbm,
     gates_hbm,
-    w0_hbm,
-    w1_hbm,
+    w_hbm,
     out_ref,
     table_ref,
-    w0_ref,
-    w1_ref,
+    w_ref,
     lengths,
     q_ref,
     nk_ref,
@@ -68,6 +66,8 @@
     num,
     tops,
     totals,
+    score,
+    weight,
     sem,
 ):
     sources = (len_hbm, nk_hbm, nv_hbm, qg_hbm, kg_hbm, ids_hbm, gates_hbm, q_hbm, k_hbm, v_hbm)
@@ -75,11 +75,8 @@
     copies = [
         pltpu.make_async_copy(a, b, sem.at[i]) for i, (a, b) in enumerate(zip(sources, targets))
     ]
-    ahead = [
-        pltpu.make_async_copy(w0_hbm, w0_ref, sem.at[10]),
-        pltpu.make_async_copy(w1_hbm, w1_ref, sem.at[11]),
-    ]
-    for c in copies + ahead:
+    ahead = pltpu.make_async_copy(w_hbm, w_ref, sem.at[10])
+    for c in copies + [ahead]:
         c.start()
     tensor_pos = lax.axis_index("tensor")
     rows, heads, hd = q_ref.shape
@@ -88,17 +85,16 @@
     parts = out_ref.shape[0]
     heads_own = heads // parts
     step = 4
-    many, cols = step * heads, step * kvh * cache
+    blocks = rows // step
+    many, cols, fresh = step * heads, step * kvh * cache, step * kvh
     scaling = hd ** (-0.5)
-    own = jnp.where(tensor_pos == 0, 1.0, 0.0).astype(F32)
 
     row_group = iota((many, cols), 0) // group
-    col = iota((many, cols), 1)
-    same = row_group == col // cache
+    same = row_group == iota((many, cols), 1) // cache
     col_row = iota((1, cols), 1) // (kvh * cache)
     col_pos = iota((1, cols), 1) % cache + tensor_pos * cache
-    new_col = iota((many, rows * kvh), 1)
-    new_row = iota((many, rows * kvh), 0) // group
+    new_col = iota((many, 2 * fresh), 1)
+    new_here = (new_col == iota((many, 2 * fresh), 0) // group) & (tensor_pos == 0)
 
     for c in copies[:7]:
         c.wait()
@@ -113,36 +109,43 @@
         nk_scr[r * kvh : (r + 1) * kvh, :] = nk_ref[r].astype(F32)
         nv_scr[r * kvh : (r + 1) * kvh, :] = nv_ref[r].astype(F32)
     query_gain = qg_ref[...]
-    new_keys = rms_scale(nk_scr[...], kg_ref[...]).astype(BF)
-    new_values = nv_scr[...].astype(BF)
+    key_norm = rms_scale(nk_scr[...], kg_ref[...])
+    empty = jnp.zeros((fresh, hd), F32)
     for c in copies[7:]:
         c.wait()
 
-    for b in range(rows // step):
-        first = b * step
-        query = q_ref[first : first + step].reshape(many, hd).astype(F32)
-        query = rms_scale(query, query_gain).astype(BF)
-        keys = k_ref[first : first + step].reshape(cols, hd)
-        values = v_ref[first : first + step].reshape(cols, hd)
+    def rows_of(ref, b, size):
+        return ref[b * step : (b + 1) * step].reshape(size, hd)
+
+    queries = []
+    for b in range(blocks):
+        query = rows_of(q_ref, b, many).astype(F32)
+        queries.append(rms_scale(query, query_gain).astype(BF))
+    for b in range(blocks):
         limit = jnp.zeros((1, cols), I32)
         for i in range(step):
-            limit = jnp.where(col_row == i, lengths[first + i], limit)
+            limit = jnp.where(col_row == i, lengths[b * step + i], limit)
         included = same & (col_pos < limit)
-        scores = matmul_t(query, keys) * scaling
-        new_here = new_col == new_row + first * kvh
-        new_score = jnp.sum(
-            jnp.where(new_here, matmul_t(query, new_keys) * scaling, 0.0), axis=1, keepdims=True
-        )
-        top = jnp.max(jnp.where(included, scores, -1e30), axis=1, keepdims=True)
-        top = jnp.maximum(top, new_score).astype(BF).astype(F32)
-        weights = jnp.where(included, jnp.exp(scores - top), 0.0).astype(BF)
-        new_weight = jnp.exp(new_score - top).astype(BF).astype(F32) * own
-        total = jnp.sum(weights.astype(F32), axis=1, keepdims=True) + new_weight
-        new_weights = jnp.where(new_here, new_weight, 0.0).astype(BF)
-        block = slice(b * many, (b + 1) * many)
-        num[block, :] = matmul(weights, values) + matmul(new_weights, new_values)
-        tops[block, :] = jnp.broadcast_to(top, (many, LANES))
-        totals[block, :] = jnp.broadcast_to(total, (many, LANES))
+        scores = matmul_t(queries[b], rows_of(k_ref, b, cols)) * scaling
+        score[b, :, :cols] = jnp.where(included, scores, -1e30)
+        new_keys = jnp.concatenate([key_norm[b * fresh : (b + 1) * fresh], empty]).astype(BF)
+        scores = matmul_t(queries[b], new_keys) * scaling
+        score[b, :, cols:] = jnp.where(new_here, scores, -1e30)
+    for b in range(blocks):
+        top = jnp.maximum(jnp.max(score[b], axis=1, keepdims=True), -1e29).astype(BF).astype(F32)
+        tops[b * many : (b + 1) * many, :] = jnp.broadcast_to(top, (many, LANES))
+    for b in range(blocks):
+        top = tops[b * many : (b + 1) * many, 0:1]
+        weights = jnp.exp(score[b] - top).astype(BF)
+        weight[b] = weights
+        total = jnp.sum(weights.astype(F32), axis=1, keepdims=True)
+        totals[b * many : (b + 1) * many, :] = jnp.broadcast_to(total, (many, LANES))
+    for b in range(blocks):
+        values = nv_scr[b * fresh : (b + 1) * fresh, :]
+        new_values = jnp.concatenate([values, empty]).astype(BF)
+        num[b * many : (b + 1) * many, :] = matmul(
+            weight[b, :, :cols], rows_of(v_ref, b, cols)
+        ) + matmul(weight[b, :, cols:], new_values)
 
     lane = iota((rows, LANES), 1)
     for t in range(parts):
@@ -157,8 +160,7 @@
             side = jnp.where(lane == heads_own + h, high, side)
             side = jnp.where(lane == 2 * heads_own + h, total - high, side)
         out_ref[slot, :, heads_own * hd :] = side.astype(BF)
-    for c in ahead:
-        c.wait()
+    ahead.wait()
 
 
 def attention(
@@ -174,10 +176,10 @@
     gate_weights,
     parts,
     lanes,
-    weights,
+    later,
 ):
     rows, heads, hd = queries.shape
-    kvh = key_cache.shape[1]
+    kvh, cache = key_cache.shape[1:3]
     args = (
         lengths,
         queries,
@@ -195,10 +197,10 @@
         out_shape=(
             jax.ShapeDtypeStruct((parts, rows, heads // parts * hd + LANES), BF),
             jax.ShapeDtypeStruct((expert_ids.shape[0], lanes), BF),
-            *[pltpu.VMEM(w.shape, w.dtype) for w in weights],
+            pltpu.VMEM(later.shape, later.dtype),
         ),
-        in_specs=[pl.BlockSpec(memory_space=pltpu.HBM)] * 12,
-        out_specs=(pl.BlockSpec(memory_space=pltpu.VMEM),) * 4,
+        in_specs=[pl.BlockSpec(memory_space=pltpu.HBM)] * 11,
+        out_specs=(pl.BlockSpec(memory_space=pltpu.VMEM),) * 3,
         scratch_shapes=[pltpu.SMEM(args[0].shape, I32)]
         + [pltpu.VMEM(a.shape, a.dtype) for a in args[1:]]
         + [
@@ -207,18 +209,24 @@
             pltpu.VMEM((rows * heads, hd), F32),
             pltpu.VMEM((rows * heads, LANES), F32),
             pltpu.VMEM((rows * heads, LANES), F32),
-            pltpu.SemaphoreType.DMA((12,)),
+            pltpu.VMEM((rows // 4, 4 * heads, 4 * kvh * (cache + 2)), F32),
+            pltpu.VMEM((rows // 4, 4 * heads, 4 * kvh * (cache + 2)), BF),
+            pltpu.SemaphoreType.DMA((11,)),
         ],
         compiler_params=pltpu.CompilerParams(vmem_limit_bytes=16 * MIB),
         name="attention",
-    )(*[in_hbm(a) for a in (*args, *weights)])
+    )(*[in_hbm(a) for a in (*args, later)])
 
 
 def projection_kernel(parts, *refs):
     got = refs[:parts]
-    w_ref, ahead_hbm, out_ref, ahead_ref, attn, sem = refs[parts:]
-    ahead = pltpu.make_async_copy(ahead_hbm, ahead_ref, sem)
-    ahead.start()
+    w_ref, w0_hbm, w1_hbm, out_ref, w0_ref, w1_ref, attn, sem = refs[parts:]
+    ahead = [
+        pltpu.make_async_copy(w0_hbm, w0_ref, sem.at[0]),
+        pltpu.make_async_copy(w1_hbm, w1_ref, sem.at[1]),
+    ]
+    for c in ahead:
+        c.start()
     tensor_pos = lax.axis_index("tensor")
     depth, width = w_ref.shape
     share = out_ref.shape[2]
@@ -245,10 +253,11 @@
         for t in range(parts):
             slot = tensor_pos ^ t
             out_ref[slot & 1, slot >> 1, :, cols] = result[t * share : (t + 1) * share].astype(BF)
-    ahead.wait()
-
-
-def projection(got, out_proj, share, weight):
+    for c in ahead:
+        c.wait()
+
+
+def projection(got, out_proj, share, later):
     parts = len(got)
     rows = got[0].shape[0]
     depth, width = out_proj.shape
@@ -257,14 +266,14 @@
         functools.partial(projection_kernel, parts),
         out_shape=(
             jax.ShapeDtypeStruct((2, parts // 2, share, width), BF),
-            pltpu.VMEM(weight.shape, weight.dtype),
+            *[pltpu.VMEM(w.shape, w.dtype) for w in later],
         ),
-        in_specs=[vmem] * (parts + 1) + [pl.BlockSpec(memory_space=pltpu.HBM)],
-        out_specs=(vmem, vmem),
-        scratch_shapes=[pltpu.VMEM((rows, depth), BF), pltpu.SemaphoreType.DMA],
+        in_specs=[vmem] * (parts + 1) + [pl.BlockSpec(memory_space=pltpu.HBM)] * 2,
+        out_specs=(vmem,) * 3,
+        scratch_shapes=[pltpu.VMEM((rows, depth), BF), pltpu.SemaphoreType.DMA((2,))],
         compiler_params=pltpu.CompilerParams(vmem_limit_bytes=12 * MIB),
         name="projection",
-    )(*got, out_proj, in_hbm(weight))
+    )(*got, out_proj, *[in_hbm(w) for w in later])
 
 
 def expert_kernel(slots, x_ref, gate, up, down_hbm, out_ref, down, xc, act, res, sem):
@@ -387,7 +396,7 @@
     share, width = residual_in.shape
     lanes = -(-dp * tensor // LANES) * LANES
 
-    local, table, out_proj, expert_gate = attention(
+    local, table, out_proj = attention(
         lengths,
         queries,
         new_keys,
@@ -400,10 +409,12 @@
         gate_weights,
         tensor,
         lanes,
-        (out_proj, expert_gate),
+        out_proj,
     )
     got = [local[0]] + plan.swaps(list(local[1:]), list(range(1, tensor)))
-    partial, expert_up = projection(got, out_proj, share, expert_up)
+    partial, expert_gate, expert_up = projection(
+        got, out_proj, share, (expert_gate, expert_up)
+    )
     pair = total_of([partial[0], plan.swap(partial[1], plan.core)])
     projected = total_of([pair[0]] + plan.swaps(list(pair[1:]), plan.y))
     hidden = residual_in.astype(F32) + projected
@@ -411,7 +422,7 @@
 
     mine = jnp.concatenate([normed, table], axis=1)
     others = plan.spread(mine, plan.z)
-    near = plan.spread(mine, plan.plane)
+    near = plan.spread(mine + others[0][:, :1] * 0, plan.plane)
     far = plan.spread(jnp.concatenate(others), plan.plane)
     pieces = [jnp.concatenate([mine] + others + near)] + far
     x = jnp.concatenate(pieces + [plan.swap(piece, plan.core) for piece in pieces])
@@ -431,10 +442,14 @@
         for i in reversed(range(len(sizes)))
     ][::-1]
     blocks = sums[0].reshape(-1, share, width)
-    far = plan.swaps(sums[1:], plan.plane)
-    others = total_of([sums[0][share : plan.zlen * share]] + far).reshape(-1, share, width)
-    near = plan.swaps(list(blocks[plan.zlen :]), plan.plane)
-    moe_sum = total_of([blocks[0]] + near + plan.swaps(list(others), plan.z))
+    sent = [
+        jnp.concatenate([near.astype(BF), far.astype(BF)])
+        for near, far in zip(blocks[plan.zlen :], sums[1:])
+    ]
+    column = total_of(
+        [sums[0][: plan.zlen * share]] + plan.swaps(sent, plan.plane)
+    ).reshape(-1, share, width)
+    moe_sum = total_of([column[0]] + plan.swaps(list(column[1:]), plan.z))
     return (hidden + moe_sum).astype(BF)
 
 

time: 78.5 us -> 81.3 us (1.036)
  waiting for transfers between devices: 33.2 us -> 38.2 us
  starting transfers between devices: 27.7 us -> 25.3 us
    ppermute x31 -> x28, waiting for transfers between devices: 33.2 us -> 38.2 us  [swap(): lax.ppermute(value, ('dp', 'tensor'), [(i, i ^ flip) for i in range(self....]
    ppermute x31 -> x28, starting transfers between devices: 27.7 us -> 25.3 us  [swap(): lax.ppermute(value, ('dp', 'tensor'), [(i, i ^ flip) for i in range(self....]
    pallas_call x1, Pallas kernels: 5.78 us -> 4.12 us  [attention(): pl.pallas_call(attention_kernel, out_shape=(jax.ShapeDtypeStruct((parts,...]
    pallas_call x1, Pallas kernels: 3.22 us -> 4.77 us  [projection(): pl.pallas_call(functools.partial(projection_kernel, parts), out_shape=(ja...]
  transfers between devices with their start and end apart: 31 -> 28, of which waited for: 17 -> 21; matrix products, arithmetic and copies ran while one was open for 1% -> 1% of each run, Pallas kernels for 0% -> 0%
where the time goes in v5:
time: 81.3 us; the launch traced here: 81.1 us
  waiting for transfers between devices  38.2 us (47%)
  starting transfers between devices  25.3 us (31%)
  Pallas kernels  15.4 us (19%)
  other arithmetic  1.61 us (2%)
    ppermute x28, waiting for transfers between devices, swap(): lax.ppermute(value, ('dp', 'tensor'), [(i, i ^ flip) for i in range(self....  38.2 us
    ppermute x28, starting transfers between devices, swap(): lax.ppermute(value, ('dp', 'tensor'), [(i, i ^ flip) for i in range(self....  25.3 us
    pallas_call x1, Pallas kernels, experts(): pl.pallas_call(functools.partial(expert_kernel, slots), out_shape=jax.Sha...  6.48 us
    pallas_call x1, Pallas kernels, projection(): pl.pallas_call(functools.partial(projection_kernel, parts), out_shape=(ja...  4.77 us
    pallas_call x1, Pallas kernels, attention(): pl.pallas_call(attention_kernel, out_shape=(jax.ShapeDtypeStruct((parts,...  4.12 us
  transfers between devices with their start and end apart: 28, of which 21 were waited for; matrix products, arithmetic and copies ran while one was open for 1% of the time, Pallas kernels for 0%

profile of v5, /device:TPU:0, one launch (start us, length us, event | category | flops | bytes accessed | tf_op | source)
XLA Modules:
  0.0 81.1 jit_solution(8137664784967546815)
XLA Ops:
  0.0 4.1 %attention.1 = (bf16[4,32,1152]{2,1,0:T(8,128)(2,1)S(1)}, bf16[8,128]{1,0:T(8,128)(2,1)S(1)}, bf16[1024,4096]{1,0:T(8,128)(2,1)S(1)}) custom-call(s32[32]{0:T(128)} %len_hbm.1, bf16[32,32,128]{2,1,0:T(8,128)(2,1)} %q_hbm.1, bf16[32,2,128]{2,1,0:T(2,128)(2,1)} %nk_hbm.1, bf16[32,2,128]{2,1,0:T(2,128)(2,1)} %nv_hbm.1, bf16[32,2,32,128]{3,2,1,0:T(8,128)(2,1)} %k_hbm.1, ...), custom_call_target="tpu_custom_call" | custom-call | tf_op jit(solution)/shard_map/attention/pallas_call | solution.py:195
  4.2 2.5 %collective-permute-start.2 = (bf16[32,1152]{1,0:T(8,128)(2,1)S(1)}, bf16[32,1152]{1,0:T(8,128)(2,1)S(1)}, u32[]{:S(2)}, u32[]{:S(2)}) collective-permute-start(bf16[32,1152]{1,0:T(8,128)(2,1)S(1)} %get-tuple-element.30), channel_id=1, source_target_pairs={{0,3},{1,2},{2,1},{3,0},{4,7},{5,6},{6,5},{7,4},{8,11},{9,10},{10,... | collective-permute-start | bytes 221192 | tf_op jit(solution)/shard_map/ppermute | solution.py:361
  7.3 2.0 %collective-permute-done.2.refs_3_ = bf16[32,1152]{1,0:T(8,128)(2,1)S(1)} collective-permute-done((bf16[32,1152]{1,0:T(8,128)(2,1)S(1)}, bf16[32,1152]{1,0:T(8,128)(2,1)S(1)}, u32[]{:S(2)}, u32[]{:S(2)}) %collective-permute-start.2) | collective-permute-done | bytes 73760 | tf_op jit(solution)/shard_map/ppermute | solution.py:361
  9.3 2.2 %collective-permute-done.1.refs_2_ = bf16[32,1152]{1,0:T(8,128)(2,1)S(1)} collective-permute-done((bf16[32,1152]{1,0:T(8,128)(2,1)S(1)}, bf16[32,1152]{1,0:T(8,128)(2,1)S(1)}, u32[]{:S(2)}, u32[]{:S(2)}) %collective-permute-start.1) | collective-permute-done | bytes 73760 | tf_op jit(solution)/shard_map/ppermute | solution.py:361
  11.5 4.8 %projection.1 = (bf16[2,2,8,4096]{3,2,1,0:T(8,128)(2,1)S(1)}, bf16[1,4096,768]{2,1,0:T(8,128)(2,1)S(1)}, bf16[1,4096,768]{2,1,0:T(8,128)(2,1)S(1)}) custom-call(bf16[32,1152]{1,0:T(8,128)(2,1)S(1)} %get-tuple-element.33.refs_0_, bf16[32,1152]{1,0:T(8,128)(2,1)S(1)} %collective-permute-done.refs_1_, bf16[32,1152]{1,0:T(8,128)(2,1)S(1)} %collective-permute-done.1.refs_2_, ...), custom_call_target="tpu_custom_call" | custom-call | tf_op jit(solution)/shard_map/projection/pallas_call | solution.py:265
  16.4 1.3 %collective-permute-done.3 = bf16[2,8,4096]{2,1,0:T(8,128)(2,1)S(1)} collective-permute-done((bf16[2,8,4096]{2,1,0:T(8,128)(2,1)S(1)}, bf16[2,8,4096]{2,1,0:T(8,128)(2,1)S(1)}, u32[]{:S(2)}, u32[]{:S(2)}) %collective-permute-start.3) | collective-permute-done | bytes 131104 | tf_op jit(solution)/shard_map/ppermute | solution.py:361
  17.7 1.9 %collective-permute-start.4 = (bf16[8,4096]{1,0:T(8,128)(2,1)S(1)}, bf16[8,4096]{1,0:T(8,128)(2,1)S(1)}, u32[]{:S(2)}, u32[]{:S(2)}) collective-permute-start(bf16[8,4096]{1,0:T(8,128)(2,1)S(1)} %fusion.8), channel_id=1, source_target_pairs={{0,2},{1,3},{2,0},{3,1},{4,6},{5,7},{6,4},{7,5},{8,10},{9,11},{10,... | collective-permute-start | bytes 196616 | tf_op jit(solution)/shard_map/ppermute | solution.py:361
  19.7 2.4 %collective-permute-done.4 = bf16[8,4096]{1,0:T(8,128)(2,1)S(1)} collective-permute-done((bf16[8,4096]{1,0:T(8,128)(2,1)S(1)}, bf16[8,4096]{1,0:T(8,128)(2,1)S(1)}, u32[]{:S(2)}, u32[]{:S(2)}) %collective-permute-start.4) | collective-permute-done | bytes 65568 | tf_op jit(solution)/shard_map/ppermute | solution.py:361
  22.4 2.0 %collective-permute-start.5 = (bf16[8,4224]{1,0:T(8,128)(2,1)S(1)}, bf16[8,4224]{1,0:T(8,128)(2,1)S(1)}, u32[]{:S(2)}, u32[]{:S(2)}) collective-permute-start(bf16[8,4224]{1,0:T(8,128)(2,1)S(1)} %pad_maximum_fusion.3), channel_id=1, source_target_pairs={{0,8},{1,9},{2,10},{3,11},{4,12},{5,13},{6,14},{7,15},{8,0},{9,1},... | collective-permute-start | bytes 202760 | tf_op jit(solution)/shard_map/ppermute | solution.py:361
  24.3 2.6 %collective-permute-start.6 = (bf16[8,4224]{1,0:T(8,128)(2,1)S(1)}, bf16[8,4224]{1,0:T(8,128)(2,1)S(1)}, u32[]{:S(2)}, u32[]{:S(2)}) collective-permute-start(bf16[8,4224]{1,0:T(8,128)(2,1)S(1)} %pad_maximum_fusion.3), channel_id=1, source_target_pairs={{0,16},{1,17},{2,18},{3,19},{4,20},{5,21},{6,22},{7,23},{8,24},{9,... | collective-permute-start | bytes 202760 | tf_op jit(solution)/shard_map/ppermute | solution.py:361
  27.6 2.8 %collective-permute-start.10 = (bf16[8,4224]{1,0:T(8,128)(2,1)S(1)}, bf16[8,4224]{1,0:T(8,128)(2,1)S(1)}, u32[]{:S(2)}, u32[]{:S(2)}) collective-permute-start(bf16[8,4224]{1,0:T(8,128)(2,1)S(1)} %get-tuple-element.54), channel_id=1, source_target_pairs={{0,6},{1,7},{2,4},{3,5},{4,2},{5,3},{6,0},{7,1},{8,14},{9,15},{10,... | collective-permute-start | bytes 202760 | tf_op jit(solution)/shard_map/ppermute | solution.py:361
  31.2 1.8 %collective-permute-done.7 = bf16[8,4224]{1,0:T(8,128)(2,1)S(1)} collective-permute-done((bf16[8,4224]{1,0:T(8,128)(2,1)S(1)}, bf16[8,4224]{1,0:T(8,128)(2,1)S(1)}, u32[]{:S(2)}, u32[]{:S(2)}) %collective-permute-start.7) | collective-permute-done | bytes 67616 | tf_op jit(solution)/shard_map/ppermute | solution.py:361
  33.0 2.5 %collective-permute-start.13 = (bf16[24,4224]{1,0:T(8,128)(2,1)S(1)}, bf16[24,4224]{1,0:T(8,128)(2,1)S(1)}, u32[]{:S(2)}, u32[]{:S(2)}) collective-permute-start(bf16[24,4224]{1,0:T(8,128)(2,1)S(1)} %get-tuple-element.45), channel_id=1, source_target_pairs={{0,6},{1,7},{2,4},{3,5},{4,2},{5,3},{6,0},{7,1},{8,14},{9,15},{10,... | collective-permute-start | bytes 608264 | tf_op jit(solution)/shard_map/ppermute | solution.py:361
  36.1 1.3 %collective-permute-done.8 = bf16[8,4224]{1,0:T(8,128)(2,1)S(1)} collective-permute-done((bf16[8,4224]{1,0:T(8,128)(2,1)S(1)}, bf16[8,4224]{1,0:T(8,128)(2,1)S(1)}, u32[]{:S(2)}, u32[]{:S(2)}) %collective-permute-start.8) | collective-permute-done | bytes 67616 | tf_op jit(solution)/shard_map/ppermute | solution.py:361
  37.6 3.7 %collective-permute-done.13 = bf16[24,4224]{1,0:T(8,128)(2,1)S(1)} collective-permute-done((bf16[24,4224]{1,0:T(8,128)(2,1)S(1)}, bf16[24,4224]{1,0:T(8,128)(2,1)S(1)}, u32[]{:S(2)}, u32[]{:S(2)}) %collective-permute-start.13) | collective-permute-done | bytes 202784 | tf_op jit(solution)/shard_map/ppermute | solution.py:361
  41.3 2.1 %collective-permute-done.12 = bf16[24,4224]{1,0:T(8,128)(2,1)S(1)} collective-permute-done((bf16[24,4224]{1,0:T(8,128)(2,1)S(1)}, bf16[24,4224]{1,0:T(8,128)(2,1)S(1)}, u32[]{:S(2)}, u32[]{:S(2)}) %collective-permute-start.12) | collective-permute-done | bytes 202784 | tf_op jit(solution)/shard_map/ppermute | solution.py:361
  45.3 6.5 %experts.1 = bf16[256,4096]{1,0:T(8,128)(2,1)S(1)} custom-call(bf16[256,4224]{1,0:T(8,128)(2,1)S(1)} %constant_dynamic-update-slice_fusion.10.x_ref, bf16[1,4096,768]{2,1,0:T(8,128)(2,1)S(1)} %get-tuple-element.15.gate, bf16[1,4096,768]{2,1,0:T(8,128)(2,1)S(1)} %get-tuple-element.16.up, bf16[1,768,4096]{2,1,0:T(8,128)(2,1)} %down_hbm.1), custom_call_target="tpu_custom_call" | custom-call | tf_op jit(solution)/shard_map/experts/pallas_call | solution.py:331
  57.1 1.3 %collective-permute-start.20 = (bf16[32,4096]{1,0:T(8,128)(2,1)S(1)}, bf16[32,4096]{1,0:T(8,128)(2,1)S(1)}, u32[]{:S(2)}, u32[]{:S(2)}) collective-permute-start(bf16[32,4096]{1,0:T(8,128)(2,1)S(1)} %pad_maximum_fusion), channel_id=1, source_target_pairs={{0,2},{1,3},{2,0},{3,1},{4,6},{5,7},{6,4},{7,5},{8,10},{9,11},{10,... | collective-permute-start | bytes 786440 | tf_op jit(solution)/shard_map/ppermute | solution.py:361
  58.4 5.5 %collective-permute-done.22 = bf16[32,4096]{1,0:T(8,128)(2,1)S(1)} collective-permute-done((bf16[32,4096]{1,0:T(8,128)(2,1)S(1)}, bf16[32,4096]{1,0:T(8,128)(2,1)S(1)}, u32[]{:S(2)}, u32[]{:S(2)}) %collective-permute-start.22) | collective-permute-done | bytes 262176 | tf_op jit(solution)/shard_map/ppermute | solution.py:361
  63.9 5.3 %collective-permute-done.24 = bf16[32,4096]{1,0:T(8,128)(2,1)S(1)} collective-permute-done((bf16[32,4096]{1,0:T(8,128)(2,1)S(1)}, bf16[32,4096]{1,0:T(8,128)(2,1)S(1)}, u32[]{:S(2)}, u32[]{:S(2)}) %collective-permute-start.24) | collective-permute-done | bytes 262176 | tf_op jit(solution)/shard_map/ppermute | solution.py:361
  69.2 1.5 %collective-permute-done.20 = bf16[32,4096]{1,0:T(8,128)(2,1)S(1)} collective-permute-done((bf16[32,4096]{1,0:T(8,128)(2,1)S(1)}, bf16[32,4096]{1,0:T(8,128)(2,1)S(1)}, u32[]{:S(2)}, u32[]{:S(2)}) %collective-permute-start.20) | collective-permute-done | bytes 262176 | tf_op jit(solution)/shard_map/ppermute | solution.py:361
  71.2 3.0 %collective-permute-start.27 = (bf16[8,4096]{1,0:T(8,128)(2,1)S(1)}, bf16[8,4096]{1,0:T(8,128)(2,1)S(1)}, u32[]{:S(2)}, u32[]{:S(2)}) collective-permute-start(bf16[8,4096]{1,0:T(8,128)(2,1)S(1)} %get-tuple-element.35), channel_id=1, source_target_pairs={{0,24},{1,25},{2,26},{3,27},{4,28},{5,29},{6,30},{7,31},{8,16},{9,... | collective-permute-start | bytes 196616 | tf_op jit(solution)/shard_map/ppermute | solution.py:361
  75.9 2.0 %collective-permute-done.27 = bf16[8,4096]{1,0:T(8,128)(2,1)S(1)} collective-permute-done((bf16[8,4096]{1,0:T(8,128)(2,1)S(1)}, bf16[8,4096]{1,0:T(8,128)(2,1)S(1)}, u32[]{:S(2)}, u32[]{:S(2)}) %collective-permute-start.27) | collective-permute-done | bytes 65568 | tf_op jit(solution)/shard_map/ppermute | solution.py:361
  77.9 2.5 %collective-permute-done.26 = bf16[8,4096]{1,0:T(8,128)(2,1)S(1)} collective-permute-done((bf16[8,4096]{1,0:T(8,128)(2,1)S(1)}, bf16[8,4096]{1,0:T(8,128)(2,1)S(1)}, u32[]{:S(2)}, u32[]{:S(2)}) %collective-permute-start.26) | collective-permute-done | bytes 65568 | tf_op jit(solution)/shard_map/ppermute | solution.py:361
  (73 shorter events, 13.1 us)
Async XLA Ops:
  4.2 5.1 %collective-permute-start.2 = (bf16[32,1152]{1,0:T(8,128)(2,1)S(1)}, bf16[32,1152]{1,0:T(8,128)(2,1)S(1)}, u32[]{:S(2)}, u32[]{:S(2)}) collective-permute-start(bf16[32,1152]{1,0:T(8,128)(2,1)S(1)} %get-tuple-element.30), channel_id=1, source_target_pairs={{0,3},{1,2},{2,1},{3,0},{4,7},{5,6},{6,5},{7,4},{8,11},{9,10},{10,... | collective-permute-start | bytes 221192 | tf_op jit(solution)/shard_map/ppermute | solution.py:361
  6.6 4.8 %collective-permute-start.1 = (bf16[32,1152]{1,0:T(8,128)(2,1)S(1)}, bf16[32,1152]{1,0:T(8,128)(2,1)S(1)}, u32[]{:S(2)}, u32[]{:S(2)}) collective-permute-start(bf16[32,1152]{1,0:T(8,128)(2,1)S(1)} %get-tuple-element.31), channel_id=1, source_target_pairs={{0,2},{1,3},{2,0},{3,1},{4,6},{5,7},{6,4},{7,5},{8,10},{9,11},{10,... | collective-permute-start | bytes 221192 | tf_op jit(solution)/shard_map/ppermute | solution.py:361
  7.3 4.2 %collective-permute-start = (bf16[32,1152]{1,0:T(8,128)(2,1)S(1)}, bf16[32,1152]{1,0:T(8,128)(2,1)S(1)}, u32[]{:S(2)}, u32[]{:S(2)}) collective-permute-start(bf16[32,1152]{1,0:T(8,128)(2,1)S(1)} %get-tuple-element.32), channel_id=1, source_target_pairs={{0,1},{1,0},{2,3},{3,2},{4,5},{5,4},{6,7},{7,6},{8,9},{9,8},{10,11... | collective-permute-start | bytes 221192 | tf_op jit(solution)/shard_map/ppermute | solution.py:361
  17.7 4.3 %collective-permute-start.4 = (bf16[8,4096]{1,0:T(8,128)(2,1)S(1)}, bf16[8,4096]{1,0:T(8,128)(2,1)S(1)}, u32[]{:S(2)}, u32[]{:S(2)}) collective-permute-start(bf16[8,4096]{1,0:T(8,128)(2,1)S(1)} %fusion.8), channel_id=1, source_target_pairs={{0,2},{1,3},{2,0},{3,1},{4,6},{5,7},{6,4},{7,5},{8,10},{9,11},{10,... | collective-permute-start | bytes 196616 | tf_op jit(solution)/shard_map/ppermute | solution.py:361
  22.4 5.0 %collective-permute-start.5 = (bf16[8,4224]{1,0:T(8,128)(2,1)S(1)}, bf16[8,4224]{1,0:T(8,128)(2,1)S(1)}, u32[]{:S(2)}, u32[]{:S(2)}) collective-permute-start(bf16[8,4224]{1,0:T(8,128)(2,1)S(1)} %pad_maximum_fusion.3), channel_id=1, source_target_pairs={{0,8},{1,9},{2,10},{3,11},{4,12},{5,13},{6,14},{7,15},{8,0},{9,1},... | collective-permute-start | bytes 202760 | tf_op jit(solution)/shard_map/ppermute | solution.py:361
  24.3 6.8 %collective-permute-start.6 = (bf16[8,4224]{1,0:T(8,128)(2,1)S(1)}, bf16[8,4224]{1,0:T(8,128)(2,1)S(1)}, u32[]{:S(2)}, u32[]{:S(2)}) collective-permute-start(bf16[8,4224]{1,0:T(8,128)(2,1)S(1)} %pad_maximum_fusion.3), channel_id=1, source_target_pairs={{0,16},{1,17},{2,18},{3,19},{4,20},{5,21},{6,22},{7,23},{8,24},{9,... | collective-permute-start | bytes 202760 | tf_op jit(solution)/shard_map/ppermute | solution.py:361
  26.9 6.1 %collective-permute-start.7 = (bf16[8,4224]{1,0:T(8,128)(2,1)S(1)}, bf16[8,4224]{1,0:T(8,128)(2,1)S(1)}, u32[]{:S(2)}, u32[]{:S(2)}) collective-permute-start(bf16[8,4224]{1,0:T(8,128)(2,1)S(1)} %pad_maximum_fusion.3), channel_id=1, source_target_pairs={{0,24},{1,25},{2,26},{3,27},{4,28},{5,29},{6,30},{7,31},{8,16},{9,... | collective-permute-start | bytes 202760 | tf_op jit(solution)/shard_map/ppermute | solution.py:361
  27.6 9.9 %collective-permute-start.10 = (bf16[8,4224]{1,0:T(8,128)(2,1)S(1)}, bf16[8,4224]{1,0:T(8,128)(2,1)S(1)}, u32[]{:S(2)}, u32[]{:S(2)}) collective-permute-start(bf16[8,4224]{1,0:T(8,128)(2,1)S(1)} %get-tuple-element.54), channel_id=1, source_target_pairs={{0,6},{1,7},{2,4},{3,5},{4,2},{5,3},{6,0},{7,1},{8,14},{9,15},{10,... | collective-permute-start | bytes 202760 | tf_op jit(solution)/shard_map/ppermute | solution.py:361
  30.4 7.0 %collective-permute-start.9 = (bf16[8,4224]{1,0:T(8,128)(2,1)S(1)}, bf16[8,4224]{1,0:T(8,128)(2,1)S(1)}, u32[]{:S(2)}, u32[]{:S(2)}) collective-permute-start(bf16[8,4224]{1,0:T(8,128)(2,1)S(1)} %get-tuple-element.54), channel_id=1, source_target_pairs={{0,4},{1,5},{2,6},{3,7},{4,0},{5,1},{6,2},{7,3},{8,12},{9,13},{10,... | collective-permute-start | bytes 202760 | tf_op jit(solution)/shard_map/ppermute | solution.py:361
  30.9 6.5 %collective-permute-start.8 = (bf16[8,4224]{1,0:T(8,128)(2,1)S(1)}, bf16[8,4224]{1,0:T(8,128)(2,1)S(1)}, u32[]{:S(2)}, u32[]{:S(2)}) collective-permute-start(bf16[8,4224]{1,0:T(8,128)(2,1)S(1)} %get-tuple-element.54), channel_id=1, source_target_pairs={{0,2},{1,3},{2,0},{3,1},{4,6},{5,7},{6,4},{7,5},{8,10},{9,11},{10,... | collective-permute-start | bytes 202760 | tf_op jit(solution)/shard_map/ppermute | solution.py:361
  33.0 8.3 %collective-permute-start.13 = (bf16[24,4224]{1,0:T(8,128)(2,1)S(1)}, bf16[24,4224]{1,0:T(8,128)(2,1)S(1)}, u32[]{:S(2)}, u32[]{:S(2)}) collective-permute-start(bf16[24,4224]{1,0:T(8,128)(2,1)S(1)} %get-tuple-element.45), channel_id=1, source_target_pairs={{0,6},{1,7},{2,4},{3,5},{4,2},{5,3},{6,0},{7,1},{8,14},{9,15},{10,... | collective-permute-start | bytes 608264 | tf_op jit(solution)/shard_map/ppermute | solution.py:361
  35.5 7.9 %collective-permute-start.12 = (bf16[24,4224]{1,0:T(8,128)(2,1)S(1)}, bf16[24,4224]{1,0:T(8,128)(2,1)S(1)}, u32[]{:S(2)}, u32[]{:S(2)}) collective-permute-start(bf16[24,4224]{1,0:T(8,128)(2,1)S(1)} %get-tuple-element.45), channel_id=1, source_target_pairs={{0,4},{1,5},{2,6},{3,7},{4,0},{5,1},{6,2},{7,3},{8,12},{9,13},{10,... | collective-permute-start | bytes 608264 | tf_op jit(solution)/shard_map/ppermute | solution.py:361
  37.4 6.3 %collective-permute-start.11 = (bf16[24,4224]{1,0:T(8,128)(2,1)S(1)}, bf16[24,4224]{1,0:T(8,128)(2,1)S(1)}, u32[]{:S(2)}, u32[]{:S(2)}) collective-permute-start(bf16[24,4224]{1,0:T(8,128)(2,1)S(1)} %get-tuple-element.45), channel_id=1, source_target_pairs={{0,2},{1,3},{2,0},{3,1},{4,6},{5,7},{6,4},{7,5},{8,10},{9,11},{10,... | collective-permute-start | bytes 608264 | tf_op jit(solution)/shard_map/ppermute | solution.py:361
  37.5 6.5 %collective-permute-start.14 = (bf16[56,4224]{1,0:T(8,128)(2,1)S(1)}, bf16[56,4224]{1,0:T(8,128)(2,1)S(1)}, u32[]{:S(2)}, u32[]{:S(2)}) collective-permute-start(bf16[56,4224]{1,0:T(8,128)(2,1)S(1)} %get-tuple-element.37), channel_id=1, source_target_pairs={{0,1},{1,0},{2,3},{3,2},{4,5},{5,4},{6,7},{7,6},{8,9},{9,8},{10,11... | collective-permute-start | bytes 1419272 | tf_op jit(solution)/shard_map/ppermute | solution.py:361
  41.3 3.9 %collective-permute-start.17 = (bf16[24,4224]{1,0:T(8,128)(2,1)S(1)}, bf16[24,4224]{1,0:T(8,128)(2,1)S(1)}, u32[]{:S(2)}, u32[]{:S(2)}) collective-permute-start(bf16[24,4224]{1,0:T(8,128)(2,1)S(1)} %collective-permute-done.13), channel_id=1, source_target_pairs={{0,1},{1,0},{2,3},{3,2},{4,5},{5,4},{6,7},{7,6},{8,9},{9,8},{10,11... | collective-permute-start | bytes 608264 | tf_op jit(solution)/shard_map/ppermute | solution.py:361
  43.4 1.8 %collective-permute-start.16 = (bf16[24,4224]{1,0:T(8,128)(2,1)S(1)}, bf16[24,4224]{1,0:T(8,128)(2,1)S(1)}, u32[]{:S(2)}, u32[]{:S(2)}) collective-permute-start(bf16[24,4224]{1,0:T(8,128)(2,1)S(1)} %collective-permute-done.12), channel_id=1, source_target_pairs={{0,1},{1,0},{2,3},{3,2},{4,5},{5,4},{6,7},{7,6},{8,9},{9,8},{10,11... | collective-permute-start | bytes 608264 | tf_op jit(solution)/shard_map/ppermute | solution.py:361
  51.8 1.5 %collective-permute-start.19 = (bf16[24,4096]{1,0:T(8,128)(2,1)S(1)}, bf16[24,4096]{1,0:T(8,128)(2,1)S(1)}, u32[]{:S(2)}, u32[]{:S(2)}) collective-permute-start(bf16[24,4096]{1,0:T(8,128)(2,1)S(1)} %get-tuple-element.24), channel_id=1, source_target_pairs={{0,1},{1,0},{2,3},{3,2},{4,5},{5,4},{6,7},{7,6},{8,9},{9,8},{10,11... | collective-permute-start | bytes 589832 | tf_op jit(solution)/shard_map/ppermute | solution.py:361
  52.6 1.9 %collective-permute-start.18 = (bf16[56,4096]{1,0:T(8,128)(2,1)S(1)}, bf16[56,4096]{1,0:T(8,128)(2,1)S(1)}, u32[]{:S(2)}, u32[]{:S(2)}) collective-permute-start(bf16[56,4096]{1,0:T(8,128)(2,1)S(1)} %slice.96), channel_id=1, source_target_pairs={{0,1},{1,0},{2,3},{3,2},{4,5},{5,4},{6,7},{7,6},{8,9},{9,8},{10,11... | collective-permute-start | bytes 1376264 | tf_op jit(solution)/shard_map/ppermute | solution.py:361
  54.7 9.2 %collective-permute-start.22 = (bf16[32,4096]{1,0:T(8,128)(2,1)S(1)}, bf16[32,4096]{1,0:T(8,128)(2,1)S(1)}, u32[]{:S(2)}, u32[]{:S(2)}) collective-permute-start(bf16[32,4096]{1,0:T(8,128)(2,1)S(1)} %pad_maximum_fusion.1), channel_id=1, source_target_pairs={{0,4},{1,5},{2,6},{3,7},{4,0},{5,1},{6,2},{7,3},{8,12},{9,13},{10,... | collective-permute-start | bytes 786440 | tf_op jit(solution)/shard_map/ppermute | solution.py:361
  56.0 13.2 %collective-permute-start.24 = (bf16[32,4096]{1,0:T(8,128)(2,1)S(1)}, bf16[32,4096]{1,0:T(8,128)(2,1)S(1)}, u32[]{:S(2)}, u32[]{:S(2)}) collective-permute-start(bf16[32,4096]{1,0:T(8,128)(2,1)S(1)} %pad_maximum_fusion.2), channel_id=1, source_target_pairs={{0,6},{1,7},{2,4},{3,5},{4,2},{5,3},{6,0},{7,1},{8,14},{9,15},{10,... | collective-permute-start | bytes 786440 | tf_op jit(solution)/shard_map/ppermute | solution.py:361
  57.1 13.6 %collective-permute-start.20 = (bf16[32,4096]{1,0:T(8,128)(2,1)S(1)}, bf16[32,4096]{1,0:T(8,128)(2,1)S(1)}, u32[]{:S(2)}, u32[]{:S(2)}) collective-permute-start(bf16[32,4096]{1,0:T(8,128)(2,1)S(1)} %pad_maximum_fusion), channel_id=1, source_target_pairs={{0,2},{1,3},{2,0},{3,1},{4,6},{5,7},{6,4},{7,5},{8,10},{9,11},{10,... | collective-permute-start | bytes 786440 | tf_op jit(solution)/shard_map/ppermute | solution.py:361
  70.9 5.0 %collective-permute-start.25 = (bf16[8,4096]{1,0:T(8,128)(2,1)S(1)}, bf16[8,4096]{1,0:T(8,128)(2,1)S(1)}, u32[]{:S(2)}, u32[]{:S(2)}) collective-permute-start(bf16[8,4096]{1,0:T(8,128)(2,1)S(1)} %get-tuple-element.34), channel_id=1, source_target_pairs={{0,8},{1,9},{2,10},{3,11},{4,12},{5,13},{6,14},{7,15},{8,0},{9,1},... | collective-permute-start | bytes 196616 | tf_op jit(solution)/shard_map/ppermute | solution.py:361
  71.2 6.8 %collective-permute-start.27 = (bf16[8,4096]{1,0:T(8,128)(2,1)S(1)}, bf16[8,4096]{1,0:T(8,128)(2,1)S(1)}, u32[]{:S(2)}, u32[]{:S(2)}) collective-permute-start(bf16[8,4096]{1,0:T(8,128)(2,1)S(1)} %get-tuple-element.35), channel_id=1, source_target_pairs={{0,24},{1,25},{2,26},{3,27},{4,28},{5,29},{6,30},{7,31},{8,16},{9,... | collective-permute-start | bytes 196616 | tf_op jit(solution)/shard_map/ppermute | solution.py:361
  74.2 6.2 %collective-permute-start.26 = (bf16[8,4096]{1,0:T(8,128)(2,1)S(1)}, bf16[8,4096]{1,0:T(8,128)(2,1)S(1)}, u32[]{:S(2)}, u32[]{:S(2)}) collective-permute-start(bf16[8,4096]{1,0:T(8,128)(2,1)S(1)} %get-tuple-element.36), channel_id=1, source_target_pairs={{0,16},{1,17},{2,18},{3,19},{4,20},{5,21},{6,22},{7,23},{8,24},{9,... | collective-permute-start | bytes 196616 | tf_op jit(solution)/shard_map/ppermute | solution.py:361
  (6 other events, 27.3 us)

commit v6 on v5

--- a/solution.py
+++ b/solution.py
@@ -220,13 +220,9 @@
 
 def projection_kernel(parts, *refs):
     got = refs[:parts]
-    w_ref, w0_hbm, w1_hbm, out_ref, w0_ref, w1_ref, attn, sem = refs[parts:]
-    ahead = [
-        pltpu.make_async_copy(w0_hbm, w0_ref, sem.at[0]),
-        pltpu.make_async_copy(w1_hbm, w1_ref, sem.at[1]),
-    ]
-    for c in ahead:
-        c.start()
+    w_ref, ahead_hbm, out_ref, ahead_ref, attn, sem = refs[parts:]
+    ahead = pltpu.make_async_copy(ahead_hbm, ahead_ref, sem)
+    ahead.start()
     tensor_pos = lax.axis_index("tensor")
     depth, width = w_ref.shape
     share = out_ref.shape[2]
@@ -253,8 +249,7 @@
         for t in range(parts):
             slot = tensor_pos ^ t
             out_ref[slot & 1, slot >> 1, :, cols] = result[t * share : (t + 1) * share].astype(BF)
-    for c in ahead:
-        c.wait()
+    ahead.wait()
 
 
 def projection(got, out_proj, share, later):
@@ -266,17 +261,19 @@
         functools.partial(projection_kernel, parts),
         out_shape=(
             jax.ShapeDtypeStruct((2, parts // 2, share, width), BF),
-            *[pltpu.VMEM(w.shape, w.dtype) for w in later],
+            pltpu.VMEM(later.shape, later.dtype),
         ),
-        in_specs=[vmem] * (parts + 1) + [pl.BlockSpec(memory_space=pltpu.HBM)] * 2,
-        out_specs=(vmem,) * 3,
-        scratch_shapes=[pltpu.VMEM((rows, depth), BF), pltpu.SemaphoreType.DMA((2,))],
+        in_specs=[vmem] * (parts + 1) + [pl.BlockSpec(memory_space=pltpu.HBM)],
+        out_specs=(vmem, vmem),
+        scratch_shapes=[pltpu.VMEM((rows, depth), BF), pltpu.SemaphoreType.DMA],
         compiler_params=pltpu.CompilerParams(vmem_limit_bytes=12 * MIB),
         name="projection",
-    )(*got, out_proj, *[in_hbm(w) for w in later])
-
-
-def expert_kernel(slots, x_ref, gate, up, down_hbm, out_ref, down, xc, act, res, sem):
+    )(*got, out_proj, in_hbm(later))
+
+
+def expert_kernel(
+    slots, x_ref, gate, up_hbm, down_hbm, o0, o1, o2, o3, up, down, xc, gated, act, res, sem
+):
     own = lax.axis_index("dp") * lax.axis_size("tensor") + lax.axis_index("tensor")
     rows = x_ref.shape[0]
     _, width, hidden = gate.shape
@@ -285,10 +282,18 @@
     dsize = 1024
     chunks = width // dsize
 
+    fchunks = hidden // fsize
+
+    def up_copy(i):
+        cols = pl.ds(i * fsize, fsize)
+        return pltpu.make_async_copy(up_hbm.at[0, :, cols], up.at[:, cols], sem.at[chunks + i])
+
     def down_copy(i):
         cols = pl.ds(i * dsize, dsize)
         return pltpu.make_async_copy(down_hbm.at[0, :, cols], down.at[:, cols], sem.at[i])
 
+    for i in range(fchunks):
+        up_copy(i).start()
     for i in range(chunks):
         down_copy(i).start()
     table = x_ref[:, width:]
@@ -311,16 +316,22 @@
     if padded > slots:
         res[slots:, :] = jnp.zeros((padded - slots, dsize), BF)
 
-    for i in range(hidden // fsize):
+    for i in range(fchunks):
         cols = slice(i * fsize, (i + 1) * fsize)
         g = matmul(xc[...], gate[0, :, cols])
-        u = matmul(xc[...], up[0, :, cols])
-        act[:, cols] = (g / (1.0 + jnp.exp(-g)) * u).astype(BF)
+        gated[:, cols] = g / (1.0 + jnp.exp(-g))
+    for i in range(fchunks):
+        up_copy(i).wait()
+        cols = slice(i * fsize, (i + 1) * fsize)
+        u = matmul(xc[...], up[:, cols])
+        act[:, cols] = (gated[:, cols] * u).astype(BF)
     for i in range(chunks):
         down_copy(i).wait()
         cols = slice(i * dsize, (i + 1) * dsize)
         res[:slots, :] = matmul(act[...], down[:, cols]).astype(BF)
-        out_ref[:, cols] = matmul(spread, res[...]).astype(BF)
+        result = matmul(spread, res[...]).astype(BF)
+        for k, out in enumerate((o0, o1, o2, o3)):
+            out[:, cols] = result[k * rows // 4 : (k + 1) * rows // 4]
 
 
 def experts(x, expert_gate, expert_up, expert_down, share):
@@ -330,19 +341,21 @@
     vmem = pl.BlockSpec(memory_space=pltpu.VMEM)
     return pl.pallas_call(
         functools.partial(expert_kernel, slots),
-        out_shape=jax.ShapeDtypeStruct((rows, width), BF),
-        in_specs=[vmem] * 3 + [pl.BlockSpec(memory_space=pltpu.HBM)],
-        out_specs=vmem,
+        out_shape=(jax.ShapeDtypeStruct((rows // 4, width), BF),) * 4,
+        in_specs=[vmem] * 2 + [pl.BlockSpec(memory_space=pltpu.HBM)] * 2,
+        out_specs=(vmem,) * 4,
         scratch_shapes=[
+            pltpu.VMEM((width, hidden), BF),
             pltpu.VMEM((hidden, width), BF),
             pltpu.VMEM((slots, width), BF),
+            pltpu.VMEM((slots, hidden), F32),
             pltpu.VMEM((slots, hidden), BF),
             pltpu.VMEM((-(-slots // LANES) * LANES, 1024), BF),
-            pltpu.SemaphoreType.DMA((width // 1024,)),
+            pltpu.SemaphoreType.DMA((width // 1024 + hidden // 256,)),
         ],
-        compiler_params=pltpu.CompilerParams(vmem_limit_bytes=(16 + rows // 32) * MIB),
+        compiler_params=pltpu.CompilerParams(vmem_limit_bytes=(22 + rows // 32) * MIB),
         name="experts",
-    )(x, expert_gate, expert_up, in_hbm(expert_down))
+    )(x, expert_gate, in_hbm(expert_up), in_hbm(expert_down))
 
 
 class Plan:
@@ -412,44 +425,54 @@
         out_proj,
     )
     got = [local[0]] + plan.swaps(list(local[1:]), list(range(1, tensor)))
-    partial, expert_gate, expert_up = projection(
-        got, out_proj, share, (expert_gate, expert_up)
-    )
+    partial, expert_gate = projection(got, out_proj, share, expert_gate)
     pair = total_of([partial[0], plan.swap(partial[1], plan.core)])
     projected = total_of([pair[0]] + plan.swaps(list(pair[1:]), plan.y))
     hidden = residual_in.astype(F32) + projected
     normed = rms_scale(hidden, norm_gain).astype(BF)
 
     mine = jnp.concatenate([normed, table], axis=1)
-    others = plan.spread(mine, plan.z)
-    near = plan.spread(mine + others[0][:, :1] * 0, plan.plane)
-    far = plan.spread(jnp.concatenate(others), plan.plane)
-    pieces = [jnp.concatenate([mine] + others + near)] + far
-    x = jnp.concatenate(pieces + [plan.swap(piece, plan.core) for piece in pieces])
-
-    result = experts(x, expert_gate, expert_up, expert_down, share)
-
-    sizes = [piece.shape[0] for piece in pieces]
-    starts = [sum(sizes[:i]) for i in range(len(sizes) + 1)]
-    every = starts[-1]
-    sums = [
-        total_of(
-            [
-                result[starts[i] : starts[i + 1]],
-                plan.swap(result[every + starts[i] : every + starts[i + 1]], plan.core),
-            ]
-        )
-        for i in reversed(range(len(sizes)))
-    ][::-1]
-    blocks = sums[0].reshape(-1, share, width)
-    sent = [
-        jnp.concatenate([near.astype(BF), far.astype(BF)])
-        for near, far in zip(blocks[plan.zlen :], sums[1:])
-    ]
-    column = total_of(
-        [sums[0][: plan.zlen * share]] + plan.swaps(sent, plan.plane)
-    ).reshape(-1, share, width)
-    moe_sum = total_of([column[0]] + plan.swaps(list(column[1:]), plan.z))
+    column = [mine] + plan.spread(mine, plan.z)
+    cut = len(column) // 2
+    near, far = jnp.concatenate(column[:cut]), jnp.concatenate(column[cut:])
+    nears = plan.spread(near, plan.plane)
+    far_in = far + nears[0][:, :1] * 0
+    fars = plan.spread(far_in, plan.plane)
+    group = far.shape[0]
+    first = plan.swap(jnp.concatenate([far, near]), plan.core)
+    first = list(first.reshape(-1, group, first.shape[1]))
+    rest = [plan.swap(piece, plan.core) for piece in nears[0:] + fars]
+    there = first + rest
+    here = [far, near] + nears + fars
+
+    def grouped(pieces, last):
+        count = len(nears)
+        pairs = zip([pieces[1]] + pieces[2 : 2 + count], [pieces[0]] + pieces[2 + count :])
+        cuts = []
+        for front, back in pairs:
+            both = jnp.concatenate([front, back])
+            if last:
+                cuts += [both[:share], both[-share:]]
+            else:
+                cuts.append(both[share:-share])
+        return cuts
+
+    x = jnp.concatenate(
+        grouped(here, True) + grouped(here, False) + grouped(there, True) + grouped(there, False)
+    )
+
+    kept_a, kept_b, sent_a, sent_b = experts(x, expert_gate, expert_up, expert_down, share)
+
+    def plane_sums(kept, sent):
+        value = total_of([kept, plan.swap(sent, plan.core)])
+        value = value.reshape(1 + len(plan.plane), -1, width)
+        value = total_of([value[0]] + plan.swaps(list(value[1:]), plan.plane))
+        return list(value.reshape(-1, share, width))
+
+    ends = plane_sums(kept_a, sent_a)
+    last = plan.swap(ends[1].astype(BF), plan.z[-1])
+    middle = plan.swaps(plane_sums(kept_b, sent_b), plan.z[:-1])
+    moe_sum = total_of([ends[0], last] + middle)
     return (hidden + moe_sum).astype(BF)
 
 

time: 81.3 us -> 80.4 us (0.989)
  waiting for transfers between devices: 38.2 us -> 25.5 us
  starting transfers between devices: 25.3 us -> 37.1 us
    ppermute x28 -> x32, waiting for transfers between devices: 38.2 us -> 25.5 us  [swap(): lax.ppermute(value, ('dp', 'tensor'), [(i, i ^ flip) for i in range(self....]
    ppermute x28 -> x32, starting transfers between devices: 25.3 us -> 37.1 us  [swap(): lax.ppermute(value, ('dp', 'tensor'), [(i, i ^ flip) for i in range(self....]
    pallas_call x1, Pallas kernels: 4.77 us -> 3.22 us  [projection(): pl.pallas_call(functools.partial(projection_kernel, parts), out_shape=(ja...]
    pallas_call x1, Pallas kernels: 6.48 us -> 7.96 us  [experts(): pl.pallas_call(functools.partial(expert_kernel, slots), out_shape=(jax.Sh...]
  transfers between devices with their start and end apart: 28 -> 32, of which waited for: 21 -> 13; matrix products, arithmetic and copies ran while one was open for 1% -> 1% of each run, Pallas kernels for 0% -> 0%
where the time goes in v6:
time: 80.4 us; the launch traced here: 80.2 us
  starting transfers between devices  37.1 us (46%)
  waiting for transfers between devices  25.5 us (32%)
  Pallas kernels  15.3 us (19%)
  other arithmetic  1.76 us (2%)
    ppermute x32, starting transfers between devices, swap(): lax.ppermute(value, ('dp', 'tensor'), [(i, i ^ flip) for i in range(self....  37.1 us
    ppermute x32, waiting for transfers between devices, swap(): lax.ppermute(value, ('dp', 'tensor'), [(i, i ^ flip) for i in range(self....  25.5 us
    pallas_call x1, Pallas kernels, experts(): pl.pallas_call(functools.partial(expert_kernel, slots), out_shape=(jax.Sh...  7.96 us
    pallas_call x1, Pallas kernels, attention(): pl.pallas_call(attention_kernel, out_shape=(jax.ShapeDtypeStruct((parts,...  4.12 us
    pallas_call x1, Pallas kernels, projection(): pl.pallas_call(functools.partial(projection_kernel, parts), out_shape=(ja...  3.22 us
  transfers between devices with their start and end apart: 32, of which 13 were waited for; matrix products, arithmetic and copies ran while one was open for 1% of the time, Pallas kernels for 0%

profile of v6, /device:TPU:0, one launch (start us, length us, event | category | flops | bytes accessed | tf_op | source)
XLA Modules:
  0.0 80.2 jit_solution(12906164032771584330)
XLA Ops:
  0.0 4.1 %attention.1 = (bf16[4,32,1152]{2,1,0:T(8,128)(2,1)S(1)}, bf16[8,128]{1,0:T(8,128)(2,1)S(1)}, bf16[1024,4096]{1,0:T(8,128)(2,1)S(1)}) custom-call(s32[32]{0:T(128)} %len_hbm.1, bf16[32,32,128]{2,1,0:T(8,128)(2,1)} %q_hbm.1, bf16[32,2,128]{2,1,0:T(2,128)(2,1)} %nk_hbm.1, bf16[32,2,128]{2,1,0:T(2,128)(2,1)} %nv_hbm.1, bf16[32,2,32,128]{3,2,1,0:T(8,128)(2,1)} %k_hbm.1, ...), custom_call_target="tpu_custom_call" | custom-call | tf_op jit(solution)/shard_map/attention/pallas_call | solution.py:195
  4.2 2.5 %collective-permute-start.2 = (bf16[32,1152]{1,0:T(8,128)(2,1)S(1)}, bf16[32,1152]{1,0:T(8,128)(2,1)S(1)}, u32[]{:S(2)}, u32[]{:S(2)}) collective-permute-start(bf16[32,1152]{1,0:T(8,128)(2,1)S(1)} %get-tuple-element.33), channel_id=1, source_target_pairs={{0,3},{1,2},{2,1},{3,0},{4,7},{5,6},{6,5},{7,4},{8,11},{9,10},{10,... | collective-permute-start | bytes 221192 | tf_op jit(solution)/shard_map/ppermute | solution.py:374
  7.3 2.0 %collective-permute-done.2.refs_3_ = bf16[32,1152]{1,0:T(8,128)(2,1)S(1)} collective-permute-done((bf16[32,1152]{1,0:T(8,128)(2,1)S(1)}, bf16[32,1152]{1,0:T(8,128)(2,1)S(1)}, u32[]{:S(2)}, u32[]{:S(2)}) %collective-permute-start.2) | collective-permute-done | bytes 73760 | tf_op jit(solution)/shard_map/ppermute | solution.py:374
  9.3 2.2 %collective-permute-done.1.refs_2_ = bf16[32,1152]{1,0:T(8,128)(2,1)S(1)} collective-permute-done((bf16[32,1152]{1,0:T(8,128)(2,1)S(1)}, bf16[32,1152]{1,0:T(8,128)(2,1)S(1)}, u32[]{:S(2)}, u32[]{:S(2)}) %collective-permute-start.1) | collective-permute-done | bytes 73760 | tf_op jit(solution)/shard_map/ppermute | solution.py:374
  11.5 3.2 %projection.1 = (bf16[2,2,8,4096]{3,2,1,0:T(8,128)(2,1)S(1)}, bf16[1,4096,768]{2,1,0:T(8,128)(2,1)S(1)}) custom-call(bf16[32,1152]{1,0:T(8,128)(2,1)S(1)} %get-tuple-element.36.refs_0_, bf16[32,1152]{1,0:T(8,128)(2,1)S(1)} %collective-permute-done.refs_1_, bf16[32,1152]{1,0:T(8,128)(2,1)S(1)} %collective-permute-done.1.refs_2_, ...), custom_call_target="tpu_custom_call" | custom-call | tf_op jit(solution)/shard_map/projection/pallas_call | solution.py:260
  14.8 1.3 %collective-permute-done.3 = bf16[2,8,4096]{2,1,0:T(8,128)(2,1)S(1)} collective-permute-done((bf16[2,8,4096]{2,1,0:T(8,128)(2,1)S(1)}, bf16[2,8,4096]{2,1,0:T(8,128)(2,1)S(1)}, u32[]{:S(2)}, u32[]{:S(2)}) %collective-permute-start.3) | collective-permute-done | bytes 131104 | tf_op jit(solution)/shard_map/ppermute | solution.py:374
  16.2 1.9 %collective-permute-start.4 = (bf16[8,4096]{1,0:T(8,128)(2,1)S(1)}, bf16[8,4096]{1,0:T(8,128)(2,1)S(1)}, u32[]{:S(2)}, u32[]{:S(2)}) collective-permute-start(bf16[8,4096]{1,0:T(8,128)(2,1)S(1)} %fusion.18), channel_id=1, source_target_pairs={{0,2},{1,3},{2,0},{3,1},{4,6},{5,7},{6,4},{7,5},{8,10},{9,11},{10,... | collective-permute-start | bytes 196616 | tf_op jit(solution)/shard_map/ppermute | solution.py:374
  18.1 2.4 %collective-permute-done.4 = bf16[8,4096]{1,0:T(8,128)(2,1)S(1)} collective-permute-done((bf16[8,4096]{1,0:T(8,128)(2,1)S(1)}, bf16[8,4096]{1,0:T(8,128)(2,1)S(1)}, u32[]{:S(2)}, u32[]{:S(2)}) %collective-permute-start.4) | collective-permute-done | bytes 65568 | tf_op jit(solution)/shard_map/ppermute | solution.py:374
  20.8 2.0 %collective-permute-start.6 = (bf16[8,4224]{1,0:T(8,128)(2,1)S(1)}, bf16[8,4224]{1,0:T(8,128)(2,1)S(1)}, u32[]{:S(2)}, u32[]{:S(2)}) collective-permute-start(bf16[8,4224]{1,0:T(8,128)(2,1)S(1)} %get-tuple-element.41), channel_id=1, source_target_pairs={{0,8},{1,9},{2,10},{3,11},{4,12},{5,13},{6,14},{7,15},{8,0},{9,1},... | collective-permute-start | bytes 202760 | tf_op jit(solution)/shard_map/ppermute | solution.py:374
  22.8 2.5 %collective-permute-start.5 = (bf16[8,4224]{1,0:T(8,128)(2,1)S(1)}, bf16[8,4224]{1,0:T(8,128)(2,1)S(1)}, u32[]{:S(2)}, u32[]{:S(2)}) collective-permute-start(bf16[8,4224]{1,0:T(8,128)(2,1)S(1)} %get-tuple-element.41), channel_id=1, source_target_pairs={{0,24},{1,25},{2,26},{3,27},{4,28},{5,29},{6,30},{7,31},{8,16},{9,... | collective-permute-start | bytes 202760 | tf_op jit(solution)/shard_map/ppermute | solution.py:374
  25.4 2.6 %collective-permute-start.12 = (bf16[16,4224]{1,0:T(8,128)(2,1)S(1)}, bf16[16,4224]{1,0:T(8,128)(2,1)S(1)}, u32[]{:S(2)}, u32[]{:S(2)}) collective-permute-start(bf16[16,4224]{1,0:T(8,128)(2,1)S(1)} %pad_maximum_fusion.8), channel_id=1, source_target_pairs={{0,6},{1,7},{2,4},{3,5},{4,2},{5,3},{6,0},{7,1},{8,14},{9,15},{10,... | collective-permute-start | bytes 405512 | tf_op jit(solution)/shard_map/ppermute | solution.py:374
  29.0 2.3 %collective-permute-done.8 = bf16[8,4224]{1,0:T(8,128)(2,1)S(1)} collective-permute-done((bf16[8,4224]{1,0:T(8,128)(2,1)S(1)}, bf16[8,4224]{1,0:T(8,128)(2,1)S(1)}, u32[]{:S(2)}, u32[]{:S(2)}) %collective-permute-start.8) | collective-permute-done | bytes 67616 | tf_op jit(solution)/shard_map/ppermute | solution.py:374
  31.4 2.2 %collective-permute-done.7 = bf16[16,4224]{1,0:T(8,128)(2,1)S(1)} collective-permute-done((bf16[16,4224]{1,0:T(8,128)(2,1)S(1)}, bf16[16,4224]{1,0:T(8,128)(2,1)S(1)}, u32[]{:S(2)}, u32[]{:S(2)}) %collective-permute-start.7) | collective-permute-done | bytes 135200 | tf_op jit(solution)/shard_map/ppermute | solution.py:374
  33.8 2.1 %collective-permute-start.13 = (bf16[16,4224]{1,0:T(8,128)(2,1)S(1)}, bf16[16,4224]{1,0:T(8,128)(2,1)S(1)}, u32[]{:S(2)}, u32[]{:S(2)}) collective-permute-start(bf16[16,4224]{1,0:T(8,128)(2,1)S(1)} %maximum_add_fusion), channel_id=1, source_target_pairs={{0,6},{1,7},{2,4},{3,5},{4,2},{5,3},{6,0},{7,1},{8,14},{9,15},{10,... | collective-permute-start | bytes 405512 | tf_op jit(solution)/shard_map/ppermute | solution.py:374
  37.4 4.4 %collective-permute-done.9 = bf16[16,4224]{1,0:T(8,128)(2,1)S(1)} collective-permute-done((bf16[16,4224]{1,0:T(8,128)(2,1)S(1)}, bf16[16,4224]{1,0:T(8,128)(2,1)S(1)}, u32[]{:S(2)}, u32[]{:S(2)}) %collective-permute-start.9) | collective-permute-done | bytes 135200 | tf_op jit(solution)/shard_map/ppermute | solution.py:374
  45.0 8.0 %experts.1 = (bf16[64,4096]{1,0:T(8,128)(2,1)S(1)}, bf16[64,4096]{1,0:T(8,128)(2,1)S(1)}, bf16[64,4096]{1,0:T(8,128)(2,1)S(1)}, bf16[64,4096]{1,0:T(8,128)(2,1)S(1)}) custom-call(bf16[256,4224]{1,0:T(8,128)(2,1)S(1)} %fusion.5.x_ref, bf16[1,4096,768]{2,1,0:T(8,128)(2,1)S(1)} %get-tuple-element.18.gate, bf16[1,4096,768]{2,1,0:T(8,128)(2,1)} %up_hbm.1, ...), custom_call_target="tpu_custom_call" | custom-call | tf_op jit(solution)/shard_map/experts/pallas_call | solution.py:342
  53.5 1.4 %collective-permute-done.21 = bf16[64,4096]{1,0:T(8,128)(2,1)S(1)} collective-permute-done((bf16[64,4096]{1,0:T(8,128)(2,1)S(1)}, bf16[64,4096]{1,0:T(8,128)(2,1)S(1)}, u32[]{:S(2)}, u32[]{:S(2)}) %collective-permute-start.21) | collective-permute-done | bytes 524320 | tf_op jit(solution)/shard_map/ppermute | solution.py:374
  55.1 1.3 %collective-permute-start.22 = (bf16[16,4096]{1,0:T(8,128)(2,1)S(1)}, bf16[16,4096]{1,0:T(8,128)(2,1)S(1)}, u32[]{:S(2)}, u32[]{:S(2)}) collective-permute-start(bf16[16,4096]{1,0:T(8,128)(2,1)S(1)} %get-tuple-element.30), channel_id=1, source_target_pairs={{0,2},{1,3},{2,0},{3,1},{4,6},{5,7},{6,4},{7,5},{8,10},{9,11},{10,... | collective-permute-start | bytes 393224 | tf_op jit(solution)/shard_map/ppermute | solution.py:374
  56.3 1.4 %collective-permute-start.24 = (bf16[16,4096]{1,0:T(8,128)(2,1)S(1)}, bf16[16,4096]{1,0:T(8,128)(2,1)S(1)}, u32[]{:S(2)}, u32[]{:S(2)}) collective-permute-start(bf16[16,4096]{1,0:T(8,128)(2,1)S(1)} %get-tuple-element.31), channel_id=1, source_target_pairs={{0,6},{1,7},{2,4},{3,5},{4,2},{5,3},{6,0},{7,1},{8,14},{9,15},{10,... | collective-permute-start | bytes 393224 | tf_op jit(solution)/shard_map/ppermute | solution.py:374
  60.1 1.4 %collective-permute-start.29 = (bf16[16,4096]{1,0:T(8,128)(2,1)S(1)}, bf16[16,4096]{1,0:T(8,128)(2,1)S(1)}, u32[]{:S(2)}, u32[]{:S(2)}) collective-permute-start(bf16[16,4096]{1,0:T(8,128)(2,1)S(1)} %get-tuple-element.28), channel_id=1, source_target_pairs={{0,6},{1,7},{2,4},{3,5},{4,2},{5,3},{6,0},{7,1},{8,14},{9,15},{10,... | collective-permute-start | bytes 393224 | tf_op jit(solution)/shard_map/ppermute | solution.py:374
  61.5 2.8 %collective-permute-done.22 = bf16[16,4096]{1,0:T(8,128)(2,1)S(1)} collective-permute-done((bf16[16,4096]{1,0:T(8,128)(2,1)S(1)}, bf16[16,4096]{1,0:T(8,128)(2,1)S(1)}, u32[]{:S(2)}, u32[]{:S(2)}) %collective-permute-start.22) | collective-permute-done | bytes 131104 | tf_op jit(solution)/shard_map/ppermute | solution.py:374
  65.9 5.3 %collective-permute-start.25 = (bf16[8,4096]{1,0:T(8,128)(2,1)S(1)}, bf16[8,4096]{1,0:T(8,128)(2,1)S(1)}, u32[]{:S(2)}, u32[]{:S(2)}) collective-permute-start(bf16[8,4096]{1,0:T(8,128)(2,1)S(1)} %unstack.110), channel_id=1, source_target_pairs={{0,24},{1,25},{2,26},{3,27},{4,28},{5,29},{6,30},{7,31},{8,16},{9,... | collective-permute-start | bytes 196616 | tf_op jit(solution)/shard_map/ppermute | solution.py:374
  72.3 4.3 %collective-permute-start.31 = (bf16[8,4096]{1,0:T(8,128)(2,1)S(1)}, bf16[8,4096]{1,0:T(8,128)(2,1)S(1)}, u32[]{:S(2)}, u32[]{:S(2)}) collective-permute-start(bf16[8,4096]{1,0:T(8,128)(2,1)S(1)} %get-tuple-element.40), channel_id=1, source_target_pairs={{0,16},{1,17},{2,18},{3,19},{4,20},{5,21},{6,22},{7,23},{8,24},{9,... | collective-permute-start | bytes 196616 | tf_op jit(solution)/shard_map/ppermute | solution.py:374
  76.6 2.9 %collective-permute-done.31 = bf16[8,4096]{1,0:T(8,128)(2,1)S(1)} collective-permute-done((bf16[8,4096]{1,0:T(8,128)(2,1)S(1)}, bf16[8,4096]{1,0:T(8,128)(2,1)S(1)}, u32[]{:S(2)}, u32[]{:S(2)}) %collective-permute-start.31) | collective-permute-done | bytes 65568 | tf_op jit(solution)/shard_map/ppermute | solution.py:374
  (93 shorter events, 13.4 us)
Async XLA Ops:
  4.2 5.1 %collective-permute-start.2 = (bf16[32,1152]{1,0:T(8,128)(2,1)S(1)}, bf16[32,1152]{1,0:T(8,128)(2,1)S(1)}, u32[]{:S(2)}, u32[]{:S(2)}) collective-permute-start(bf16[32,1152]{1,0:T(8,128)(2,1)S(1)} %get-tuple-element.33), channel_id=1, source_target_pairs={{0,3},{1,2},{2,1},{3,0},{4,7},{5,6},{6,5},{7,4},{8,11},{9,10},{10,... | collective-permute-start | bytes 221192 | tf_op jit(solution)/shard_map/ppermute | solution.py:374
  6.6 4.8 %collective-permute-start.1 = (bf16[32,1152]{1,0:T(8,128)(2,1)S(1)}, bf16[32,1152]{1,0:T(8,128)(2,1)S(1)}, u32[]{:S(2)}, u32[]{:S(2)}) collective-permute-start(bf16[32,1152]{1,0:T(8,128)(2,1)S(1)} %get-tuple-element.34), channel_id=1, source_target_pairs={{0,2},{1,3},{2,0},{3,1},{4,6},{5,7},{6,4},{7,5},{8,10},{9,11},{10,... | collective-permute-start | bytes 221192 | tf_op jit(solution)/shard_map/ppermute | solution.py:374
  7.3 4.2 %collective-permute-start = (bf16[32,1152]{1,0:T(8,128)(2,1)S(1)}, bf16[32,1152]{1,0:T(8,128)(2,1)S(1)}, u32[]{:S(2)}, u32[]{:S(2)}) collective-permute-start(bf16[32,1152]{1,0:T(8,128)(2,1)S(1)} %get-tuple-element.35), channel_id=1, source_target_pairs={{0,1},{1,0},{2,3},{3,2},{4,5},{5,4},{6,7},{7,6},{8,9},{9,8},{10,11... | collective-permute-start | bytes 221192 | tf_op jit(solution)/shard_map/ppermute | solution.py:374
  16.2 4.3 %collective-permute-start.4 = (bf16[8,4096]{1,0:T(8,128)(2,1)S(1)}, bf16[8,4096]{1,0:T(8,128)(2,1)S(1)}, u32[]{:S(2)}, u32[]{:S(2)}) collective-permute-start(bf16[8,4096]{1,0:T(8,128)(2,1)S(1)} %fusion.18), channel_id=1, source_target_pairs={{0,2},{1,3},{2,0},{3,1},{4,6},{5,7},{6,4},{7,5},{8,10},{9,11},{10,... | collective-permute-start | bytes 196616 | tf_op jit(solution)/shard_map/ppermute | solution.py:374
  20.8 4.6 %collective-permute-start.6 = (bf16[8,4224]{1,0:T(8,128)(2,1)S(1)}, bf16[8,4224]{1,0:T(8,128)(2,1)S(1)}, u32[]{:S(2)}, u32[]{:S(2)}) collective-permute-start(bf16[8,4224]{1,0:T(8,128)(2,1)S(1)} %get-tuple-element.41), channel_id=1, source_target_pairs={{0,8},{1,9},{2,10},{3,11},{4,12},{5,13},{6,14},{7,15},{8,0},{9,1},... | collective-permute-start | bytes 202760 | tf_op jit(solution)/shard_map/ppermute | solution.py:374
  22.8 6.2 %collective-permute-start.5 = (bf16[8,4224]{1,0:T(8,128)(2,1)S(1)}, bf16[8,4224]{1,0:T(8,128)(2,1)S(1)}, u32[]{:S(2)}, u32[]{:S(2)}) collective-permute-start(bf16[8,4224]{1,0:T(8,128)(2,1)S(1)} %get-tuple-element.41), channel_id=1, source_target_pairs={{0,24},{1,25},{2,26},{3,27},{4,28},{5,29},{6,30},{7,31},{8,16},{9,... | collective-permute-start | bytes 202760 | tf_op jit(solution)/shard_map/ppermute | solution.py:374
  25.3 6.0 %collective-permute-start.8 = (bf16[8,4224]{1,0:T(8,128)(2,1)S(1)}, bf16[8,4224]{1,0:T(8,128)(2,1)S(1)}, u32[]{:S(2)}, u32[]{:S(2)}) collective-permute-start(bf16[8,4224]{1,0:T(8,128)(2,1)S(1)} %get-tuple-element.41), channel_id=1, source_target_pairs={{0,16},{1,17},{2,18},{3,19},{4,20},{5,21},{6,22},{7,23},{8,24},{9,... | collective-permute-start | bytes 202760 | tf_op jit(solution)/shard_map/ppermute | solution.py:374
  25.4 16.4 %collective-permute-start.12 = (bf16[16,4224]{1,0:T(8,128)(2,1)S(1)}, bf16[16,4224]{1,0:T(8,128)(2,1)S(1)}, u32[]{:S(2)}, u32[]{:S(2)}) collective-permute-start(bf16[16,4224]{1,0:T(8,128)(2,1)S(1)} %pad_maximum_fusion.8), channel_id=1, source_target_pairs={{0,6},{1,7},{2,4},{3,5},{4,2},{5,3},{6,0},{7,1},{8,14},{9,15},{10,... | collective-permute-start | bytes 405512 | tf_op jit(solution)/shard_map/ppermute | solution.py:374
  28.0 8.8 %collective-permute-start.10 = (bf16[16,4224]{1,0:T(8,128)(2,1)S(1)}, bf16[16,4224]{1,0:T(8,128)(2,1)S(1)}, u32[]{:S(2)}, u32[]{:S(2)}) collective-permute-start(bf16[16,4224]{1,0:T(8,128)(2,1)S(1)} %pad_maximum_fusion.8), channel_id=1, source_target_pairs={{0,4},{1,5},{2,6},{3,7},{4,0},{5,1},{6,2},{7,3},{8,12},{9,13},{10,... | collective-permute-start | bytes 405512 | tf_op jit(solution)/shard_map/ppermute | solution.py:374
  28.6 5.0 %collective-permute-start.7 = (bf16[16,4224]{1,0:T(8,128)(2,1)S(1)}, bf16[16,4224]{1,0:T(8,128)(2,1)S(1)}, u32[]{:S(2)}, u32[]{:S(2)}) collective-permute-start(bf16[16,4224]{1,0:T(8,128)(2,1)S(1)} %pad_maximum_fusion.8), channel_id=1, source_target_pairs={{0,2},{1,3},{2,0},{3,1},{4,6},{5,7},{6,4},{7,5},{8,10},{9,11},{10,... | collective-permute-start | bytes 405512 | tf_op jit(solution)/shard_map/ppermute | solution.py:374
  31.3 11.8 %collective-permute-start.14 = (bf16[32,4224]{1,0:T(8,128)(2,1)S(1)}, bf16[32,4224]{1,0:T(8,128)(2,1)S(1)}, u32[]{:S(2)}, u32[]{:S(2)}) collective-permute-start(bf16[32,4224]{1,0:T(8,128)(2,1)S(1)} %pad_maximum_fusion), channel_id=1, source_target_pairs={{0,1},{1,0},{2,3},{3,2},{4,5},{5,4},{6,7},{7,6},{8,9},{9,8},{10,11... | collective-permute-start | bytes 811016 | tf_op jit(solution)/shard_map/ppermute | solution.py:374
  33.8 8.6 %collective-permute-start.13 = (bf16[16,4224]{1,0:T(8,128)(2,1)S(1)}, bf16[16,4224]{1,0:T(8,128)(2,1)S(1)}, u32[]{:S(2)}, u32[]{:S(2)}) collective-permute-start(bf16[16,4224]{1,0:T(8,128)(2,1)S(1)} %maximum_add_fusion), channel_id=1, source_target_pairs={{0,6},{1,7},{2,4},{3,5},{4,2},{5,3},{6,0},{7,1},{8,14},{9,15},{10,... | collective-permute-start | bytes 405512 | tf_op jit(solution)/shard_map/ppermute | solution.py:374
  35.9 5.9 %collective-permute-start.9 = (bf16[16,4224]{1,0:T(8,128)(2,1)S(1)}, bf16[16,4224]{1,0:T(8,128)(2,1)S(1)}, u32[]{:S(2)}, u32[]{:S(2)}) collective-permute-start(bf16[16,4224]{1,0:T(8,128)(2,1)S(1)} %maximum_add_fusion), channel_id=1, source_target_pairs={{0,2},{1,3},{2,0},{3,1},{4,6},{5,7},{6,4},{7,5},{8,10},{9,11},{10,... | collective-permute-start | bytes 405512 | tf_op jit(solution)/shard_map/ppermute | solution.py:374
  36.8 5.7 %collective-permute-start.11 = (bf16[16,4224]{1,0:T(8,128)(2,1)S(1)}, bf16[16,4224]{1,0:T(8,128)(2,1)S(1)}, u32[]{:S(2)}, u32[]{:S(2)}) collective-permute-start(bf16[16,4224]{1,0:T(8,128)(2,1)S(1)} %maximum_add_fusion), channel_id=1, source_target_pairs={{0,4},{1,5},{2,6},{3,7},{4,0},{5,1},{6,2},{7,3},{8,12},{9,13},{10,... | collective-permute-start | bytes 405512 | tf_op jit(solution)/shard_map/ppermute | solution.py:374
  53.4 5.3 %collective-permute-start.26 = (bf16[64,4096]{1,0:T(8,128)(2,1)S(1)}, bf16[64,4096]{1,0:T(8,128)(2,1)S(1)}, u32[]{:S(2)}, u32[]{:S(2)}) collective-permute-start(bf16[64,4096]{1,0:T(8,128)(2,1)S(1)} %get-tuple-element.22), channel_id=1, source_target_pairs={{0,1},{1,0},{2,3},{3,2},{4,5},{5,4},{6,7},{7,6},{8,9},{9,8},{10,11... | collective-permute-start | bytes 1572872 | tf_op jit(solution)/shard_map/ppermute | solution.py:374
  55.1 9.2 %collective-permute-start.22 = (bf16[16,4096]{1,0:T(8,128)(2,1)S(1)}, bf16[16,4096]{1,0:T(8,128)(2,1)S(1)}, u32[]{:S(2)}, u32[]{:S(2)}) collective-permute-start(bf16[16,4096]{1,0:T(8,128)(2,1)S(1)} %get-tuple-element.30), channel_id=1, source_target_pairs={{0,2},{1,3},{2,0},{3,1},{4,6},{5,7},{6,4},{7,5},{8,10},{9,11},{10,... | collective-permute-start | bytes 393224 | tf_op jit(solution)/shard_map/ppermute | solution.py:374
  56.3 9.1 %collective-permute-start.24 = (bf16[16,4096]{1,0:T(8,128)(2,1)S(1)}, bf16[16,4096]{1,0:T(8,128)(2,1)S(1)}, u32[]{:S(2)}, u32[]{:S(2)}) collective-permute-start(bf16[16,4096]{1,0:T(8,128)(2,1)S(1)} %get-tuple-element.31), channel_id=1, source_target_pairs={{0,6},{1,7},{2,4},{3,5},{4,2},{5,3},{6,0},{7,1},{8,14},{9,15},{10,... | collective-permute-start | bytes 393224 | tf_op jit(solution)/shard_map/ppermute | solution.py:374
  57.8 8.1 %collective-permute-start.23 = (bf16[16,4096]{1,0:T(8,128)(2,1)S(1)}, bf16[16,4096]{1,0:T(8,128)(2,1)S(1)}, u32[]{:S(2)}, u32[]{:S(2)}) collective-permute-start(bf16[16,4096]{1,0:T(8,128)(2,1)S(1)} %get-tuple-element.32), channel_id=1, source_target_pairs={{0,4},{1,5},{2,6},{3,7},{4,0},{5,1},{6,2},{7,3},{8,12},{9,13},{10,... | collective-permute-start | bytes 393224 | tf_op jit(solution)/shard_map/ppermute | solution.py:374
  58.8 12.4 %collective-permute-start.27 = (bf16[16,4096]{1,0:T(8,128)(2,1)S(1)}, bf16[16,4096]{1,0:T(8,128)(2,1)S(1)}, u32[]{:S(2)}, u32[]{:S(2)}) collective-permute-start(bf16[16,4096]{1,0:T(8,128)(2,1)S(1)} %get-tuple-element.27), channel_id=1, source_target_pairs={{0,2},{1,3},{2,0},{3,1},{4,6},{5,7},{6,4},{7,5},{8,10},{9,11},{10,... | collective-permute-start | bytes 393224 | tf_op jit(solution)/shard_map/ppermute | solution.py:374
  60.1 11.2 %collective-permute-start.29 = (bf16[16,4096]{1,0:T(8,128)(2,1)S(1)}, bf16[16,4096]{1,0:T(8,128)(2,1)S(1)}, u32[]{:S(2)}, u32[]{:S(2)}) collective-permute-start(bf16[16,4096]{1,0:T(8,128)(2,1)S(1)} %get-tuple-element.28), channel_id=1, source_target_pairs={{0,6},{1,7},{2,4},{3,5},{4,2},{5,3},{6,0},{7,1},{8,14},{9,15},{10,... | collective-permute-start | bytes 393224 | tf_op jit(solution)/shard_map/ppermute | solution.py:374
  64.3 7.0 %collective-permute-start.28 = (bf16[16,4096]{1,0:T(8,128)(2,1)S(1)}, bf16[16,4096]{1,0:T(8,128)(2,1)S(1)}, u32[]{:S(2)}, u32[]{:S(2)}) collective-permute-start(bf16[16,4096]{1,0:T(8,128)(2,1)S(1)} %get-tuple-element.29), channel_id=1, source_target_pairs={{0,4},{1,5},{2,6},{3,7},{4,0},{5,1},{6,2},{7,3},{8,12},{9,13},{10,... | collective-permute-start | bytes 393224 | tf_op jit(solution)/shard_map/ppermute | solution.py:374
  65.9 10.7 %collective-permute-start.25 = (bf16[8,4096]{1,0:T(8,128)(2,1)S(1)}, bf16[8,4096]{1,0:T(8,128)(2,1)S(1)}, u32[]{:S(2)}, u32[]{:S(2)}) collective-permute-start(bf16[8,4096]{1,0:T(8,128)(2,1)S(1)} %unstack.110), channel_id=1, source_target_pairs={{0,24},{1,25},{2,26},{3,27},{4,28},{5,29},{6,30},{7,31},{8,16},{9,... | collective-permute-start | bytes 196616 | tf_op jit(solution)/shard_map/ppermute | solution.py:374
  71.3 5.2 %collective-permute-start.30 = (bf16[8,4096]{1,0:T(8,128)(2,1)S(1)}, bf16[8,4096]{1,0:T(8,128)(2,1)S(1)}, u32[]{:S(2)}, u32[]{:S(2)}) collective-permute-start(bf16[8,4096]{1,0:T(8,128)(2,1)S(1)} %get-tuple-element.39), channel_id=1, source_target_pairs={{0,8},{1,9},{2,10},{3,11},{4,12},{5,13},{6,14},{7,15},{8,0},{9,1},... | collective-permute-start | bytes 196616 | tf_op jit(solution)/shard_map/ppermute | solution.py:374
  72.3 7.3 %collective-permute-start.31 = (bf16[8,4096]{1,0:T(8,128)(2,1)S(1)}, bf16[8,4096]{1,0:T(8,128)(2,1)S(1)}, u32[]{:S(2)}, u32[]{:S(2)}) collective-permute-start(bf16[8,4096]{1,0:T(8,128)(2,1)S(1)} %get-tuple-element.40), channel_id=1, source_target_pairs={{0,16},{1,17},{2,18},{3,19},{4,20},{5,21},{6,22},{7,23},{8,24},{9,... | collective-permute-start | bytes 196616 | tf_op jit(solution)/shard_map/ppermute | solution.py:374
  (10 other events, 34.0 us)

commit v7 on v5

--- a/solution.py
+++ b/solution.py
@@ -220,13 +220,9 @@
 
 def projection_kernel(parts, *refs):
     got = refs[:parts]
-    w_ref, w0_hbm, w1_hbm, out_ref, w0_ref, w1_ref, attn, sem = refs[parts:]
-    ahead = [
-        pltpu.make_async_copy(w0_hbm, w0_ref, sem.at[0]),
-        pltpu.make_async_copy(w1_hbm, w1_ref, sem.at[1]),
-    ]
-    for c in ahead:
-        c.start()
+    w_ref, ahead_hbm, out_ref, ahead_ref, attn, sem = refs[parts:]
+    ahead = pltpu.make_async_copy(ahead_hbm, ahead_ref, sem)
+    ahead.start()
     tensor_pos = lax.axis_index("tensor")
     depth, width = w_ref.shape
     share = out_ref.shape[2]
@@ -253,8 +249,7 @@
         for t in range(parts):
             slot = tensor_pos ^ t
             out_ref[slot & 1, slot >> 1, :, cols] = result[t * share : (t + 1) * share].astype(BF)
-    for c in ahead:
-        c.wait()
+    ahead.wait()
 
 
 def projection(got, out_proj, share, later):
@@ -266,14 +261,14 @@
         functools.partial(projection_kernel, parts),
         out_shape=(
             jax.ShapeDtypeStruct((2, parts // 2, share, width), BF),
-            *[pltpu.VMEM(w.shape, w.dtype) for w in later],
+            pltpu.VMEM(later.shape, later.dtype),
         ),
-        in_specs=[vmem] * (parts + 1) + [pl.BlockSpec(memory_space=pltpu.HBM)] * 2,
-        out_specs=(vmem,) * 3,
-        scratch_shapes=[pltpu.VMEM((rows, depth), BF), pltpu.SemaphoreType.DMA((2,))],
+        in_specs=[vmem] * (parts + 1) + [pl.BlockSpec(memory_space=pltpu.HBM)],
+        out_specs=(vmem, vmem),
+        scratch_shapes=[pltpu.VMEM((rows, depth), BF), pltpu.SemaphoreType.DMA],
         compiler_params=pltpu.CompilerParams(vmem_limit_bytes=12 * MIB),
         name="projection",
-    )(*got, out_proj, *[in_hbm(w) for w in later])
+    )(*got, out_proj, in_hbm(later))
 
 
 def expert_kernel(slots, x_ref, gate, up, down_hbm, out_ref, down, xc, act, res, sem):
@@ -281,7 +276,7 @@
     rows = x_ref.shape[0]
     _, width, hidden = gate.shape
     padded = res.shape[0]
-    fsize = 256
+    fsize = 384
     dsize = 1024
     chunks = width // dsize
 
@@ -412,9 +407,7 @@
         out_proj,
     )
     got = [local[0]] + plan.swaps(list(local[1:]), list(range(1, tensor)))
-    partial, expert_gate, expert_up = projection(
-        got, out_proj, share, (expert_gate, expert_up)
-    )
+    partial, expert_gate = projection(got, out_proj, share, expert_gate)
     pair = total_of([partial[0], plan.swap(partial[1], plan.core)])
     projected = total_of([pair[0]] + plan.swaps(list(pair[1:]), plan.y))
     hidden = residual_in.astype(F32) + projected
@@ -442,14 +435,10 @@
         for i in reversed(range(len(sizes)))
     ][::-1]
     blocks = sums[0].reshape(-1, share, width)
-    sent = [
-        jnp.concatenate([near.astype(BF), far.astype(BF)])
-        for near, far in zip(blocks[plan.zlen :], sums[1:])
-    ]
-    column = total_of(
-        [sums[0][: plan.zlen * share]] + plan.swaps(sent, plan.plane)
-    ).reshape(-1, share, width)
-    moe_sum = total_of([column[0]] + plan.swaps(list(column[1:]), plan.z))
+    far = plan.swaps(sums[1:], plan.plane)
+    others = total_of([sums[0][share : plan.zlen * share]] + far).reshape(-1, share, width)
+    near = plan.swaps(list(blocks[plan.zlen :]), plan.plane)
+    moe_sum = total_of([blocks[0]] + near + plan.swaps(list(others), plan.z))
     return (hidden + moe_sum).astype(BF)
 
 

time: 81.3 us -> 76.5 us (0.941)
  waiting for transfers between devices: 38.2 us -> 30.8 us
  starting transfers between devices: 25.3 us -> 29.2 us
  Pallas kernels: 15.4 us -> 14.1 us
    ppermute x28 -> x31, waiting for transfers between devices: 38.2 us -> 30.8 us  [swap(): lax.ppermute(value, ('dp', 'tensor'), [(i, i ^ flip) for i in range(self....]
    ppermute x28 -> x31, starting transfers between devices: 25.3 us -> 29.2 us  [swap(): lax.ppermute(value, ('dp', 'tensor'), [(i, i ^ flip) for i in range(self....]
    pallas_call x1, Pallas kernels: 4.77 us -> 3.46 us  [projection(): pl.pallas_call(functools.partial(projection_kernel, parts), out_shape=(ja...]
  transfers between devices with their start and end apart: 28 -> 31, of which waited for: 21 -> 18; matrix products, arithmetic and copies ran while one was open for 1% -> 1% of each run, Pallas kernels for 0% -> 0%
where the time goes in v7:
time: 76.5 us; the launch traced here: 76.4 us
  waiting for transfers between devices  30.8 us (40%)
  starting transfers between devices  29.2 us (38%)
  Pallas kernels  14.1 us (18%)
  other arithmetic  1.55 us (2%)
    ppermute x31, waiting for transfers between devices, swap(): lax.ppermute(value, ('dp', 'tensor'), [(i, i ^ flip) for i in range(self....  30.8 us
    ppermute x31, starting transfers between devices, swap(): lax.ppermute(value, ('dp', 'tensor'), [(i, i ^ flip) for i in range(self....  29.2 us
    pallas_call x1, Pallas kernels, experts(): pl.pallas_call(functools.partial(expert_kernel, slots), out_shape=jax.Sha...  6.49 us
    pallas_call x1, Pallas kernels, attention(): pl.pallas_call(attention_kernel, out_shape=(jax.ShapeDtypeStruct((parts,...  4.12 us
    pallas_call x1, Pallas kernels, projection(): pl.pallas_call(functools.partial(projection_kernel, parts), out_shape=(ja...  3.46 us
  transfers between devices with their start and end apart: 31, of which 18 were waited for; matrix products, arithmetic and copies ran while one was open for 1% of the time, Pallas kernels for 0%

profile of v7, /device:TPU:0, one launch (start us, length us, event | category | flops | bytes accessed | tf_op | source)
XLA Modules:
  0.0 76.4 jit_solution(8430180255989053815)
XLA Ops:
  0.0 4.1 %attention.1 = (bf16[4,32,1152]{2,1,0:T(8,128)(2,1)S(1)}, bf16[8,128]{1,0:T(8,128)(2,1)S(1)}, bf16[1024,4096]{1,0:T(8,128)(2,1)S(1)}) custom-call(s32[32]{0:T(128)} %len_hbm.1, bf16[32,32,128]{2,1,0:T(8,128)(2,1)} %q_hbm.1, bf16[32,2,128]{2,1,0:T(2,128)(2,1)} %nk_hbm.1, bf16[32,2,128]{2,1,0:T(2,128)(2,1)} %nv_hbm.1, bf16[32,2,32,128]{3,2,1,0:T(8,128)(2,1)} %k_hbm.1, ...), custom_call_target="tpu_custom_call" | custom-call | tf_op jit(solution)/shard_map/attention/pallas_call | solution.py:195
  4.2 2.5 %collective-permute-start.2 = (bf16[32,1152]{1,0:T(8,128)(2,1)S(1)}, bf16[32,1152]{1,0:T(8,128)(2,1)S(1)}, u32[]{:S(2)}, u32[]{:S(2)}) collective-permute-start(bf16[32,1152]{1,0:T(8,128)(2,1)S(1)} %get-tuple-element.26), channel_id=1, source_target_pairs={{0,3},{1,2},{2,1},{3,0},{4,7},{5,6},{6,5},{7,4},{8,11},{9,10},{10,... | collective-permute-start | bytes 221192 | tf_op jit(solution)/shard_map/ppermute | solution.py:356
  7.3 2.0 %collective-permute-done.2.refs_3_ = bf16[32,1152]{1,0:T(8,128)(2,1)S(1)} collective-permute-done((bf16[32,1152]{1,0:T(8,128)(2,1)S(1)}, bf16[32,1152]{1,0:T(8,128)(2,1)S(1)}, u32[]{:S(2)}, u32[]{:S(2)}) %collective-permute-start.2) | collective-permute-done | bytes 73760 | tf_op jit(solution)/shard_map/ppermute | solution.py:356
  9.3 2.2 %collective-permute-done.1.refs_2_ = bf16[32,1152]{1,0:T(8,128)(2,1)S(1)} collective-permute-done((bf16[32,1152]{1,0:T(8,128)(2,1)S(1)}, bf16[32,1152]{1,0:T(8,128)(2,1)S(1)}, u32[]{:S(2)}, u32[]{:S(2)}) %collective-permute-start.1) | collective-permute-done | bytes 73760 | tf_op jit(solution)/shard_map/ppermute | solution.py:356
  11.5 3.5 %projection.1 = (bf16[2,2,8,4096]{3,2,1,0:T(8,128)(2,1)S(1)}, bf16[1,4096,768]{2,1,0:T(8,128)(2,1)S(1)}) custom-call(bf16[32,1152]{1,0:T(8,128)(2,1)S(1)} %get-tuple-element.29.refs_0_, bf16[32,1152]{1,0:T(8,128)(2,1)S(1)} %collective-permute-done.refs_1_, bf16[32,1152]{1,0:T(8,128)(2,1)S(1)} %collective-permute-done.1.refs_2_, ...), custom_call_target="tpu_custom_call" | custom-call | tf_op jit(solution)/shard_map/projection/pallas_call | solution.py:260
  15.1 1.3 %collective-permute-done.3 = bf16[2,8,4096]{2,1,0:T(8,128)(2,1)S(1)} collective-permute-done((bf16[2,8,4096]{2,1,0:T(8,128)(2,1)S(1)}, bf16[2,8,4096]{2,1,0:T(8,128)(2,1)S(1)}, u32[]{:S(2)}, u32[]{:S(2)}) %collective-permute-start.3) | collective-permute-done | bytes 131104 | tf_op jit(solution)/shard_map/ppermute | solution.py:356
  16.5 1.9 %collective-permute-start.4 = (bf16[8,4096]{1,0:T(8,128)(2,1)S(1)}, bf16[8,4096]{1,0:T(8,128)(2,1)S(1)}, u32[]{:S(2)}, u32[]{:S(2)}) collective-permute-start(bf16[8,4096]{1,0:T(8,128)(2,1)S(1)} %fusion.12), channel_id=1, source_target_pairs={{0,2},{1,3},{2,0},{3,1},{4,6},{5,7},{6,4},{7,5},{8,10},{9,11},{10,... | collective-permute-start | bytes 196616 | tf_op jit(solution)/shard_map/ppermute | solution.py:356
  18.4 2.4 %collective-permute-done.4 = bf16[8,4096]{1,0:T(8,128)(2,1)S(1)} collective-permute-done((bf16[8,4096]{1,0:T(8,128)(2,1)S(1)}, bf16[8,4096]{1,0:T(8,128)(2,1)S(1)}, u32[]{:S(2)}, u32[]{:S(2)}) %collective-permute-start.4) | collective-permute-done | bytes 65568 | tf_op jit(solution)/shard_map/ppermute | solution.py:356
  21.1 2.0 %collective-permute-start.5 = (bf16[8,4224]{1,0:T(8,128)(2,1)S(1)}, bf16[8,4224]{1,0:T(8,128)(2,1)S(1)}, u32[]{:S(2)}, u32[]{:S(2)}) collective-permute-start(bf16[8,4224]{1,0:T(8,128)(2,1)S(1)} %pad_maximum_fusion), channel_id=1, source_target_pairs={{0,8},{1,9},{2,10},{3,11},{4,12},{5,13},{6,14},{7,15},{8,0},{9,1},... | collective-permute-start | bytes 202760 | tf_op jit(solution)/shard_map/ppermute | solution.py:356
  23.1 2.6 %collective-permute-start.6 = (bf16[8,4224]{1,0:T(8,128)(2,1)S(1)}, bf16[8,4224]{1,0:T(8,128)(2,1)S(1)}, u32[]{:S(2)}, u32[]{:S(2)}) collective-permute-start(bf16[8,4224]{1,0:T(8,128)(2,1)S(1)} %pad_maximum_fusion), channel_id=1, source_target_pairs={{0,16},{1,17},{2,18},{3,19},{4,20},{5,21},{6,22},{7,23},{8,24},{9,... | collective-permute-start | bytes 202760 | tf_op jit(solution)/shard_map/ppermute | solution.py:356
  26.3 2.8 %collective-permute-start.10 = (bf16[8,4224]{1,0:T(8,128)(2,1)S(1)}, bf16[8,4224]{1,0:T(8,128)(2,1)S(1)}, u32[]{:S(2)}, u32[]{:S(2)}) collective-permute-start(bf16[8,4224]{1,0:T(8,128)(2,1)S(1)} %get-tuple-element.50), channel_id=1, source_target_pairs={{0,6},{1,7},{2,4},{3,5},{4,2},{5,3},{6,0},{7,1},{8,14},{9,15},{10,... | collective-permute-start | bytes 202760 | tf_op jit(solution)/shard_map/ppermute | solution.py:356
  29.9 1.8 %collective-permute-done.7 = bf16[8,4224]{1,0:T(8,128)(2,1)S(1)} collective-permute-done((bf16[8,4224]{1,0:T(8,128)(2,1)S(1)}, bf16[8,4224]{1,0:T(8,128)(2,1)S(1)}, u32[]{:S(2)}, u32[]{:S(2)}) %collective-permute-start.7) | collective-permute-done | bytes 67616 | tf_op jit(solution)/shard_map/ppermute | solution.py:356
  31.7 2.5 %collective-permute-start.13 = (bf16[24,4224]{1,0:T(8,128)(2,1)S(1)}, bf16[24,4224]{1,0:T(8,128)(2,1)S(1)}, u32[]{:S(2)}, u32[]{:S(2)}) collective-permute-start(bf16[24,4224]{1,0:T(8,128)(2,1)S(1)} %get-tuple-element.41), channel_id=1, source_target_pairs={{0,6},{1,7},{2,4},{3,5},{4,2},{5,3},{6,0},{7,1},{8,14},{9,15},{10,... | collective-permute-start | bytes 608264 | tf_op jit(solution)/shard_map/ppermute | solution.py:356
  34.8 1.3 %collective-permute-done.8 = bf16[8,4224]{1,0:T(8,128)(2,1)S(1)} collective-permute-done((bf16[8,4224]{1,0:T(8,128)(2,1)S(1)}, bf16[8,4224]{1,0:T(8,128)(2,1)S(1)}, u32[]{:S(2)}, u32[]{:S(2)}) %collective-permute-start.8) | collective-permute-done | bytes 67616 | tf_op jit(solution)/shard_map/ppermute | solution.py:356
  36.3 3.7 %collective-permute-done.13 = bf16[24,4224]{1,0:T(8,128)(2,1)S(1)} collective-permute-done((bf16[24,4224]{1,0:T(8,128)(2,1)S(1)}, bf16[24,4224]{1,0:T(8,128)(2,1)S(1)}, u32[]{:S(2)}, u32[]{:S(2)}) %collective-permute-start.13) | collective-permute-done | bytes 202784 | tf_op jit(solution)/shard_map/ppermute | solution.py:356
  40.0 2.1 %collective-permute-done.12 = bf16[24,4224]{1,0:T(8,128)(2,1)S(1)} collective-permute-done((bf16[24,4224]{1,0:T(8,128)(2,1)S(1)}, bf16[24,4224]{1,0:T(8,128)(2,1)S(1)}, u32[]{:S(2)}, u32[]{:S(2)}) %collective-permute-start.12) | collective-permute-done | bytes 202784 | tf_op jit(solution)/shard_map/ppermute | solution.py:356
  42.8 1.1 %collective-permute-done.15 = bf16[24,4224]{1,0:T(8,128)(2,1)S(1)} collective-permute-done((bf16[24,4224]{1,0:T(8,128)(2,1)S(1)}, bf16[24,4224]{1,0:T(8,128)(2,1)S(1)}, u32[]{:S(2)}, u32[]{:S(2)}) %collective-permute-start.15) | collective-permute-done | bytes 202784 | tf_op jit(solution)/shard_map/ppermute | solution.py:356
  44.0 6.5 %experts.1 = bf16[256,4096]{1,0:T(8,128)(2,1)S(1)} custom-call(bf16[256,4224]{1,0:T(8,128)(2,1)S(1)} %constant_dynamic-update-slice_fusion.10.x_ref, bf16[1,4096,768]{2,1,0:T(8,128)(2,1)S(1)} %get-tuple-element.14.gate, bf16[1,4096,768]{2,1,0:T(8,128)(2,1)S(1)} %bitcast.30, bf16[1,768,4096]{2,1,0:T(8,128)(2,1)} %down_hbm.1), custom_call_target="tpu_custom_call" | custom-call | tf_op jit(solution)/shard_map/experts/pallas_call | solution.py:326
  53.6 1.9 %collective-permute-start.27 = (bf16[24,4096]{1,0:T(8,128)(2,1)S(1)}, bf16[24,4096]{1,0:T(8,128)(2,1)S(1)}, u32[]{:S(2)}, u32[]{:S(2)}) collective-permute-start(bf16[24,4096]{1,0:T(8,128)(2,1)S(1)} %get-tuple-element.18), channel_id=1, source_target_pairs={{0,6},{1,7},{2,4},{3,5},{4,2},{5,3},{6,0},{7,1},{8,14},{9,15},{10,... | collective-permute-start | bytes 589832 | tf_op jit(solution)/shard_map/ppermute | solution.py:356
  57.3 1.9 %collective-permute-start.21 = (bf16[8,4096]{1,0:T(8,128)(2,1)S(1)}, bf16[8,4096]{1,0:T(8,128)(2,1)S(1)}, u32[]{:S(2)}, u32[]{:S(2)}) collective-permute-start(bf16[8,4096]{1,0:T(8,128)(2,1)S(1)} %get-tuple-element.24), channel_id=1, source_target_pairs={{0,6},{1,7},{2,4},{3,5},{4,2},{5,3},{6,0},{7,1},{8,14},{9,15},{10,... | collective-permute-start | bytes 196616 | tf_op jit(solution)/shard_map/ppermute | solution.py:356
  59.2 5.8 %collective-permute-done.23 = bf16[24,4096]{1,0:T(8,128)(2,1)S(1)} collective-permute-done((bf16[24,4096]{1,0:T(8,128)(2,1)S(1)}, bf16[24,4096]{1,0:T(8,128)(2,1)S(1)}, u32[]{:S(2)}, u32[]{:S(2)}) %collective-permute-start.23) | collective-permute-done | bytes 196640 | tf_op jit(solution)/shard_map/ppermute | solution.py:356
  66.5 3.3 %collective-permute-start.30 = (bf16[8,4096]{1,0:T(8,128)(2,1)S(1)}, bf16[8,4096]{1,0:T(8,128)(2,1)S(1)}, u32[]{:S(2)}, u32[]{:S(2)}) collective-permute-start(bf16[8,4096]{1,0:T(8,128)(2,1)S(1)} %get-tuple-element.31), channel_id=1, source_target_pairs={{0,24},{1,25},{2,26},{3,27},{4,28},{5,29},{6,30},{7,31},{8,16},{9,... | collective-permute-start | bytes 196616 | tf_op jit(solution)/shard_map/ppermute | solution.py:356
  71.0 2.4 %collective-permute-done.30 = bf16[8,4096]{1,0:T(8,128)(2,1)S(1)} collective-permute-done((bf16[8,4096]{1,0:T(8,128)(2,1)S(1)}, bf16[8,4096]{1,0:T(8,128)(2,1)S(1)}, u32[]{:S(2)}, u32[]{:S(2)}) %collective-permute-start.30) | collective-permute-done | bytes 65568 | tf_op jit(solution)/shard_map/ppermute | solution.py:356
  73.4 2.2 %collective-permute-done.29 = bf16[8,4096]{1,0:T(8,128)(2,1)S(1)} collective-permute-done((bf16[8,4096]{1,0:T(8,128)(2,1)S(1)}, bf16[8,4096]{1,0:T(8,128)(2,1)S(1)}, u32[]{:S(2)}, u32[]{:S(2)}) %collective-permute-start.29) | collective-permute-done | bytes 65568 | tf_op jit(solution)/shard_map/ppermute | solution.py:356
  (81 shorter events, 12.1 us)
Async XLA Ops:
  4.2 5.1 %collective-permute-start.2 = (bf16[32,1152]{1,0:T(8,128)(2,1)S(1)}, bf16[32,1152]{1,0:T(8,128)(2,1)S(1)}, u32[]{:S(2)}, u32[]{:S(2)}) collective-permute-start(bf16[32,1152]{1,0:T(8,128)(2,1)S(1)} %get-tuple-element.26), channel_id=1, source_target_pairs={{0,3},{1,2},{2,1},{3,0},{4,7},{5,6},{6,5},{7,4},{8,11},{9,10},{10,... | collective-permute-start | bytes 221192 | tf_op jit(solution)/shard_map/ppermute | solution.py:356
  6.6 4.8 %collective-permute-start.1 = (bf16[32,1152]{1,0:T(8,128)(2,1)S(1)}, bf16[32,1152]{1,0:T(8,128)(2,1)S(1)}, u32[]{:S(2)}, u32[]{:S(2)}) collective-permute-start(bf16[32,1152]{1,0:T(8,128)(2,1)S(1)} %get-tuple-element.27), channel_id=1, source_target_pairs={{0,2},{1,3},{2,0},{3,1},{4,6},{5,7},{6,4},{7,5},{8,10},{9,11},{10,... | collective-permute-start | bytes 221192 | tf_op jit(solution)/shard_map/ppermute | solution.py:356
  7.3 4.2 %collective-permute-start = (bf16[32,1152]{1,0:T(8,128)(2,1)S(1)}, bf16[32,1152]{1,0:T(8,128)(2,1)S(1)}, u32[]{:S(2)}, u32[]{:S(2)}) collective-permute-start(bf16[32,1152]{1,0:T(8,128)(2,1)S(1)} %get-tuple-element.28), channel_id=1, source_target_pairs={{0,1},{1,0},{2,3},{3,2},{4,5},{5,4},{6,7},{7,6},{8,9},{9,8},{10,11... | collective-permute-start | bytes 221192 | tf_op jit(solution)/shard_map/ppermute | solution.py:356
  16.5 4.3 %collective-permute-start.4 = (bf16[8,4096]{1,0:T(8,128)(2,1)S(1)}, bf16[8,4096]{1,0:T(8,128)(2,1)S(1)}, u32[]{:S(2)}, u32[]{:S(2)}) collective-permute-start(bf16[8,4096]{1,0:T(8,128)(2,1)S(1)} %fusion.12), channel_id=1, source_target_pairs={{0,2},{1,3},{2,0},{3,1},{4,6},{5,7},{6,4},{7,5},{8,10},{9,11},{10,... | collective-permute-start | bytes 196616 | tf_op jit(solution)/shard_map/ppermute | solution.py:356
  21.1 5.0 %collective-permute-start.5 = (bf16[8,4224]{1,0:T(8,128)(2,1)S(1)}, bf16[8,4224]{1,0:T(8,128)(2,1)S(1)}, u32[]{:S(2)}, u32[]{:S(2)}) collective-permute-start(bf16[8,4224]{1,0:T(8,128)(2,1)S(1)} %pad_maximum_fusion), channel_id=1, source_target_pairs={{0,8},{1,9},{2,10},{3,11},{4,12},{5,13},{6,14},{7,15},{8,0},{9,1},... | collective-permute-start | bytes 202760 | tf_op jit(solution)/shard_map/ppermute | solution.py:356
  23.1 6.8 %collective-permute-start.6 = (bf16[8,4224]{1,0:T(8,128)(2,1)S(1)}, bf16[8,4224]{1,0:T(8,128)(2,1)S(1)}, u32[]{:S(2)}, u32[]{:S(2)}) collective-permute-start(bf16[8,4224]{1,0:T(8,128)(2,1)S(1)} %pad_maximum_fusion), channel_id=1, source_target_pairs={{0,16},{1,17},{2,18},{3,19},{4,20},{5,21},{6,22},{7,23},{8,24},{9,... | collective-permute-start | bytes 202760 | tf_op jit(solution)/shard_map/ppermute | solution.py:356
  25.6 6.1 %collective-permute-start.7 = (bf16[8,4224]{1,0:T(8,128)(2,1)S(1)}, bf16[8,4224]{1,0:T(8,128)(2,1)S(1)}, u32[]{:S(2)}, u32[]{:S(2)}) collective-permute-start(bf16[8,4224]{1,0:T(8,128)(2,1)S(1)} %pad_maximum_fusion), channel_id=1, source_target_pairs={{0,24},{1,25},{2,26},{3,27},{4,28},{5,29},{6,30},{7,31},{8,16},{9,... | collective-permute-start | bytes 202760 | tf_op jit(solution)/shard_map/ppermute | solution.py:356
  26.3 9.9 %collective-permute-start.10 = (bf16[8,4224]{1,0:T(8,128)(2,1)S(1)}, bf16[8,4224]{1,0:T(8,128)(2,1)S(1)}, u32[]{:S(2)}, u32[]{:S(2)}) collective-permute-start(bf16[8,4224]{1,0:T(8,128)(2,1)S(1)} %get-tuple-element.50), channel_id=1, source_target_pairs={{0,6},{1,7},{2,4},{3,5},{4,2},{5,3},{6,0},{7,1},{8,14},{9,15},{10,... | collective-permute-start | bytes 202760 | tf_op jit(solution)/shard_map/ppermute | solution.py:356
  29.1 7.0 %collective-permute-start.9 = (bf16[8,4224]{1,0:T(8,128)(2,1)S(1)}, bf16[8,4224]{1,0:T(8,128)(2,1)S(1)}, u32[]{:S(2)}, u32[]{:S(2)}) collective-permute-start(bf16[8,4224]{1,0:T(8,128)(2,1)S(1)} %get-tuple-element.50), channel_id=1, source_target_pairs={{0,4},{1,5},{2,6},{3,7},{4,0},{5,1},{6,2},{7,3},{8,12},{9,13},{10,... | collective-permute-start | bytes 202760 | tf_op jit(solution)/shard_map/ppermute | solution.py:356
  29.7 6.5 %collective-permute-start.8 = (bf16[8,4224]{1,0:T(8,128)(2,1)S(1)}, bf16[8,4224]{1,0:T(8,128)(2,1)S(1)}, u32[]{:S(2)}, u32[]{:S(2)}) collective-permute-start(bf16[8,4224]{1,0:T(8,128)(2,1)S(1)} %get-tuple-element.50), channel_id=1, source_target_pairs={{0,2},{1,3},{2,0},{3,1},{4,6},{5,7},{6,4},{7,5},{8,10},{9,11},{10,... | collective-permute-start | bytes 202760 | tf_op jit(solution)/shard_map/ppermute | solution.py:356
  31.7 8.3 %collective-permute-start.13 = (bf16[24,4224]{1,0:T(8,128)(2,1)S(1)}, bf16[24,4224]{1,0:T(8,128)(2,1)S(1)}, u32[]{:S(2)}, u32[]{:S(2)}) collective-permute-start(bf16[24,4224]{1,0:T(8,128)(2,1)S(1)} %get-tuple-element.41), channel_id=1, source_target_pairs={{0,6},{1,7},{2,4},{3,5},{4,2},{5,3},{6,0},{7,1},{8,14},{9,15},{10,... | collective-permute-start | bytes 608264 | tf_op jit(solution)/shard_map/ppermute | solution.py:356
  34.3 7.9 %collective-permute-start.12 = (bf16[24,4224]{1,0:T(8,128)(2,1)S(1)}, bf16[24,4224]{1,0:T(8,128)(2,1)S(1)}, u32[]{:S(2)}, u32[]{:S(2)}) collective-permute-start(bf16[24,4224]{1,0:T(8,128)(2,1)S(1)} %get-tuple-element.41), channel_id=1, source_target_pairs={{0,4},{1,5},{2,6},{3,7},{4,0},{5,1},{6,2},{7,3},{8,12},{9,13},{10,... | collective-permute-start | bytes 608264 | tf_op jit(solution)/shard_map/ppermute | solution.py:356
  36.1 6.3 %collective-permute-start.11 = (bf16[24,4224]{1,0:T(8,128)(2,1)S(1)}, bf16[24,4224]{1,0:T(8,128)(2,1)S(1)}, u32[]{:S(2)}, u32[]{:S(2)}) collective-permute-start(bf16[24,4224]{1,0:T(8,128)(2,1)S(1)} %get-tuple-element.41), channel_id=1, source_target_pairs={{0,2},{1,3},{2,0},{3,1},{4,6},{5,7},{6,4},{7,5},{8,10},{9,11},{10,... | collective-permute-start | bytes 608264 | tf_op jit(solution)/shard_map/ppermute | solution.py:356
  36.2 6.5 %collective-permute-start.14 = (bf16[56,4224]{1,0:T(8,128)(2,1)S(1)}, bf16[56,4224]{1,0:T(8,128)(2,1)S(1)}, u32[]{:S(2)}, u32[]{:S(2)}) collective-permute-start(bf16[56,4224]{1,0:T(8,128)(2,1)S(1)} %get-tuple-element.33), channel_id=1, source_target_pairs={{0,1},{1,0},{2,3},{3,2},{4,5},{5,4},{6,7},{7,6},{8,9},{9,8},{10,11... | collective-permute-start | bytes 1419272 | tf_op jit(solution)/shard_map/ppermute | solution.py:356
  51.4 4.9 %collective-permute-start.18 = (bf16[56,4096]{1,0:T(8,128)(2,1)S(1)}, bf16[56,4096]{1,0:T(8,128)(2,1)S(1)}, u32[]{:S(2)}, u32[]{:S(2)}) collective-permute-start(bf16[56,4096]{1,0:T(8,128)(2,1)S(1)} %slice.91), channel_id=1, source_target_pairs={{0,1},{1,0},{2,3},{3,2},{4,5},{5,4},{6,7},{7,6},{8,9},{9,8},{10,11... | collective-permute-start | bytes 1376264 | tf_op jit(solution)/shard_map/ppermute | solution.py:356
  52.8 12.3 %collective-permute-start.23 = (bf16[24,4096]{1,0:T(8,128)(2,1)S(1)}, bf16[24,4096]{1,0:T(8,128)(2,1)S(1)}, u32[]{:S(2)}, u32[]{:S(2)}) collective-permute-start(bf16[24,4096]{1,0:T(8,128)(2,1)S(1)} %get-tuple-element.17), channel_id=1, source_target_pairs={{0,2},{1,3},{2,0},{3,1},{4,6},{5,7},{6,4},{7,5},{8,10},{9,11},{10,... | collective-permute-start | bytes 589832 | tf_op jit(solution)/shard_map/ppermute | solution.py:356
  53.6 12.4 %collective-permute-start.27 = (bf16[24,4096]{1,0:T(8,128)(2,1)S(1)}, bf16[24,4096]{1,0:T(8,128)(2,1)S(1)}, u32[]{:S(2)}, u32[]{:S(2)}) collective-permute-start(bf16[24,4096]{1,0:T(8,128)(2,1)S(1)} %get-tuple-element.18), channel_id=1, source_target_pairs={{0,6},{1,7},{2,4},{3,5},{4,2},{5,3},{6,0},{7,1},{8,14},{9,15},{10,... | collective-permute-start | bytes 589832 | tf_op jit(solution)/shard_map/ppermute | solution.py:356
  55.5 10.5 %collective-permute-start.25 = (bf16[24,4096]{1,0:T(8,128)(2,1)S(1)}, bf16[24,4096]{1,0:T(8,128)(2,1)S(1)}, u32[]{:S(2)}, u32[]{:S(2)}) collective-permute-start(bf16[24,4096]{1,0:T(8,128)(2,1)S(1)} %get-tuple-element.19), channel_id=1, source_target_pairs={{0,4},{1,5},{2,6},{3,7},{4,0},{5,1},{6,2},{7,3},{8,12},{9,13},{10,... | collective-permute-start | bytes 589832 | tf_op jit(solution)/shard_map/ppermute | solution.py:356
  56.5 13.3 %collective-permute-start.19 = (bf16[8,4096]{1,0:T(8,128)(2,1)S(1)}, bf16[8,4096]{1,0:T(8,128)(2,1)S(1)}, u32[]{:S(2)}, u32[]{:S(2)}) collective-permute-start(bf16[8,4096]{1,0:T(8,128)(2,1)S(1)} %get-tuple-element.23), channel_id=1, source_target_pairs={{0,2},{1,3},{2,0},{3,1},{4,6},{5,7},{6,4},{7,5},{8,10},{9,11},{10,... | collective-permute-start | bytes 196616 | tf_op jit(solution)/shard_map/ppermute | solution.py:356
  57.3 13.0 %collective-permute-start.21 = (bf16[8,4096]{1,0:T(8,128)(2,1)S(1)}, bf16[8,4096]{1,0:T(8,128)(2,1)S(1)}, u32[]{:S(2)}, u32[]{:S(2)}) collective-permute-start(bf16[8,4096]{1,0:T(8,128)(2,1)S(1)} %get-tuple-element.24), channel_id=1, source_target_pairs={{0,6},{1,7},{2,4},{3,5},{4,2},{5,3},{6,0},{7,1},{8,14},{9,15},{10,... | collective-permute-start | bytes 196616 | tf_op jit(solution)/shard_map/ppermute | solution.py:356
  65.0 5.2 %collective-permute-start.20 = (bf16[8,4096]{1,0:T(8,128)(2,1)S(1)}, bf16[8,4096]{1,0:T(8,128)(2,1)S(1)}, u32[]{:S(2)}, u32[]{:S(2)}) collective-permute-start(bf16[8,4096]{1,0:T(8,128)(2,1)S(1)} %get-tuple-element.25), channel_id=1, source_target_pairs={{0,4},{1,5},{2,6},{3,7},{4,0},{5,1},{6,2},{7,3},{8,12},{9,13},{10,... | collective-permute-start | bytes 196616 | tf_op jit(solution)/shard_map/ppermute | solution.py:356
  66.1 4.9 %collective-permute-start.28 = (bf16[8,4096]{1,0:T(8,128)(2,1)S(1)}, bf16[8,4096]{1,0:T(8,128)(2,1)S(1)}, u32[]{:S(2)}, u32[]{:S(2)}) collective-permute-start(bf16[8,4096]{1,0:T(8,128)(2,1)S(1)} %get-tuple-element.30), channel_id=1, source_target_pairs={{0,8},{1,9},{2,10},{3,11},{4,12},{5,13},{6,14},{7,15},{8,0},{9,1},... | collective-permute-start | bytes 196616 | tf_op jit(solution)/shard_map/ppermute | solution.py:356
  66.5 7.0 %collective-permute-start.30 = (bf16[8,4096]{1,0:T(8,128)(2,1)S(1)}, bf16[8,4096]{1,0:T(8,128)(2,1)S(1)}, u32[]{:S(2)}, u32[]{:S(2)}) collective-permute-start(bf16[8,4096]{1,0:T(8,128)(2,1)S(1)} %get-tuple-element.31), channel_id=1, source_target_pairs={{0,24},{1,25},{2,26},{3,27},{4,28},{5,29},{6,30},{7,31},{8,16},{9,... | collective-permute-start | bytes 196616 | tf_op jit(solution)/shard_map/ppermute | solution.py:356
  69.8 5.9 %collective-permute-start.29 = (bf16[8,4096]{1,0:T(8,128)(2,1)S(1)}, bf16[8,4096]{1,0:T(8,128)(2,1)S(1)}, u32[]{:S(2)}, u32[]{:S(2)}) collective-permute-start(bf16[8,4096]{1,0:T(8,128)(2,1)S(1)} %get-tuple-element.32), channel_id=1, source_target_pairs={{0,16},{1,17},{2,18},{3,19},{4,20},{5,21},{6,22},{7,23},{8,24},{9,... | collective-permute-start | bytes 196616 | tf_op jit(solution)/shard_map/ppermute | solution.py:356
  (11 other events, 96.9 us)

commit v8 on v7

--- a/solution.py
+++ b/solution.py
@@ -36,86 +36,80 @@
     return pltpu.with_memory_space_constraint(value, pltpu.HBM)
 
 
-def attention_kernel(
-    len_hbm,
-    q_hbm,
-    nk_hbm,
-    nv_hbm,
-    k_hbm,
-    v_hbm,
-    qg_hbm,
-    kg_hbm,
-    ids_hbm,
-    gates_hbm,
-    w_hbm,
-    out_ref,
-    table_ref,
-    w_ref,
-    lengths,
-    q_ref,
-    nk_ref,
-    nv_ref,
-    k_ref,
-    v_ref,
-    qg_ref,
-    kg_ref,
-    ids_ref,
-    gates_ref,
-    nk_scr,
-    nv_scr,
-    num,
-    tops,
-    totals,
-    score,
-    weight,
-    sem,
-):
-    sources = (len_hbm, nk_hbm, nv_hbm, qg_hbm, kg_hbm, ids_hbm, gates_hbm, q_hbm, k_hbm, v_hbm)
-    targets = (lengths, nk_ref, nv_ref, qg_ref, kg_ref, ids_ref, gates_ref, q_ref, k_ref, v_ref)
-    copies = [
-        pltpu.make_async_copy(a, b, sem.at[i]) for i, (a, b) in enumerate(zip(sources, targets))
+def attention_kernel(flip, *refs):
+    sources, refs = refs[:8], refs[8:]
+    if flip == 0:
+        ids_hbm, gates_hbm, w_hbm, _, out_ref, table_ref, w_ref = refs[:7]
+        refs = refs[7:]
+    else:
+        out_ref, refs = refs[0], refs[1:]
+    len_hbm, q_hbm, nk_hbm, nv_hbm, k_hbm, v_hbm, qg_hbm, kg_hbm = sources
+    lengths, q_ref, nk_ref, nv_ref, k_ref, v_ref, qg_ref, kg_ref = refs[:8]
+    nk_scr, nv_scr, num, tops, totals, score, weight, sem = refs[8:16]
+    tensor_pos = lax.axis_index("tensor")
+    rows, group, hd = q_ref.shape
+    kvh, cache = k_hbm.shape[1], k_ref.shape[1]
+    heads_own = q_hbm.shape[1] // lax.axis_size("tensor")
+    parts = group // heads_own
+    which = (tensor_pos // parts) ^ flip
+    heads = pl.ds(pl.multiple_of(which * group, group), group)
+    pairs = [
+        (len_hbm, lengths),
+        (nk_hbm, nk_ref),
+        (nv_hbm, nv_ref),
+        (qg_hbm, qg_ref),
+        (kg_hbm, kg_ref),
+        (q_hbm.at[:, heads], q_ref),
+        (k_hbm.at[:, which], k_ref),
+        (v_hbm.at[:, which], v_ref),
     ]
-    ahead = pltpu.make_async_copy(w_hbm, w_ref, sem.at[10])
-    for c in copies + [ahead]:
+    if flip == 0:
+        ids_ref, gates_ref = refs[16:]
+        pairs = [(ids_hbm, ids_ref), (gates_hbm, gates_ref)] + pairs + [(w_hbm, w_ref)]
+    copies = [pltpu.make_async_copy(src, dst, sem.at[i]) for i, (src, dst) in enumerate(pairs)]
+    for c in copies:
         c.start()
-    tensor_pos = lax.axis_index("tensor")
-    rows, heads, hd = q_ref.shape
-    kvh, cache = k_ref.shape[1], k_ref.shape[2]
-    group = heads // kvh
-    parts = out_ref.shape[0]
-    heads_own = heads // parts
-    step = 4
+    if flip == 0:
+        for c in copies[:2]:
+            c.wait()
+        ahead = copies[-1]
+        copies = copies[2:-1]
+        gates = gates_ref[...]
+        route = (gates / jnp.sum(gates, axis=1, keepdims=True)).astype(BF).astype(F32)
+        expert = iota(table_ref.shape, 1)
+        table = jnp.zeros(table_ref.shape, F32)
+        for k in range(gates.shape[1]):
+            table = jnp.where(expert == ids_ref[:, k : k + 1], route[:, k : k + 1], table)
+        table_ref[...] = table.astype(BF)
+
+    step = 8
     blocks = rows // step
-    many, cols, fresh = step * heads, step * kvh * cache, step * kvh
+    many, cols = step * group, step * cache
     scaling = hd ** (-0.5)
-
-    row_group = iota((many, cols), 0) // group
-    same = row_group == iota((many, cols), 1) // cache
-    col_row = iota((1, cols), 1) // (kvh * cache)
+    same = iota((many, cols), 0) // group == iota((many, cols), 1) // cache
+    col_row = iota((1, cols), 1) // cache
     col_pos = iota((1, cols), 1) % cache + tensor_pos * cache
-    new_col = iota((many, 2 * fresh), 1)
-    new_here = (new_col == iota((many, 2 * fresh), 0) // group) & (tensor_pos == 0)
-
-    for c in copies[:7]:
+    new_here = iota((many, 2 * step), 1) == iota((many, 2 * step), 0) // group
+    new_here = new_here & (tensor_pos == 0)
+
+    for c in copies[:5]:
         c.wait()
-    gates = gates_ref[...]
-    route = (gates / jnp.sum(gates, axis=1, keepdims=True)).astype(BF).astype(F32)
-    expert = iota(table_ref.shape, 1)
-    table = jnp.zeros(table_ref.shape, F32)
-    for k in range(gates.shape[1]):
-        table = jnp.where(expert == ids_ref[:, k : k + 1], route[:, k : k + 1], table)
-    table_ref[...] = table.astype(BF)
     for r in range(rows):
         nk_scr[r * kvh : (r + 1) * kvh, :] = nk_ref[r].astype(F32)
         nv_scr[r * kvh : (r + 1) * kvh, :] = nv_ref[r].astype(F32)
     query_gain = qg_ref[...]
-    key_norm = rms_scale(nk_scr[...], kg_ref[...])
-    empty = jnp.zeros((fresh, hd), F32)
-    for c in copies[7:]:
+    new_rows = pl.ds(which, rows, stride=kvh)
+    key_norm = rms_scale(nk_scr[new_rows, :], kg_ref[...])
+    new_value = nv_scr[new_rows, :]
+    empty = jnp.zeros((step, hd), F32)
+    for c in copies[5:]:
         c.wait()
 
     def rows_of(ref, b, size):
         return ref[b * step : (b + 1) * step].reshape(size, hd)
+
+    def with_empty(value, b):
+        return jnp.concatenate([value[b * step : (b + 1) * step], empty]).astype(BF)
 
     queries = []
     for b in range(blocks):
@@ -128,8 +122,7 @@
         included = same & (col_pos < limit)
         scores = matmul_t(queries[b], rows_of(k_ref, b, cols)) * scaling
         score[b, :, :cols] = jnp.where(included, scores, -1e30)
-        new_keys = jnp.concatenate([key_norm[b * fresh : (b + 1) * fresh], empty]).astype(BF)
-        scores = matmul_t(queries[b], new_keys) * scaling
+        scores = matmul_t(queries[b], with_empty(key_norm, b)) * scaling
         score[b, :, cols:] = jnp.where(new_here, scores, -1e30)
     for b in range(blocks):
         top = jnp.maximum(jnp.max(score[b], axis=1, keepdims=True), -1e29).astype(BF).astype(F32)
@@ -141,81 +134,75 @@
         total = jnp.sum(weights.astype(F32), axis=1, keepdims=True)
         totals[b * many : (b + 1) * many, :] = jnp.broadcast_to(total, (many, LANES))
     for b in range(blocks):
-        values = nv_scr[b * fresh : (b + 1) * fresh, :]
-        new_values = jnp.concatenate([values, empty]).astype(BF)
         num[b * many : (b + 1) * many, :] = matmul(
             weight[b, :, :cols], rows_of(v_ref, b, cols)
-        ) + matmul(weight[b, :, cols:], new_values)
+        ) + matmul(weight[b, :, cols:], with_empty(new_value, b))
 
     lane = iota((rows, LANES), 1)
     for t in range(parts):
-        slot = tensor_pos ^ t
+        slot = (tensor_pos % parts) ^ t
         side = jnp.zeros((rows, LANES), F32)
         for h in range(heads_own):
-            which = pl.ds(t * heads_own + h, rows, stride=heads)
-            out_ref[slot, :, h * hd : (h + 1) * hd] = num[which, :].astype(BF)
-            total = totals[which, :]
+            own = pl.ds(t * heads_own + h, rows, stride=group)
+            out_ref[slot, :, h * hd : (h + 1) * hd] = num[own, :].astype(BF)
+            total = totals[own, :]
             high = total.astype(BF).astype(F32)
-            side = jnp.where(lane == h, tops[which, :], side)
+            side = jnp.where(lane == h, tops[own, :], side)
             side = jnp.where(lane == heads_own + h, high, side)
             side = jnp.where(lane == 2 * heads_own + h, total - high, side)
         out_ref[slot, :, heads_own * hd :] = side.astype(BF)
-    ahead.wait()
+    if flip == 0:
+        ahead.wait()
 
 
 def attention(
-    lengths,
-    queries,
-    new_keys,
-    new_values,
-    key_cache,
-    value_cache,
-    qg,
-    kg,
-    expert_ids,
-    gate_weights,
-    parts,
-    lanes,
-    later,
+    flip, lengths, queries, new_keys, new_values, key_cache, value_cache, qg, kg, parts, more
 ):
     rows, heads, hd = queries.shape
     kvh, cache = key_cache.shape[1:3]
-    args = (
-        lengths,
-        queries,
-        new_keys,
-        new_values,
-        key_cache,
-        value_cache,
-        qg.reshape(1, -1),
-        kg.reshape(1, -1),
-        expert_ids,
-        gate_weights,
-    )
+    group = heads // kvh
+    blocks = rows // 8
+    args = [lengths, queries, new_keys, new_values, key_cache, value_cache]
+    args = [in_hbm(a) for a in (*args, qg.reshape(1, -1), kg.reshape(1, -1))]
+    outs = [jax.ShapeDtypeStruct((parts // kvh, rows, heads // parts * hd + LANES), BF)]
+    scratch = [
+        pltpu.SMEM((rows,), I32),
+        pltpu.VMEM((rows, group, hd), BF),
+        pltpu.VMEM(new_keys.shape, BF),
+        pltpu.VMEM(new_values.shape, BF),
+        pltpu.VMEM((rows, cache, hd), BF),
+        pltpu.VMEM((rows, cache, hd), BF),
+        pltpu.VMEM((1, hd), F32),
+        pltpu.VMEM((1, hd), F32),
+        pltpu.VMEM((rows * kvh, hd), F32),
+        pltpu.VMEM((rows * kvh, hd), F32),
+        pltpu.VMEM((rows * group, hd), F32),
+        pltpu.VMEM((rows * group, LANES), F32),
+        pltpu.VMEM((rows * group, LANES), F32),
+        pltpu.VMEM((blocks, 8 * group, 8 * (cache + 2)), F32),
+        pltpu.VMEM((blocks, 8 * group, 8 * (cache + 2)), BF),
+        pltpu.SemaphoreType.DMA((11,)),
+    ]
+    specs = [pl.BlockSpec(memory_space=pltpu.HBM)] * len(args)
+    size = 2 * rows * group * hd * 8
+    if flip == 0:
+        expert_ids, gate_weights, lanes, later, earlier = more
+        args += [in_hbm(a) for a in (expert_ids, gate_weights, later)] + [earlier]
+        specs += [pl.BlockSpec(memory_space=pltpu.HBM)] * 3 + [pl.BlockSpec(memory_space=pl.ANY)]
+        outs.append(jax.ShapeDtypeStruct((expert_ids.shape[0], lanes), BF))
+        outs.append(pltpu.VMEM(later.shape, later.dtype))
+        scratch += [pltpu.VMEM(expert_ids.shape, I32), pltpu.VMEM(gate_weights.shape, F32)]
+        size = size + 2 * later.size
     return pl.pallas_call(
-        attention_kernel,
-        out_shape=(
-            jax.ShapeDtypeStruct((parts, rows, heads // parts * hd + LANES), BF),
-            jax.ShapeDtypeStruct((expert_ids.shape[0], lanes), BF),
-            pltpu.VMEM(later.shape, later.dtype),
-        ),
-        in_specs=[pl.BlockSpec(memory_space=pltpu.HBM)] * 11,
-        out_specs=(pl.BlockSpec(memory_space=pltpu.VMEM),) * 3,
-        scratch_shapes=[pltpu.SMEM(args[0].shape, I32)]
-        + [pltpu.VMEM(a.shape, a.dtype) for a in args[1:]]
-        + [
-            pltpu.VMEM((rows * kvh, hd), F32),
-            pltpu.VMEM((rows * kvh, hd), F32),
-            pltpu.VMEM((rows * heads, hd), F32),
-            pltpu.VMEM((rows * heads, LANES), F32),
-            pltpu.VMEM((rows * heads, LANES), F32),
-            pltpu.VMEM((rows // 4, 4 * heads, 4 * kvh * (cache + 2)), F32),
-            pltpu.VMEM((rows // 4, 4 * heads, 4 * kvh * (cache + 2)), BF),
-            pltpu.SemaphoreType.DMA((11,)),
-        ],
+        functools.partial(attention_kernel, flip),
+        out_shape=tuple(outs),
+        in_specs=specs,
+        out_specs=(pl.BlockSpec(memory_space=pltpu.VMEM),) * len(outs),
+        scratch_shapes=scratch,
         compiler_params=pltpu.CompilerParams(vmem_limit_bytes=16 * MIB),
+        cost_estimate=pl.CostEstimate(flops=size, bytes_accessed=size, transcendentals=0),
         name="attention",
-    )(*[in_hbm(a) for a in (*args, later)])
+    )(*args)
 
 
 def projection_kernel(parts, *refs):
@@ -271,7 +258,10 @@
     )(*got, out_proj, in_hbm(later))
 
 
-def expert_kernel(slots, x_ref, gate, up, down_hbm, out_ref, down, xc, act, res, sem):
+def expert_kernel(slots, sizes, *refs):
+    x_ref, gate, up, down_hbm = refs[:4]
+    outs = refs[4 : 4 + len(sizes)]
+    down, xc, act, res, sem = refs[4 + len(sizes) :]
     own = lax.axis_index("dp") * lax.axis_size("tensor") + lax.axis_index("tensor")
     rows = x_ref.shape[0]
     _, width, hidden = gate.shape
@@ -315,19 +305,22 @@
         down_copy(i).wait()
         cols = slice(i * dsize, (i + 1) * dsize)
         res[:slots, :] = matmul(act[...], down[:, cols]).astype(BF)
-        out_ref[:, cols] = matmul(spread, res[...]).astype(BF)
-
-
-def experts(x, expert_gate, expert_up, expert_down, share):
+        result, start = matmul(spread, res[...]), 0
+        for size, out in zip(sizes, outs):
+            out[:, cols] = result[start : start + size].astype(BF)
+            start += size
+
+
+def experts(x, expert_gate, expert_up, expert_down, share, sizes):
     rows = x.shape[0]
     _, width, hidden = expert_gate.shape
     slots = rows // share * CAP
     vmem = pl.BlockSpec(memory_space=pltpu.VMEM)
     return pl.pallas_call(
-        functools.partial(expert_kernel, slots),
-        out_shape=jax.ShapeDtypeStruct((rows, width), BF),
+        functools.partial(expert_kernel, slots, sizes),
+        out_shape=tuple(jax.ShapeDtypeStruct((size, width), BF) for size in sizes),
         in_specs=[vmem] * 3 + [pl.BlockSpec(memory_space=pltpu.HBM)],
-        out_specs=vmem,
+        out_specs=(vmem,) * len(sizes),
         scratch_shapes=[
             pltpu.VMEM((hidden, width), BF),
             pltpu.VMEM((slots, width), BF),
@@ -391,22 +384,20 @@
     share, width = residual_in.shape
     lanes = -(-dp * tensor // LANES) * LANES
 
-    local, table, out_proj = attention(
-        lengths,
-        queries,
-        new_keys,
-        new_values,
-        key_cache,
-        value_cache,
-        query_gain,
-        key_gain,
-        expert_ids,
-        gate_weights,
-        tensor,
-        lanes,
-        out_proj,
-    )
-    got = [local[0]] + plan.swaps(list(local[1:]), list(range(1, tensor)))
+    inputs = (lengths, queries, new_keys, new_values, key_cache, value_cache, query_gain, key_gain)
+    groups = key_cache.shape[1]
+    got, local = [], None
+    for flip in reversed(range(groups)):
+        more = (expert_ids, gate_weights, lanes, out_proj, local)
+        results = attention(flip, *inputs, tensor, more)
+        local = results[0]
+        for j in range(0, tensor // groups, 2):
+            far = flip * (tensor // groups) + j
+            pair = local[j : j + 2]
+            if far:
+                pair = plan.swap(pair, far)
+            got += [pair[0], plan.swap(pair[1], plan.core)]
+    _, table, out_proj = results
     partial, expert_gate = projection(got, out_proj, share, expert_gate)
     pair = total_of([partial[0], plan.swap(partial[1], plan.core)])
     projected = total_of([pair[0]] + plan.swaps(list(pair[1:]), plan.y))
@@ -420,19 +411,13 @@
     pieces = [jnp.concatenate([mine] + others + near)] + far
     x = jnp.concatenate(pieces + [plan.swap(piece, plan.core) for piece in pieces])
 
-    result = experts(x, expert_gate, expert_up, expert_down, share)
-
-    sizes = [piece.shape[0] for piece in pieces]
-    starts = [sum(sizes[:i]) for i in range(len(sizes) + 1)]
-    every = starts[-1]
+    sizes = [piece.shape[0] for piece in pieces] * 2
+    results = experts(x, expert_gate, expert_up, expert_down, share, sizes)
+
+    half = len(pieces)
     sums = [
-        total_of(
-            [
-                result[starts[i] : starts[i + 1]],
-                plan.swap(result[every + starts[i] : every + starts[i + 1]], plan.core),
-            ]
-        )
-        for i in reversed(range(len(sizes)))
+        total_of([results[i], plan.swap(results[half + i], plan.core)])
+        for i in reversed(range(half))
     ][::-1]
     blocks = sums[0].reshape(-1, share, width)
     far = plan.swaps(sums[1:], plan.plane)

time: 76.5 us -> 76 us (level)
  waiting for transfers between devices: 30.8 us -> 28.4 us
  Pallas kernels: 14.1 us -> 16.2 us
    ppermute x31, waiting for transfers between devices: 30.8 us -> 28.4 us  [swap(): lax.ppermute(value, ('dp', 'tensor'), [(i, i ^ flip) for i in range(self....]
    pallas_call x2 -> x3, Pallas kernels: 10.6 us -> 12.7 us  [the longest x1 6.49 us: experts(): pl.pallas_call(functools.partial(expert_kernel, slots, sizes), out_shape=...]
  transfers between devices with their start and end apart: 31 -> 31, of which waited for: 18 -> 18; matrix products, arithmetic and copies ran while one was open for 1% -> 1% of each run, Pallas kernels for 0% -> 5%
where the time goes in v8:
time: 76 us; the launch traced here: 75.9 us
  starting transfers between devices  29.1 us (38%)
  waiting for transfers between devices  28.4 us (37%)
  Pallas kernels  16.2 us (21%)
  other arithmetic  1.55 us (2%)
    ppermute x31, starting transfers between devices, swap(): lax.ppermute(value, ('dp', 'tensor'), [(i, i ^ flip) for i in range(self....  29.1 us
    ppermute x31, waiting for transfers between devices, swap(): lax.ppermute(value, ('dp', 'tensor'), [(i, i ^ flip) for i in range(self....  28.4 us
    pallas_call x1, Pallas kernels, experts(): pl.pallas_call(functools.partial(expert_kernel, slots, sizes), out_shape=...  6.49 us
    pallas_call x2, Pallas kernels, attention(): pl.pallas_call(functools.partial(attention_kernel, flip), out_shape=tuple...  6.23 us
    pallas_call x1, Pallas kernels, projection(): pl.pallas_call(functools.partial(projection_kernel, parts), out_shape=(ja...  3.45 us
  transfers between devices with their start and end apart: 31, of which 18 were waited for; matrix products, arithmetic and copies ran while one was open for 1% of the time, Pallas kernels for 5%

profile of v8, /device:TPU:0, one launch (start us, length us, event | category | flops | bytes accessed | tf_op | source)
XLA Modules:
  0.0 75.9 jit_solution(273661325370427045)
XLA Ops:
  0.0 2.4 %attention.2.refs_11_ = bf16[2,32,1152]{2,1,0:T(8,128)(2,1)S(1)} custom-call(s32[32]{0:T(128)} %refs_0_.3, bf16[32,32,128]{2,1,0:T(8,128)(2,1)} %refs_1_.3, bf16[32,2,128]{2,1,0:T(2,128)(2,1)} %refs_2_.4, bf16[32,2,128]{2,1,0:T(2,128)(2,1)} %refs_3_.4, bf16[32,2,32,128]{3,2,1,0:T(8,128)(2,1)} %refs_4_.3, bf16[32,2,32,128]{3,2,1,0:T(8,128)(2,1)} %refs_5_.4, ...), custom_call_target="tpu_custom_call" | custom-call | flops 1048576 | bytes 1048576 | tf_op jit(solution)/shard_map/attention/pallas_call | solution.py:196
  2.4 3.0 %collective-permute-start = (bf16[2,32,1152]{2,1,0:T(8,128)(2,1)S(1)}, bf16[2,32,1152]{2,1,0:T(8,128)(2,1)S(1)}, u32[]{:S(2)}, u32[]{:S(2)}) collective-permute-start(bf16[2,32,1152]{2,1,0:T(8,128)(2,1)S(1)} %attention.2.refs_11_), channel_id=1, source_target_pairs={{0,2},{1,3},{2,0},{3,1},{4,6},{5,7},{6,4},{7,5},{8,10},{9,11},{10,... | collective-permute-start | bytes 442376 | tf_op jit(solution)/shard_map/ppermute | solution.py:349
  5.5 3.8 %attention.3 = (bf16[2,32,1152]{2,1,0:T(8,128)(2,1)S(1)}, bf16[8,128]{1,0:T(8,128)(2,1)S(1)}, bf16[1024,4096]{1,0:T(8,128)(2,1)S(1)}) custom-call(s32[32]{0:T(128)} %refs_0_.3, bf16[32,32,128]{2,1,0:T(8,128)(2,1)} %refs_1_.3, bf16[32,2,128]{2,1,0:T(2,128)(2,1)} %refs_2_.4, bf16[32,2,128]{2,1,0:T(2,128)(2,1)} %refs_3_.4, bf16[32,2,32,128]{3,2,1,0:T(8,128)(2,1)} %refs_4_.3, ...), custom_call_target="tpu_custom_call" | custom-call | flops 9437184 | bytes 9437184 | tf_op jit(solution)/shard_map/attention/pallas_call | solution.py:196
  10.9 3.5 %projection.1 = (bf16[2,2,8,4096]{3,2,1,0:T(8,128)(2,1)S(1)}, bf16[1,4096,768]{2,1,0:T(8,128)(2,1)S(1)}) custom-call(bf16[32,1152]{1,0:T(8,128)(2,1)S(1)} %get-tuple-element.42.refs_0_, bf16[32,1152]{1,0:T(8,128)(2,1)S(1)} %collective-permute-done.1.refs_1_, bf16[32,1152]{1,0:T(8,128)(2,1)S(1)} %get-tuple-element.40.refs_2_, ...), custom_call_target="tpu_custom_call" | custom-call | tf_op jit(solution)/shard_map/projection/pallas_call | solution.py:247
  15.8 1.6 %collective-permute-start.4 = (bf16[8,4096]{1,0:T(8,128)(2,1)S(1)}, bf16[8,4096]{1,0:T(8,128)(2,1)S(1)}, u32[]{:S(2)}, u32[]{:S(2)}) collective-permute-start(bf16[8,4096]{1,0:T(8,128)(2,1)S(1)} %fusion.12), channel_id=1, source_target_pairs={{0,2},{1,3},{2,0},{3,1},{4,6},{5,7},{6,4},{7,5},{8,10},{9,11},{10,... | collective-permute-start | bytes 196616 | tf_op jit(solution)/shard_map/ppermute | solution.py:349
  17.4 2.8 %collective-permute-done.4 = bf16[8,4096]{1,0:T(8,128)(2,1)S(1)} collective-permute-done((bf16[8,4096]{1,0:T(8,128)(2,1)S(1)}, bf16[8,4096]{1,0:T(8,128)(2,1)S(1)}, u32[]{:S(2)}, u32[]{:S(2)}) %collective-permute-start.4) | collective-permute-done | bytes 65568 | tf_op jit(solution)/shard_map/ppermute | solution.py:349
  20.5 1.6 %collective-permute-start.5 = (bf16[8,4224]{1,0:T(8,128)(2,1)S(1)}, bf16[8,4224]{1,0:T(8,128)(2,1)S(1)}, u32[]{:S(2)}, u32[]{:S(2)}) collective-permute-start(bf16[8,4224]{1,0:T(8,128)(2,1)S(1)} %pad_maximum_fusion), channel_id=1, source_target_pairs={{0,8},{1,9},{2,10},{3,11},{4,12},{5,13},{6,14},{7,15},{8,0},{9,1},... | collective-permute-start | bytes 202760 | tf_op jit(solution)/shard_map/ppermute | solution.py:349
  22.2 2.6 %collective-permute-start.6 = (bf16[8,4224]{1,0:T(8,128)(2,1)S(1)}, bf16[8,4224]{1,0:T(8,128)(2,1)S(1)}, u32[]{:S(2)}, u32[]{:S(2)}) collective-permute-start(bf16[8,4224]{1,0:T(8,128)(2,1)S(1)} %pad_maximum_fusion), channel_id=1, source_target_pairs={{0,16},{1,17},{2,18},{3,19},{4,20},{5,21},{6,22},{7,23},{8,24},{9,... | collective-permute-start | bytes 202760 | tf_op jit(solution)/shard_map/ppermute | solution.py:349
  25.2 3.0 %collective-permute-start.10 = (bf16[8,4224]{1,0:T(8,128)(2,1)S(1)}, bf16[8,4224]{1,0:T(8,128)(2,1)S(1)}, u32[]{:S(2)}, u32[]{:S(2)}) collective-permute-start(bf16[8,4224]{1,0:T(8,128)(2,1)S(1)} %get-tuple-element.60), channel_id=1, source_target_pairs={{0,6},{1,7},{2,4},{3,5},{4,2},{5,3},{6,0},{7,1},{8,14},{9,15},{10,... | collective-permute-start | bytes 202760 | tf_op jit(solution)/shard_map/ppermute | solution.py:349
  29.3 1.6 %collective-permute-done.7 = bf16[8,4224]{1,0:T(8,128)(2,1)S(1)} collective-permute-done((bf16[8,4224]{1,0:T(8,128)(2,1)S(1)}, bf16[8,4224]{1,0:T(8,128)(2,1)S(1)}, u32[]{:S(2)}, u32[]{:S(2)}) %collective-permute-start.7) | collective-permute-done | bytes 67616 | tf_op jit(solution)/shard_map/ppermute | solution.py:349
  30.9 2.4 %collective-permute-start.13 = (bf16[24,4224]{1,0:T(8,128)(2,1)S(1)}, bf16[24,4224]{1,0:T(8,128)(2,1)S(1)}, u32[]{:S(2)}, u32[]{:S(2)}) collective-permute-start(bf16[24,4224]{1,0:T(8,128)(2,1)S(1)} %get-tuple-element.51), channel_id=1, source_target_pairs={{0,6},{1,7},{2,4},{3,5},{4,2},{5,3},{6,0},{7,1},{8,14},{9,15},{10,... | collective-permute-start | bytes 608264 | tf_op jit(solution)/shard_map/ppermute | solution.py:349
  33.8 2.3 %collective-permute-done.8 = bf16[8,4224]{1,0:T(8,128)(2,1)S(1)} collective-permute-done((bf16[8,4224]{1,0:T(8,128)(2,1)S(1)}, bf16[8,4224]{1,0:T(8,128)(2,1)S(1)}, u32[]{:S(2)}, u32[]{:S(2)}) %collective-permute-start.8) | collective-permute-done | bytes 67616 | tf_op jit(solution)/shard_map/ppermute | solution.py:349
  36.3 2.7 %collective-permute-done.13 = bf16[24,4224]{1,0:T(8,128)(2,1)S(1)} collective-permute-done((bf16[24,4224]{1,0:T(8,128)(2,1)S(1)}, bf16[24,4224]{1,0:T(8,128)(2,1)S(1)}, u32[]{:S(2)}, u32[]{:S(2)}) %collective-permute-start.13) | collective-permute-done | bytes 202784 | tf_op jit(solution)/shard_map/ppermute | solution.py:349
  38.9 2.3 %collective-permute-done.12 = bf16[24,4224]{1,0:T(8,128)(2,1)S(1)} collective-permute-done((bf16[24,4224]{1,0:T(8,128)(2,1)S(1)}, bf16[24,4224]{1,0:T(8,128)(2,1)S(1)}, u32[]{:S(2)}, u32[]{:S(2)}) %collective-permute-start.12) | collective-permute-done | bytes 202784 | tf_op jit(solution)/shard_map/ppermute | solution.py:349
  42.0 1.3 %collective-permute-done.15 = bf16[24,4224]{1,0:T(8,128)(2,1)S(1)} collective-permute-done((bf16[24,4224]{1,0:T(8,128)(2,1)S(1)}, bf16[24,4224]{1,0:T(8,128)(2,1)S(1)}, u32[]{:S(2)}, u32[]{:S(2)}) %collective-permute-start.15) | collective-permute-done | bytes 202784 | tf_op jit(solution)/shard_map/ppermute | solution.py:349
  43.4 6.5 %experts.1 = (bf16[56,4096]{1,0:T(8,128)(2,1)S(1)}, bf16[24,4096]{1,0:T(8,128)(2,1)S(1)}, bf16[24,4096]{1,0:T(8,128)(2,1)S(1)}, bf16[24,4096]{1,0:T(8,128)(2,1)S...) custom-call(bf16[256,4224]{1,0:T(8,128)(2,1)S(1)} %constant_dynamic-, ...), custom_call_target="tpu_custom_call" | custom-call | tf_op jit(solution)/shard_map/experts/pallas_call | solution.py:319
  53.4 1.9 %collective-permute-start.27 = (bf16[24,4096]{1,0:T(8,128)(2,1)S(1)}, bf16[24,4096]{1,0:T(8,128)(2,1)S(1)}, u32[]{:S(2)}, u32[]{:S(2)}) collective-permute-start(bf16[24,4096]{1,0:T(8,128)(2,1)S(1)} %add_convert_fusion), channel_id=1, source_target_pairs={{0,6},{1,7},{2,4},{3,5},{4,2},{5,3},{6,0},{7,1},{8,14},{9,15},{10,... | collective-permute-start | bytes 589832 | tf_op jit(solution)/shard_map/ppermute | solution.py:349
  55.4 3.1 %collective-permute-done.23 = bf16[24,4096]{1,0:T(8,128)(2,1)S(1)} collective-permute-done((bf16[24,4096]{1,0:T(8,128)(2,1)S(1)}, bf16[24,4096]{1,0:T(8,128)(2,1)S(1)}, u32[]{:S(2)}, u32[]{:S(2)}) %collective-permute-start.23) | collective-permute-done | bytes 196640 | tf_op jit(solution)/shard_map/ppermute | solution.py:349
  58.5 1.7 %collective-permute-done.25 = bf16[24,4096]{1,0:T(8,128)(2,1)S(1)} collective-permute-done((bf16[24,4096]{1,0:T(8,128)(2,1)S(1)}, bf16[24,4096]{1,0:T(8,128)(2,1)S(1)}, u32[]{:S(2)}, u32[]{:S(2)}) %collective-permute-start.25) | collective-permute-done | bytes 196640 | tf_op jit(solution)/shard_map/ppermute | solution.py:349
  60.2 3.8 %collective-permute-done.27 = bf16[24,4096]{1,0:T(8,128)(2,1)S(1)} collective-permute-done((bf16[24,4096]{1,0:T(8,128)(2,1)S(1)}, bf16[24,4096]{1,0:T(8,128)(2,1)S(1)}, u32[]{:S(2)}, u32[]{:S(2)}) %collective-permute-start.27) | collective-permute-done | bytes 196640 | tf_op jit(solution)/shard_map/ppermute | solution.py:349
  64.1 2.5 %collective-permute-start.28 = (bf16[8,4096]{1,0:T(8,128)(2,1)S(1)}, bf16[8,4096]{1,0:T(8,128)(2,1)S(1)}, u32[]{:S(2)}, u32[]{:S(2)}) collective-permute-start(bf16[8,4096]{1,0:T(8,128)(2,1)S(1)} %get-tuple-element.36), channel_id=1, source_target_pairs={{0,8},{1,9},{2,10},{3,11},{4,12},{5,13},{6,14},{7,15},{8,0},{9,1},... | collective-permute-start | bytes 196616 | tf_op jit(solution)/shard_map/ppermute | solution.py:349
  68.7 2.2 %collective-permute-start.21 = (bf16[8,4096]{1,0:T(8,128)(2,1)S(1)}, bf16[8,4096]{1,0:T(8,128)(2,1)S(1)}, u32[]{:S(2)}, u32[]{:S(2)}) collective-permute-start(bf16[8,4096]{1,0:T(8,128)(2,1)S(1)} %get-tuple-element.34), channel_id=1, source_target_pairs={{0,6},{1,7},{2,4},{3,5},{4,2},{5,3},{6,0},{7,1},{8,14},{9,15},{10,... | collective-permute-start | bytes 196616 | tf_op jit(solution)/shard_map/ppermute | solution.py:349
  71.7 1.2 %collective-permute-done.30 = bf16[8,4096]{1,0:T(8,128)(2,1)S(1)} collective-permute-done((bf16[8,4096]{1,0:T(8,128)(2,1)S(1)}, bf16[8,4096]{1,0:T(8,128)(2,1)S(1)}, u32[]{:S(2)}, u32[]{:S(2)}) %collective-permute-start.30) | collective-permute-done | bytes 65568 | tf_op jit(solution)/shard_map/ppermute | solution.py:349
  72.8 1.6 %collective-permute-done.29 = bf16[8,4096]{1,0:T(8,128)(2,1)S(1)} collective-permute-done((bf16[8,4096]{1,0:T(8,128)(2,1)S(1)}, bf16[8,4096]{1,0:T(8,128)(2,1)S(1)}, u32[]{:S(2)}, u32[]{:S(2)}) %collective-permute-start.29) | collective-permute-done | bytes 65568 | tf_op jit(solution)/shard_map/ppermute | solution.py:349
  (83 shorter events, 14.3 us)
Async XLA Ops:
  2.4 7.0 %collective-permute-start = (bf16[2,32,1152]{2,1,0:T(8,128)(2,1)S(1)}, bf16[2,32,1152]{2,1,0:T(8,128)(2,1)S(1)}, u32[]{:S(2)}, u32[]{:S(2)}) collective-permute-start(bf16[2,32,1152]{2,1,0:T(8,128)(2,1)S(1)} %attention.2.refs_11_), channel_id=1, source_target_pairs={{0,2},{1,3},{2,0},{3,1},{4,6},{5,7},{6,4},{7,5},{8,10},{9,11},{10,... | collective-permute-start | bytes 442376 | tf_op jit(solution)/shard_map/ppermute | solution.py:349
  15.8 4.4 %collective-permute-start.4 = (bf16[8,4096]{1,0:T(8,128)(2,1)S(1)}, bf16[8,4096]{1,0:T(8,128)(2,1)S(1)}, u32[]{:S(2)}, u32[]{:S(2)}) collective-permute-start(bf16[8,4096]{1,0:T(8,128)(2,1)S(1)} %fusion.12), channel_id=1, source_target_pairs={{0,2},{1,3},{2,0},{3,1},{4,6},{5,7},{6,4},{7,5},{8,10},{9,11},{10,... | collective-permute-start | bytes 196616 | tf_op jit(solution)/shard_map/ppermute | solution.py:349
  20.5 4.5 %collective-permute-start.5 = (bf16[8,4224]{1,0:T(8,128)(2,1)S(1)}, bf16[8,4224]{1,0:T(8,128)(2,1)S(1)}, u32[]{:S(2)}, u32[]{:S(2)}) collective-permute-start(bf16[8,4224]{1,0:T(8,128)(2,1)S(1)} %pad_maximum_fusion), channel_id=1, source_target_pairs={{0,8},{1,9},{2,10},{3,11},{4,12},{5,13},{6,14},{7,15},{8,0},{9,1},... | collective-permute-start | bytes 202760 | tf_op jit(solution)/shard_map/ppermute | solution.py:349
  22.2 7.1 %collective-permute-start.6 = (bf16[8,4224]{1,0:T(8,128)(2,1)S(1)}, bf16[8,4224]{1,0:T(8,128)(2,1)S(1)}, u32[]{:S(2)}, u32[]{:S(2)}) collective-permute-start(bf16[8,4224]{1,0:T(8,128)(2,1)S(1)} %pad_maximum_fusion), channel_id=1, source_target_pairs={{0,16},{1,17},{2,18},{3,19},{4,20},{5,21},{6,22},{7,23},{8,24},{9,... | collective-permute-start | bytes 202760 | tf_op jit(solution)/shard_map/ppermute | solution.py:349
  24.8 6.1 %collective-permute-start.7 = (bf16[8,4224]{1,0:T(8,128)(2,1)S(1)}, bf16[8,4224]{1,0:T(8,128)(2,1)S(1)}, u32[]{:S(2)}, u32[]{:S(2)}) collective-permute-start(bf16[8,4224]{1,0:T(8,128)(2,1)S(1)} %pad_maximum_fusion), channel_id=1, source_target_pairs={{0,24},{1,25},{2,26},{3,27},{4,28},{5,29},{6,30},{7,31},{8,16},{9,... | collective-permute-start | bytes 202760 | tf_op jit(solution)/shard_map/ppermute | solution.py:349
  25.2 11.0 %collective-permute-start.10 = (bf16[8,4224]{1,0:T(8,128)(2,1)S(1)}, bf16[8,4224]{1,0:T(8,128)(2,1)S(1)}, u32[]{:S(2)}, u32[]{:S(2)}) collective-permute-start(bf16[8,4224]{1,0:T(8,128)(2,1)S(1)} %get-tuple-element.60), channel_id=1, source_target_pairs={{0,6},{1,7},{2,4},{3,5},{4,2},{5,3},{6,0},{7,1},{8,14},{9,15},{10,... | collective-permute-start | bytes 202760 | tf_op jit(solution)/shard_map/ppermute | solution.py:349
  28.2 8.0 %collective-permute-start.9 = (bf16[8,4224]{1,0:T(8,128)(2,1)S(1)}, bf16[8,4224]{1,0:T(8,128)(2,1)S(1)}, u32[]{:S(2)}, u32[]{:S(2)}) collective-permute-start(bf16[8,4224]{1,0:T(8,128)(2,1)S(1)} %get-tuple-element.60), channel_id=1, source_target_pairs={{0,4},{1,5},{2,6},{3,7},{4,0},{5,1},{6,2},{7,3},{8,12},{9,13},{10,... | collective-permute-start | bytes 202760 | tf_op jit(solution)/shard_map/ppermute | solution.py:349
  28.7 7.4 %collective-permute-start.8 = (bf16[8,4224]{1,0:T(8,128)(2,1)S(1)}, bf16[8,4224]{1,0:T(8,128)(2,1)S(1)}, u32[]{:S(2)}, u32[]{:S(2)}) collective-permute-start(bf16[8,4224]{1,0:T(8,128)(2,1)S(1)} %get-tuple-element.60), channel_id=1, source_target_pairs={{0,2},{1,3},{2,0},{3,1},{4,6},{5,7},{6,4},{7,5},{8,10},{9,11},{10,... | collective-permute-start | bytes 202760 | tf_op jit(solution)/shard_map/ppermute | solution.py:349
  30.9 8.1 %collective-permute-start.13 = (bf16[24,4224]{1,0:T(8,128)(2,1)S(1)}, bf16[24,4224]{1,0:T(8,128)(2,1)S(1)}, u32[]{:S(2)}, u32[]{:S(2)}) collective-permute-start(bf16[24,4224]{1,0:T(8,128)(2,1)S(1)} %get-tuple-element.51), channel_id=1, source_target_pairs={{0,6},{1,7},{2,4},{3,5},{4,2},{5,3},{6,0},{7,1},{8,14},{9,15},{10,... | collective-permute-start | bytes 608264 | tf_op jit(solution)/shard_map/ppermute | solution.py:349
  33.3 7.9 %collective-permute-start.12 = (bf16[24,4224]{1,0:T(8,128)(2,1)S(1)}, bf16[24,4224]{1,0:T(8,128)(2,1)S(1)}, u32[]{:S(2)}, u32[]{:S(2)}) collective-permute-start(bf16[24,4224]{1,0:T(8,128)(2,1)S(1)} %get-tuple-element.51), channel_id=1, source_target_pairs={{0,4},{1,5},{2,6},{3,7},{4,0},{5,1},{6,2},{7,3},{8,12},{9,13},{10,... | collective-permute-start | bytes 608264 | tf_op jit(solution)/shard_map/ppermute | solution.py:349
  36.1 5.7 %collective-permute-start.11 = (bf16[24,4224]{1,0:T(8,128)(2,1)S(1)}, bf16[24,4224]{1,0:T(8,128)(2,1)S(1)}, u32[]{:S(2)}, u32[]{:S(2)}) collective-permute-start(bf16[24,4224]{1,0:T(8,128)(2,1)S(1)} %get-tuple-element.51), channel_id=1, source_target_pairs={{0,2},{1,3},{2,0},{3,1},{4,6},{5,7},{6,4},{7,5},{8,10},{9,11},{10,... | collective-permute-start | bytes 608264 | tf_op jit(solution)/shard_map/ppermute | solution.py:349
  36.2 5.7 %collective-permute-start.14 = (bf16[56,4224]{1,0:T(8,128)(2,1)S(1)}, bf16[56,4224]{1,0:T(8,128)(2,1)S(1)}, u32[]{:S(2)}, u32[]{:S(2)}) collective-permute-start(bf16[56,4224]{1,0:T(8,128)(2,1)S(1)} %get-tuple-element.43), channel_id=1, source_target_pairs={{0,1},{1,0},{2,3},{3,2},{4,5},{5,4},{6,7},{7,6},{8,9},{9,8},{10,11... | collective-permute-start | bytes 1419272 | tf_op jit(solution)/shard_map/ppermute | solution.py:349
  38.9 4.4 %collective-permute-start.17 = (bf16[24,4224]{1,0:T(8,128)(2,1)S(1)}, bf16[24,4224]{1,0:T(8,128)(2,1)S(1)}, u32[]{:S(2)}, u32[]{:S(2)}) collective-permute-start(bf16[24,4224]{1,0:T(8,128)(2,1)S(1)} %collective-permute-done.13), channel_id=1, source_target_pairs={{0,1},{1,0},{2,3},{3,2},{4,5},{5,4},{6,7},{7,6},{8,9},{9,8},{10,11... | collective-permute-start | bytes 608264 | tf_op jit(solution)/shard_map/ppermute | solution.py:349
  50.5 2.8 %collective-permute-start.26 = (bf16[24,4096]{1,0:T(8,128)(2,1)S(1)}, bf16[24,4096]{1,0:T(8,128)(2,1)S(1)}, u32[]{:S(2)}, u32[]{:S(2)}) collective-permute-start(bf16[24,4096]{1,0:T(8,128)(2,1)S(1)} %get-tuple-element.30), channel_id=1, source_target_pairs={{0,1},{1,0},{2,3},{3,2},{4,5},{5,4},{6,7},{7,6},{8,9},{9,8},{10,11... | collective-permute-start | bytes 589832 | tf_op jit(solution)/shard_map/ppermute | solution.py:349
  50.6 4.6 %collective-permute-start.18 = (bf16[56,4096]{1,0:T(8,128)(2,1)S(1)}, bf16[56,4096]{1,0:T(8,128)(2,1)S(1)}, u32[]{:S(2)}, u32[]{:S(2)}) collective-permute-start(bf16[56,4096]{1,0:T(8,128)(2,1)S(1)} %get-tuple-element.24), channel_id=1, source_target_pairs={{0,1},{1,0},{2,3},{3,2},{4,5},{5,4},{6,7},{7,6},{8,9},{9,8},{10,11... | collective-permute-start | bytes 1376264 | tf_op jit(solution)/shard_map/ppermute | solution.py:349
  51.5 7.0 %collective-permute-start.23 = (bf16[24,4096]{1,0:T(8,128)(2,1)S(1)}, bf16[24,4096]{1,0:T(8,128)(2,1)S(1)}, u32[]{:S(2)}, u32[]{:S(2)}) collective-permute-start(bf16[24,4096]{1,0:T(8,128)(2,1)S(1)} %add_convert_fusion.2), channel_id=1, source_target_pairs={{0,2},{1,3},{2,0},{3,1},{4,6},{5,7},{6,4},{7,5},{8,10},{9,11},{10,... | collective-permute-start | bytes 589832 | tf_op jit(solution)/shard_map/ppermute | solution.py:349
  52.4 7.9 %collective-permute-start.25 = (bf16[24,4096]{1,0:T(8,128)(2,1)S(1)}, bf16[24,4096]{1,0:T(8,128)(2,1)S(1)}, u32[]{:S(2)}, u32[]{:S(2)}) collective-permute-start(bf16[24,4096]{1,0:T(8,128)(2,1)S(1)} %add_convert_fusion.1), channel_id=1, source_target_pairs={{0,4},{1,5},{2,6},{3,7},{4,0},{5,1},{6,2},{7,3},{8,12},{9,13},{10,... | collective-permute-start | bytes 589832 | tf_op jit(solution)/shard_map/ppermute | solution.py:349
  53.4 10.6 %collective-permute-start.27 = (bf16[24,4096]{1,0:T(8,128)(2,1)S(1)}, bf16[24,4096]{1,0:T(8,128)(2,1)S(1)}, u32[]{:S(2)}, u32[]{:S(2)}) collective-permute-start(bf16[24,4096]{1,0:T(8,128)(2,1)S(1)} %add_convert_fusion), channel_id=1, source_target_pairs={{0,6},{1,7},{2,4},{3,5},{4,2},{5,3},{6,0},{7,1},{8,14},{9,15},{10,... | collective-permute-start | bytes 589832 | tf_op jit(solution)/shard_map/ppermute | solution.py:349
  64.1 6.8 %collective-permute-start.28 = (bf16[8,4096]{1,0:T(8,128)(2,1)S(1)}, bf16[8,4096]{1,0:T(8,128)(2,1)S(1)}, u32[]{:S(2)}, u32[]{:S(2)}) collective-permute-start(bf16[8,4096]{1,0:T(8,128)(2,1)S(1)} %get-tuple-element.36), channel_id=1, source_target_pairs={{0,8},{1,9},{2,10},{3,11},{4,12},{5,13},{6,14},{7,15},{8,0},{9,1},... | collective-permute-start | bytes 196616 | tf_op jit(solution)/shard_map/ppermute | solution.py:349
  66.6 6.2 %collective-permute-start.30 = (bf16[8,4096]{1,0:T(8,128)(2,1)S(1)}, bf16[8,4096]{1,0:T(8,128)(2,1)S(1)}, u32[]{:S(2)}, u32[]{:S(2)}) collective-permute-start(bf16[8,4096]{1,0:T(8,128)(2,1)S(1)} %get-tuple-element.37), channel_id=1, source_target_pairs={{0,24},{1,25},{2,26},{3,27},{4,28},{5,29},{6,30},{7,31},{8,16},{9,... | collective-permute-start | bytes 196616 | tf_op jit(solution)/shard_map/ppermute | solution.py:349
  67.6 6.8 %collective-permute-start.29 = (bf16[8,4096]{1,0:T(8,128)(2,1)S(1)}, bf16[8,4096]{1,0:T(8,128)(2,1)S(1)}, u32[]{:S(2)}, u32[]{:S(2)}) collective-permute-start(bf16[8,4096]{1,0:T(8,128)(2,1)S(1)} %get-tuple-element.38), channel_id=1, source_target_pairs={{0,16},{1,17},{2,18},{3,19},{4,20},{5,21},{6,22},{7,23},{8,24},{9,... | collective-permute-start | bytes 196616 | tf_op jit(solution)/shard_map/ppermute | solution.py:349
  68.2 6.3 %collective-permute-start.19 = (bf16[8,4096]{1,0:T(8,128)(2,1)S(1)}, bf16[8,4096]{1,0:T(8,128)(2,1)S(1)}, u32[]{:S(2)}, u32[]{:S(2)}) collective-permute-start(bf16[8,4096]{1,0:T(8,128)(2,1)S(1)} %get-tuple-element.33), channel_id=1, source_target_pairs={{0,2},{1,3},{2,0},{3,1},{4,6},{5,7},{6,4},{7,5},{8,10},{9,11},{10,... | collective-permute-start | bytes 196616 | tf_op jit(solution)/shard_map/ppermute | solution.py:349
  68.7 5.8 %collective-permute-start.21 = (bf16[8,4096]{1,0:T(8,128)(2,1)S(1)}, bf16[8,4096]{1,0:T(8,128)(2,1)S(1)}, u32[]{:S(2)}, u32[]{:S(2)}) collective-permute-start(bf16[8,4096]{1,0:T(8,128)(2,1)S(1)} %get-tuple-element.34), channel_id=1, source_target_pairs={{0,6},{1,7},{2,4},{3,5},{4,2},{5,3},{6,0},{7,1},{8,14},{9,15},{10,... | collective-permute-start | bytes 196616 | tf_op jit(solution)/shard_map/ppermute | solution.py:349
  70.9 4.3 %collective-permute-start.20 = (bf16[8,4096]{1,0:T(8,128)(2,1)S(1)}, bf16[8,4096]{1,0:T(8,128)(2,1)S(1)}, u32[]{:S(2)}, u32[]{:S(2)}) collective-permute-start(bf16[8,4096]{1,0:T(8,128)(2,1)S(1)} %get-tuple-element.35), channel_id=1, source_target_pairs={{0,4},{1,5},{2,6},{3,7},{4,0},{5,1},{6,2},{7,3},{8,12},{9,13},{10,... | collective-permute-start | bytes 196616 | tf_op jit(solution)/shard_map/ppermute | solution.py:349
  (11 other events, 95.4 us)

commit v9 on v8

--- a/solution.py
+++ b/solution.py
@@ -38,11 +38,13 @@
 
 def attention_kernel(flip, *refs):
     sources, refs = refs[:8], refs[8:]
+    w_hbm, refs = refs[0], refs[1:]
     if flip == 0:
-        ids_hbm, gates_hbm, w_hbm, _, out_ref, table_ref, w_ref = refs[:7]
-        refs = refs[7:]
+        ids_hbm, gates_hbm, _, out_ref, w_ref, table_ref = refs[:6]
+        refs = refs[6:]
     else:
-        out_ref, refs = refs[0], refs[1:]
+        out_ref, w_ref = refs[:2]
+        refs = refs[2:]
     len_hbm, q_hbm, nk_hbm, nv_hbm, k_hbm, v_hbm, qg_hbm, kg_hbm = sources
     lengths, q_ref, nk_ref, nv_ref, k_ref, v_ref, qg_ref, kg_ref = refs[:8]
     nk_scr, nv_scr, num, tops, totals, score, weight, sem = refs[8:16]
@@ -65,15 +67,16 @@
     ]
     if flip == 0:
         ids_ref, gates_ref = refs[16:]
-        pairs = [(ids_hbm, ids_ref), (gates_hbm, gates_ref)] + pairs + [(w_hbm, w_ref)]
+        pairs = [(ids_hbm, ids_ref), (gates_hbm, gates_ref)] + pairs
     copies = [pltpu.make_async_copy(src, dst, sem.at[i]) for i, (src, dst) in enumerate(pairs)]
+    width = w_ref.shape[1]
+    ahead = pltpu.make_async_copy(w_hbm.at[:, pl.ds(flip * width, width)], w_ref, sem.at[10])
     for c in copies:
         c.start()
     if flip == 0:
         for c in copies[:2]:
             c.wait()
-        ahead = copies[-1]
-        copies = copies[2:-1]
+        copies = copies[2:]
         gates = gates_ref[...]
         route = (gates / jnp.sum(gates, axis=1, keepdims=True)).astype(BF).astype(F32)
         expert = iota(table_ref.shape, 1)
@@ -104,6 +107,7 @@
     empty = jnp.zeros((step, hd), F32)
     for c in copies[5:]:
         c.wait()
+    ahead.start()
 
     def rows_of(ref, b, size):
         return ref[b * step : (b + 1) * step].reshape(size, hd)
@@ -151,20 +155,23 @@
             side = jnp.where(lane == heads_own + h, high, side)
             side = jnp.where(lane == 2 * heads_own + h, total - high, side)
         out_ref[slot, :, heads_own * hd :] = side.astype(BF)
-    if flip == 0:
-        ahead.wait()
+    ahead.wait()
 
 
 def attention(
-    flip, lengths, queries, new_keys, new_values, key_cache, value_cache, qg, kg, parts, more
+    flip, lengths, queries, new_keys, new_values, key_cache, value_cache, qg, kg, out_proj, parts, more
 ):
     rows, heads, hd = queries.shape
     kvh, cache = key_cache.shape[1:3]
     group = heads // kvh
     blocks = rows // 8
     args = [lengths, queries, new_keys, new_values, key_cache, value_cache]
-    args = [in_hbm(a) for a in (*args, qg.reshape(1, -1), kg.reshape(1, -1))]
-    outs = [jax.ShapeDtypeStruct((parts // kvh, rows, heads // parts * hd + LANES), BF)]
+    args = [in_hbm(a) for a in (*args, qg.reshape(1, -1), kg.reshape(1, -1), out_proj)]
+    columns = out_proj.shape[1] // kvh
+    outs = [
+        jax.ShapeDtypeStruct((parts // kvh, rows, heads // parts * hd + LANES), BF),
+        pltpu.VMEM((out_proj.shape[0], columns), BF),
+    ]
     scratch = [
         pltpu.SMEM((rows,), I32),
         pltpu.VMEM((rows, group, hd), BF),
@@ -184,15 +191,13 @@
         pltpu.SemaphoreType.DMA((11,)),
     ]
     specs = [pl.BlockSpec(memory_space=pltpu.HBM)] * len(args)
-    size = 2 * rows * group * hd * 8
+    size = 2 * out_proj.shape[0] * columns
     if flip == 0:
-        expert_ids, gate_weights, lanes, later, earlier = more
-        args += [in_hbm(a) for a in (expert_ids, gate_weights, later)] + [earlier]
-        specs += [pl.BlockSpec(memory_space=pltpu.HBM)] * 3 + [pl.BlockSpec(memory_space=pl.ANY)]
+        expert_ids, gate_weights, lanes, earlier = more
+        args += [in_hbm(expert_ids), in_hbm(gate_weights), earlier]
+        specs += [pl.BlockSpec(memory_space=pltpu.HBM)] * 2 + [pl.BlockSpec(memory_space=pl.ANY)]
         outs.append(jax.ShapeDtypeStruct((expert_ids.shape[0], lanes), BF))
-        outs.append(pltpu.VMEM(later.shape, later.dtype))
         scratch += [pltpu.VMEM(expert_ids.shape, I32), pltpu.VMEM(gate_weights.shape, F32)]
-        size = size + 2 * later.size
     return pl.pallas_call(
         functools.partial(attention_kernel, flip),
         out_shape=tuple(outs),
@@ -205,13 +210,14 @@
     )(*args)
 
 
-def projection_kernel(parts, *refs):
+def projection_kernel(parts, cuts, *refs):
     got = refs[:parts]
-    w_ref, ahead_hbm, out_ref, ahead_ref, attn, sem = refs[parts:]
+    w_refs, refs = refs[parts : parts + cuts], refs[parts + cuts :]
+    ahead_hbm, out_ref, ahead_ref, attn, sem = refs
     ahead = pltpu.make_async_copy(ahead_hbm, ahead_ref, sem)
     ahead.start()
     tensor_pos = lax.axis_index("tensor")
-    depth, width = w_ref.shape
+    depth, width = w_refs[0].shape
     share = out_ref.shape[2]
     hd = LANES
     heads_own = depth // hd
@@ -230,32 +236,35 @@
         cols = slice(h * hd, (h + 1) * hd)
         terms = [g[:, cols].astype(F32) * f[:, h : h + 1] for g, f in zip(got, factors)]
         attn[:, cols] = functools.reduce(jnp.add, terms).astype(BF)
-    for i in range(width // size):
-        cols = slice(i * size, (i + 1) * size)
-        result = matmul(attn[...], w_ref[:, cols])
-        for t in range(parts):
-            slot = tensor_pos ^ t
-            out_ref[slot & 1, slot >> 1, :, cols] = result[t * share : (t + 1) * share].astype(BF)
+    for k, w_ref in enumerate(w_refs):
+        for start in range(0, width, size):
+            result = matmul(attn[...], w_ref[:, start : start + size])
+            cols = slice(k * width + start, k * width + start + size)
+            for t in range(parts):
+                slot = tensor_pos ^ t
+                block = result[t * share : (t + 1) * share].astype(BF)
+                out_ref[slot & 1, slot >> 1, :, cols] = block
     ahead.wait()
 
 
-def projection(got, out_proj, share, later):
+def projection(got, weights, share, later):
     parts = len(got)
     rows = got[0].shape[0]
-    depth, width = out_proj.shape
+    depth = weights[0].shape[0]
+    width = sum(w.shape[1] for w in weights)
     vmem = pl.BlockSpec(memory_space=pltpu.VMEM)
     return pl.pallas_call(
-        functools.partial(projection_kernel, parts),
+        functools.partial(projection_kernel, parts, len(weights)),
         out_shape=(
             jax.ShapeDtypeStruct((2, parts // 2, share, width), BF),
             pltpu.VMEM(later.shape, later.dtype),
         ),
-        in_specs=[vmem] * (parts + 1) + [pl.BlockSpec(memory_space=pltpu.HBM)],
+        in_specs=[vmem] * (parts + len(weights)) + [pl.BlockSpec(memory_space=pltpu.HBM)],
         out_specs=(vmem, vmem),
         scratch_shapes=[pltpu.VMEM((rows, depth), BF), pltpu.SemaphoreType.DMA],
         compiler_params=pltpu.CompilerParams(vmem_limit_bytes=12 * MIB),
         name="projection",
-    )(*got, out_proj, in_hbm(later))
+    )(*got, *weights, in_hbm(later))
 
 
 def expert_kernel(slots, sizes, *refs):
@@ -386,19 +395,20 @@
 
     inputs = (lengths, queries, new_keys, new_values, key_cache, value_cache, query_gain, key_gain)
     groups = key_cache.shape[1]
-    got, local = [], None
+    got, local, weights = [], None, []
     for flip in reversed(range(groups)):
-        more = (expert_ids, gate_weights, lanes, out_proj, local)
-        results = attention(flip, *inputs, tensor, more)
+        more = (expert_ids, gate_weights, lanes, local)
+        results = attention(flip, *inputs, out_proj, tensor, more)
         local = results[0]
+        weights.insert(0, results[1])
         for j in range(0, tensor // groups, 2):
             far = flip * (tensor // groups) + j
             pair = local[j : j + 2]
             if far:
                 pair = plan.swap(pair, far)
             got += [pair[0], plan.swap(pair[1], plan.core)]
-    _, table, out_proj = results
-    partial, expert_gate = projection(got, out_proj, share, expert_gate)
+    table = results[2]
+    partial, expert_gate = projection(got, weights, share, expert_gate)
     pair = total_of([partial[0], plan.swap(partial[1], plan.core)])
     projected = total_of([pair[0]] + plan.swaps(list(pair[1:]), plan.y))
     hidden = residual_in.astype(F32) + projected
@@ -420,10 +430,10 @@
         for i in reversed(range(half))
     ][::-1]
     blocks = sums[0].reshape(-1, share, width)
-    far = plan.swaps(sums[1:], plan.plane)
-    others = total_of([sums[0][share : plan.zlen * share]] + far).reshape(-1, share, width)
-    near = plan.swaps(list(blocks[plan.zlen :]), plan.plane)
-    moe_sum = total_of([blocks[0]] + near + plan.swaps(list(others), plan.z))
+    far = plan.swaps(sums[1:], plan.plane)[::-1]
+    others = total_of(far + [sums[0][share : plan.zlen * share]]).reshape(-1, share, width)
+    near = plan.swaps(list(blocks[plan.zlen :]), plan.plane)[::-1]
+    moe_sum = total_of(plan.swaps(list(others), plan.z)[::-1] + near + [blocks[0]])
     return (hidden + moe_sum).astype(BF)
 
 

time: 76 us -> 77 us (1.013)
  starting transfers between devices: 29.1 us -> 30 us
  waiting for transfers between devices: 28.4 us -> 27.6 us
    pallas_call x2, Pallas kernels: 6.23 us -> 7.5 us  [attention(): pl.pallas_call(functools.partial(attention_kernel, flip), out_shape=tuple...]
    ppermute x31, starting transfers between devices: 29.1 us -> 30 us  [swap(): lax.ppermute(value, ('dp', 'tensor'), [(i, i ^ flip) for i in range(self....]
    ppermute x31, waiting for transfers between devices: 28.4 us -> 27.6 us  [swap(): lax.ppermute(value, ('dp', 'tensor'), [(i, i ^ flip) for i in range(self....]
where the time goes in v9:
time: 77 us; the launch traced here: 76.8 us
  starting transfers between devices  30 us (39%)
  waiting for transfers between devices  27.6 us (36%)
  Pallas kernels  16.9 us (22%)
  other arithmetic  1.55 us (2%)
    ppermute x31, starting transfers between devices, swap(): lax.ppermute(value, ('dp', 'tensor'), [(i, i ^ flip) for i in range(self....  30 us
    ppermute x31, waiting for transfers between devices, swap(): lax.ppermute(value, ('dp', 'tensor'), [(i, i ^ flip) for i in range(self....  27.6 us
    pallas_call x2, Pallas kernels, attention(): pl.pallas_call(functools.partial(attention_kernel, flip), out_shape=tuple...  7.5 us
    pallas_call x1, Pallas kernels, experts(): pl.pallas_call(functools.partial(expert_kernel, slots, sizes), out_shape=...  6.49 us
    pallas_call x1, Pallas kernels, projection(): pl.pallas_call(functools.partial(projection_kernel, parts, len(weights)),...  2.94 us
  transfers between devices with their start and end apart: 31, of which 18 were waited for; matrix products, arithmetic and copies ran while one was open for 1% of the time, Pallas kernels for 5%

profile of v9, /device:TPU:0, one launch (start us, length us, event | category | flops | bytes accessed | tf_op | source)
XLA Modules:
  0.0 76.8 jit_solution(6869506657150148047)
XLA Ops:
  0.0 3.8 %attention.2 = (bf16[2,32,1152]{2,1,0:T(8,128)(2,1)S(1)}, bf16[1024,2048]{1,0:T(8,128)(2,1)S(1)}) custom-call(s32[32]{0:T(128)} %refs_0_.3, bf16[32,32,128]{2,1,0:T(8,128)(2,1)} %refs_1_.3, bf16[32,2,128]{2,1,0:T(2,128)(2,1)} %refs_2_.4, bf16[32,2,128]{2,1,0:T(2,128)(2,1)} %refs_3_.4, bf16[32,2,32,128]{3,2,1,0:T(8,128)(2,1)} %refs_4_.3, ...), custom_call_target="tpu_custom_call" | custom-call | flops 4194304 | bytes 4194304 | tf_op jit(solution)/shard_map/attention/pallas_call | solution.py:201
  3.8 3.0 %collective-permute-start = (bf16[2,32,1152]{2,1,0:T(8,128)(2,1)S(1)}, bf16[2,32,1152]{2,1,0:T(8,128)(2,1)S(1)}, u32[]{:S(2)}, u32[]{:S(2)}) collective-permute-start(bf16[2,32,1152]{2,1,0:T(8,128)(2,1)S(1)} %get-tuple-element.20.refs_11_), channel_id=1, source_target_pairs={{0,2},{1,3},{2,0},{3,1},{4,6},{5,7},{6,4},{7,5},{8,10},{9,11},{10,... | collective-permute-start | bytes 442376 | tf_op jit(solution)/shard_map/ppermute | solution.py:358
  6.8 3.7 %attention.3 = (bf16[2,32,1152]{2,1,0:T(8,128)(2,1)S(1)}, bf16[1024,2048]{1,0:T(8,128)(2,1)S(1)}, bf16[8,128]{1,0:T(8,128)(2,1)S(1)}) custom-call(s32[32]{0:T(128)} %refs_0_.3, bf16[32,32,128]{2,1,0:T(8,128)(2,1)} %refs_1_.3, bf16[32,2,128]{2,1,0:T(2,128)(2,1)} %refs_2_.4, bf16[32,2,128]{2,1,0:T(2,128)(2,1)} %refs_3_.4, bf16[32,2,32,128]{3,2,1,0:T(8,128)(2,1)} %refs_4_.3, ...), custom_call_target="tpu_custom_call" | custom-call | flops 4194304 | bytes 4194304 | tf_op jit(solution)/shard_map/attention/pallas_call | solution.py:201
  12.2 2.9 %projection.1 = (bf16[2,2,8,4096]{3,2,1,0:T(8,128)(2,1)S(1)}, bf16[1,4096,768]{2,1,0:T(8,128)(2,1)S(1)}) custom-call(bf16[32,1152]{1,0:T(8,128)(2,1)S(1)} %get-tuple-element.46.refs_0_, bf16[32,1152]{1,0:T(8,128)(2,1)S(1)} %collective-permute-done.1.refs_1_, bf16[32,1152]{1,0:T(8,128)(2,1)S(1)} %get-tuple-element.44.refs_2_, ...), custom_call_target="tpu_custom_call" | custom-call | tf_op jit(solution)/shard_map/projection/pallas_call | solution.py:256
  16.6 1.7 %collective-permute-start.4 = (bf16[8,4096]{1,0:T(8,128)(2,1)S(1)}, bf16[8,4096]{1,0:T(8,128)(2,1)S(1)}, u32[]{:S(2)}, u32[]{:S(2)}) collective-permute-start(bf16[8,4096]{1,0:T(8,128)(2,1)S(1)} %fusion.5), channel_id=1, source_target_pairs={{0,2},{1,3},{2,0},{3,1},{4,6},{5,7},{6,4},{7,5},{8,10},{9,11},{10,... | collective-permute-start | bytes 196616 | tf_op jit(solution)/shard_map/ppermute | solution.py:358
  18.3 2.8 %collective-permute-done.4 = bf16[8,4096]{1,0:T(8,128)(2,1)S(1)} collective-permute-done((bf16[8,4096]{1,0:T(8,128)(2,1)S(1)}, bf16[8,4096]{1,0:T(8,128)(2,1)S(1)}, u32[]{:S(2)}, u32[]{:S(2)}) %collective-permute-start.4) | collective-permute-done | bytes 65568 | tf_op jit(solution)/shard_map/ppermute | solution.py:358
  21.3 1.6 %collective-permute-start.5 = (bf16[8,4224]{1,0:T(8,128)(2,1)S(1)}, bf16[8,4224]{1,0:T(8,128)(2,1)S(1)}, u32[]{:S(2)}, u32[]{:S(2)}) collective-permute-start(bf16[8,4224]{1,0:T(8,128)(2,1)S(1)} %pad_maximum_fusion), channel_id=1, source_target_pairs={{0,8},{1,9},{2,10},{3,11},{4,12},{5,13},{6,14},{7,15},{8,0},{9,1},... | collective-permute-start | bytes 202760 | tf_op jit(solution)/shard_map/ppermute | solution.py:358
  22.9 2.6 %collective-permute-start.6 = (bf16[8,4224]{1,0:T(8,128)(2,1)S(1)}, bf16[8,4224]{1,0:T(8,128)(2,1)S(1)}, u32[]{:S(2)}, u32[]{:S(2)}) collective-permute-start(bf16[8,4224]{1,0:T(8,128)(2,1)S(1)} %pad_maximum_fusion), channel_id=1, source_target_pairs={{0,16},{1,17},{2,18},{3,19},{4,20},{5,21},{6,22},{7,23},{8,24},{9,... | collective-permute-start | bytes 202760 | tf_op jit(solution)/shard_map/ppermute | solution.py:358
  25.9 3.1 %collective-permute-start.10 = (bf16[8,4224]{1,0:T(8,128)(2,1)S(1)}, bf16[8,4224]{1,0:T(8,128)(2,1)S(1)}, u32[]{:S(2)}, u32[]{:S(2)}) collective-permute-start(bf16[8,4224]{1,0:T(8,128)(2,1)S(1)} %get-tuple-element.64), channel_id=1, source_target_pairs={{0,6},{1,7},{2,4},{3,5},{4,2},{5,3},{6,0},{7,1},{8,14},{9,15},{10,... | collective-permute-start | bytes 202760 | tf_op jit(solution)/shard_map/ppermute | solution.py:358
  30.0 1.6 %collective-permute-done.7 = bf16[8,4224]{1,0:T(8,128)(2,1)S(1)} collective-permute-done((bf16[8,4224]{1,0:T(8,128)(2,1)S(1)}, bf16[8,4224]{1,0:T(8,128)(2,1)S(1)}, u32[]{:S(2)}, u32[]{:S(2)}) %collective-permute-start.7) | collective-permute-done | bytes 67616 | tf_op jit(solution)/shard_map/ppermute | solution.py:358
  31.6 2.5 %collective-permute-start.13 = (bf16[24,4224]{1,0:T(8,128)(2,1)S(1)}, bf16[24,4224]{1,0:T(8,128)(2,1)S(1)}, u32[]{:S(2)}, u32[]{:S(2)}) collective-permute-start(bf16[24,4224]{1,0:T(8,128)(2,1)S(1)} %get-tuple-element.55), channel_id=1, source_target_pairs={{0,6},{1,7},{2,4},{3,5},{4,2},{5,3},{6,0},{7,1},{8,14},{9,15},{10,... | collective-permute-start | bytes 608264 | tf_op jit(solution)/shard_map/ppermute | solution.py:358
  34.7 2.0 %collective-permute-done.8 = bf16[8,4224]{1,0:T(8,128)(2,1)S(1)} collective-permute-done((bf16[8,4224]{1,0:T(8,128)(2,1)S(1)}, bf16[8,4224]{1,0:T(8,128)(2,1)S(1)}, u32[]{:S(2)}, u32[]{:S(2)}) %collective-permute-start.8) | collective-permute-done | bytes 67616 | tf_op jit(solution)/shard_map/ppermute | solution.py:358
  36.9 2.7 %collective-permute-done.13 = bf16[24,4224]{1,0:T(8,128)(2,1)S(1)} collective-permute-done((bf16[24,4224]{1,0:T(8,128)(2,1)S(1)}, bf16[24,4224]{1,0:T(8,128)(2,1)S(1)}, u32[]{:S(2)}, u32[]{:S(2)}) %collective-permute-start.13) | collective-permute-done | bytes 202784 | tf_op jit(solution)/shard_map/ppermute | solution.py:358
  39.6 2.4 %collective-permute-done.12 = bf16[24,4224]{1,0:T(8,128)(2,1)S(1)} collective-permute-done((bf16[24,4224]{1,0:T(8,128)(2,1)S(1)}, bf16[24,4224]{1,0:T(8,128)(2,1)S(1)}, u32[]{:S(2)}, u32[]{:S(2)}) %collective-permute-start.12) | collective-permute-done | bytes 202784 | tf_op jit(solution)/shard_map/ppermute | solution.py:358
  42.7 1.2 %collective-permute-done.15 = bf16[24,4224]{1,0:T(8,128)(2,1)S(1)} collective-permute-done((bf16[24,4224]{1,0:T(8,128)(2,1)S(1)}, bf16[24,4224]{1,0:T(8,128)(2,1)S(1)}, u32[]{:S(2)}, u32[]{:S(2)}) %collective-permute-start.15) | collective-permute-done | bytes 202784 | tf_op jit(solution)/shard_map/ppermute | solution.py:358
  44.0 6.5 %experts.1 = (bf16[56,4096]{1,0:T(8,128)(2,1)S(1)}, bf16[24,4096]{1,0:T(8,128)(2,1)S(1)}, bf16[24,4096]{1,0:T(8,128)(2,1)S(1)}, bf16[24,4096]{1,0:T(8,128)(2,1)S...) custom-call(bf16[256,4224]{1,0:T(8,128)(2,1)S(1)} %constant_dynamic-, ...), custom_call_target="tpu_custom_call" | custom-call | tf_op jit(solution)/shard_map/experts/pallas_call | solution.py:328
  52.1 1.4 %collective-permute-start.19 = (bf16[24,4096]{1,0:T(8,128)(2,1)S(1)}, bf16[24,4096]{1,0:T(8,128)(2,1)S(1)}, u32[]{:S(2)}, u32[]{:S(2)}) collective-permute-start(bf16[24,4096]{1,0:T(8,128)(2,1)S(1)} %add_convert_fusion.2), channel_id=1, source_target_pairs={{0,6},{1,7},{2,4},{3,5},{4,2},{5,3},{6,0},{7,1},{8,14},{9,15},{10,... | collective-permute-start | bytes 589832 | tf_op jit(solution)/shard_map/ppermute | solution.py:358
  56.0 4.8 %collective-permute-done.19 = bf16[24,4096]{1,0:T(8,128)(2,1)S(1)} collective-permute-done((bf16[24,4096]{1,0:T(8,128)(2,1)S(1)}, bf16[24,4096]{1,0:T(8,128)(2,1)S(1)}, u32[]{:S(2)}, u32[]{:S(2)}) %collective-permute-start.19) | collective-permute-done | bytes 196640 | tf_op jit(solution)/shard_map/ppermute | solution.py:358
  60.8 2.9 %collective-permute-done.21 = bf16[24,4096]{1,0:T(8,128)(2,1)S(1)} collective-permute-done((bf16[24,4096]{1,0:T(8,128)(2,1)S(1)}, bf16[24,4096]{1,0:T(8,128)(2,1)S(1)}, u32[]{:S(2)}, u32[]{:S(2)}) %collective-permute-start.21) | collective-permute-done | bytes 196640 | tf_op jit(solution)/shard_map/ppermute | solution.py:358
  64.3 3.0 %collective-permute-start.25 = (bf16[8,4096]{1,0:T(8,128)(2,1)S(1)}, bf16[8,4096]{1,0:T(8,128)(2,1)S(1)}, u32[]{:S(2)}, u32[]{:S(2)}) collective-permute-start(bf16[8,4096]{1,0:T(8,128)(2,1)S(1)} %get-tuple-element.40), channel_id=1, source_target_pairs={{0,24},{1,25},{2,26},{3,27},{4,28},{5,29},{6,30},{7,31},{8,16},{9,... | collective-permute-start | bytes 196616 | tf_op jit(solution)/shard_map/ppermute | solution.py:358
  67.5 1.4 %collective-permute-start.26 = (bf16[8,4096]{1,0:T(8,128)(2,1)S(1)}, bf16[8,4096]{1,0:T(8,128)(2,1)S(1)}, u32[]{:S(2)}, u32[]{:S(2)}) collective-permute-start(bf16[8,4096]{1,0:T(8,128)(2,1)S(1)} %get-tuple-element.42), channel_id=1, source_target_pairs={{0,16},{1,17},{2,18},{3,19},{4,20},{5,21},{6,22},{7,23},{8,24},{9,... | collective-permute-start | bytes 196616 | tf_op jit(solution)/shard_map/ppermute | solution.py:358
  68.8 1.5 %collective-permute-start.28 = (bf16[8,4096]{1,0:T(8,128)(2,1)S(1)}, bf16[8,4096]{1,0:T(8,128)(2,1)S(1)}, u32[]{:S(2)}, u32[]{:S(2)}) collective-permute-start(bf16[8,4096]{1,0:T(8,128)(2,1)S(1)} %get-tuple-element.37), channel_id=1, source_target_pairs={{0,6},{1,7},{2,4},{3,5},{4,2},{5,3},{6,0},{7,1},{8,14},{9,15},{10,... | collective-permute-start | bytes 196616 | tf_op jit(solution)/shard_map/ppermute | solution.py:358
  70.4 1.4 %collective-permute-start.30 = (bf16[8,4096]{1,0:T(8,128)(2,1)S(1)}, bf16[8,4096]{1,0:T(8,128)(2,1)S(1)}, u32[]{:S(2)}, u32[]{:S(2)}) collective-permute-start(bf16[8,4096]{1,0:T(8,128)(2,1)S(1)} %get-tuple-element.38), channel_id=1, source_target_pairs={{0,2},{1,3},{2,0},{3,1},{4,6},{5,7},{6,4},{7,5},{8,10},{9,11},{10,... | collective-permute-start | bytes 196616 | tf_op jit(solution)/shard_map/ppermute | solution.py:358
  72.5 1.9 %collective-permute-done.26 = bf16[8,4096]{1,0:T(8,128)(2,1)S(1)} collective-permute-done((bf16[8,4096]{1,0:T(8,128)(2,1)S(1)}, bf16[8,4096]{1,0:T(8,128)(2,1)S(1)}, u32[]{:S(2)}, u32[]{:S(2)}) %collective-permute-start.26) | collective-permute-done | bytes 65568 | tf_op jit(solution)/shard_map/ppermute | solution.py:358
  (83 shorter events, 14.1 us)
Async XLA Ops:
  3.8 6.9 %collective-permute-start = (bf16[2,32,1152]{2,1,0:T(8,128)(2,1)S(1)}, bf16[2,32,1152]{2,1,0:T(8,128)(2,1)S(1)}, u32[]{:S(2)}, u32[]{:S(2)}) collective-permute-start(bf16[2,32,1152]{2,1,0:T(8,128)(2,1)S(1)} %get-tuple-element.20.refs_11_), channel_id=1, source_target_pairs={{0,2},{1,3},{2,0},{3,1},{4,6},{5,7},{6,4},{7,5},{8,10},{9,11},{10,... | collective-permute-start | bytes 442376 | tf_op jit(solution)/shard_map/ppermute | solution.py:358
  16.6 4.4 %collective-permute-start.4 = (bf16[8,4096]{1,0:T(8,128)(2,1)S(1)}, bf16[8,4096]{1,0:T(8,128)(2,1)S(1)}, u32[]{:S(2)}, u32[]{:S(2)}) collective-permute-start(bf16[8,4096]{1,0:T(8,128)(2,1)S(1)} %fusion.5), channel_id=1, source_target_pairs={{0,2},{1,3},{2,0},{3,1},{4,6},{5,7},{6,4},{7,5},{8,10},{9,11},{10,... | collective-permute-start | bytes 196616 | tf_op jit(solution)/shard_map/ppermute | solution.py:358
  21.3 4.5 %collective-permute-start.5 = (bf16[8,4224]{1,0:T(8,128)(2,1)S(1)}, bf16[8,4224]{1,0:T(8,128)(2,1)S(1)}, u32[]{:S(2)}, u32[]{:S(2)}) collective-permute-start(bf16[8,4224]{1,0:T(8,128)(2,1)S(1)} %pad_maximum_fusion), channel_id=1, source_target_pairs={{0,8},{1,9},{2,10},{3,11},{4,12},{5,13},{6,14},{7,15},{8,0},{9,1},... | collective-permute-start | bytes 202760 | tf_op jit(solution)/shard_map/ppermute | solution.py:358
  22.9 7.0 %collective-permute-start.6 = (bf16[8,4224]{1,0:T(8,128)(2,1)S(1)}, bf16[8,4224]{1,0:T(8,128)(2,1)S(1)}, u32[]{:S(2)}, u32[]{:S(2)}) collective-permute-start(bf16[8,4224]{1,0:T(8,128)(2,1)S(1)} %pad_maximum_fusion), channel_id=1, source_target_pairs={{0,16},{1,17},{2,18},{3,19},{4,20},{5,21},{6,22},{7,23},{8,24},{9,... | collective-permute-start | bytes 202760 | tf_op jit(solution)/shard_map/ppermute | solution.py:358
  25.5 6.1 %collective-permute-start.7 = (bf16[8,4224]{1,0:T(8,128)(2,1)S(1)}, bf16[8,4224]{1,0:T(8,128)(2,1)S(1)}, u32[]{:S(2)}, u32[]{:S(2)}) collective-permute-start(bf16[8,4224]{1,0:T(8,128)(2,1)S(1)} %pad_maximum_fusion), channel_id=1, source_target_pairs={{0,24},{1,25},{2,26},{3,27},{4,28},{5,29},{6,30},{7,31},{8,16},{9,... | collective-permute-start | bytes 202760 | tf_op jit(solution)/shard_map/ppermute | solution.py:358
  25.9 10.8 %collective-permute-start.10 = (bf16[8,4224]{1,0:T(8,128)(2,1)S(1)}, bf16[8,4224]{1,0:T(8,128)(2,1)S(1)}, u32[]{:S(2)}, u32[]{:S(2)}) collective-permute-start(bf16[8,4224]{1,0:T(8,128)(2,1)S(1)} %get-tuple-element.64), channel_id=1, source_target_pairs={{0,6},{1,7},{2,4},{3,5},{4,2},{5,3},{6,0},{7,1},{8,14},{9,15},{10,... | collective-permute-start | bytes 202760 | tf_op jit(solution)/shard_map/ppermute | solution.py:358
  29.0 7.7 %collective-permute-start.9 = (bf16[8,4224]{1,0:T(8,128)(2,1)S(1)}, bf16[8,4224]{1,0:T(8,128)(2,1)S(1)}, u32[]{:S(2)}, u32[]{:S(2)}) collective-permute-start(bf16[8,4224]{1,0:T(8,128)(2,1)S(1)} %get-tuple-element.64), channel_id=1, source_target_pairs={{0,4},{1,5},{2,6},{3,7},{4,0},{5,1},{6,2},{7,3},{8,12},{9,13},{10,... | collective-permute-start | bytes 202760 | tf_op jit(solution)/shard_map/ppermute | solution.py:358
  29.5 7.2 %collective-permute-start.8 = (bf16[8,4224]{1,0:T(8,128)(2,1)S(1)}, bf16[8,4224]{1,0:T(8,128)(2,1)S(1)}, u32[]{:S(2)}, u32[]{:S(2)}) collective-permute-start(bf16[8,4224]{1,0:T(8,128)(2,1)S(1)} %get-tuple-element.64), channel_id=1, source_target_pairs={{0,2},{1,3},{2,0},{3,1},{4,6},{5,7},{6,4},{7,5},{8,10},{9,11},{10,... | collective-permute-start | bytes 202760 | tf_op jit(solution)/shard_map/ppermute | solution.py:358
  31.6 8.0 %collective-permute-start.13 = (bf16[24,4224]{1,0:T(8,128)(2,1)S(1)}, bf16[24,4224]{1,0:T(8,128)(2,1)S(1)}, u32[]{:S(2)}, u32[]{:S(2)}) collective-permute-start(bf16[24,4224]{1,0:T(8,128)(2,1)S(1)} %get-tuple-element.55), channel_id=1, source_target_pairs={{0,6},{1,7},{2,4},{3,5},{4,2},{5,3},{6,0},{7,1},{8,14},{9,15},{10,... | collective-permute-start | bytes 608264 | tf_op jit(solution)/shard_map/ppermute | solution.py:358
  34.1 7.9 %collective-permute-start.12 = (bf16[24,4224]{1,0:T(8,128)(2,1)S(1)}, bf16[24,4224]{1,0:T(8,128)(2,1)S(1)}, u32[]{:S(2)}, u32[]{:S(2)}) collective-permute-start(bf16[24,4224]{1,0:T(8,128)(2,1)S(1)} %get-tuple-element.55), channel_id=1, source_target_pairs={{0,4},{1,5},{2,6},{3,7},{4,0},{5,1},{6,2},{7,3},{8,12},{9,13},{10,... | collective-permute-start | bytes 608264 | tf_op jit(solution)/shard_map/ppermute | solution.py:358
  36.7 5.7 %collective-permute-start.11 = (bf16[24,4224]{1,0:T(8,128)(2,1)S(1)}, bf16[24,4224]{1,0:T(8,128)(2,1)S(1)}, u32[]{:S(2)}, u32[]{:S(2)}) collective-permute-start(bf16[24,4224]{1,0:T(8,128)(2,1)S(1)} %get-tuple-element.55), channel_id=1, source_target_pairs={{0,2},{1,3},{2,0},{3,1},{4,6},{5,7},{6,4},{7,5},{8,10},{9,11},{10,... | collective-permute-start | bytes 608264 | tf_op jit(solution)/shard_map/ppermute | solution.py:358
  36.8 5.8 %collective-permute-start.14 = (bf16[56,4224]{1,0:T(8,128)(2,1)S(1)}, bf16[56,4224]{1,0:T(8,128)(2,1)S(1)}, u32[]{:S(2)}, u32[]{:S(2)}) collective-permute-start(bf16[56,4224]{1,0:T(8,128)(2,1)S(1)} %get-tuple-element.47), channel_id=1, source_target_pairs={{0,1},{1,0},{2,3},{3,2},{4,5},{5,4},{6,7},{7,6},{8,9},{9,8},{10,11... | collective-permute-start | bytes 1419272 | tf_op jit(solution)/shard_map/ppermute | solution.py:358
  39.6 4.3 %collective-permute-start.17 = (bf16[24,4224]{1,0:T(8,128)(2,1)S(1)}, bf16[24,4224]{1,0:T(8,128)(2,1)S(1)}, u32[]{:S(2)}, u32[]{:S(2)}) collective-permute-start(bf16[24,4224]{1,0:T(8,128)(2,1)S(1)} %collective-permute-done.13), channel_id=1, source_target_pairs={{0,1},{1,0},{2,3},{3,2},{4,5},{5,4},{6,7},{7,6},{8,9},{9,8},{10,11... | collective-permute-start | bytes 608264 | tf_op jit(solution)/shard_map/ppermute | solution.py:358
  51.1 3.5 %collective-permute-start.22 = (bf16[24,4096]{1,0:T(8,128)(2,1)S(1)}, bf16[24,4096]{1,0:T(8,128)(2,1)S(1)}, u32[]{:S(2)}, u32[]{:S(2)}) collective-permute-start(bf16[24,4096]{1,0:T(8,128)(2,1)S(1)} %get-tuple-element.32), channel_id=1, source_target_pairs={{0,1},{1,0},{2,3},{3,2},{4,5},{5,4},{6,7},{7,6},{8,9},{9,8},{10,11... | collective-permute-start | bytes 589832 | tf_op jit(solution)/shard_map/ppermute | solution.py:358
  51.2 4.6 %collective-permute-start.24 = (bf16[56,4096]{1,0:T(8,128)(2,1)S(1)}, bf16[56,4096]{1,0:T(8,128)(2,1)S(1)}, u32[]{:S(2)}, u32[]{:S(2)}) collective-permute-start(bf16[56,4096]{1,0:T(8,128)(2,1)S(1)} %get-tuple-element.34), channel_id=1, source_target_pairs={{0,1},{1,0},{2,3},{3,2},{4,5},{5,4},{6,7},{7,6},{8,9},{9,8},{10,11... | collective-permute-start | bytes 1376264 | tf_op jit(solution)/shard_map/ppermute | solution.py:358
  52.1 8.8 %collective-permute-start.19 = (bf16[24,4096]{1,0:T(8,128)(2,1)S(1)}, bf16[24,4096]{1,0:T(8,128)(2,1)S(1)}, u32[]{:S(2)}, u32[]{:S(2)}) collective-permute-start(bf16[24,4096]{1,0:T(8,128)(2,1)S(1)} %add_convert_fusion.2), channel_id=1, source_target_pairs={{0,6},{1,7},{2,4},{3,5},{4,2},{5,3},{6,0},{7,1},{8,14},{9,15},{10,... | collective-permute-start | bytes 589832 | tf_op jit(solution)/shard_map/ppermute | solution.py:358
  53.5 10.2 %collective-permute-start.21 = (bf16[24,4096]{1,0:T(8,128)(2,1)S(1)}, bf16[24,4096]{1,0:T(8,128)(2,1)S(1)}, u32[]{:S(2)}, u32[]{:S(2)}) collective-permute-start(bf16[24,4096]{1,0:T(8,128)(2,1)S(1)} %add_convert_fusion.1), channel_id=1, source_target_pairs={{0,4},{1,5},{2,6},{3,7},{4,0},{5,1},{6,2},{7,3},{8,12},{9,13},{10,... | collective-permute-start | bytes 589832 | tf_op jit(solution)/shard_map/ppermute | solution.py:358
  54.7 9.5 %collective-permute-start.23 = (bf16[24,4096]{1,0:T(8,128)(2,1)S(1)}, bf16[24,4096]{1,0:T(8,128)(2,1)S(1)}, u32[]{:S(2)}, u32[]{:S(2)}) collective-permute-start(bf16[24,4096]{1,0:T(8,128)(2,1)S(1)} %add_convert_fusion), channel_id=1, source_target_pairs={{0,2},{1,3},{2,0},{3,1},{4,6},{5,7},{6,4},{7,5},{8,10},{9,11},{10,... | collective-permute-start | bytes 589832 | tf_op jit(solution)/shard_map/ppermute | solution.py:358
  64.3 7.5 %collective-permute-start.25 = (bf16[8,4096]{1,0:T(8,128)(2,1)S(1)}, bf16[8,4096]{1,0:T(8,128)(2,1)S(1)}, u32[]{:S(2)}, u32[]{:S(2)}) collective-permute-start(bf16[8,4096]{1,0:T(8,128)(2,1)S(1)} %get-tuple-element.40), channel_id=1, source_target_pairs={{0,24},{1,25},{2,26},{3,27},{4,28},{5,29},{6,30},{7,31},{8,16},{9,... | collective-permute-start | bytes 196616 | tf_op jit(solution)/shard_map/ppermute | solution.py:358
  67.3 5.2 %collective-permute-start.27 = (bf16[8,4096]{1,0:T(8,128)(2,1)S(1)}, bf16[8,4096]{1,0:T(8,128)(2,1)S(1)}, u32[]{:S(2)}, u32[]{:S(2)}) collective-permute-start(bf16[8,4096]{1,0:T(8,128)(2,1)S(1)} %get-tuple-element.41), channel_id=1, source_target_pairs={{0,8},{1,9},{2,10},{3,11},{4,12},{5,13},{6,14},{7,15},{8,0},{9,1},... | collective-permute-start | bytes 196616 | tf_op jit(solution)/shard_map/ppermute | solution.py:358
  67.5 6.9 %collective-permute-start.26 = (bf16[8,4096]{1,0:T(8,128)(2,1)S(1)}, bf16[8,4096]{1,0:T(8,128)(2,1)S(1)}, u32[]{:S(2)}, u32[]{:S(2)}) collective-permute-start(bf16[8,4096]{1,0:T(8,128)(2,1)S(1)} %get-tuple-element.42), channel_id=1, source_target_pairs={{0,16},{1,17},{2,18},{3,19},{4,20},{5,21},{6,22},{7,23},{8,24},{9,... | collective-permute-start | bytes 196616 | tf_op jit(solution)/shard_map/ppermute | solution.py:358
  68.8 5.6 %collective-permute-start.28 = (bf16[8,4096]{1,0:T(8,128)(2,1)S(1)}, bf16[8,4096]{1,0:T(8,128)(2,1)S(1)}, u32[]{:S(2)}, u32[]{:S(2)}) collective-permute-start(bf16[8,4096]{1,0:T(8,128)(2,1)S(1)} %get-tuple-element.37), channel_id=1, source_target_pairs={{0,6},{1,7},{2,4},{3,5},{4,2},{5,3},{6,0},{7,1},{8,14},{9,15},{10,... | collective-permute-start | bytes 196616 | tf_op jit(solution)/shard_map/ppermute | solution.py:358
  70.4 4.5 %collective-permute-start.30 = (bf16[8,4096]{1,0:T(8,128)(2,1)S(1)}, bf16[8,4096]{1,0:T(8,128)(2,1)S(1)}, u32[]{:S(2)}, u32[]{:S(2)}) collective-permute-start(bf16[8,4096]{1,0:T(8,128)(2,1)S(1)} %get-tuple-element.38), channel_id=1, source_target_pairs={{0,2},{1,3},{2,0},{3,1},{4,6},{5,7},{6,4},{7,5},{8,10},{9,11},{10,... | collective-permute-start | bytes 196616 | tf_op jit(solution)/shard_map/ppermute | solution.py:358
  71.8 4.3 %collective-permute-start.29 = (bf16[8,4096]{1,0:T(8,128)(2,1)S(1)}, bf16[8,4096]{1,0:T(8,128)(2,1)S(1)}, u32[]{:S(2)}, u32[]{:S(2)}) collective-permute-start(bf16[8,4096]{1,0:T(8,128)(2,1)S(1)} %get-tuple-element.39), channel_id=1, source_target_pairs={{0,4},{1,5},{2,6},{3,7},{4,0},{5,1},{6,2},{7,3},{8,12},{9,13},{10,... | collective-permute-start | bytes 196616 | tf_op jit(solution)/shard_map/ppermute | solution.py:358
  (11 other events, 93.4 us)

commit v10 on v7

--- a/solution.py
+++ b/solution.py
@@ -36,86 +36,29 @@
     return pltpu.with_memory_space_constraint(value, pltpu.HBM)
 
 
-def attention_kernel(
-    len_hbm,
-    q_hbm,
-    nk_hbm,
-    nv_hbm,
-    k_hbm,
-    v_hbm,
-    qg_hbm,
-    kg_hbm,
-    ids_hbm,
-    gates_hbm,
-    w_hbm,
-    out_ref,
-    table_ref,
-    w_ref,
-    lengths,
-    q_ref,
-    nk_ref,
-    nv_ref,
-    k_ref,
-    v_ref,
-    qg_ref,
-    kg_ref,
-    ids_ref,
-    gates_ref,
-    nk_scr,
-    nv_scr,
-    num,
-    tops,
-    totals,
-    score,
-    weight,
-    sem,
-):
-    sources = (len_hbm, nk_hbm, nv_hbm, qg_hbm, kg_hbm, ids_hbm, gates_hbm, q_hbm, k_hbm, v_hbm)
-    targets = (lengths, nk_ref, nv_ref, qg_ref, kg_ref, ids_ref, gates_ref, q_ref, k_ref, v_ref)
-    copies = [
-        pltpu.make_async_copy(a, b, sem.at[i]) for i, (a, b) in enumerate(zip(sources, targets))
-    ]
-    ahead = pltpu.make_async_copy(w_hbm, w_ref, sem.at[10])
-    for c in copies + [ahead]:
-        c.start()
+def attend(lengths, q_ref, k_ref, v_ref, key_norm, new_value, query_gain, out_ref, scratch):
+    num, tops, totals, score, weight = scratch
     tensor_pos = lax.axis_index("tensor")
-    rows, heads, hd = q_ref.shape
-    kvh, cache = k_ref.shape[1], k_ref.shape[2]
-    group = heads // kvh
+    rows, group, hd = q_ref.shape
+    cache = k_ref.shape[1]
     parts = out_ref.shape[0]
-    heads_own = heads // parts
-    step = 4
+    heads_own = group // parts
+    step = 8
     blocks = rows // step
-    many, cols, fresh = step * heads, step * kvh * cache, step * kvh
+    many, cols = step * group, step * cache
     scaling = hd ** (-0.5)
-
-    row_group = iota((many, cols), 0) // group
-    same = row_group == iota((many, cols), 1) // cache
-    col_row = iota((1, cols), 1) // (kvh * cache)
+    same = iota((many, cols), 0) // group == iota((many, cols), 1) // cache
+    col_row = iota((1, cols), 1) // cache
     col_pos = iota((1, cols), 1) % cache + tensor_pos * cache
-    new_col = iota((many, 2 * fresh), 1)
-    new_here = (new_col == iota((many, 2 * fresh), 0) // group) & (tensor_pos == 0)
-
-    for c in copies[:7]:
-        c.wait()
-    gates = gates_ref[...]
-    route = (gates / jnp.sum(gates, axis=1, keepdims=True)).astype(BF).astype(F32)
-    expert = iota(table_ref.shape, 1)
-    table = jnp.zeros(table_ref.shape, F32)
-    for k in range(gates.shape[1]):
-        table = jnp.where(expert == ids_ref[:, k : k + 1], route[:, k : k + 1], table)
-    table_ref[...] = table.astype(BF)
-    for r in range(rows):
-        nk_scr[r * kvh : (r + 1) * kvh, :] = nk_ref[r].astype(F32)
-        nv_scr[r * kvh : (r + 1) * kvh, :] = nv_ref[r].astype(F32)
-    query_gain = qg_ref[...]
-    key_norm = rms_scale(nk_scr[...], kg_ref[...])
-    empty = jnp.zeros((fresh, hd), F32)
-    for c in copies[7:]:
-        c.wait()
+    new_here = iota((many, 2 * step), 1) == iota((many, 2 * step), 0) // group
+    new_here = new_here & (tensor_pos == 0)
+    empty = jnp.zeros((step, hd), F32)
 
     def rows_of(ref, b, size):
         return ref[b * step : (b + 1) * step].reshape(size, hd)
+
+    def with_empty(value, b):
+        return jnp.concatenate([value[b * step : (b + 1) * step], empty]).astype(BF)
 
     queries = []
     for b in range(blocks):
@@ -128,8 +71,7 @@
         included = same & (col_pos < limit)
         scores = matmul_t(queries[b], rows_of(k_ref, b, cols)) * scaling
         score[b, :, :cols] = jnp.where(included, scores, -1e30)
-        new_keys = jnp.concatenate([key_norm[b * fresh : (b + 1) * fresh], empty]).astype(BF)
-        scores = matmul_t(queries[b], new_keys) * scaling
+        scores = matmul_t(queries[b], with_empty(key_norm, b)) * scaling
         score[b, :, cols:] = jnp.where(new_here, scores, -1e30)
     for b in range(blocks):
         top = jnp.maximum(jnp.max(score[b], axis=1, keepdims=True), -1e29).astype(BF).astype(F32)
@@ -141,26 +83,168 @@
         total = jnp.sum(weights.astype(F32), axis=1, keepdims=True)
         totals[b * many : (b + 1) * many, :] = jnp.broadcast_to(total, (many, LANES))
     for b in range(blocks):
-        values = nv_scr[b * fresh : (b + 1) * fresh, :]
-        new_values = jnp.concatenate([values, empty]).astype(BF)
         num[b * many : (b + 1) * many, :] = matmul(
             weight[b, :, :cols], rows_of(v_ref, b, cols)
-        ) + matmul(weight[b, :, cols:], new_values)
+        ) + matmul(weight[b, :, cols:], with_empty(new_value, b))
 
     lane = iota((rows, LANES), 1)
     for t in range(parts):
-        slot = tensor_pos ^ t
+        slot = (tensor_pos % parts) ^ t
         side = jnp.zeros((rows, LANES), F32)
         for h in range(heads_own):
-            which = pl.ds(t * heads_own + h, rows, stride=heads)
-            out_ref[slot, :, h * hd : (h + 1) * hd] = num[which, :].astype(BF)
-            total = totals[which, :]
+            own = pl.ds(t * heads_own + h, rows, stride=group)
+            out_ref[slot, :, h * hd : (h + 1) * hd] = num[own, :].astype(BF)
+            total = totals[own, :]
             high = total.astype(BF).astype(F32)
-            side = jnp.where(lane == h, tops[which, :], side)
+            side = jnp.where(lane == h, tops[own, :], side)
             side = jnp.where(lane == heads_own + h, high, side)
             side = jnp.where(lane == 2 * heads_own + h, total - high, side)
         out_ref[slot, :, heads_own * hd :] = side.astype(BF)
-    ahead.wait()
+
+
+WEIGHT_COPIES = 4
+
+
+def weight_copies(w_hbm, w_ref, half, sem):
+    rows = w_ref.shape[0]
+    size = rows // WEIGHT_COPIES
+    return [
+        pltpu.make_async_copy(
+            w_hbm.at[pl.ds(half * rows + i * size, size)], w_ref.at[pl.ds(i * size, size)], sem.at[i]
+        )
+        for i in range(WEIGHT_COPIES)
+    ]
+
+
+def other_kernel(
+    len_hbm,
+    nk_hbm,
+    nv_hbm,
+    qg_hbm,
+    kg_hbm,
+    q_hbm,
+    k_hbm,
+    v_hbm,
+    w_hbm,
+    out_ref,
+    w_ref,
+    q_own,
+    k_own,
+    v_own,
+    nk_scr,
+    nv_scr,
+    qg_ref,
+    lengths,
+    nk_ref,
+    nv_ref,
+    kg_ref,
+    q_ref,
+    k_ref,
+    v_ref,
+    *refs,
+):
+    scratch, (sem, wsem) = refs[:5], refs[5:]
+    tensor_pos = lax.axis_index("tensor")
+    rows, group, _ = q_ref.shape
+    kvh = k_hbm.shape[1]
+    mine = tensor_pos // out_ref.shape[0]
+    which = mine ^ 1
+
+    def heads(index):
+        return pl.ds(pl.multiple_of(index * group, group), group)
+
+    pairs = [
+        (len_hbm, lengths),
+        (nk_hbm, nk_ref),
+        (nv_hbm, nv_ref),
+        (qg_hbm, qg_ref),
+        (kg_hbm, kg_ref),
+        (q_hbm.at[:, heads(which)], q_ref),
+        (k_hbm.at[:, which], k_ref),
+        (v_hbm.at[:, which], v_ref),
+        (q_hbm.at[:, heads(mine)], q_own),
+        (k_hbm.at[:, mine], k_own),
+        (v_hbm.at[:, mine], v_own),
+    ]
+    copies = [pltpu.make_async_copy(src, dst, sem.at[i]) for i, (src, dst) in enumerate(pairs)]
+    weights = weight_copies(w_hbm, w_ref, 0, wsem)
+    for c in copies:
+        c.start()
+    for c in copies[:5]:
+        c.wait()
+    for r in range(rows):
+        nk_scr[r * kvh : (r + 1) * kvh, :] = nk_ref[r].astype(F32)
+        nv_scr[r * kvh : (r + 1) * kvh, :] = nv_ref[r].astype(F32)
+    nk_scr[...] = rms_scale(nk_scr[...], kg_ref[...])
+    for c in copies[5:8]:
+        c.wait()
+    for c in weights:
+        c.start()
+    new_rows = pl.ds(which, rows, stride=kvh)
+    attend(
+        lengths,
+        q_ref,
+        k_ref,
+        v_ref,
+        nk_scr[new_rows, :],
+        nv_scr[new_rows, :],
+        qg_ref[...],
+        out_ref,
+        scratch,
+    )
+    for c in copies[8:] + weights:
+        c.wait()
+
+
+def own_kernel(
+    len_hbm,
+    ids_hbm,
+    gates_hbm,
+    w_hbm,
+    q_ref,
+    k_ref,
+    v_ref,
+    nk_scr,
+    nv_scr,
+    qg_ref,
+    out_ref,
+    w_ref,
+    table_ref,
+    lengths,
+    ids_ref,
+    gates_ref,
+    *refs,
+):
+    scratch, (sem, wsem) = refs[:5], refs[5:]
+    pairs = [(len_hbm, lengths), (ids_hbm, ids_ref), (gates_hbm, gates_ref)]
+    copies = [pltpu.make_async_copy(src, dst, sem.at[i]) for i, (src, dst) in enumerate(pairs)]
+    copies += weight_copies(w_hbm, w_ref, 1, wsem)
+    for c in copies:
+        c.start()
+    rows = q_ref.shape[0]
+    kvh = nk_scr.shape[0] // rows
+    new_rows = pl.ds(lax.axis_index("tensor") // out_ref.shape[0], rows, stride=kvh)
+    copies[0].wait()
+    attend(
+        lengths,
+        q_ref,
+        k_ref,
+        v_ref,
+        nk_scr[new_rows, :],
+        nv_scr[new_rows, :],
+        qg_ref[...],
+        out_ref,
+        scratch,
+    )
+    for c in copies[1:]:
+        c.wait()
+    gates = gates_ref[...]
+    route = (gates / jnp.sum(gates, axis=1, keepdims=True)).astype(BF).astype(F32)
+    expert = iota(table_ref.shape, 1)
+    table = jnp.zeros(table_ref.shape, F32)
+    for k in range(gates.shape[1]):
+        table = jnp.where(expert == ids_ref[:, k : k + 1], route[:, k : k + 1], table)
+    table_ref[...] = table.astype(BF)
 
 
 def attention(
@@ -170,61 +254,84 @@
     new_values,
     key_cache,
     value_cache,
-    qg,
-    kg,
+    query_gain,
+    key_gain,
     expert_ids,
     gate_weights,
+    out_proj,
     parts,
     lanes,
-    later,
 ):
     rows, heads, hd = queries.shape
     kvh, cache = key_cache.shape[1:3]
-    args = (
-        lengths,
-        queries,
-        new_keys,
-        new_values,
-        key_cache,
-        value_cache,
-        qg.reshape(1, -1),
-        kg.reshape(1, -1),
-        expert_ids,
-        gate_weights,
+    group = heads // kvh
+    blocks = rows // 8
+    hbm = pl.BlockSpec(memory_space=pltpu.HBM)
+    vmem = pl.BlockSpec(memory_space=pltpu.VMEM)
+    sums = jax.ShapeDtypeStruct((parts // kvh, rows, heads // parts * hd + LANES), BF)
+    half = pltpu.VMEM((out_proj.shape[0] // 2, out_proj.shape[1]), BF)
+    operands = [pltpu.VMEM((rows, group, hd), BF)] + [pltpu.VMEM((rows, cache, hd), BF)] * 2
+    news = [pltpu.VMEM((rows * kvh, hd), F32)] * 2
+    gain = pltpu.VMEM((1, hd), F32)
+    scratch = [
+        pltpu.VMEM((rows * group, hd), F32),
+        pltpu.VMEM((rows * group, LANES), F32),
+        pltpu.VMEM((rows * group, LANES), F32),
+        pltpu.VMEM((blocks, 8 * group, 8 * (cache + 2)), F32),
+        pltpu.VMEM((blocks, 8 * group, 8 * (cache + 2)), BF),
+        pltpu.SemaphoreType.DMA((11,)),
+        pltpu.SemaphoreType.DMA((WEIGHT_COPIES,)),
+    ]
+    size = out_proj.size
+    settings = dict(
+        compiler_params=pltpu.CompilerParams(vmem_limit_bytes=16 * MIB),
+        cost_estimate=pl.CostEstimate(flops=size, bytes_accessed=size, transcendentals=0),
     )
-    return pl.pallas_call(
-        attention_kernel,
-        out_shape=(
-            jax.ShapeDtypeStruct((parts, rows, heads // parts * hd + LANES), BF),
-            jax.ShapeDtypeStruct((expert_ids.shape[0], lanes), BF),
-            pltpu.VMEM(later.shape, later.dtype),
-        ),
-        in_specs=[pl.BlockSpec(memory_space=pltpu.HBM)] * 11,
-        out_specs=(pl.BlockSpec(memory_space=pltpu.VMEM),) * 3,
-        scratch_shapes=[pltpu.SMEM(args[0].shape, I32)]
-        + [pltpu.VMEM(a.shape, a.dtype) for a in args[1:]]
-        + [
-            pltpu.VMEM((rows * kvh, hd), F32),
-            pltpu.VMEM((rows * kvh, hd), F32),
-            pltpu.VMEM((rows * heads, hd), F32),
-            pltpu.VMEM((rows * heads, LANES), F32),
-            pltpu.VMEM((rows * heads, LANES), F32),
-            pltpu.VMEM((rows // 4, 4 * heads, 4 * kvh * (cache + 2)), F32),
-            pltpu.VMEM((rows // 4, 4 * heads, 4 * kvh * (cache + 2)), BF),
-            pltpu.SemaphoreType.DMA((11,)),
+    args = (lengths, new_keys, new_values, query_gain.reshape(1, -1), key_gain.reshape(1, -1))
+    args = args + (queries, key_cache, value_cache, out_proj)
+    other, first, *held = pl.pallas_call(
+        other_kernel,
+        out_shape=(sums, half, *operands, *news, gain),
+        in_specs=[hbm] * len(args),
+        out_specs=(vmem,) * 8,
+        scratch_shapes=[
+            pltpu.SMEM((rows,), I32),
+            pltpu.VMEM(new_keys.shape, BF),
+            pltpu.VMEM(new_values.shape, BF),
+            gain,
+            *operands,
+            *scratch,
         ],
-        compiler_params=pltpu.CompilerParams(vmem_limit_bytes=16 * MIB),
-        name="attention",
-    )(*[in_hbm(a) for a in (*args, later)])
-
-
-def projection_kernel(parts, *refs):
+        name="attention_other",
+        **settings,
+    )(*[in_hbm(a) for a in args])
+    args = (lengths, expert_ids, gate_weights, out_proj)
+    own, second, table = pl.pallas_call(
+        own_kernel,
+        out_shape=(sums, half, jax.ShapeDtypeStruct((expert_ids.shape[0], lanes), BF)),
+        in_specs=[hbm] * len(args) + [vmem] * len(held),
+        out_specs=(vmem,) * 3,
+        scratch_shapes=[
+            pltpu.SMEM((rows,), I32),
+            pltpu.VMEM(expert_ids.shape, I32),
+            pltpu.VMEM(gate_weights.shape, F32),
+            *scratch,
+        ],
+        name="attention_own",
+        **settings,
+    )(*[in_hbm(a) for a in args], *held)
+    return (other, own), (first, second), table
+
+
+def projection_kernel(parts, cuts, *refs):
     got = refs[:parts]
-    w_ref, ahead_hbm, out_ref, ahead_ref, attn, sem = refs[parts:]
+    w_refs, refs = refs[parts : parts + cuts], refs[parts + cuts :]
+    ahead_hbm, out_ref, ahead_ref, attn, sem = refs
     ahead = pltpu.make_async_copy(ahead_hbm, ahead_ref, sem)
     ahead.start()
     tensor_pos = lax.axis_index("tensor")
-    depth, width = w_ref.shape
+    width = w_refs[0].shape[1]
+    depth = attn.shape[1]
     share = out_ref.shape[2]
     hd = LANES
     heads_own = depth // hd
@@ -243,32 +350,41 @@
         cols = slice(h * hd, (h + 1) * hd)
         terms = [g[:, cols].astype(F32) * f[:, h : h + 1] for g, f in zip(got, factors)]
         attn[:, cols] = functools.reduce(jnp.add, terms).astype(BF)
-    for i in range(width // size):
-        cols = slice(i * size, (i + 1) * size)
-        result = matmul(attn[...], w_ref[:, cols])
+    part = depth // cuts
+    for start in range(0, width, size):
+        cols = slice(start, start + size)
+        result = functools.reduce(
+            jnp.add,
+            [
+                matmul(attn[:, k * part : (k + 1) * part], w_ref[:, cols])
+                for k, w_ref in enumerate(w_refs)
+            ],
+        )
         for t in range(parts):
             slot = tensor_pos ^ t
-            out_ref[slot & 1, slot >> 1, :, cols] = result[t * share : (t + 1) * share].astype(BF)
+            block = result[t * share : (t + 1) * share].astype(BF)
+            out_ref[slot & 1, slot >> 1, :, cols] = block
     ahead.wait()
 
 
-def projection(got, out_proj, share, later):
+def projection(got, weights, share, later):
     parts = len(got)
     rows = got[0].shape[0]
-    depth, width = out_proj.shape
+    depth = sum(w.shape[0] for w in weights)
+    width = weights[0].shape[1]
     vmem = pl.BlockSpec(memory_space=pltpu.VMEM)
     return pl.pallas_call(
-        functools.partial(projection_kernel, parts),
+        functools.partial(projection_kernel, parts, len(weights)),
         out_shape=(
             jax.ShapeDtypeStruct((2, parts // 2, share, width), BF),
             pltpu.VMEM(later.shape, later.dtype),
         ),
-        in_specs=[vmem] * (parts + 1) + [pl.BlockSpec(memory_space=pltpu.HBM)],
+        in_specs=[vmem] * (parts + len(weights)) + [pl.BlockSpec(memory_space=pltpu.HBM)],
         out_specs=(vmem, vmem),
         scratch_shapes=[pltpu.VMEM((rows, depth), BF), pltpu.SemaphoreType.DMA],
         compiler_params=pltpu.CompilerParams(vmem_limit_bytes=12 * MIB),
         name="projection",
-    )(*got, out_proj, in_hbm(later))
+    )(*got, *weights, in_hbm(later))
 
 
 def expert_kernel(slots, x_ref, gate, up, down_hbm, out_ref, down, xc, act, res, sem):
@@ -391,7 +507,7 @@
     share, width = residual_in.shape
     lanes = -(-dp * tensor // LANES) * LANES
 
-    local, table, out_proj = attention(
+    sums, weights, table = attention(
         lengths,
         queries,
         new_keys,
@@ -402,12 +518,19 @@
         key_gain,
         expert_ids,
         gate_weights,
+        out_proj,
         tensor,
         lanes,
-        out_proj,
     )
-    got = [local[0]] + plan.swaps(list(local[1:]), list(range(1, tensor)))
-    partial, expert_gate = projection(got, out_proj, share, expert_gate)
+    got = []
+    for flip, local in zip((1, 0), sums):
+        for j in range(0, local.shape[0], 2):
+            far = flip * local.shape[0] + j
+            pair = local[j : j + 2]
+            if far:
+                pair = plan.swap(pair, far)
+            got += [pair[0], plan.swap(pair[1], plan.core)]
+    partial, expert_gate = projection(got, weights, share, expert_gate)
     pair = total_of([partial[0], plan.swap(partial[1], plan.core)])
     projected = total_of([pair[0]] + plan.swaps(list(pair[1:]), plan.y))
     hidden = residual_in.astype(F32) + projected

time: 76.5 us -> 76.4 us (level)
  waiting for transfers between devices: 30.8 us -> 29.1 us
  Pallas kernels: 14.1 us -> 15.7 us
    ppermute x31, waiting for transfers between devices: 30.8 us -> 29.1 us  [swap(): lax.ppermute(value, ('dp', 'tensor'), [(i, i ^ flip) for i in range(self....]
    pallas_call x2 -> x3, Pallas kernels: 7.58 us -> 9.26 us  [the longest x1 3.79 us: attention(): pl.pallas_call(other_kernel, out_shape=(sums, half, *operands, *news, gai...]
  transfers between devices with their start and end apart: 31 -> 31, of which waited for: 18 -> 18; matrix products, arithmetic and copies ran while one was open for 1% -> 1% of each run, Pallas kernels for 0% -> 3%
where the time goes in v10:
time: 76.4 us; the launch traced here: 76.3 us
  starting transfers between devices  29.1 us (38%)
  waiting for transfers between devices  29.1 us (38%)
  Pallas kernels  15.7 us (21%)
  other arithmetic  1.55 us (2%)
    ppermute x31, starting transfers between devices, swap(): lax.ppermute(value, ('dp', 'tensor'), [(i, i ^ flip) for i in range(self....  29.1 us
    ppermute x31, waiting for transfers between devices, swap(): lax.ppermute(value, ('dp', 'tensor'), [(i, i ^ flip) for i in range(self....  29.1 us
    pallas_call x1, Pallas kernels, experts(): pl.pallas_call(functools.partial(expert_kernel, slots), out_shape=jax.Sha...  6.48 us
    pallas_call x1, Pallas kernels, attention(): pl.pallas_call(other_kernel, out_shape=(sums, half, *operands, *news, gai...  3.79 us
    pallas_call x1, Pallas kernels, projection(): pl.pallas_call(functools.partial(projection_kernel, parts, len(weights)),...  2.95 us
    pallas_call x1, Pallas kernels, attention(): pl.pallas_call(own_kernel, out_shape=(sums, half, jax.ShapeDtypeStruct((e...  2.52 us
  transfers between devices with their start and end apart: 31, of which 18 were waited for; matrix products, arithmetic and copies ran while one was open for 1% of the time, Pallas kernels for 3%

profile of v10, /device:TPU:0, one launch (start us, length us, event | category | flops | bytes accessed | tf_op | source)
XLA Modules:
  0.0 76.3 jit_solution(2302823040216231152)
XLA Ops:
  0.0 3.8 %attention_other.1 = (bf16[2,32,1152]{2,1,0:T(8,128)(2,1)S(1)}, bf16[512,4096]{1,0:T(8,128)(2,1)S(1)}, bf16[32,16,128]{2,1,0:T(8,128)(2,1)S(1)}, bf16[32,32,128]...) custom-call(s32[32]{0:T(128)} %len_hbm.3, ...), custom_call_target="tpu_custom_call" | custom-call | flops 4194304 | bytes 4194304 | tf_op jit(solution)/shard_map/attention_other/pallas_call | solution.py:292
  3.8 3.0 %collective-permute-start = (bf16[2,32,1152]{2,1,0:T(8,128)(2,1)S(1)}, bf16[2,32,1152]{2,1,0:T(8,128)(2,1)S(1)}, u32[]{:S(2)}, u32[]{:S(2)}) collective-permute-start(bf16[2,32,1152]{2,1,0:T(8,128)(2,1)S(1)} %get-tuple-element.18), channel_id=1, source_target_pairs={{0,2},{1,3},{2,0},{3,1},{4,6},{5,7},{6,4},{7,5},{8,10},{9,11},{10,... | collective-permute-start | bytes 442376 | tf_op jit(solution)/shard_map/ppermute | solution.py:472
  6.8 2.5 %attention_own.1 = (bf16[2,32,1152]{2,1,0:T(8,128)(2,1)S(1)}, bf16[512,4096]{1,0:T(8,128)(2,1)S(1)}, bf16[8,128]{1,0:T(8,128)(2,1)S(1)}) custom-call(s32[32]{0:T(128)} %len_hbm.3, s32[8,8]{1,0:T(8,128)} %ids_hbm.1, f32[8,8]{1,0:T(8,128)} %gates_hbm.1, bf16[1024,4096]{1,0:T(8,128)(2,1)} %w_hbm.3, bf16[32,16,128]{2,1,0:T(8,128)(2,1)S(1)} %get-tuple-element.19.q_ref, ...), custom_call_target="tpu_custom_call" | custom-call | flops 4194304 | bytes 4194304 | tf_op jit(solution)/shard_map/attention_own/pallas_call | solution.py:309
  9.5 1.2 %collective-permute-done = bf16[2,32,1152]{2,1,0:T(8,128)(2,1)S(1)} collective-permute-done((bf16[2,32,1152]{2,1,0:T(8,128)(2,1)S(1)}, bf16[2,32,1152]{2,1,0:T(8,128)(2,1)S(1)}, u32[]{:S(2)}, u32[]{:S(2)}) %collective-permute-start) | collective-permute-done | bytes 147488 | tf_op jit(solution)/shard_map/ppermute | solution.py:472
  10.8 1.2 %collective-permute-done.1.refs_1_ = bf16[32,1152]{1,0:T(8,128)(2,1)S(1)} collective-permute-done((bf16[32,1152]{1,0:T(8,128)(2,1)S(1)}, bf16[32,1152]{1,0:T(8,128)(2,1)S(1)}, u32[]{:S(2)}, u32[]{:S(2)}) %collective-permute-start.1) | collective-permute-done | bytes 73760 | tf_op jit(solution)/shard_map/ppermute | solution.py:472
  12.0 2.9 %projection.1 = (bf16[2,2,8,4096]{3,2,1,0:T(8,128)(2,1)S(1)}, bf16[1,4096,768]{2,1,0:T(8,128)(2,1)S(1)}) custom-call(bf16[32,1152]{1,0:T(8,128)(2,1)S(1)} %get-tuple-element.48.refs_0_, bf16[32,1152]{1,0:T(8,128)(2,1)S(1)} %collective-permute-done.1.refs_1_, bf16[32,1152]{1,0:T(8,128)(2,1)S(1)} %get-tuple-element.46.refs_2_, ...), custom_call_target="tpu_custom_call" | custom-call | tf_op jit(solution)/shard_map/projection/pallas_call | solution.py:376
  15.2 1.2 %collective-permute-done.3 = bf16[2,8,4096]{2,1,0:T(8,128)(2,1)S(1)} collective-permute-done((bf16[2,8,4096]{2,1,0:T(8,128)(2,1)S(1)}, bf16[2,8,4096]{2,1,0:T(8,128)(2,1)S(1)}, u32[]{:S(2)}, u32[]{:S(2)}) %collective-permute-start.3) | collective-permute-done | bytes 131104 | tf_op jit(solution)/shard_map/ppermute | solution.py:472
  16.5 1.8 %collective-permute-start.4 = (bf16[8,4096]{1,0:T(8,128)(2,1)S(1)}, bf16[8,4096]{1,0:T(8,128)(2,1)S(1)}, u32[]{:S(2)}, u32[]{:S(2)}) collective-permute-start(bf16[8,4096]{1,0:T(8,128)(2,1)S(1)} %fusion.12), channel_id=1, source_target_pairs={{0,2},{1,3},{2,0},{3,1},{4,6},{5,7},{6,4},{7,5},{8,10},{9,11},{10,... | collective-permute-start | bytes 196616 | tf_op jit(solution)/shard_map/ppermute | solution.py:472
  18.3 2.5 %collective-permute-done.4 = bf16[8,4096]{1,0:T(8,128)(2,1)S(1)} collective-permute-done((bf16[8,4096]{1,0:T(8,128)(2,1)S(1)}, bf16[8,4096]{1,0:T(8,128)(2,1)S(1)}, u32[]{:S(2)}, u32[]{:S(2)}) %collective-permute-start.4) | collective-permute-done | bytes 65568 | tf_op jit(solution)/shard_map/ppermute | solution.py:472
  21.1 1.9 %collective-permute-start.5 = (bf16[8,4224]{1,0:T(8,128)(2,1)S(1)}, bf16[8,4224]{1,0:T(8,128)(2,1)S(1)}, u32[]{:S(2)}, u32[]{:S(2)}) collective-permute-start(bf16[8,4224]{1,0:T(8,128)(2,1)S(1)} %pad_maximum_fusion), channel_id=1, source_target_pairs={{0,8},{1,9},{2,10},{3,11},{4,12},{5,13},{6,14},{7,15},{8,0},{9,1},... | collective-permute-start | bytes 202760 | tf_op jit(solution)/shard_map/ppermute | solution.py:472
  23.0 2.6 %collective-permute-start.6 = (bf16[8,4224]{1,0:T(8,128)(2,1)S(1)}, bf16[8,4224]{1,0:T(8,128)(2,1)S(1)}, u32[]{:S(2)}, u32[]{:S(2)}) collective-permute-start(bf16[8,4224]{1,0:T(8,128)(2,1)S(1)} %pad_maximum_fusion), channel_id=1, source_target_pairs={{0,16},{1,17},{2,18},{3,19},{4,20},{5,21},{6,22},{7,23},{8,24},{9,... | collective-permute-start | bytes 202760 | tf_op jit(solution)/shard_map/ppermute | solution.py:472
  26.3 2.7 %collective-permute-start.10 = (bf16[8,4224]{1,0:T(8,128)(2,1)S(1)}, bf16[8,4224]{1,0:T(8,128)(2,1)S(1)}, u32[]{:S(2)}, u32[]{:S(2)}) collective-permute-start(bf16[8,4224]{1,0:T(8,128)(2,1)S(1)} %get-tuple-element.66), channel_id=1, source_target_pairs={{0,6},{1,7},{2,4},{3,5},{4,2},{5,3},{6,0},{7,1},{8,14},{9,15},{10,... | collective-permute-start | bytes 202760 | tf_op jit(solution)/shard_map/ppermute | solution.py:472
  29.9 1.7 %collective-permute-done.7 = bf16[8,4224]{1,0:T(8,128)(2,1)S(1)} collective-permute-done((bf16[8,4224]{1,0:T(8,128)(2,1)S(1)}, bf16[8,4224]{1,0:T(8,128)(2,1)S(1)}, u32[]{:S(2)}, u32[]{:S(2)}) %collective-permute-start.7) | collective-permute-done | bytes 67616 | tf_op jit(solution)/shard_map/ppermute | solution.py:472
  31.6 2.5 %collective-permute-start.13 = (bf16[24,4224]{1,0:T(8,128)(2,1)S(1)}, bf16[24,4224]{1,0:T(8,128)(2,1)S(1)}, u32[]{:S(2)}, u32[]{:S(2)}) collective-permute-start(bf16[24,4224]{1,0:T(8,128)(2,1)S(1)} %get-tuple-element.57), channel_id=1, source_target_pairs={{0,6},{1,7},{2,4},{3,5},{4,2},{5,3},{6,0},{7,1},{8,14},{9,15},{10,... | collective-permute-start | bytes 608264 | tf_op jit(solution)/shard_map/ppermute | solution.py:472
  34.7 1.3 %collective-permute-done.8 = bf16[8,4224]{1,0:T(8,128)(2,1)S(1)} collective-permute-done((bf16[8,4224]{1,0:T(8,128)(2,1)S(1)}, bf16[8,4224]{1,0:T(8,128)(2,1)S(1)}, u32[]{:S(2)}, u32[]{:S(2)}) %collective-permute-start.8) | collective-permute-done | bytes 67616 | tf_op jit(solution)/shard_map/ppermute | solution.py:472
  36.2 3.7 %collective-permute-done.13 = bf16[24,4224]{1,0:T(8,128)(2,1)S(1)} collective-permute-done((bf16[24,4224]{1,0:T(8,128)(2,1)S(1)}, bf16[24,4224]{1,0:T(8,128)(2,1)S(1)}, u32[]{:S(2)}, u32[]{:S(2)}) %collective-permute-start.13) | collective-permute-done | bytes 202784 | tf_op jit(solution)/shard_map/ppermute | solution.py:472
  39.9 2.1 %collective-permute-done.12 = bf16[24,4224]{1,0:T(8,128)(2,1)S(1)} collective-permute-done((bf16[24,4224]{1,0:T(8,128)(2,1)S(1)}, bf16[24,4224]{1,0:T(8,128)(2,1)S(1)}, u32[]{:S(2)}, u32[]{:S(2)}) %collective-permute-start.12) | collective-permute-done | bytes 202784 | tf_op jit(solution)/shard_map/ppermute | solution.py:472
  43.9 6.5 %experts.1 = bf16[256,4096]{1,0:T(8,128)(2,1)S(1)} custom-call(bf16[256,4224]{1,0:T(8,128)(2,1)S(1)} %constant_dynamic-update-slice_fusion.10.x_ref, bf16[1,4096,768]{2,1,0:T(8,128)(2,1)S(1)} %get-tuple-element.30.gate, bf16[1,4096,768]{2,1,0:T(8,128)(2,1)S(1)} %bitcast.30, bf16[1,768,4096]{2,1,0:T(8,128)(2,1)} %down_hbm.1), custom_call_target="tpu_custom_call" | custom-call | tf_op jit(solution)/shard_map/experts/pallas_call | solution.py:442
  53.5 1.9 %collective-permute-start.27 = (bf16[24,4096]{1,0:T(8,128)(2,1)S(1)}, bf16[24,4096]{1,0:T(8,128)(2,1)S(1)}, u32[]{:S(2)}, u32[]{:S(2)}) collective-permute-start(bf16[24,4096]{1,0:T(8,128)(2,1)S(1)} %get-tuple-element.34), channel_id=1, source_target_pairs={{0,6},{1,7},{2,4},{3,5},{4,2},{5,3},{6,0},{7,1},{8,14},{9,15},{10,... | collective-permute-start | bytes 589832 | tf_op jit(solution)/shard_map/ppermute | solution.py:472
  57.2 1.9 %collective-permute-start.21 = (bf16[8,4096]{1,0:T(8,128)(2,1)S(1)}, bf16[8,4096]{1,0:T(8,128)(2,1)S(1)}, u32[]{:S(2)}, u32[]{:S(2)}) collective-permute-start(bf16[8,4096]{1,0:T(8,128)(2,1)S(1)} %get-tuple-element.40), channel_id=1, source_target_pairs={{0,6},{1,7},{2,4},{3,5},{4,2},{5,3},{6,0},{7,1},{8,14},{9,15},{10,... | collective-permute-start | bytes 196616 | tf_op jit(solution)/shard_map/ppermute | solution.py:472
  59.1 5.8 %collective-permute-done.23 = bf16[24,4096]{1,0:T(8,128)(2,1)S(1)} collective-permute-done((bf16[24,4096]{1,0:T(8,128)(2,1)S(1)}, bf16[24,4096]{1,0:T(8,128)(2,1)S(1)}, u32[]{:S(2)}, u32[]{:S(2)}) %collective-permute-start.23) | collective-permute-done | bytes 196640 | tf_op jit(solution)/shard_map/ppermute | solution.py:472
  66.4 3.3 %collective-permute-start.30 = (bf16[8,4096]{1,0:T(8,128)(2,1)S(1)}, bf16[8,4096]{1,0:T(8,128)(2,1)S(1)}, u32[]{:S(2)}, u32[]{:S(2)}) collective-permute-start(bf16[8,4096]{1,0:T(8,128)(2,1)S(1)} %get-tuple-element.43), channel_id=1, source_target_pairs={{0,24},{1,25},{2,26},{3,27},{4,28},{5,29},{6,30},{7,31},{8,16},{9,... | collective-permute-start | bytes 196616 | tf_op jit(solution)/shard_map/ppermute | solution.py:472
  71.0 2.4 %collective-permute-done.30 = bf16[8,4096]{1,0:T(8,128)(2,1)S(1)} collective-permute-done((bf16[8,4096]{1,0:T(8,128)(2,1)S(1)}, bf16[8,4096]{1,0:T(8,128)(2,1)S(1)}, u32[]{:S(2)}, u32[]{:S(2)}) %collective-permute-start.30) | collective-permute-done | bytes 65568 | tf_op jit(solution)/shard_map/ppermute | solution.py:472
  73.4 2.2 %collective-permute-done.29 = bf16[8,4096]{1,0:T(8,128)(2,1)S(1)} collective-permute-done((bf16[8,4096]{1,0:T(8,128)(2,1)S(1)}, bf16[8,4096]{1,0:T(8,128)(2,1)S(1)}, u32[]{:S(2)}, u32[]{:S(2)}) %collective-permute-start.29) | collective-permute-done | bytes 65568 | tf_op jit(solution)/shard_map/ppermute | solution.py:472
  (83 shorter events, 13.1 us)
Async XLA Ops:
  3.8 6.9 %collective-permute-start = (bf16[2,32,1152]{2,1,0:T(8,128)(2,1)S(1)}, bf16[2,32,1152]{2,1,0:T(8,128)(2,1)S(1)}, u32[]{:S(2)}, u32[]{:S(2)}) collective-permute-start(bf16[2,32,1152]{2,1,0:T(8,128)(2,1)S(1)} %get-tuple-element.18), channel_id=1, source_target_pairs={{0,2},{1,3},{2,0},{3,1},{4,6},{5,7},{6,4},{7,5},{8,10},{9,11},{10,... | collective-permute-start | bytes 442376 | tf_op jit(solution)/shard_map/ppermute | solution.py:472
  16.5 4.3 %collective-permute-start.4 = (bf16[8,4096]{1,0:T(8,128)(2,1)S(1)}, bf16[8,4096]{1,0:T(8,128)(2,1)S(1)}, u32[]{:S(2)}, u32[]{:S(2)}) collective-permute-start(bf16[8,4096]{1,0:T(8,128)(2,1)S(1)} %fusion.12), channel_id=1, source_target_pairs={{0,2},{1,3},{2,0},{3,1},{4,6},{5,7},{6,4},{7,5},{8,10},{9,11},{10,... | collective-permute-start | bytes 196616 | tf_op jit(solution)/shard_map/ppermute | solution.py:472
  21.1 5.0 %collective-permute-start.5 = (bf16[8,4224]{1,0:T(8,128)(2,1)S(1)}, bf16[8,4224]{1,0:T(8,128)(2,1)S(1)}, u32[]{:S(2)}, u32[]{:S(2)}) collective-permute-start(bf16[8,4224]{1,0:T(8,128)(2,1)S(1)} %pad_maximum_fusion), channel_id=1, source_target_pairs={{0,8},{1,9},{2,10},{3,11},{4,12},{5,13},{6,14},{7,15},{8,0},{9,1},... | collective-permute-start | bytes 202760 | tf_op jit(solution)/shard_map/ppermute | solution.py:472
  23.0 6.9 %collective-permute-start.6 = (bf16[8,4224]{1,0:T(8,128)(2,1)S(1)}, bf16[8,4224]{1,0:T(8,128)(2,1)S(1)}, u32[]{:S(2)}, u32[]{:S(2)}) collective-permute-start(bf16[8,4224]{1,0:T(8,128)(2,1)S(1)} %pad_maximum_fusion), channel_id=1, source_target_pairs={{0,16},{1,17},{2,18},{3,19},{4,20},{5,21},{6,22},{7,23},{8,24},{9,... | collective-permute-start | bytes 202760 | tf_op jit(solution)/shard_map/ppermute | solution.py:472
  25.5 6.1 %collective-permute-start.7 = (bf16[8,4224]{1,0:T(8,128)(2,1)S(1)}, bf16[8,4224]{1,0:T(8,128)(2,1)S(1)}, u32[]{:S(2)}, u32[]{:S(2)}) collective-permute-start(bf16[8,4224]{1,0:T(8,128)(2,1)S(1)} %pad_maximum_fusion), channel_id=1, source_target_pairs={{0,24},{1,25},{2,26},{3,27},{4,28},{5,29},{6,30},{7,31},{8,16},{9,... | collective-permute-start | bytes 202760 | tf_op jit(solution)/shard_map/ppermute | solution.py:472
  26.3 9.8 %collective-permute-start.10 = (bf16[8,4224]{1,0:T(8,128)(2,1)S(1)}, bf16[8,4224]{1,0:T(8,128)(2,1)S(1)}, u32[]{:S(2)}, u32[]{:S(2)}) collective-permute-start(bf16[8,4224]{1,0:T(8,128)(2,1)S(1)} %get-tuple-element.66), channel_id=1, source_target_pairs={{0,6},{1,7},{2,4},{3,5},{4,2},{5,3},{6,0},{7,1},{8,14},{9,15},{10,... | collective-permute-start | bytes 202760 | tf_op jit(solution)/shard_map/ppermute | solution.py:472
  29.0 7.0 %collective-permute-start.9 = (bf16[8,4224]{1,0:T(8,128)(2,1)S(1)}, bf16[8,4224]{1,0:T(8,128)(2,1)S(1)}, u32[]{:S(2)}, u32[]{:S(2)}) collective-permute-start(bf16[8,4224]{1,0:T(8,128)(2,1)S(1)} %get-tuple-element.66), channel_id=1, source_target_pairs={{0,4},{1,5},{2,6},{3,7},{4,0},{5,1},{6,2},{7,3},{8,12},{9,13},{10,... | collective-permute-start | bytes 202760 | tf_op jit(solution)/shard_map/ppermute | solution.py:472
  29.6 6.5 %collective-permute-start.8 = (bf16[8,4224]{1,0:T(8,128)(2,1)S(1)}, bf16[8,4224]{1,0:T(8,128)(2,1)S(1)}, u32[]{:S(2)}, u32[]{:S(2)}) collective-permute-start(bf16[8,4224]{1,0:T(8,128)(2,1)S(1)} %get-tuple-element.66), channel_id=1, source_target_pairs={{0,2},{1,3},{2,0},{3,1},{4,6},{5,7},{6,4},{7,5},{8,10},{9,11},{10,... | collective-permute-start | bytes 202760 | tf_op jit(solution)/shard_map/ppermute | solution.py:472
  31.6 8.3 %collective-permute-start.13 = (bf16[24,4224]{1,0:T(8,128)(2,1)S(1)}, bf16[24,4224]{1,0:T(8,128)(2,1)S(1)}, u32[]{:S(2)}, u32[]{:S(2)}) collective-permute-start(bf16[24,4224]{1,0:T(8,128)(2,1)S(1)} %get-tuple-element.57), channel_id=1, source_target_pairs={{0,6},{1,7},{2,4},{3,5},{4,2},{5,3},{6,0},{7,1},{8,14},{9,15},{10,... | collective-permute-start | bytes 608264 | tf_op jit(solution)/shard_map/ppermute | solution.py:472
  34.2 7.9 %collective-permute-start.12 = (bf16[24,4224]{1,0:T(8,128)(2,1)S(1)}, bf16[24,4224]{1,0:T(8,128)(2,1)S(1)}, u32[]{:S(2)}, u32[]{:S(2)}) collective-permute-start(bf16[24,4224]{1,0:T(8,128)(2,1)S(1)} %get-tuple-element.57), channel_id=1, source_target_pairs={{0,4},{1,5},{2,6},{3,7},{4,0},{5,1},{6,2},{7,3},{8,12},{9,13},{10,... | collective-permute-start | bytes 608264 | tf_op jit(solution)/shard_map/ppermute | solution.py:472
  36.0 6.3 %collective-permute-start.11 = (bf16[24,4224]{1,0:T(8,128)(2,1)S(1)}, bf16[24,4224]{1,0:T(8,128)(2,1)S(1)}, u32[]{:S(2)}, u32[]{:S(2)}) collective-permute-start(bf16[24,4224]{1,0:T(8,128)(2,1)S(1)} %get-tuple-element.57), channel_id=1, source_target_pairs={{0,2},{1,3},{2,0},{3,1},{4,6},{5,7},{6,4},{7,5},{8,10},{9,11},{10,... | collective-permute-start | bytes 608264 | tf_op jit(solution)/shard_map/ppermute | solution.py:472
  36.1 6.5 %collective-permute-start.14 = (bf16[56,4224]{1,0:T(8,128)(2,1)S(1)}, bf16[56,4224]{1,0:T(8,128)(2,1)S(1)}, u32[]{:S(2)}, u32[]{:S(2)}) collective-permute-start(bf16[56,4224]{1,0:T(8,128)(2,1)S(1)} %get-tuple-element.49), channel_id=1, source_target_pairs={{0,1},{1,0},{2,3},{3,2},{4,5},{5,4},{6,7},{7,6},{8,9},{9,8},{10,11... | collective-permute-start | bytes 1419272 | tf_op jit(solution)/shard_map/ppermute | solution.py:472
  39.9 3.9 %collective-permute-start.17 = (bf16[24,4224]{1,0:T(8,128)(2,1)S(1)}, bf16[24,4224]{1,0:T(8,128)(2,1)S(1)}, u32[]{:S(2)}, u32[]{:S(2)}) collective-permute-start(bf16[24,4224]{1,0:T(8,128)(2,1)S(1)} %collective-permute-done.13), channel_id=1, source_target_pairs={{0,1},{1,0},{2,3},{3,2},{4,5},{5,4},{6,7},{7,6},{8,9},{9,8},{10,11... | collective-permute-start | bytes 608264 | tf_op jit(solution)/shard_map/ppermute | solution.py:472
  42.0 1.8 %collective-permute-start.16 = (bf16[24,4224]{1,0:T(8,128)(2,1)S(1)}, bf16[24,4224]{1,0:T(8,128)(2,1)S(1)}, u32[]{:S(2)}, u32[]{:S(2)}) collective-permute-start(bf16[24,4224]{1,0:T(8,128)(2,1)S(1)} %collective-permute-done.12), channel_id=1, source_target_pairs={{0,1},{1,0},{2,3},{3,2},{4,5},{5,4},{6,7},{7,6},{8,9},{9,8},{10,11... | collective-permute-start | bytes 608264 | tf_op jit(solution)/shard_map/ppermute | solution.py:472
  51.3 4.9 %collective-permute-start.18 = (bf16[56,4096]{1,0:T(8,128)(2,1)S(1)}, bf16[56,4096]{1,0:T(8,128)(2,1)S(1)}, u32[]{:S(2)}, u32[]{:S(2)}) collective-permute-start(bf16[56,4096]{1,0:T(8,128)(2,1)S(1)} %slice.101), channel_id=1, source_target_pairs={{0,1},{1,0},{2,3},{3,2},{4,5},{5,4},{6,7},{7,6},{8,9},{9,8},{10,11... | collective-permute-start | bytes 1376264 | tf_op jit(solution)/shard_map/ppermute | solution.py:472
  52.7 12.3 %collective-permute-start.23 = (bf16[24,4096]{1,0:T(8,128)(2,1)S(1)}, bf16[24,4096]{1,0:T(8,128)(2,1)S(1)}, u32[]{:S(2)}, u32[]{:S(2)}) collective-permute-start(bf16[24,4096]{1,0:T(8,128)(2,1)S(1)} %get-tuple-element.33), channel_id=1, source_target_pairs={{0,2},{1,3},{2,0},{3,1},{4,6},{5,7},{6,4},{7,5},{8,10},{9,11},{10,... | collective-permute-start | bytes 589832 | tf_op jit(solution)/shard_map/ppermute | solution.py:472
  53.5 12.4 %collective-permute-start.27 = (bf16[24,4096]{1,0:T(8,128)(2,1)S(1)}, bf16[24,4096]{1,0:T(8,128)(2,1)S(1)}, u32[]{:S(2)}, u32[]{:S(2)}) collective-permute-start(bf16[24,4096]{1,0:T(8,128)(2,1)S(1)} %get-tuple-element.34), channel_id=1, source_target_pairs={{0,6},{1,7},{2,4},{3,5},{4,2},{5,3},{6,0},{7,1},{8,14},{9,15},{10,... | collective-permute-start | bytes 589832 | tf_op jit(solution)/shard_map/ppermute | solution.py:472
  55.4 10.5 %collective-permute-start.25 = (bf16[24,4096]{1,0:T(8,128)(2,1)S(1)}, bf16[24,4096]{1,0:T(8,128)(2,1)S(1)}, u32[]{:S(2)}, u32[]{:S(2)}) collective-permute-start(bf16[24,4096]{1,0:T(8,128)(2,1)S(1)} %get-tuple-element.35), channel_id=1, source_target_pairs={{0,4},{1,5},{2,6},{3,7},{4,0},{5,1},{6,2},{7,3},{8,12},{9,13},{10,... | collective-permute-start | bytes 589832 | tf_op jit(solution)/shard_map/ppermute | solution.py:472
  56.4 13.3 %collective-permute-start.19 = (bf16[8,4096]{1,0:T(8,128)(2,1)S(1)}, bf16[8,4096]{1,0:T(8,128)(2,1)S(1)}, u32[]{:S(2)}, u32[]{:S(2)}) collective-permute-start(bf16[8,4096]{1,0:T(8,128)(2,1)S(1)} %get-tuple-element.39), channel_id=1, source_target_pairs={{0,2},{1,3},{2,0},{3,1},{4,6},{5,7},{6,4},{7,5},{8,10},{9,11},{10,... | collective-permute-start | bytes 196616 | tf_op jit(solution)/shard_map/ppermute | solution.py:472
  57.2 13.0 %collective-permute-start.21 = (bf16[8,4096]{1,0:T(8,128)(2,1)S(1)}, bf16[8,4096]{1,0:T(8,128)(2,1)S(1)}, u32[]{:S(2)}, u32[]{:S(2)}) collective-permute-start(bf16[8,4096]{1,0:T(8,128)(2,1)S(1)} %get-tuple-element.40), channel_id=1, source_target_pairs={{0,6},{1,7},{2,4},{3,5},{4,2},{5,3},{6,0},{7,1},{8,14},{9,15},{10,... | collective-permute-start | bytes 196616 | tf_op jit(solution)/shard_map/ppermute | solution.py:472
  64.9 5.3 %collective-permute-start.20 = (bf16[8,4096]{1,0:T(8,128)(2,1)S(1)}, bf16[8,4096]{1,0:T(8,128)(2,1)S(1)}, u32[]{:S(2)}, u32[]{:S(2)}) collective-permute-start(bf16[8,4096]{1,0:T(8,128)(2,1)S(1)} %get-tuple-element.41), channel_id=1, source_target_pairs={{0,4},{1,5},{2,6},{3,7},{4,0},{5,1},{6,2},{7,3},{8,12},{9,13},{10,... | collective-permute-start | bytes 196616 | tf_op jit(solution)/shard_map/ppermute | solution.py:472
  66.0 4.9 %collective-permute-start.28 = (bf16[8,4096]{1,0:T(8,128)(2,1)S(1)}, bf16[8,4096]{1,0:T(8,128)(2,1)S(1)}, u32[]{:S(2)}, u32[]{:S(2)}) collective-permute-start(bf16[8,4096]{1,0:T(8,128)(2,1)S(1)} %get-tuple-element.42), channel_id=1, source_target_pairs={{0,8},{1,9},{2,10},{3,11},{4,12},{5,13},{6,14},{7,15},{8,0},{9,1},... | collective-permute-start | bytes 196616 | tf_op jit(solution)/shard_map/ppermute | solution.py:472
  66.4 7.0 %collective-permute-start.30 = (bf16[8,4096]{1,0:T(8,128)(2,1)S(1)}, bf16[8,4096]{1,0:T(8,128)(2,1)S(1)}, u32[]{:S(2)}, u32[]{:S(2)}) collective-permute-start(bf16[8,4096]{1,0:T(8,128)(2,1)S(1)} %get-tuple-element.43), channel_id=1, source_target_pairs={{0,24},{1,25},{2,26},{3,27},{4,28},{5,29},{6,30},{7,31},{8,16},{9,... | collective-permute-start | bytes 196616 | tf_op jit(solution)/shard_map/ppermute | solution.py:472
  69.7 5.9 %collective-permute-start.29 = (bf16[8,4096]{1,0:T(8,128)(2,1)S(1)}, bf16[8,4096]{1,0:T(8,128)(2,1)S(1)}, u32[]{:S(2)}, u32[]{:S(2)}) collective-permute-start(bf16[8,4096]{1,0:T(8,128)(2,1)S(1)} %get-tuple-element.44), channel_id=1, source_target_pairs={{0,16},{1,17},{2,18},{3,19},{4,20},{5,21},{6,22},{7,23},{8,24},{9,... | collective-permute-start | bytes 196616 | tf_op jit(solution)/shard_map/ppermute | solution.py:472
  (11 other events, 91.6 us)

commit v11 on v8

--- a/solution.py
+++ b/solution.py
@@ -12,7 +12,6 @@
 I32 = jnp.int32
 MIB = 1 << 20
 LANES = 128
-CAP = 3
 
 
 def rms_scale(values, gain):
@@ -39,8 +38,8 @@
 def attention_kernel(flip, *refs):
     sources, refs = refs[:8], refs[8:]
     if flip == 0:
-        ids_hbm, gates_hbm, w_hbm, _, out_ref, table_ref, w_ref = refs[:7]
-        refs = refs[7:]
+        ids_hbm, gates_hbm, w_hbm, _, out_ref, table_ref, *w_refs = refs[:8]
+        refs = refs[8:]
     else:
         out_ref, refs = refs[0], refs[1:]
     len_hbm, q_hbm, nk_hbm, nv_hbm, k_hbm, v_hbm, qg_hbm, kg_hbm = sources
@@ -65,15 +64,17 @@
     ]
     if flip == 0:
         ids_ref, gates_ref = refs[16:]
-        pairs = [(ids_hbm, ids_ref), (gates_hbm, gates_ref)] + pairs + [(w_hbm, w_ref)]
+        pairs = [(ids_hbm, ids_ref), (gates_hbm, gates_ref)] + pairs
+        size = w_refs[0].shape[0]
+        pairs += [(w_hbm.at[pl.ds(i * size, size)], ref) for i, ref in enumerate(w_refs)]
     copies = [pltpu.make_async_copy(src, dst, sem.at[i]) for i, (src, dst) in enumerate(pairs)]
     for c in copies:
         c.start()
     if flip == 0:
         for c in copies[:2]:
             c.wait()
-        ahead = copies[-1]
-        copies = copies[2:-1]
+        ahead = copies[-2:]
+        copies = copies[2:-2]
         gates = gates_ref[...]
         route = (gates / jnp.sum(gates, axis=1, keepdims=True)).astype(BF).astype(F32)
         expert = iota(table_ref.shape, 1)
@@ -152,7 +153,8 @@
             side = jnp.where(lane == 2 * heads_own + h, total - high, side)
         out_ref[slot, :, heads_own * hd :] = side.astype(BF)
     if flip == 0:
-        ahead.wait()
+        for c in ahead:
+            c.wait()
 
 
 def attention(
@@ -181,7 +183,7 @@
         pltpu.VMEM((rows * group, LANES), F32),
         pltpu.VMEM((blocks, 8 * group, 8 * (cache + 2)), F32),
         pltpu.VMEM((blocks, 8 * group, 8 * (cache + 2)), BF),
-        pltpu.SemaphoreType.DMA((11,)),
+        pltpu.SemaphoreType.DMA((12,)),
     ]
     specs = [pl.BlockSpec(memory_space=pltpu.HBM)] * len(args)
     size = 2 * rows * group * hd * 8
@@ -190,7 +192,7 @@
         args += [in_hbm(a) for a in (expert_ids, gate_weights, later)] + [earlier]
         specs += [pl.BlockSpec(memory_space=pltpu.HBM)] * 3 + [pl.BlockSpec(memory_space=pl.ANY)]
         outs.append(jax.ShapeDtypeStruct((expert_ids.shape[0], lanes), BF))
-        outs.append(pltpu.VMEM(later.shape, later.dtype))
+        outs += [pltpu.VMEM((later.shape[0] // 2, later.shape[1]), later.dtype)] * 2
         scratch += [pltpu.VMEM(expert_ids.shape, I32), pltpu.VMEM(gate_weights.shape, F32)]
         size = size + 2 * later.size
     return pl.pallas_call(
@@ -205,13 +207,15 @@
     )(*args)
 
 
-def projection_kernel(parts, *refs):
+def projection_kernel(parts, cuts, *refs):
     got = refs[:parts]
-    w_ref, ahead_hbm, out_ref, ahead_ref, attn, sem = refs[parts:]
+    w_refs, refs = refs[parts : parts + cuts], refs[parts + cuts :]
+    ahead_hbm, out_ref, ahead_ref, attn, sem = refs
     ahead = pltpu.make_async_copy(ahead_hbm, ahead_ref, sem)
     ahead.start()
     tensor_pos = lax.axis_index("tensor")
-    depth, width = w_ref.shape
+    width = w_refs[0].shape[1]
+    depth = attn.shape[1]
     share = out_ref.shape[2]
     hd = LANES
     heads_own = depth // hd
@@ -230,42 +234,46 @@
         cols = slice(h * hd, (h + 1) * hd)
         terms = [g[:, cols].astype(F32) * f[:, h : h + 1] for g, f in zip(got, factors)]
         attn[:, cols] = functools.reduce(jnp.add, terms).astype(BF)
-    for i in range(width // size):
-        cols = slice(i * size, (i + 1) * size)
-        result = matmul(attn[...], w_ref[:, cols])
+    part = depth // cuts
+    for start in range(0, width, size):
+        cols = slice(start, start + size)
+        result = functools.reduce(
+            jnp.add,
+            [
+                matmul(attn[:, k * part : (k + 1) * part], w_ref[:, cols])
+                for k, w_ref in enumerate(w_refs)
+            ],
+        )
         for t in range(parts):
             slot = tensor_pos ^ t
-            out_ref[slot & 1, slot >> 1, :, cols] = result[t * share : (t + 1) * share].astype(BF)
+            block = result[t * share : (t + 1) * share].astype(BF)
+            out_ref[slot & 1, slot >> 1, :, cols] = block
     ahead.wait()
 
 
-def projection(got, out_proj, share, later):
+def projection(got, weights, share, later):
     parts = len(got)
     rows = got[0].shape[0]
-    depth, width = out_proj.shape
+    depth = sum(w.shape[0] for w in weights)
+    width = weights[0].shape[1]
     vmem = pl.BlockSpec(memory_space=pltpu.VMEM)
     return pl.pallas_call(
-        functools.partial(projection_kernel, parts),
+        functools.partial(projection_kernel, parts, len(weights)),
         out_shape=(
             jax.ShapeDtypeStruct((2, parts // 2, share, width), BF),
             pltpu.VMEM(later.shape, later.dtype),
         ),
-        in_specs=[vmem] * (parts + 1) + [pl.BlockSpec(memory_space=pltpu.HBM)],
+        in_specs=[vmem] * (parts + len(weights)) + [pl.BlockSpec(memory_space=pltpu.HBM)],
         out_specs=(vmem, vmem),
         scratch_shapes=[pltpu.VMEM((rows, depth), BF), pltpu.SemaphoreType.DMA],
         compiler_params=pltpu.CompilerParams(vmem_limit_bytes=12 * MIB),
         name="projection",
-    )(*got, out_proj, in_hbm(later))
-
-
-def expert_kernel(slots, sizes, *refs):
-    x_ref, gate, up, down_hbm = refs[:4]
-    outs = refs[4 : 4 + len(sizes)]
-    down, xc, act, res, sem = refs[4 + len(sizes) :]
+    )(*got, *weights, in_hbm(later))
+
+
+def expert_kernel(x_ref, gate, up, down_hbm, out_ref, down, act, sem):
     own = lax.axis_index("dp") * lax.axis_size("tensor") + lax.axis_index("tensor")
-    rows = x_ref.shape[0]
     _, width, hidden = gate.shape
-    padded = res.shape[0]
     fsize = 384
     dsize = 1024
     chunks = width // dsize
@@ -276,56 +284,32 @@
 
     for i in range(chunks):
         down_copy(i).start()
-    table = x_ref[:, width:]
-    pick = (iota((16, table.shape[1]), 1) == own).astype(F32).astype(BF)
-    named = matmul_t(pick, table) != 0.0
-    before = (iota((rows, rows), 0) < iota((rows, rows), 1)).astype(F32).astype(BF)
-    place = matmul(named.astype(F32).astype(BF), before)
-    place = jnp.where(named, place, -1.0)[:1]
-    take = (iota((slots, rows), 0).astype(F32) == place).astype(F32).astype(BF)
-    for i in range(chunks):
-        cols = slice(i * dsize, (i + 1) * dsize)
-        xc[:, cols] = matmul(take, x_ref[:, cols]).astype(BF)
-
-    lane = iota(table.shape, 1)
-    weight = jnp.sum(jnp.where(lane == own, table.astype(F32), 0.0), axis=1, keepdims=True)
-    named = jnp.broadcast_to((weight != 0.0).astype(F32), (rows, LANES)).astype(BF)
-    after = (iota((rows, rows), 1) < iota((rows, rows), 0)).astype(F32).astype(BF)
-    place = matmul(after, named)[:, :1]
-    spread = jnp.where(iota((rows, padded), 1).astype(F32) == place, weight, 0.0).astype(BF)
-    if padded > slots:
-        res[slots:, :] = jnp.zeros((padded - slots, dsize), BF)
-
     for i in range(hidden // fsize):
         cols = slice(i * fsize, (i + 1) * fsize)
-        g = matmul(xc[...], gate[0, :, cols])
-        u = matmul(xc[...], up[0, :, cols])
+        g = matmul(x_ref[:, :width], gate[0, :, cols])
+        u = matmul(x_ref[:, :width], up[0, :, cols])
         act[:, cols] = (g / (1.0 + jnp.exp(-g)) * u).astype(BF)
+    table = x_ref[:, width:].astype(F32)
+    named = iota(table.shape, 1) == own
+    weight = jnp.sum(jnp.where(named, table, 0.0), axis=1, keepdims=True)
     for i in range(chunks):
         down_copy(i).wait()
         cols = slice(i * dsize, (i + 1) * dsize)
-        res[:slots, :] = matmul(act[...], down[:, cols]).astype(BF)
-        result, start = matmul(spread, res[...]), 0
-        for size, out in zip(sizes, outs):
-            out[:, cols] = result[start : start + size].astype(BF)
-            start += size
-
-
-def experts(x, expert_gate, expert_up, expert_down, share, sizes):
+        out_ref[:, cols] = (matmul(act[...], down[:, cols]) * weight).astype(BF)
+
+
+def experts(x, expert_gate, expert_up, expert_down):
     rows = x.shape[0]
     _, width, hidden = expert_gate.shape
-    slots = rows // share * CAP
     vmem = pl.BlockSpec(memory_space=pltpu.VMEM)
     return pl.pallas_call(
-        functools.partial(expert_kernel, slots, sizes),
-        out_shape=tuple(jax.ShapeDtypeStruct((size, width), BF) for size in sizes),
+        expert_kernel,
+        out_shape=jax.ShapeDtypeStruct((rows, width), BF),
         in_specs=[vmem] * 3 + [pl.BlockSpec(memory_space=pltpu.HBM)],
-        out_specs=(vmem,) * len(sizes),
+        out_specs=vmem,
         scratch_shapes=[
             pltpu.VMEM((hidden, width), BF),
-            pltpu.VMEM((slots, width), BF),
-            pltpu.VMEM((slots, hidden), BF),
-            pltpu.VMEM((-(-slots // LANES) * LANES, 1024), BF),
+            pltpu.VMEM((rows, hidden), BF),
             pltpu.SemaphoreType.DMA((width // 1024,)),
         ],
         compiler_params=pltpu.CompilerParams(vmem_limit_bytes=(16 + rows // 32) * MIB),
@@ -397,8 +381,8 @@
             if far:
                 pair = plan.swap(pair, far)
             got += [pair[0], plan.swap(pair[1], plan.core)]
-    _, table, out_proj = results
-    partial, expert_gate = projection(got, out_proj, share, expert_gate)
+    _, table, *weights = results
+    partial, expert_gate = projection(got, weights, share, expert_gate)
     pair = total_of([partial[0], plan.swap(partial[1], plan.core)])
     projected = total_of([pair[0]] + plan.swaps(list(pair[1:]), plan.y))
     hidden = residual_in.astype(F32) + projected
@@ -411,13 +395,19 @@
     pieces = [jnp.concatenate([mine] + others + near)] + far
     x = jnp.concatenate(pieces + [plan.swap(piece, plan.core) for piece in pieces])
 
-    sizes = [piece.shape[0] for piece in pieces] * 2
-    results = experts(x, expert_gate, expert_up, expert_down, share, sizes)
-
-    half = len(pieces)
+    result = experts(x, expert_gate, expert_up, expert_down)
+
+    sizes = [piece.shape[0] for piece in pieces]
+    starts = [sum(sizes[:i]) for i in range(len(sizes) + 1)]
+    every = starts[-1]
     sums = [
-        total_of([results[i], plan.swap(results[half + i], plan.core)])
-        for i in reversed(range(half))
+        total_of(
+            [
+                result[starts[i] : starts[i + 1]],
+                plan.swap(result[every + starts[i] : every + starts[i + 1]], plan.core),
+            ]
+        )
+        for i in reversed(range(len(sizes)))
     ][::-1]
     blocks = sums[0].reshape(-1, share, width)
     far = plan.swaps(sums[1:], plan.plane)

time: 76 us -> 77.7 us (1.022)
  Pallas kernels: 16.2 us -> 17.4 us
  starting transfers between devices: 29.1 us -> 29.9 us
    pallas_call x2, Pallas kernels: 9.94 us -> 11.1 us  [the longest x1 8.17 us: experts(): pl.pallas_call(expert_kernel, out_shape=jax.ShapeDtypeStruct((rows, width...]
    ppermute x31, starting transfers between devices: 29.1 us -> 29.9 us  [swap(): lax.ppermute(value, ('dp', 'tensor'), [(i, i ^ flip) for i in range(self....]
where the time goes in v11:
time: 77.7 us; the launch traced here: 77.5 us
  starting transfers between devices  29.9 us (38%)
  waiting for transfers between devices  27.9 us (36%)
  Pallas kernels  17.4 us (22%)
  other arithmetic  1.55 us (2%)
    ppermute x31, starting transfers between devices, swap(): lax.ppermute(value, ('dp', 'tensor'), [(i, i ^ flip) for i in range(self....  29.9 us
    ppermute x31, waiting for transfers between devices, swap(): lax.ppermute(value, ('dp', 'tensor'), [(i, i ^ flip) for i in range(self....  27.9 us
    pallas_call x1, Pallas kernels, experts(): pl.pallas_call(expert_kernel, out_shape=jax.ShapeDtypeStruct((rows, width...  8.17 us
    pallas_call x2, Pallas kernels, attention(): pl.pallas_call(functools.partial(attention_kernel, flip), out_shape=tuple...  6.31 us
    pallas_call x1, Pallas kernels, projection(): pl.pallas_call(functools.partial(projection_kernel, parts, len(weights)),...  2.94 us
  transfers between devices with their start and end apart: 31, of which 18 were waited for; matrix products, arithmetic and copies ran while one was open for 1% of the time, Pallas kernels for 5%

profile of v11, /device:TPU:0, one launch (start us, length us, event | category | flops | bytes accessed | tf_op | source)
XLA Modules:
  0.0 77.5 jit_solution(1404028644885135360)
XLA Ops:
  0.0 2.4 %attention.2.refs_11_ = bf16[2,32,1152]{2,1,0:T(8,128)(2,1)S(1)} custom-call(s32[32]{0:T(128)} %refs_0_.3, bf16[32,32,128]{2,1,0:T(8,128)(2,1)} %refs_1_.3, bf16[32,2,128]{2,1,0:T(2,128)(2,1)} %refs_2_.3, bf16[32,2,128]{2,1,0:T(2,128)(2,1)} %refs_3_.3, bf16[32,2,32,128]{3,2,1,0:T(8,128)(2,1)} %refs_4_.3, bf16[32,2,32,128]{3,2,1,0:T(8,128)(2,1)} %refs_5_.3, ...), custom_call_target="tpu_custom_call" | custom-call | flops 1048576 | bytes 1048576 | tf_op jit(solution)/shard_map/attention/pallas_call | solution.py:198
  2.4 3.0 %collective-permute-start = (bf16[2,32,1152]{2,1,0:T(8,128)(2,1)S(1)}, bf16[2,32,1152]{2,1,0:T(8,128)(2,1)S(1)}, u32[]{:S(2)}, u32[]{:S(2)}) collective-permute-start(bf16[2,32,1152]{2,1,0:T(8,128)(2,1)S(1)} %attention.2.refs_11_), channel_id=1, source_target_pairs={{0,2},{1,3},{2,0},{3,1},{4,6},{5,7},{6,4},{7,5},{8,10},{9,11},{10,... | collective-permute-start | bytes 442376 | tf_op jit(solution)/shard_map/ppermute | solution.py:333
  5.5 3.9 %attention.3 = (bf16[2,32,1152]{2,1,0:T(8,128)(2,1)S(1)}, bf16[8,128]{1,0:T(8,128)(2,1)S(1)}, bf16[512,4096]{1,0:T(8,128)(2,1)S(1)}, bf16[512,4096]{1,0:T(8,128)(2,1)S(1)}) custom-call(s32[32]{0:T(128)} %refs_0_.3, bf16[32,32,128]{2,1,0:T(8,128)(2,1)} %refs_1_.3, bf16[32,2,128]{2,1,0:T(2,128)(2,1)} %refs_2_.3, bf16[32,2,128]{2,1,0:T(2,128)(2,1)} %refs_3_.3, ...), custom_call_target="tpu_custom_call" | custom-call | flops 9437184 | bytes 9437184 | tf_op jit(solution)/shard_map/attention/pallas_call | solution.py:198
  11.0 2.9 %projection.1 = (bf16[2,2,8,4096]{3,2,1,0:T(8,128)(2,1)S(1)}, bf16[1,4096,768]{2,1,0:T(8,128)(2,1)S(1)}) custom-call(bf16[32,1152]{1,0:T(8,128)(2,1)S(1)} %get-tuple-element.34.refs_0_, bf16[32,1152]{1,0:T(8,128)(2,1)S(1)} %collective-permute-done.1.refs_1_, bf16[32,1152]{1,0:T(8,128)(2,1)S(1)} %get-tuple-element.32.refs_2_, ...), custom_call_target="tpu_custom_call" | custom-call | tf_op jit(solution)/shard_map/projection/pallas_call | solution.py:260
  15.4 1.5 %collective-permute-start.4 = (bf16[8,4096]{1,0:T(8,128)(2,1)S(1)}, bf16[8,4096]{1,0:T(8,128)(2,1)S(1)}, u32[]{:S(2)}, u32[]{:S(2)}) collective-permute-start(bf16[8,4096]{1,0:T(8,128)(2,1)S(1)} %fusion.12), channel_id=1, source_target_pairs={{0,2},{1,3},{2,0},{3,1},{4,6},{5,7},{6,4},{7,5},{8,10},{9,11},{10,... | collective-permute-start | bytes 196616 | tf_op jit(solution)/shard_map/ppermute | solution.py:333
  16.9 2.9 %collective-permute-done.4 = bf16[8,4096]{1,0:T(8,128)(2,1)S(1)} collective-permute-done((bf16[8,4096]{1,0:T(8,128)(2,1)S(1)}, bf16[8,4096]{1,0:T(8,128)(2,1)S(1)}, u32[]{:S(2)}, u32[]{:S(2)}) %collective-permute-start.4) | collective-permute-done | bytes 65568 | tf_op jit(solution)/shard_map/ppermute | solution.py:333
  20.1 1.6 %collective-permute-start.5 = (bf16[8,4224]{1,0:T(8,128)(2,1)S(1)}, bf16[8,4224]{1,0:T(8,128)(2,1)S(1)}, u32[]{:S(2)}, u32[]{:S(2)}) collective-permute-start(bf16[8,4224]{1,0:T(8,128)(2,1)S(1)} %pad_maximum_fusion), channel_id=1, source_target_pairs={{0,8},{1,9},{2,10},{3,11},{4,12},{5,13},{6,14},{7,15},{8,0},{9,1},... | collective-permute-start | bytes 202760 | tf_op jit(solution)/shard_map/ppermute | solution.py:333
  21.7 2.6 %collective-permute-start.6 = (bf16[8,4224]{1,0:T(8,128)(2,1)S(1)}, bf16[8,4224]{1,0:T(8,128)(2,1)S(1)}, u32[]{:S(2)}, u32[]{:S(2)}) collective-permute-start(bf16[8,4224]{1,0:T(8,128)(2,1)S(1)} %pad_maximum_fusion), channel_id=1, source_target_pairs={{0,16},{1,17},{2,18},{3,19},{4,20},{5,21},{6,22},{7,23},{8,24},{9,... | collective-permute-start | bytes 202760 | tf_op jit(solution)/shard_map/ppermute | solution.py:333
  24.8 2.9 %collective-permute-start.10 = (bf16[8,4224]{1,0:T(8,128)(2,1)S(1)}, bf16[8,4224]{1,0:T(8,128)(2,1)S(1)}, u32[]{:S(2)}, u32[]{:S(2)}) collective-permute-start(bf16[8,4224]{1,0:T(8,128)(2,1)S(1)} %get-tuple-element.52), channel_id=1, source_target_pairs={{0,6},{1,7},{2,4},{3,5},{4,2},{5,3},{6,0},{7,1},{8,14},{9,15},{10,... | collective-permute-start | bytes 202760 | tf_op jit(solution)/shard_map/ppermute | solution.py:333
  28.9 1.6 %collective-permute-done.7 = bf16[8,4224]{1,0:T(8,128)(2,1)S(1)} collective-permute-done((bf16[8,4224]{1,0:T(8,128)(2,1)S(1)}, bf16[8,4224]{1,0:T(8,128)(2,1)S(1)}, u32[]{:S(2)}, u32[]{:S(2)}) %collective-permute-start.7) | collective-permute-done | bytes 67616 | tf_op jit(solution)/shard_map/ppermute | solution.py:333
  30.4 2.4 %collective-permute-start.13 = (bf16[24,4224]{1,0:T(8,128)(2,1)S(1)}, bf16[24,4224]{1,0:T(8,128)(2,1)S(1)}, u32[]{:S(2)}, u32[]{:S(2)}) collective-permute-start(bf16[24,4224]{1,0:T(8,128)(2,1)S(1)} %get-tuple-element.43), channel_id=1, source_target_pairs={{0,6},{1,7},{2,4},{3,5},{4,2},{5,3},{6,0},{7,1},{8,14},{9,15},{10,... | collective-permute-start | bytes 608264 | tf_op jit(solution)/shard_map/ppermute | solution.py:333
  33.3 2.1 %collective-permute-done.8 = bf16[8,4224]{1,0:T(8,128)(2,1)S(1)} collective-permute-done((bf16[8,4224]{1,0:T(8,128)(2,1)S(1)}, bf16[8,4224]{1,0:T(8,128)(2,1)S(1)}, u32[]{:S(2)}, u32[]{:S(2)}) %collective-permute-start.8) | collective-permute-done | bytes 67616 | tf_op jit(solution)/shard_map/ppermute | solution.py:333
  35.6 2.9 %collective-permute-done.13 = bf16[24,4224]{1,0:T(8,128)(2,1)S(1)} collective-permute-done((bf16[24,4224]{1,0:T(8,128)(2,1)S(1)}, bf16[24,4224]{1,0:T(8,128)(2,1)S(1)}, u32[]{:S(2)}, u32[]{:S(2)}) %collective-permute-start.13) | collective-permute-done | bytes 202784 | tf_op jit(solution)/shard_map/ppermute | solution.py:333
  38.5 2.2 %collective-permute-done.12 = bf16[24,4224]{1,0:T(8,128)(2,1)S(1)} collective-permute-done((bf16[24,4224]{1,0:T(8,128)(2,1)S(1)}, bf16[24,4224]{1,0:T(8,128)(2,1)S(1)}, u32[]{:S(2)}, u32[]{:S(2)}) %collective-permute-start.12) | collective-permute-done | bytes 202784 | tf_op jit(solution)/shard_map/ppermute | solution.py:333
  41.3 1.3 %collective-permute-done.15 = bf16[24,4224]{1,0:T(8,128)(2,1)S(1)} collective-permute-done((bf16[24,4224]{1,0:T(8,128)(2,1)S(1)}, bf16[24,4224]{1,0:T(8,128)(2,1)S(1)}, u32[]{:S(2)}, u32[]{:S(2)}) %collective-permute-start.15) | collective-permute-done | bytes 202784 | tf_op jit(solution)/shard_map/ppermute | solution.py:333
  42.8 8.2 %experts.1 = bf16[256,4096]{1,0:T(8,128)(2,1)S(1)} custom-call(bf16[256,4224]{1,0:T(8,128)(2,1)S(1)} %constant_dynamic-update-slice_fusion.10.x_ref, bf16[1,4096,768]{2,1,0:T(8,128)(2,1)S(1)} %get-tuple-element.16.gate, bf16[1,4096,768]{2,1,0:T(8,128)(2,1)S(1)} %bitcast.30, bf16[1,768,4096]{2,1,0:T(8,128)(2,1)} %down_hbm.1), custom_call_target="tpu_custom_call" | custom-call | tf_op jit(solution)/shard_map/experts/pallas_call | solution.py:305
  54.1 2.1 %collective-permute-start.27 = (bf16[24,4096]{1,0:T(8,128)(2,1)S(1)}, bf16[24,4096]{1,0:T(8,128)(2,1)S(1)}, u32[]{:S(2)}, u32[]{:S(2)}) collective-permute-start(bf16[24,4096]{1,0:T(8,128)(2,1)S(1)} %get-tuple-element.20), channel_id=1, source_target_pairs={{0,6},{1,7},{2,4},{3,5},{4,2},{5,3},{6,0},{7,1},{8,14},{9,15},{10,... | collective-permute-start | bytes 589832 | tf_op jit(solution)/shard_map/ppermute | solution.py:333
  57.8 2.1 %collective-permute-start.21 = (bf16[8,4096]{1,0:T(8,128)(2,1)S(1)}, bf16[8,4096]{1,0:T(8,128)(2,1)S(1)}, u32[]{:S(2)}, u32[]{:S(2)}) collective-permute-start(bf16[8,4096]{1,0:T(8,128)(2,1)S(1)} %get-tuple-element.26), channel_id=1, source_target_pairs={{0,6},{1,7},{2,4},{3,5},{4,2},{5,3},{6,0},{7,1},{8,14},{9,15},{10,... | collective-permute-start | bytes 196616 | tf_op jit(solution)/shard_map/ppermute | solution.py:333
  59.9 5.4 %collective-permute-done.23 = bf16[24,4096]{1,0:T(8,128)(2,1)S(1)} collective-permute-done((bf16[24,4096]{1,0:T(8,128)(2,1)S(1)}, bf16[24,4096]{1,0:T(8,128)(2,1)S(1)}, u32[]{:S(2)}, u32[]{:S(2)}) %collective-permute-start.23) | collective-permute-done | bytes 196640 | tf_op jit(solution)/shard_map/ppermute | solution.py:333
  65.4 2.0 %collective-permute-start.20 = (bf16[8,4096]{1,0:T(8,128)(2,1)S(1)}, bf16[8,4096]{1,0:T(8,128)(2,1)S(1)}, u32[]{:S(2)}, u32[]{:S(2)}) collective-permute-start(bf16[8,4096]{1,0:T(8,128)(2,1)S(1)} %get-tuple-element.27), channel_id=1, source_target_pairs={{0,4},{1,5},{2,6},{3,7},{4,0},{5,1},{6,2},{7,3},{8,12},{9,13},{10,... | collective-permute-start | bytes 196616 | tf_op jit(solution)/shard_map/ppermute | solution.py:333
  67.5 1.9 %collective-permute-start.28 = (bf16[8,4096]{1,0:T(8,128)(2,1)S(1)}, bf16[8,4096]{1,0:T(8,128)(2,1)S(1)}, u32[]{:S(2)}, u32[]{:S(2)}) collective-permute-start(bf16[8,4096]{1,0:T(8,128)(2,1)S(1)} %get-tuple-element.28), channel_id=1, source_target_pairs={{0,8},{1,9},{2,10},{3,11},{4,12},{5,13},{6,14},{7,15},{8,0},{9,1},... | collective-permute-start | bytes 196616 | tf_op jit(solution)/shard_map/ppermute | solution.py:333
  69.3 1.4 %collective-permute-start.30 = (bf16[8,4096]{1,0:T(8,128)(2,1)S(1)}, bf16[8,4096]{1,0:T(8,128)(2,1)S(1)}, u32[]{:S(2)}, u32[]{:S(2)}) collective-permute-start(bf16[8,4096]{1,0:T(8,128)(2,1)S(1)} %get-tuple-element.29), channel_id=1, source_target_pairs={{0,24},{1,25},{2,26},{3,27},{4,28},{5,29},{6,30},{7,31},{8,16},{9,... | collective-permute-start | bytes 196616 | tf_op jit(solution)/shard_map/ppermute | solution.py:333
  71.8 3.6 %collective-permute-done.30 = bf16[8,4096]{1,0:T(8,128)(2,1)S(1)} collective-permute-done((bf16[8,4096]{1,0:T(8,128)(2,1)S(1)}, bf16[8,4096]{1,0:T(8,128)(2,1)S(1)}, u32[]{:S(2)}, u32[]{:S(2)}) %collective-permute-start.30) | collective-permute-done | bytes 65568 | tf_op jit(solution)/shard_map/ppermute | solution.py:333
  75.4 1.4 %collective-permute-done.29 = bf16[8,4096]{1,0:T(8,128)(2,1)S(1)} collective-permute-done((bf16[8,4096]{1,0:T(8,128)(2,1)S(1)}, bf16[8,4096]{1,0:T(8,128)(2,1)S(1)}, u32[]{:S(2)}, u32[]{:S(2)}) %collective-permute-start.29) | collective-permute-done | bytes 65568 | tf_op jit(solution)/shard_map/ppermute | solution.py:333
  (83 shorter events, 12.9 us)
Async XLA Ops:
  2.4 7.0 %collective-permute-start = (bf16[2,32,1152]{2,1,0:T(8,128)(2,1)S(1)}, bf16[2,32,1152]{2,1,0:T(8,128)(2,1)S(1)}, u32[]{:S(2)}, u32[]{:S(2)}) collective-permute-start(bf16[2,32,1152]{2,1,0:T(8,128)(2,1)S(1)} %attention.2.refs_11_), channel_id=1, source_target_pairs={{0,2},{1,3},{2,0},{3,1},{4,6},{5,7},{6,4},{7,5},{8,10},{9,11},{10,... | collective-permute-start | bytes 442376 | tf_op jit(solution)/shard_map/ppermute | solution.py:333
  15.4 4.4 %collective-permute-start.4 = (bf16[8,4096]{1,0:T(8,128)(2,1)S(1)}, bf16[8,4096]{1,0:T(8,128)(2,1)S(1)}, u32[]{:S(2)}, u32[]{:S(2)}) collective-permute-start(bf16[8,4096]{1,0:T(8,128)(2,1)S(1)} %fusion.12), channel_id=1, source_target_pairs={{0,2},{1,3},{2,0},{3,1},{4,6},{5,7},{6,4},{7,5},{8,10},{9,11},{10,... | collective-permute-start | bytes 196616 | tf_op jit(solution)/shard_map/ppermute | solution.py:333
  20.1 4.5 %collective-permute-start.5 = (bf16[8,4224]{1,0:T(8,128)(2,1)S(1)}, bf16[8,4224]{1,0:T(8,128)(2,1)S(1)}, u32[]{:S(2)}, u32[]{:S(2)}) collective-permute-start(bf16[8,4224]{1,0:T(8,128)(2,1)S(1)} %pad_maximum_fusion), channel_id=1, source_target_pairs={{0,8},{1,9},{2,10},{3,11},{4,12},{5,13},{6,14},{7,15},{8,0},{9,1},... | collective-permute-start | bytes 202760 | tf_op jit(solution)/shard_map/ppermute | solution.py:333
  21.7 7.1 %collective-permute-start.6 = (bf16[8,4224]{1,0:T(8,128)(2,1)S(1)}, bf16[8,4224]{1,0:T(8,128)(2,1)S(1)}, u32[]{:S(2)}, u32[]{:S(2)}) collective-permute-start(bf16[8,4224]{1,0:T(8,128)(2,1)S(1)} %pad_maximum_fusion), channel_id=1, source_target_pairs={{0,16},{1,17},{2,18},{3,19},{4,20},{5,21},{6,22},{7,23},{8,24},{9,... | collective-permute-start | bytes 202760 | tf_op jit(solution)/shard_map/ppermute | solution.py:333
  24.3 6.1 %collective-permute-start.7 = (bf16[8,4224]{1,0:T(8,128)(2,1)S(1)}, bf16[8,4224]{1,0:T(8,128)(2,1)S(1)}, u32[]{:S(2)}, u32[]{:S(2)}) collective-permute-start(bf16[8,4224]{1,0:T(8,128)(2,1)S(1)} %pad_maximum_fusion), channel_id=1, source_target_pairs={{0,24},{1,25},{2,26},{3,27},{4,28},{5,29},{6,30},{7,31},{8,16},{9,... | collective-permute-start | bytes 202760 | tf_op jit(solution)/shard_map/ppermute | solution.py:333
  24.8 10.7 %collective-permute-start.10 = (bf16[8,4224]{1,0:T(8,128)(2,1)S(1)}, bf16[8,4224]{1,0:T(8,128)(2,1)S(1)}, u32[]{:S(2)}, u32[]{:S(2)}) collective-permute-start(bf16[8,4224]{1,0:T(8,128)(2,1)S(1)} %get-tuple-element.52), channel_id=1, source_target_pairs={{0,6},{1,7},{2,4},{3,5},{4,2},{5,3},{6,0},{7,1},{8,14},{9,15},{10,... | collective-permute-start | bytes 202760 | tf_op jit(solution)/shard_map/ppermute | solution.py:333
  27.7 7.8 %collective-permute-start.9 = (bf16[8,4224]{1,0:T(8,128)(2,1)S(1)}, bf16[8,4224]{1,0:T(8,128)(2,1)S(1)}, u32[]{:S(2)}, u32[]{:S(2)}) collective-permute-start(bf16[8,4224]{1,0:T(8,128)(2,1)S(1)} %get-tuple-element.52), channel_id=1, source_target_pairs={{0,4},{1,5},{2,6},{3,7},{4,0},{5,1},{6,2},{7,3},{8,12},{9,13},{10,... | collective-permute-start | bytes 202760 | tf_op jit(solution)/shard_map/ppermute | solution.py:333
  28.2 7.2 %collective-permute-start.8 = (bf16[8,4224]{1,0:T(8,128)(2,1)S(1)}, bf16[8,4224]{1,0:T(8,128)(2,1)S(1)}, u32[]{:S(2)}, u32[]{:S(2)}) collective-permute-start(bf16[8,4224]{1,0:T(8,128)(2,1)S(1)} %get-tuple-element.52), channel_id=1, source_target_pairs={{0,2},{1,3},{2,0},{3,1},{4,6},{5,7},{6,4},{7,5},{8,10},{9,11},{10,... | collective-permute-start | bytes 202760 | tf_op jit(solution)/shard_map/ppermute | solution.py:333
  30.4 8.1 %collective-permute-start.13 = (bf16[24,4224]{1,0:T(8,128)(2,1)S(1)}, bf16[24,4224]{1,0:T(8,128)(2,1)S(1)}, u32[]{:S(2)}, u32[]{:S(2)}) collective-permute-start(bf16[24,4224]{1,0:T(8,128)(2,1)S(1)} %get-tuple-element.43), channel_id=1, source_target_pairs={{0,6},{1,7},{2,4},{3,5},{4,2},{5,3},{6,0},{7,1},{8,14},{9,15},{10,... | collective-permute-start | bytes 608264 | tf_op jit(solution)/shard_map/ppermute | solution.py:333
  32.8 7.9 %collective-permute-start.12 = (bf16[24,4224]{1,0:T(8,128)(2,1)S(1)}, bf16[24,4224]{1,0:T(8,128)(2,1)S(1)}, u32[]{:S(2)}, u32[]{:S(2)}) collective-permute-start(bf16[24,4224]{1,0:T(8,128)(2,1)S(1)} %get-tuple-element.43), channel_id=1, source_target_pairs={{0,4},{1,5},{2,6},{3,7},{4,0},{5,1},{6,2},{7,3},{8,12},{9,13},{10,... | collective-permute-start | bytes 608264 | tf_op jit(solution)/shard_map/ppermute | solution.py:333
  35.4 5.8 %collective-permute-start.11 = (bf16[24,4224]{1,0:T(8,128)(2,1)S(1)}, bf16[24,4224]{1,0:T(8,128)(2,1)S(1)}, u32[]{:S(2)}, u32[]{:S(2)}) collective-permute-start(bf16[24,4224]{1,0:T(8,128)(2,1)S(1)} %get-tuple-element.43), channel_id=1, source_target_pairs={{0,2},{1,3},{2,0},{3,1},{4,6},{5,7},{6,4},{7,5},{8,10},{9,11},{10,... | collective-permute-start | bytes 608264 | tf_op jit(solution)/shard_map/ppermute | solution.py:333
  35.5 5.8 %collective-permute-start.14 = (bf16[56,4224]{1,0:T(8,128)(2,1)S(1)}, bf16[56,4224]{1,0:T(8,128)(2,1)S(1)}, u32[]{:S(2)}, u32[]{:S(2)}) collective-permute-start(bf16[56,4224]{1,0:T(8,128)(2,1)S(1)} %get-tuple-element.35), channel_id=1, source_target_pairs={{0,1},{1,0},{2,3},{3,2},{4,5},{5,4},{6,7},{7,6},{8,9},{9,8},{10,11... | collective-permute-start | bytes 1419272 | tf_op jit(solution)/shard_map/ppermute | solution.py:333
  38.5 4.2 %collective-permute-start.17 = (bf16[24,4224]{1,0:T(8,128)(2,1)S(1)}, bf16[24,4224]{1,0:T(8,128)(2,1)S(1)}, u32[]{:S(2)}, u32[]{:S(2)}) collective-permute-start(bf16[24,4224]{1,0:T(8,128)(2,1)S(1)} %collective-permute-done.13), channel_id=1, source_target_pairs={{0,1},{1,0},{2,3},{3,2},{4,5},{5,4},{6,7},{7,6},{8,9},{9,8},{10,11... | collective-permute-start | bytes 608264 | tf_op jit(solution)/shard_map/ppermute | solution.py:333
  40.7 2.0 %collective-permute-start.16 = (bf16[24,4224]{1,0:T(8,128)(2,1)S(1)}, bf16[24,4224]{1,0:T(8,128)(2,1)S(1)}, u32[]{:S(2)}, u32[]{:S(2)}) collective-permute-start(bf16[24,4224]{1,0:T(8,128)(2,1)S(1)} %collective-permute-done.12), channel_id=1, source_target_pairs={{0,1},{1,0},{2,3},{3,2},{4,5},{5,4},{6,7},{7,6},{8,9},{9,8},{10,11... | collective-permute-start | bytes 608264 | tf_op jit(solution)/shard_map/ppermute | solution.py:333
  51.7 5.0 %collective-permute-start.18 = (bf16[56,4096]{1,0:T(8,128)(2,1)S(1)}, bf16[56,4096]{1,0:T(8,128)(2,1)S(1)}, u32[]{:S(2)}, u32[]{:S(2)}) collective-permute-start(bf16[56,4096]{1,0:T(8,128)(2,1)S(1)} %slice.101), channel_id=1, source_target_pairs={{0,1},{1,0},{2,3},{3,2},{4,5},{5,4},{6,7},{7,6},{8,9},{9,8},{10,11... | collective-permute-start | bytes 1376264 | tf_op jit(solution)/shard_map/ppermute | solution.py:333
  53.2 12.2 %collective-permute-start.23 = (bf16[24,4096]{1,0:T(8,128)(2,1)S(1)}, bf16[24,4096]{1,0:T(8,128)(2,1)S(1)}, u32[]{:S(2)}, u32[]{:S(2)}) collective-permute-start(bf16[24,4096]{1,0:T(8,128)(2,1)S(1)} %get-tuple-element.19), channel_id=1, source_target_pairs={{0,2},{1,3},{2,0},{3,1},{4,6},{5,7},{6,4},{7,5},{8,10},{9,11},{10,... | collective-permute-start | bytes 589832 | tf_op jit(solution)/shard_map/ppermute | solution.py:333
  54.1 13.2 %collective-permute-start.27 = (bf16[24,4096]{1,0:T(8,128)(2,1)S(1)}, bf16[24,4096]{1,0:T(8,128)(2,1)S(1)}, u32[]{:S(2)}, u32[]{:S(2)}) collective-permute-start(bf16[24,4096]{1,0:T(8,128)(2,1)S(1)} %get-tuple-element.20), channel_id=1, source_target_pairs={{0,6},{1,7},{2,4},{3,5},{4,2},{5,3},{6,0},{7,1},{8,14},{9,15},{10,... | collective-permute-start | bytes 589832 | tf_op jit(solution)/shard_map/ppermute | solution.py:333
  56.2 11.1 %collective-permute-start.25 = (bf16[24,4096]{1,0:T(8,128)(2,1)S(1)}, bf16[24,4096]{1,0:T(8,128)(2,1)S(1)}, u32[]{:S(2)}, u32[]{:S(2)}) collective-permute-start(bf16[24,4096]{1,0:T(8,128)(2,1)S(1)} %get-tuple-element.21), channel_id=1, source_target_pairs={{0,4},{1,5},{2,6},{3,7},{4,0},{5,1},{6,2},{7,3},{8,12},{9,13},{10,... | collective-permute-start | bytes 589832 | tf_op jit(solution)/shard_map/ppermute | solution.py:333
  56.9 13.8 %collective-permute-start.19 = (bf16[8,4096]{1,0:T(8,128)(2,1)S(1)}, bf16[8,4096]{1,0:T(8,128)(2,1)S(1)}, u32[]{:S(2)}, u32[]{:S(2)}) collective-permute-start(bf16[8,4096]{1,0:T(8,128)(2,1)S(1)} %get-tuple-element.25), channel_id=1, source_target_pairs={{0,2},{1,3},{2,0},{3,1},{4,6},{5,7},{6,4},{7,5},{8,10},{9,11},{10,... | collective-permute-start | bytes 196616 | tf_op jit(solution)/shard_map/ppermute | solution.py:333
  57.8 13.2 %collective-permute-start.21 = (bf16[8,4096]{1,0:T(8,128)(2,1)S(1)}, bf16[8,4096]{1,0:T(8,128)(2,1)S(1)}, u32[]{:S(2)}, u32[]{:S(2)}) collective-permute-start(bf16[8,4096]{1,0:T(8,128)(2,1)S(1)} %get-tuple-element.26), channel_id=1, source_target_pairs={{0,6},{1,7},{2,4},{3,5},{4,2},{5,3},{6,0},{7,1},{8,14},{9,15},{10,... | collective-permute-start | bytes 196616 | tf_op jit(solution)/shard_map/ppermute | solution.py:333
  65.4 5.7 %collective-permute-start.20 = (bf16[8,4096]{1,0:T(8,128)(2,1)S(1)}, bf16[8,4096]{1,0:T(8,128)(2,1)S(1)}, u32[]{:S(2)}, u32[]{:S(2)}) collective-permute-start(bf16[8,4096]{1,0:T(8,128)(2,1)S(1)} %get-tuple-element.27), channel_id=1, source_target_pairs={{0,4},{1,5},{2,6},{3,7},{4,0},{5,1},{6,2},{7,3},{8,12},{9,13},{10,... | collective-permute-start | bytes 196616 | tf_op jit(solution)/shard_map/ppermute | solution.py:333
  67.5 4.3 %collective-permute-start.28 = (bf16[8,4096]{1,0:T(8,128)(2,1)S(1)}, bf16[8,4096]{1,0:T(8,128)(2,1)S(1)}, u32[]{:S(2)}, u32[]{:S(2)}) collective-permute-start(bf16[8,4096]{1,0:T(8,128)(2,1)S(1)} %get-tuple-element.28), channel_id=1, source_target_pairs={{0,8},{1,9},{2,10},{3,11},{4,12},{5,13},{6,14},{7,15},{8,0},{9,1},... | collective-permute-start | bytes 196616 | tf_op jit(solution)/shard_map/ppermute | solution.py:333
  69.3 6.1 %collective-permute-start.30 = (bf16[8,4096]{1,0:T(8,128)(2,1)S(1)}, bf16[8,4096]{1,0:T(8,128)(2,1)S(1)}, u32[]{:S(2)}, u32[]{:S(2)}) collective-permute-start(bf16[8,4096]{1,0:T(8,128)(2,1)S(1)} %get-tuple-element.29), channel_id=1, source_target_pairs={{0,24},{1,25},{2,26},{3,27},{4,28},{5,29},{6,30},{7,31},{8,16},{9,... | collective-permute-start | bytes 196616 | tf_op jit(solution)/shard_map/ppermute | solution.py:333
  70.7 6.1 %collective-permute-start.29 = (bf16[8,4096]{1,0:T(8,128)(2,1)S(1)}, bf16[8,4096]{1,0:T(8,128)(2,1)S(1)}, u32[]{:S(2)}, u32[]{:S(2)}) collective-permute-start(bf16[8,4096]{1,0:T(8,128)(2,1)S(1)} %get-tuple-element.30), channel_id=1, source_target_pairs={{0,16},{1,17},{2,18},{3,19},{4,20},{5,21},{6,22},{7,23},{8,24},{9,... | collective-permute-start | bytes 196616 | tf_op jit(solution)/shard_map/ppermute | solution.py:333
  (11 other events, 91.7 us)

commit v12 on v11

--- a/solution.py
+++ b/solution.py
@@ -12,6 +12,7 @@
 I32 = jnp.int32
 MIB = 1 << 20
 LANES = 128
+CAP = 3
 
 
 def rms_scale(values, gain):
@@ -271,9 +272,11 @@
     )(*got, *weights, in_hbm(later))
 
 
-def expert_kernel(x_ref, gate, up, down_hbm, out_ref, down, act, sem):
+def expert_kernel(slots, x_ref, gate, up, down_hbm, out_ref, down, xc, act, res, sem):
     own = lax.axis_index("dp") * lax.axis_size("tensor") + lax.axis_index("tensor")
+    rows = x_ref.shape[0]
     _, width, hidden = gate.shape
+    padded = res.shape[0]
     fsize = 384
     dsize = 1024
     chunks = width // dsize
@@ -284,32 +287,53 @@
 
     for i in range(chunks):
         down_copy(i).start()
+    table = x_ref[:, width:]
+    pick = (iota((16, table.shape[1]), 1) == own).astype(F32).astype(BF)
+    named = matmul_t(pick, table) != 0.0
+    before = (iota((rows, rows), 0) < iota((rows, rows), 1)).astype(F32).astype(BF)
+    place = matmul(named.astype(F32).astype(BF), before)
+    place = jnp.where(named, place, -1.0)[:1]
+    take = (iota((slots, rows), 0).astype(F32) == place).astype(F32).astype(BF)
+    for i in range(chunks):
+        cols = slice(i * dsize, (i + 1) * dsize)
+        xc[:, cols] = matmul(take, x_ref[:, cols]).astype(BF)
+
+    lane = iota(table.shape, 1)
+    weight = jnp.sum(jnp.where(lane == own, table.astype(F32), 0.0), axis=1, keepdims=True)
+    named = jnp.broadcast_to((weight != 0.0).astype(F32), (rows, LANES)).astype(BF)
+    after = (iota((rows, rows), 1) < iota((rows, rows), 0)).astype(F32).astype(BF)
+    place = matmul(after, named)[:, :1]
+    spread = jnp.where(iota((rows, padded), 1).astype(F32) == place, weight, 0.0).astype(BF)
+    if padded > slots:
+        res[slots:, :] = jnp.zeros((padded - slots, dsize), BF)
+
     for i in range(hidden // fsize):
         cols = slice(i * fsize, (i + 1) * fsize)
-        g = matmul(x_ref[:, :width], gate[0, :, cols])
-        u = matmul(x_ref[:, :width], up[0, :, cols])
+        g = matmul(xc[...], gate[0, :, cols])
+        u = matmul(xc[...], up[0, :, cols])
         act[:, cols] = (g / (1.0 + jnp.exp(-g)) * u).astype(BF)
-    table = x_ref[:, width:].astype(F32)
-    named = iota(table.shape, 1) == own
-    weight = jnp.sum(jnp.where(named, table, 0.0), axis=1, keepdims=True)
     for i in range(chunks):
         down_copy(i).wait()
         cols = slice(i * dsize, (i + 1) * dsize)
-        out_ref[:, cols] = (matmul(act[...], down[:, cols]) * weight).astype(BF)
-
-
-def experts(x, expert_gate, expert_up, expert_down):
+        res[:slots, :] = matmul(act[...], down[:, cols]).astype(BF)
+        out_ref[:, cols] = matmul(spread, res[...]).astype(BF)
+
+
+def experts(x, expert_gate, expert_up, expert_down, share):
     rows = x.shape[0]
     _, width, hidden = expert_gate.shape
+    slots = rows // share * CAP
     vmem = pl.BlockSpec(memory_space=pltpu.VMEM)
     return pl.pallas_call(
-        expert_kernel,
+        functools.partial(expert_kernel, slots),
         out_shape=jax.ShapeDtypeStruct((rows, width), BF),
         in_specs=[vmem] * 3 + [pl.BlockSpec(memory_space=pltpu.HBM)],
         out_specs=vmem,
         scratch_shapes=[
             pltpu.VMEM((hidden, width), BF),
-            pltpu.VMEM((rows, hidden), BF),
+            pltpu.VMEM((slots, width), BF),
+            pltpu.VMEM((slots, hidden), BF),
+            pltpu.VMEM((-(-slots // LANES) * LANES, 1024), BF),
             pltpu.SemaphoreType.DMA((width // 1024,)),
         ],
         compiler_params=pltpu.CompilerParams(vmem_limit_bytes=(16 + rows // 32) * MIB),
@@ -325,9 +349,8 @@
         self.core = 1
         self.y = [2 * j for j in range(1, ylen)]
         self.z = [tensor * xlen * j for j in range(1, self.zlen)]
-        self.plane = [
-            tensor * jx + 2 * jy for jx in range(xlen) for jy in range(ylen) if jx or jy
-        ]
+        self.x = [tensor * j for j in range(1, xlen)]
+        self.diagonal = [jx + jy for jx in self.x for jy in self.y]
 
     def swap(self, value, flip):
         return lax.ppermute(value, ("dp", "tensor"), [(i, i ^ flip) for i in range(self.count)])
@@ -390,12 +413,17 @@
 
     mine = jnp.concatenate([normed, table], axis=1)
     others = plan.spread(mine, plan.z)
-    near = plan.spread(mine + others[0][:, :1] * 0, plan.plane)
-    far = plan.spread(jnp.concatenate(others), plan.plane)
-    pieces = [jnp.concatenate([mine] + others + near)] + far
+    first = mine + others[0][:, :1] * 0
+    near_x = plan.spread(first, plan.x)
+    near_y = plan.spread(first, plan.y)
+    rest = jnp.concatenate(others)
+    far_diagonal = plan.spread(rest, plan.diagonal)
+    far_y = plan.spread(rest, plan.y)
+    far_x = plan.spread(jnp.concatenate(others + near_y), plan.x)
+    pieces = [jnp.concatenate([mine] + others + near_x + near_y)] + far_y + far_x + far_diagonal
     x = jnp.concatenate(pieces + [plan.swap(piece, plan.core) for piece in pieces])
 
-    result = experts(x, expert_gate, expert_up, expert_down)
+    result = experts(x, expert_gate, expert_up, expert_down, share)
 
     sizes = [piece.shape[0] for piece in pieces]
     starts = [sum(sizes[:i]) for i in range(len(sizes) + 1)]
@@ -409,11 +437,17 @@
         )
         for i in reversed(range(len(sizes)))
     ][::-1]
-    blocks = sums[0].reshape(-1, share, width)
-    far = plan.swaps(sums[1:], plan.plane)
-    others = total_of([sums[0][share : plan.zlen * share]] + far).reshape(-1, share, width)
-    near = plan.swaps(list(blocks[plan.zlen :]), plan.plane)
-    moe_sum = total_of([blocks[0]] + near + plan.swaps(list(others), plan.z))
+    back = plan.swaps(sums[1:], plan.y + plan.x + plan.diagonal)
+    height, x_end = rest.shape[0], len(plan.y) + len(plan.x)
+    column = sums[0][: share + height]
+    near = sums[0][share + height :].reshape(-1, share, width)
+    through = [v[height:] for v in back[len(plan.y) : x_end]]
+    through = total_of([near[len(plan.x) :].reshape(-1, width)] + through)
+    others = total_of([column[share:]] + [v[:height] for v in back])
+    others = plan.swaps(list(others.reshape(-1, share, width)), plan.z)
+    near_x = plan.swaps(list(near[: len(plan.x)]), plan.x)
+    near_y = plan.swaps(list(through.reshape(-1, share, width)), plan.y)
+    moe_sum = total_of([column[:share]] + near_x + near_y + others)
     return (hidden + moe_sum).astype(BF)
 
 

time: 77.7 us -> 76.1 us (0.979)
  Pallas kernels: 17.4 us -> 15.7 us
  waiting for transfers between devices: 27.9 us -> 29.4 us
  starting transfers between devices: 29.9 us -> 28.5 us
    pallas_call x1, Pallas kernels: 8.17 us -> 6.49 us  [experts(): pl.pallas_call(functools.partial(expert_kernel, slots), out_shape=jax.Sha...]
    ppermute x31 -> x29, waiting for transfers between devices: 27.9 us -> 29.4 us  [swap(): lax.ppermute(value, ('dp', 'tensor'), [(i, i ^ flip) for i in range(self....]
    ppermute x31 -> x29, starting transfers between devices: 29.9 us -> 28.5 us  [swap(): lax.ppermute(value, ('dp', 'tensor'), [(i, i ^ flip) for i in range(self....]
  transfers between devices with their start and end apart: 31 -> 29, of which waited for: 18 -> 17; matrix products, arithmetic and copies ran while one was open for 1% -> 1% of each run, Pallas kernels for 5% -> 5%
where the time goes in v12:
time: 76.1 us; the launch traced here: 75.9 us
  waiting for transfers between devices  29.4 us (39%)
  starting transfers between devices  28.5 us (37%)
  Pallas kernels  15.7 us (21%)
  other arithmetic  1.58 us (2%)
    ppermute x29, waiting for transfers between devices, swap(): lax.ppermute(value, ('dp', 'tensor'), [(i, i ^ flip) for i in range(self....  29.4 us
    ppermute x29, starting transfers between devices, swap(): lax.ppermute(value, ('dp', 'tensor'), [(i, i ^ flip) for i in range(self....  28.5 us
    pallas_call x1, Pallas kernels, experts(): pl.pallas_call(functools.partial(expert_kernel, slots), out_shape=jax.Sha...  6.49 us
    pallas_call x2, Pallas kernels, attention(): pl.pallas_call(functools.partial(attention_kernel, flip), out_shape=tuple...  6.31 us
    pallas_call x1, Pallas kernels, projection(): pl.pallas_call(functools.partial(projection_kernel, parts, len(weights)),...  2.94 us
  transfers between devices with their start and end apart: 29, of which 17 were waited for; matrix products, arithmetic and copies ran while one was open for 1% of the time, Pallas kernels for 5%

profile of v12, /device:TPU:0, one launch (start us, length us, event | category | flops | bytes accessed | tf_op | source)
XLA Modules:
  0.0 75.9 jit_solution(4357215797663775097)
XLA Ops:
  0.0 2.4 %attention.2.refs_11_ = bf16[2,32,1152]{2,1,0:T(8,128)(2,1)S(1)} custom-call(s32[32]{0:T(128)} %refs_0_.3, bf16[32,32,128]{2,1,0:T(8,128)(2,1)} %refs_1_.3, bf16[32,2,128]{2,1,0:T(2,128)(2,1)} %refs_2_.3, bf16[32,2,128]{2,1,0:T(2,128)(2,1)} %refs_3_.3, bf16[32,2,32,128]{3,2,1,0:T(8,128)(2,1)} %refs_4_.3, bf16[32,2,32,128]{3,2,1,0:T(8,128)(2,1)} %refs_5_.3, ...), custom_call_target="tpu_custom_call" | custom-call | flops 1048576 | bytes 1048576 | tf_op jit(solution)/shard_map/attention/pallas_call | solution.py:199
  2.4 3.0 %collective-permute-start = (bf16[2,32,1152]{2,1,0:T(8,128)(2,1)S(1)}, bf16[2,32,1152]{2,1,0:T(8,128)(2,1)S(1)}, u32[]{:S(2)}, u32[]{:S(2)}) collective-permute-start(bf16[2,32,1152]{2,1,0:T(8,128)(2,1)S(1)} %attention.2.refs_11_), channel_id=1, source_target_pairs={{0,2},{1,3},{2,0},{3,1},{4,6},{5,7},{6,4},{7,5},{8,10},{9,11},{10,... | collective-permute-start | bytes 442376 | tf_op jit(solution)/shard_map/ppermute | solution.py:356
  5.5 3.9 %attention.3 = (bf16[2,32,1152]{2,1,0:T(8,128)(2,1)S(1)}, bf16[8,128]{1,0:T(8,128)(2,1)S(1)}, bf16[512,4096]{1,0:T(8,128)(2,1)S(1)}, bf16[512,4096]{1,0:T(8,128)(2,1)S(1)}) custom-call(s32[32]{0:T(128)} %refs_0_.3, bf16[32,32,128]{2,1,0:T(8,128)(2,1)} %refs_1_.3, bf16[32,2,128]{2,1,0:T(2,128)(2,1)} %refs_2_.3, bf16[32,2,128]{2,1,0:T(2,128)(2,1)} %refs_3_.3, ...), custom_call_target="tpu_custom_call" | custom-call | flops 9437184 | bytes 9437184 | tf_op jit(solution)/shard_map/attention/pallas_call | solution.py:199
  11.0 2.9 %projection.1 = (bf16[2,2,8,4096]{3,2,1,0:T(8,128)(2,1)S(1)}, bf16[1,4096,768]{2,1,0:T(8,128)(2,1)S(1)}) custom-call(bf16[32,1152]{1,0:T(8,128)(2,1)S(1)} %get-tuple-element.27.refs_0_, bf16[32,1152]{1,0:T(8,128)(2,1)S(1)} %collective-permute-done.1.refs_1_, bf16[32,1152]{1,0:T(8,128)(2,1)S(1)} %get-tuple-element.25.refs_2_, ...), custom_call_target="tpu_custom_call" | custom-call | tf_op jit(solution)/shard_map/projection/pallas_call | solution.py:261
  15.4 1.5 %collective-permute-start.4 = (bf16[8,4096]{1,0:T(8,128)(2,1)S(1)}, bf16[8,4096]{1,0:T(8,128)(2,1)S(1)}, u32[]{:S(2)}, u32[]{:S(2)}) collective-permute-start(bf16[8,4096]{1,0:T(8,128)(2,1)S(1)} %fusion.12), channel_id=1, source_target_pairs={{0,2},{1,3},{2,0},{3,1},{4,6},{5,7},{6,4},{7,5},{8,10},{9,11},{10,... | collective-permute-start | bytes 196616 | tf_op jit(solution)/shard_map/ppermute | solution.py:356
  16.9 2.9 %collective-permute-done.4 = bf16[8,4096]{1,0:T(8,128)(2,1)S(1)} collective-permute-done((bf16[8,4096]{1,0:T(8,128)(2,1)S(1)}, bf16[8,4096]{1,0:T(8,128)(2,1)S(1)}, u32[]{:S(2)}, u32[]{:S(2)}) %collective-permute-start.4) | collective-permute-done | bytes 65568 | tf_op jit(solution)/shard_map/ppermute | solution.py:356
  20.1 1.6 %collective-permute-start.5 = (bf16[8,4224]{1,0:T(8,128)(2,1)S(1)}, bf16[8,4224]{1,0:T(8,128)(2,1)S(1)}, u32[]{:S(2)}, u32[]{:S(2)}) collective-permute-start(bf16[8,4224]{1,0:T(8,128)(2,1)S(1)} %pad_maximum_fusion.1), channel_id=1, source_target_pairs={{0,8},{1,9},{2,10},{3,11},{4,12},{5,13},{6,14},{7,15},{8,0},{9,1},... | collective-permute-start | bytes 202760 | tf_op jit(solution)/shard_map/ppermute | solution.py:356
  21.7 2.6 %collective-permute-start.6 = (bf16[8,4224]{1,0:T(8,128)(2,1)S(1)}, bf16[8,4224]{1,0:T(8,128)(2,1)S(1)}, u32[]{:S(2)}, u32[]{:S(2)}) collective-permute-start(bf16[8,4224]{1,0:T(8,128)(2,1)S(1)} %pad_maximum_fusion.1), channel_id=1, source_target_pairs={{0,16},{1,17},{2,18},{3,19},{4,20},{5,21},{6,22},{7,23},{8,24},{9,... | collective-permute-start | bytes 202760 | tf_op jit(solution)/shard_map/ppermute | solution.py:356
  24.8 2.0 %collective-permute-start.9 = (bf16[8,4224]{1,0:T(8,128)(2,1)S(1)}, bf16[8,4224]{1,0:T(8,128)(2,1)S(1)}, u32[]{:S(2)}, u32[]{:S(2)}) collective-permute-start(bf16[8,4224]{1,0:T(8,128)(2,1)S(1)} %get-tuple-element.43), channel_id=1, source_target_pairs={{0,2},{1,3},{2,0},{3,1},{4,6},{5,7},{6,4},{7,5},{8,10},{9,11},{10,... | collective-permute-start | bytes 202760 | tf_op jit(solution)/shard_map/ppermute | solution.py:356
  26.7 1.5 %collective-permute-start.8 = (bf16[8,4224]{1,0:T(8,128)(2,1)S(1)}, bf16[8,4224]{1,0:T(8,128)(2,1)S(1)}, u32[]{:S(2)}, u32[]{:S(2)}) collective-permute-start(bf16[8,4224]{1,0:T(8,128)(2,1)S(1)} %get-tuple-element.43), channel_id=1, source_target_pairs={{0,4},{1,5},{2,6},{3,7},{4,0},{5,1},{6,2},{7,3},{8,12},{9,13},{10,... | collective-permute-start | bytes 202760 | tf_op jit(solution)/shard_map/ppermute | solution.py:356
  28.9 1.5 %collective-permute-done.7 = bf16[8,4224]{1,0:T(8,128)(2,1)S(1)} collective-permute-done((bf16[8,4224]{1,0:T(8,128)(2,1)S(1)}, bf16[8,4224]{1,0:T(8,128)(2,1)S(1)}, u32[]{:S(2)}, u32[]{:S(2)}) %collective-permute-start.7) | collective-permute-done | bytes 67616 | tf_op jit(solution)/shard_map/ppermute | solution.py:356
  30.4 2.3 %collective-permute-start.12 = (bf16[24,4224]{1,0:T(8,128)(2,1)S(1)}, bf16[24,4224]{1,0:T(8,128)(2,1)S(1)}, u32[]{:S(2)}, u32[]{:S(2)}) collective-permute-start(bf16[24,4224]{1,0:T(8,128)(2,1)S(1)} %get-tuple-element.34), channel_id=1, source_target_pairs={{0,6},{1,7},{2,4},{3,5},{4,2},{5,3},{6,0},{7,1},{8,14},{9,15},{10,... | collective-permute-start | bytes 608264 | tf_op jit(solution)/shard_map/ppermute | solution.py:356
  34.2 5.0 %collective-permute-done.12 = bf16[24,4224]{1,0:T(8,128)(2,1)S(1)} collective-permute-done((bf16[24,4224]{1,0:T(8,128)(2,1)S(1)}, bf16[24,4224]{1,0:T(8,128)(2,1)S(1)}, u32[]{:S(2)}, u32[]{:S(2)}) %collective-permute-start.12) | collective-permute-done | bytes 202784 | tf_op jit(solution)/shard_map/ppermute | solution.py:356
  39.2 1.3 %collective-permute-done.10 = bf16[24,4224]{1,0:T(8,128)(2,1)S(1)} collective-permute-done((bf16[24,4224]{1,0:T(8,128)(2,1)S(1)}, bf16[24,4224]{1,0:T(8,128)(2,1)S(1)}, u32[]{:S(2)}, u32[]{:S(2)}) %collective-permute-start.10) | collective-permute-done | bytes 202784 | tf_op jit(solution)/shard_map/ppermute | solution.py:356
  43.1 6.5 %experts.1 = bf16[256,4096]{1,0:T(8,128)(2,1)S(1)} custom-call(bf16[256,4224]{1,0:T(8,128)(2,1)S(1)} %constant_dynamic-update-slice_fusion.9.x_ref, bf16[1,4096,768]{2,1,0:T(8,128)(2,1)S(1)} %get-tuple-element.16.gate, bf16[1,4096,768]{2,1,0:T(8,128)(2,1)S(1)} %bitcast.30, bf16[1,768,4096]{2,1,0:T(8,128)(2,1)} %down_hbm.1), custom_call_target="tpu_custom_call" | custom-call | tf_op jit(solution)/shard_map/experts/pallas_call | solution.py:327
  51.5 1.1 %collective-permute-start.23 = (bf16[24,4096]{1,0:T(8,128)(2,1)S(1)}, bf16[24,4096]{1,0:T(8,128)(2,1)S(1)}, u32[]{:S(2)}, u32[]{:S(2)}) collective-permute-start(bf16[24,4096]{1,0:T(8,128)(2,1)S(1)} %get-tuple-element.17), channel_id=1, source_target_pairs={{0,2},{1,3},{2,0},{3,1},{4,6},{5,7},{6,4},{7,5},{8,10},{9,11},{10,... | collective-permute-start | bytes 589832 | tf_op jit(solution)/shard_map/ppermute | solution.py:356
  52.7 1.9 %collective-permute-start.25 = (bf16[24,4096]{1,0:T(8,128)(2,1)S(1)}, bf16[24,4096]{1,0:T(8,128)(2,1)S(1)}, u32[]{:S(2)}, u32[]{:S(2)}) collective-permute-start(bf16[24,4096]{1,0:T(8,128)(2,1)S(1)} %get-tuple-element.18), channel_id=1, source_target_pairs={{0,6},{1,7},{2,4},{3,5},{4,2},{5,3},{6,0},{7,1},{8,14},{9,15},{10,... | collective-permute-start | bytes 589832 | tf_op jit(solution)/shard_map/ppermute | solution.py:356
  55.3 1.6 %collective-permute-start.18 = (bf16[8,4096]{1,0:T(8,128)(2,1)S(1)}, bf16[8,4096]{1,0:T(8,128)(2,1)S(1)}, u32[]{:S(2)}, u32[]{:S(2)}) collective-permute-start(bf16[8,4096]{1,0:T(8,128)(2,1)S(1)} %slice.180), channel_id=1, source_target_pairs={{0,4},{1,5},{2,6},{3,7},{4,0},{5,1},{6,2},{7,3},{8,12},{9,13},{10,... | collective-permute-start | bytes 196616 | tf_op jit(solution)/shard_map/ppermute | solution.py:356
  56.9 5.9 %collective-permute-done.23 = bf16[24,4096]{1,0:T(8,128)(2,1)S(1)} collective-permute-done((bf16[24,4096]{1,0:T(8,128)(2,1)S(1)}, bf16[24,4096]{1,0:T(8,128)(2,1)S(1)}, u32[]{:S(2)}, u32[]{:S(2)}) %collective-permute-start.23) | collective-permute-done | bytes 196640 | tf_op jit(solution)/shard_map/ppermute | solution.py:356
  62.8 3.3 %collective-permute-done.20 = bf16[32,4096]{1,0:T(8,128)(2,1)S(1)} collective-permute-done((bf16[32,4096]{1,0:T(8,128)(2,1)S(1)}, bf16[32,4096]{1,0:T(8,128)(2,1)S(1)}, u32[]{:S(2)}, u32[]{:S(2)}) %collective-permute-start.20) | collective-permute-done | bytes 262176 | tf_op jit(solution)/shard_map/ppermute | solution.py:356
  67.2 2.9 %collective-permute-start.28 = (bf16[8,4096]{1,0:T(8,128)(2,1)S(1)}, bf16[8,4096]{1,0:T(8,128)(2,1)S(1)}, u32[]{:S(2)}, u32[]{:S(2)}) collective-permute-start(bf16[8,4096]{1,0:T(8,128)(2,1)S(1)} %get-tuple-element.22), channel_id=1, source_target_pairs={{0,24},{1,25},{2,26},{3,27},{4,28},{5,29},{6,30},{7,31},{8,16},{9,... | collective-permute-start | bytes 196616 | tf_op jit(solution)/shard_map/ppermute | solution.py:356
  70.0 1.3 %collective-permute-start.21 = (bf16[8,4096]{1,0:T(8,128)(2,1)S(1)}, bf16[8,4096]{1,0:T(8,128)(2,1)S(1)}, u32[]{:S(2)}, u32[]{:S(2)}) collective-permute-start(bf16[8,4096]{1,0:T(8,128)(2,1)S(1)} %fusion.3), channel_id=1, source_target_pairs={{0,2},{1,3},{2,0},{3,1},{4,6},{5,7},{6,4},{7,5},{8,10},{9,11},{10,... | collective-permute-start | bytes 196616 | tf_op jit(solution)/shard_map/ppermute | solution.py:356
  71.3 2.0 %collective-permute-done.28 = bf16[8,4096]{1,0:T(8,128)(2,1)S(1)} collective-permute-done((bf16[8,4096]{1,0:T(8,128)(2,1)S(1)}, bf16[8,4096]{1,0:T(8,128)(2,1)S(1)}, u32[]{:S(2)}, u32[]{:S(2)}) %collective-permute-start.28) | collective-permute-done | bytes 65568 | tf_op jit(solution)/shard_map/ppermute | solution.py:356
  73.3 1.9 %collective-permute-done.27 = bf16[8,4096]{1,0:T(8,128)(2,1)S(1)} collective-permute-done((bf16[8,4096]{1,0:T(8,128)(2,1)S(1)}, bf16[8,4096]{1,0:T(8,128)(2,1)S(1)}, u32[]{:S(2)}, u32[]{:S(2)}) %collective-permute-start.27) | collective-permute-done | bytes 65568 | tf_op jit(solution)/shard_map/ppermute | solution.py:356
  (82 shorter events, 12.6 us)
Async XLA Ops:
  2.4 7.0 %collective-permute-start = (bf16[2,32,1152]{2,1,0:T(8,128)(2,1)S(1)}, bf16[2,32,1152]{2,1,0:T(8,128)(2,1)S(1)}, u32[]{:S(2)}, u32[]{:S(2)}) collective-permute-start(bf16[2,32,1152]{2,1,0:T(8,128)(2,1)S(1)} %attention.2.refs_11_), channel_id=1, source_target_pairs={{0,2},{1,3},{2,0},{3,1},{4,6},{5,7},{6,4},{7,5},{8,10},{9,11},{10,... | collective-permute-start | bytes 442376 | tf_op jit(solution)/shard_map/ppermute | solution.py:356
  15.4 4.4 %collective-permute-start.4 = (bf16[8,4096]{1,0:T(8,128)(2,1)S(1)}, bf16[8,4096]{1,0:T(8,128)(2,1)S(1)}, u32[]{:S(2)}, u32[]{:S(2)}) collective-permute-start(bf16[8,4096]{1,0:T(8,128)(2,1)S(1)} %fusion.12), channel_id=1, source_target_pairs={{0,2},{1,3},{2,0},{3,1},{4,6},{5,7},{6,4},{7,5},{8,10},{9,11},{10,... | collective-permute-start | bytes 196616 | tf_op jit(solution)/shard_map/ppermute | solution.py:356
  20.1 4.5 %collective-permute-start.5 = (bf16[8,4224]{1,0:T(8,128)(2,1)S(1)}, bf16[8,4224]{1,0:T(8,128)(2,1)S(1)}, u32[]{:S(2)}, u32[]{:S(2)}) collective-permute-start(bf16[8,4224]{1,0:T(8,128)(2,1)S(1)} %pad_maximum_fusion.1), channel_id=1, source_target_pairs={{0,8},{1,9},{2,10},{3,11},{4,12},{5,13},{6,14},{7,15},{8,0},{9,1},... | collective-permute-start | bytes 202760 | tf_op jit(solution)/shard_map/ppermute | solution.py:356
  21.7 7.1 %collective-permute-start.6 = (bf16[8,4224]{1,0:T(8,128)(2,1)S(1)}, bf16[8,4224]{1,0:T(8,128)(2,1)S(1)}, u32[]{:S(2)}, u32[]{:S(2)}) collective-permute-start(bf16[8,4224]{1,0:T(8,128)(2,1)S(1)} %pad_maximum_fusion.1), channel_id=1, source_target_pairs={{0,16},{1,17},{2,18},{3,19},{4,20},{5,21},{6,22},{7,23},{8,24},{9,... | collective-permute-start | bytes 202760 | tf_op jit(solution)/shard_map/ppermute | solution.py:356
  24.3 6.1 %collective-permute-start.7 = (bf16[8,4224]{1,0:T(8,128)(2,1)S(1)}, bf16[8,4224]{1,0:T(8,128)(2,1)S(1)}, u32[]{:S(2)}, u32[]{:S(2)}) collective-permute-start(bf16[8,4224]{1,0:T(8,128)(2,1)S(1)} %pad_maximum_fusion.1), channel_id=1, source_target_pairs={{0,24},{1,25},{2,26},{3,27},{4,28},{5,29},{6,30},{7,31},{8,16},{9,... | collective-permute-start | bytes 202760 | tf_op jit(solution)/shard_map/ppermute | solution.py:356
  24.8 8.7 %collective-permute-start.9 = (bf16[8,4224]{1,0:T(8,128)(2,1)S(1)}, bf16[8,4224]{1,0:T(8,128)(2,1)S(1)}, u32[]{:S(2)}, u32[]{:S(2)}) collective-permute-start(bf16[8,4224]{1,0:T(8,128)(2,1)S(1)} %get-tuple-element.43), channel_id=1, source_target_pairs={{0,2},{1,3},{2,0},{3,1},{4,6},{5,7},{6,4},{7,5},{8,10},{9,11},{10,... | collective-permute-start | bytes 202760 | tf_op jit(solution)/shard_map/ppermute | solution.py:356
  26.7 7.4 %collective-permute-start.8 = (bf16[8,4224]{1,0:T(8,128)(2,1)S(1)}, bf16[8,4224]{1,0:T(8,128)(2,1)S(1)}, u32[]{:S(2)}, u32[]{:S(2)}) collective-permute-start(bf16[8,4224]{1,0:T(8,128)(2,1)S(1)} %get-tuple-element.43), channel_id=1, source_target_pairs={{0,4},{1,5},{2,6},{3,7},{4,0},{5,1},{6,2},{7,3},{8,12},{9,13},{10,... | collective-permute-start | bytes 202760 | tf_op jit(solution)/shard_map/ppermute | solution.py:356
  30.4 8.7 %collective-permute-start.12 = (bf16[24,4224]{1,0:T(8,128)(2,1)S(1)}, bf16[24,4224]{1,0:T(8,128)(2,1)S(1)}, u32[]{:S(2)}, u32[]{:S(2)}) collective-permute-start(bf16[24,4224]{1,0:T(8,128)(2,1)S(1)} %get-tuple-element.34), channel_id=1, source_target_pairs={{0,6},{1,7},{2,4},{3,5},{4,2},{5,3},{6,0},{7,1},{8,14},{9,15},{10,... | collective-permute-start | bytes 608264 | tf_op jit(solution)/shard_map/ppermute | solution.py:356
  32.8 7.7 %collective-permute-start.10 = (bf16[24,4224]{1,0:T(8,128)(2,1)S(1)}, bf16[24,4224]{1,0:T(8,128)(2,1)S(1)}, u32[]{:S(2)}, u32[]{:S(2)}) collective-permute-start(bf16[24,4224]{1,0:T(8,128)(2,1)S(1)} %get-tuple-element.34), channel_id=1, source_target_pairs={{0,2},{1,3},{2,0},{3,1},{4,6},{5,7},{6,4},{7,5},{8,10},{9,11},{10,... | collective-permute-start | bytes 608264 | tf_op jit(solution)/shard_map/ppermute | solution.py:356
  33.5 8.0 %collective-permute-start.11 = (bf16[32,4224]{1,0:T(8,128)(2,1)S(1)}, bf16[32,4224]{1,0:T(8,128)(2,1)S(1)}, u32[]{:S(2)}, u32[]{:S(2)}) collective-permute-start(bf16[32,4224]{1,0:T(8,128)(2,1)S(1)} %pad_maximum_fusion), channel_id=1, source_target_pairs={{0,4},{1,5},{2,6},{3,7},{4,0},{5,1},{6,2},{7,3},{8,12},{9,13},{10,... | collective-permute-start | bytes 811016 | tf_op jit(solution)/shard_map/ppermute | solution.py:356
  34.1 7.4 %collective-permute-start.13 = (bf16[48,4224]{1,0:T(8,128)(2,1)S(1)}, bf16[48,4224]{1,0:T(8,128)(2,1)S(1)}, u32[]{:S(2)}, u32[]{:S(2)}) collective-permute-start(bf16[48,4224]{1,0:T(8,128)(2,1)S(1)} %get-tuple-element.28), channel_id=1, source_target_pairs={{0,1},{1,0},{2,3},{3,2},{4,5},{5,4},{6,7},{7,6},{8,9},{9,8},{10,11... | collective-permute-start | bytes 1216520 | tf_op jit(solution)/shard_map/ppermute | solution.py:356
  39.2 3.8 %collective-permute-start.16 = (bf16[24,4224]{1,0:T(8,128)(2,1)S(1)}, bf16[24,4224]{1,0:T(8,128)(2,1)S(1)}, u32[]{:S(2)}, u32[]{:S(2)}) collective-permute-start(bf16[24,4224]{1,0:T(8,128)(2,1)S(1)} %collective-permute-done.12), channel_id=1, source_target_pairs={{0,1},{1,0},{2,3},{3,2},{4,5},{5,4},{6,7},{7,6},{8,9},{9,8},{10,11... | collective-permute-start | bytes 608264 | tf_op jit(solution)/shard_map/ppermute | solution.py:356
  41.5 1.5 %collective-permute-start.15 = (bf16[32,4224]{1,0:T(8,128)(2,1)S(1)}, bf16[32,4224]{1,0:T(8,128)(2,1)S(1)}, u32[]{:S(2)}, u32[]{:S(2)}) collective-permute-start(bf16[32,4224]{1,0:T(8,128)(2,1)S(1)} %collective-permute-done.11), channel_id=1, source_target_pairs={{0,1},{1,0},{2,3},{3,2},{4,5},{5,4},{6,7},{7,6},{8,9},{9,8},{10,11... | collective-permute-start | bytes 811016 | tf_op jit(solution)/shard_map/ppermute | solution.py:356
  49.8 1.6 %collective-permute-start.24 = (bf16[24,4096]{1,0:T(8,128)(2,1)S(1)}, bf16[24,4096]{1,0:T(8,128)(2,1)S(1)}, u32[]{:S(2)}, u32[]{:S(2)}) collective-permute-start(bf16[24,4096]{1,0:T(8,128)(2,1)S(1)} %get-tuple-element.20), channel_id=1, source_target_pairs={{0,1},{1,0},{2,3},{3,2},{4,5},{5,4},{6,7},{7,6},{8,9},{9,8},{10,11... | collective-permute-start | bytes 589832 | tf_op jit(solution)/shard_map/ppermute | solution.py:356
  50.3 4.3 %collective-permute-start.19 = (bf16[32,4096]{1,0:T(8,128)(2,1)S(1)}, bf16[32,4096]{1,0:T(8,128)(2,1)S(1)}, u32[]{:S(2)}, u32[]{:S(2)}) collective-permute-start(bf16[32,4096]{1,0:T(8,128)(2,1)S(1)} %slice.119), channel_id=1, source_target_pairs={{0,1},{1,0},{2,3},{3,2},{4,5},{5,4},{6,7},{7,6},{8,9},{9,8},{10,11... | collective-permute-start | bytes 786440 | tf_op jit(solution)/shard_map/ppermute | solution.py:356
  50.5 4.8 %collective-permute-start.17 = (bf16[48,4096]{1,0:T(8,128)(2,1)S(1)}, bf16[48,4096]{1,0:T(8,128)(2,1)S(1)}, u32[]{:S(2)}, u32[]{:S(2)}) collective-permute-start(bf16[48,4096]{1,0:T(8,128)(2,1)S(1)} %slice.114), channel_id=1, source_target_pairs={{0,1},{1,0},{2,3},{3,2},{4,5},{5,4},{6,7},{7,6},{8,9},{9,8},{10,11... | collective-permute-start | bytes 1179656 | tf_op jit(solution)/shard_map/ppermute | solution.py:356
  51.5 11.3 %collective-permute-start.23 = (bf16[24,4096]{1,0:T(8,128)(2,1)S(1)}, bf16[24,4096]{1,0:T(8,128)(2,1)S(1)}, u32[]{:S(2)}, u32[]{:S(2)}) collective-permute-start(bf16[24,4096]{1,0:T(8,128)(2,1)S(1)} %get-tuple-element.17), channel_id=1, source_target_pairs={{0,2},{1,3},{2,0},{3,1},{4,6},{5,7},{6,4},{7,5},{8,10},{9,11},{10,... | collective-permute-start | bytes 589832 | tf_op jit(solution)/shard_map/ppermute | solution.py:356
  52.7 10.2 %collective-permute-start.25 = (bf16[24,4096]{1,0:T(8,128)(2,1)S(1)}, bf16[24,4096]{1,0:T(8,128)(2,1)S(1)}, u32[]{:S(2)}, u32[]{:S(2)}) collective-permute-start(bf16[24,4096]{1,0:T(8,128)(2,1)S(1)} %get-tuple-element.18), channel_id=1, source_target_pairs={{0,6},{1,7},{2,4},{3,5},{4,2},{5,3},{6,0},{7,1},{8,14},{9,15},{10,... | collective-permute-start | bytes 589832 | tf_op jit(solution)/shard_map/ppermute | solution.py:356
  54.7 11.5 %collective-permute-start.20 = (bf16[32,4096]{1,0:T(8,128)(2,1)S(1)}, bf16[32,4096]{1,0:T(8,128)(2,1)S(1)}, u32[]{:S(2)}, u32[]{:S(2)}) collective-permute-start(bf16[32,4096]{1,0:T(8,128)(2,1)S(1)} %add_convert_fusion), channel_id=1, source_target_pairs={{0,4},{1,5},{2,6},{3,7},{4,0},{5,1},{6,2},{7,3},{8,12},{9,13},{10,... | collective-permute-start | bytes 786440 | tf_op jit(solution)/shard_map/ppermute | solution.py:356
  55.3 16.0 %collective-permute-start.18 = (bf16[8,4096]{1,0:T(8,128)(2,1)S(1)}, bf16[8,4096]{1,0:T(8,128)(2,1)S(1)}, u32[]{:S(2)}, u32[]{:S(2)}) collective-permute-start(bf16[8,4096]{1,0:T(8,128)(2,1)S(1)} %slice.180), channel_id=1, source_target_pairs={{0,4},{1,5},{2,6},{3,7},{4,0},{5,1},{6,2},{7,3},{8,12},{9,13},{10,... | collective-permute-start | bytes 196616 | tf_op jit(solution)/shard_map/ppermute | solution.py:356
  66.3 5.0 %collective-permute-start.26 = (bf16[8,4096]{1,0:T(8,128)(2,1)S(1)}, bf16[8,4096]{1,0:T(8,128)(2,1)S(1)}, u32[]{:S(2)}, u32[]{:S(2)}) collective-permute-start(bf16[8,4096]{1,0:T(8,128)(2,1)S(1)} %get-tuple-element.21), channel_id=1, source_target_pairs={{0,8},{1,9},{2,10},{3,11},{4,12},{5,13},{6,14},{7,15},{8,0},{9,1},... | collective-permute-start | bytes 196616 | tf_op jit(solution)/shard_map/ppermute | solution.py:356
  67.2 6.2 %collective-permute-start.28 = (bf16[8,4096]{1,0:T(8,128)(2,1)S(1)}, bf16[8,4096]{1,0:T(8,128)(2,1)S(1)}, u32[]{:S(2)}, u32[]{:S(2)}) collective-permute-start(bf16[8,4096]{1,0:T(8,128)(2,1)S(1)} %get-tuple-element.22), channel_id=1, source_target_pairs={{0,24},{1,25},{2,26},{3,27},{4,28},{5,29},{6,30},{7,31},{8,16},{9,... | collective-permute-start | bytes 196616 | tf_op jit(solution)/shard_map/ppermute | solution.py:356
  70.0 5.2 %collective-permute-start.27 = (bf16[8,4096]{1,0:T(8,128)(2,1)S(1)}, bf16[8,4096]{1,0:T(8,128)(2,1)S(1)}, u32[]{:S(2)}, u32[]{:S(2)}) collective-permute-start(bf16[8,4096]{1,0:T(8,128)(2,1)S(1)} %get-tuple-element.23), channel_id=1, source_target_pairs={{0,16},{1,17},{2,18},{3,19},{4,20},{5,21},{6,22},{7,23},{8,24},{9,... | collective-permute-start | bytes 196616 | tf_op jit(solution)/shard_map/ppermute | solution.py:356
  70.0 5.1 %collective-permute-start.21 = (bf16[8,4096]{1,0:T(8,128)(2,1)S(1)}, bf16[8,4096]{1,0:T(8,128)(2,1)S(1)}, u32[]{:S(2)}, u32[]{:S(2)}) collective-permute-start(bf16[8,4096]{1,0:T(8,128)(2,1)S(1)} %fusion.3), channel_id=1, source_target_pairs={{0,2},{1,3},{2,0},{3,1},{4,6},{5,7},{6,4},{7,5},{8,10},{9,11},{10,... | collective-permute-start | bytes 196616 | tf_op jit(solution)/shard_map/ppermute | solution.py:356
  (9 other events, 90.9 us)

commit v13 on v12

--- a/solution.py
+++ b/solution.py
@@ -443,9 +443,10 @@
     near = sums[0][share + height :].reshape(-1, share, width)
     through = [v[height:] for v in back[len(plan.y) : x_end]]
     through = total_of([near[len(plan.x) :].reshape(-1, width)] + through)
-    others = total_of([column[share:]] + [v[:height] for v in back])
+    others = total_of([v[:height] for v in back[::-1]] + [column[share:]])
     others = plan.swaps(list(others.reshape(-1, share, width)), plan.z)
-    near_x = plan.swaps(list(near[: len(plan.x)]), plan.x)
+    wait = back[len(plan.y)][:share, :1] * 0
+    near_x = plan.swaps([value + wait for value in near[: len(plan.x)]], plan.x)
     near_y = plan.swaps(list(through.reshape(-1, share, width)), plan.y)
     moe_sum = total_of([column[:share]] + near_x + near_y + others)
     return (hidden + moe_sum).astype(BF)

time: 76.1 us -> 75.7 us (level)
  transfers between devices with their start and end apart: 29 -> 29, of which waited for: 17 -> 19; matrix products, arithmetic and copies ran while one was open for 1% -> 1% of each run, Pallas kernels for 5% -> 5%
where the time goes in v13:
time: 75.7 us; the launch traced here: 75.5 us
  waiting for transfers between devices  29.3 us (39%)
  starting transfers between devices  28 us (37%)
  Pallas kernels  15.7 us (21%)
  other arithmetic  1.76 us (2%)
    ppermute x29, waiting for transfers between devices, swap(): lax.ppermute(value, ('dp', 'tensor'), [(i, i ^ flip) for i in range(self....  29.3 us
    ppermute x29, starting transfers between devices, swap(): lax.ppermute(value, ('dp', 'tensor'), [(i, i ^ flip) for i in range(self....  28 us
    pallas_call x1, Pallas kernels, experts(): pl.pallas_call(functools.partial(expert_kernel, slots), out_shape=jax.Sha...  6.49 us
    pallas_call x2, Pallas kernels, attention(): pl.pallas_call(functools.partial(attention_kernel, flip), out_shape=tuple...  6.31 us
    pallas_call x1, Pallas kernels, projection(): pl.pallas_call(functools.partial(projection_kernel, parts, len(weights)),...  2.94 us
  transfers between devices with their start and end apart: 29, of which 19 were waited for; matrix products, arithmetic and copies ran while one was open for 1% of the time, Pallas kernels for 5%

profile of v13, /device:TPU:0, one launch (start us, length us, event | category | flops | bytes accessed | tf_op | source)
XLA Modules:
  0.0 75.5 jit_solution(1454901379679733384)
XLA Ops:
  0.0 2.4 %attention.2.refs_11_ = bf16[2,32,1152]{2,1,0:T(8,128)(2,1)S(1)} custom-call(s32[32]{0:T(128)} %refs_0_.3, bf16[32,32,128]{2,1,0:T(8,128)(2,1)} %refs_1_.3, bf16[32,2,128]{2,1,0:T(2,128)(2,1)} %refs_2_.3, bf16[32,2,128]{2,1,0:T(2,128)(2,1)} %refs_3_.3, bf16[32,2,32,128]{3,2,1,0:T(8,128)(2,1)} %refs_4_.3, bf16[32,2,32,128]{3,2,1,0:T(8,128)(2,1)} %refs_5_.3, ...), custom_call_target="tpu_custom_call" | custom-call | flops 1048576 | bytes 1048576 | tf_op jit(solution)/shard_map/attention/pallas_call | solution.py:199
  2.4 3.0 %collective-permute-start = (bf16[2,32,1152]{2,1,0:T(8,128)(2,1)S(1)}, bf16[2,32,1152]{2,1,0:T(8,128)(2,1)S(1)}, u32[]{:S(2)}, u32[]{:S(2)}) collective-permute-start(bf16[2,32,1152]{2,1,0:T(8,128)(2,1)S(1)} %attention.2.refs_11_), channel_id=1, source_target_pairs={{0,2},{1,3},{2,0},{3,1},{4,6},{5,7},{6,4},{7,5},{8,10},{9,11},{10,... | collective-permute-start | bytes 442376 | tf_op jit(solution)/shard_map/ppermute | solution.py:356
  5.5 3.9 %attention.3 = (bf16[2,32,1152]{2,1,0:T(8,128)(2,1)S(1)}, bf16[8,128]{1,0:T(8,128)(2,1)S(1)}, bf16[512,4096]{1,0:T(8,128)(2,1)S(1)}, bf16[512,4096]{1,0:T(8,128)(2,1)S(1)}) custom-call(s32[32]{0:T(128)} %refs_0_.3, bf16[32,32,128]{2,1,0:T(8,128)(2,1)} %refs_1_.3, bf16[32,2,128]{2,1,0:T(2,128)(2,1)} %refs_2_.3, bf16[32,2,128]{2,1,0:T(2,128)(2,1)} %refs_3_.3, ...), custom_call_target="tpu_custom_call" | custom-call | flops 9437184 | bytes 9437184 | tf_op jit(solution)/shard_map/attention/pallas_call | solution.py:199
  11.0 2.9 %projection.1 = (bf16[2,2,8,4096]{3,2,1,0:T(8,128)(2,1)S(1)}, bf16[1,4096,768]{2,1,0:T(8,128)(2,1)S(1)}) custom-call(bf16[32,1152]{1,0:T(8,128)(2,1)S(1)} %get-tuple-element.29.refs_0_, bf16[32,1152]{1,0:T(8,128)(2,1)S(1)} %collective-permute-done.1.refs_1_, bf16[32,1152]{1,0:T(8,128)(2,1)S(1)} %get-tuple-element.27.refs_2_, ...), custom_call_target="tpu_custom_call" | custom-call | tf_op jit(solution)/shard_map/projection/pallas_call | solution.py:261
  15.4 1.5 %collective-permute-start.4 = (bf16[8,4096]{1,0:T(8,128)(2,1)S(1)}, bf16[8,4096]{1,0:T(8,128)(2,1)S(1)}, u32[]{:S(2)}, u32[]{:S(2)}) collective-permute-start(bf16[8,4096]{1,0:T(8,128)(2,1)S(1)} %fusion.11), channel_id=1, source_target_pairs={{0,2},{1,3},{2,0},{3,1},{4,6},{5,7},{6,4},{7,5},{8,10},{9,11},{10,... | collective-permute-start | bytes 196616 | tf_op jit(solution)/shard_map/ppermute | solution.py:356
  16.9 2.9 %collective-permute-done.4 = bf16[8,4096]{1,0:T(8,128)(2,1)S(1)} collective-permute-done((bf16[8,4096]{1,0:T(8,128)(2,1)S(1)}, bf16[8,4096]{1,0:T(8,128)(2,1)S(1)}, u32[]{:S(2)}, u32[]{:S(2)}) %collective-permute-start.4) | collective-permute-done | bytes 65568 | tf_op jit(solution)/shard_map/ppermute | solution.py:356
  20.1 1.6 %collective-permute-start.5 = (bf16[8,4224]{1,0:T(8,128)(2,1)S(1)}, bf16[8,4224]{1,0:T(8,128)(2,1)S(1)}, u32[]{:S(2)}, u32[]{:S(2)}) collective-permute-start(bf16[8,4224]{1,0:T(8,128)(2,1)S(1)} %pad_maximum_fusion.1), channel_id=1, source_target_pairs={{0,8},{1,9},{2,10},{3,11},{4,12},{5,13},{6,14},{7,15},{8,0},{9,1},... | collective-permute-start | bytes 202760 | tf_op jit(solution)/shard_map/ppermute | solution.py:356
  21.7 2.6 %collective-permute-start.6 = (bf16[8,4224]{1,0:T(8,128)(2,1)S(1)}, bf16[8,4224]{1,0:T(8,128)(2,1)S(1)}, u32[]{:S(2)}, u32[]{:S(2)}) collective-permute-start(bf16[8,4224]{1,0:T(8,128)(2,1)S(1)} %pad_maximum_fusion.1), channel_id=1, source_target_pairs={{0,16},{1,17},{2,18},{3,19},{4,20},{5,21},{6,22},{7,23},{8,24},{9,... | collective-permute-start | bytes 202760 | tf_op jit(solution)/shard_map/ppermute | solution.py:356
  24.8 2.0 %collective-permute-start.9 = (bf16[8,4224]{1,0:T(8,128)(2,1)S(1)}, bf16[8,4224]{1,0:T(8,128)(2,1)S(1)}, u32[]{:S(2)}, u32[]{:S(2)}) collective-permute-start(bf16[8,4224]{1,0:T(8,128)(2,1)S(1)} %get-tuple-element.45), channel_id=1, source_target_pairs={{0,2},{1,3},{2,0},{3,1},{4,6},{5,7},{6,4},{7,5},{8,10},{9,11},{10,... | collective-permute-start | bytes 202760 | tf_op jit(solution)/shard_map/ppermute | solution.py:356
  26.7 1.5 %collective-permute-start.8 = (bf16[8,4224]{1,0:T(8,128)(2,1)S(1)}, bf16[8,4224]{1,0:T(8,128)(2,1)S(1)}, u32[]{:S(2)}, u32[]{:S(2)}) collective-permute-start(bf16[8,4224]{1,0:T(8,128)(2,1)S(1)} %get-tuple-element.45), channel_id=1, source_target_pairs={{0,4},{1,5},{2,6},{3,7},{4,0},{5,1},{6,2},{7,3},{8,12},{9,13},{10,... | collective-permute-start | bytes 202760 | tf_op jit(solution)/shard_map/ppermute | solution.py:356
  28.9 1.5 %collective-permute-done.7 = bf16[8,4224]{1,0:T(8,128)(2,1)S(1)} collective-permute-done((bf16[8,4224]{1,0:T(8,128)(2,1)S(1)}, bf16[8,4224]{1,0:T(8,128)(2,1)S(1)}, u32[]{:S(2)}, u32[]{:S(2)}) %collective-permute-start.7) | collective-permute-done | bytes 67616 | tf_op jit(solution)/shard_map/ppermute | solution.py:356
  30.4 2.3 %collective-permute-start.12 = (bf16[24,4224]{1,0:T(8,128)(2,1)S(1)}, bf16[24,4224]{1,0:T(8,128)(2,1)S(1)}, u32[]{:S(2)}, u32[]{:S(2)}) collective-permute-start(bf16[24,4224]{1,0:T(8,128)(2,1)S(1)} %get-tuple-element.36), channel_id=1, source_target_pairs={{0,6},{1,7},{2,4},{3,5},{4,2},{5,3},{6,0},{7,1},{8,14},{9,15},{10,... | collective-permute-start | bytes 608264 | tf_op jit(solution)/shard_map/ppermute | solution.py:356
  34.2 5.0 %collective-permute-done.12 = bf16[24,4224]{1,0:T(8,128)(2,1)S(1)} collective-permute-done((bf16[24,4224]{1,0:T(8,128)(2,1)S(1)}, bf16[24,4224]{1,0:T(8,128)(2,1)S(1)}, u32[]{:S(2)}, u32[]{:S(2)}) %collective-permute-start.12) | collective-permute-done | bytes 202784 | tf_op jit(solution)/shard_map/ppermute | solution.py:356
  39.2 1.3 %collective-permute-done.10 = bf16[24,4224]{1,0:T(8,128)(2,1)S(1)} collective-permute-done((bf16[24,4224]{1,0:T(8,128)(2,1)S(1)}, bf16[24,4224]{1,0:T(8,128)(2,1)S(1)}, u32[]{:S(2)}, u32[]{:S(2)}) %collective-permute-start.10) | collective-permute-done | bytes 202784 | tf_op jit(solution)/shard_map/ppermute | solution.py:356
  42.0 1.0 %collective-permute-done.15 = bf16[32,4224]{1,0:T(8,128)(2,1)S(1)} collective-permute-done((bf16[32,4224]{1,0:T(8,128)(2,1)S(1)}, bf16[32,4224]{1,0:T(8,128)(2,1)S(1)}, u32[]{:S(2)}, u32[]{:S(2)}) %collective-permute-start.15) | collective-permute-done | bytes 270368 | tf_op jit(solution)/shard_map/ppermute | solution.py:356
  43.1 6.5 %experts.1 = bf16[256,4096]{1,0:T(8,128)(2,1)S(1)} custom-call(bf16[256,4224]{1,0:T(8,128)(2,1)S(1)} %constant_dynamic-update-slice_fusion.9.x_ref, bf16[1,4096,768]{2,1,0:T(8,128)(2,1)S(1)} %get-tuple-element.16.gate, bf16[1,4096,768]{2,1,0:T(8,128)(2,1)S(1)} %bitcast.30, bf16[1,768,4096]{2,1,0:T(8,128)(2,1)} %down_hbm.1), custom_call_target="tpu_custom_call" | custom-call | tf_op jit(solution)/shard_map/experts/pallas_call | solution.py:327
  51.5 2.1 %collective-permute-start.23 = (bf16[24,4096]{1,0:T(8,128)(2,1)S(1)}, bf16[24,4096]{1,0:T(8,128)(2,1)S(1)}, u32[]{:S(2)}, u32[]{:S(2)}) collective-permute-start(bf16[24,4096]{1,0:T(8,128)(2,1)S(1)} %get-tuple-element.17), channel_id=1, source_target_pairs={{0,6},{1,7},{2,4},{3,5},{4,2},{5,3},{6,0},{7,1},{8,14},{9,15},{10,... | collective-permute-start | bytes 589832 | tf_op jit(solution)/shard_map/ppermute | solution.py:356
  55.3 5.0 %collective-permute-done.23 = bf16[24,4096]{1,0:T(8,128)(2,1)S(1)} collective-permute-done((bf16[24,4096]{1,0:T(8,128)(2,1)S(1)}, bf16[24,4096]{1,0:T(8,128)(2,1)S(1)}, u32[]{:S(2)}, u32[]{:S(2)}) %collective-permute-start.23) | collective-permute-done | bytes 196640 | tf_op jit(solution)/shard_map/ppermute | solution.py:356
  60.3 3.5 %collective-permute-done.25 = bf16[24,4096]{1,0:T(8,128)(2,1)S(1)} collective-permute-done((bf16[24,4096]{1,0:T(8,128)(2,1)S(1)}, bf16[24,4096]{1,0:T(8,128)(2,1)S(1)}, u32[]{:S(2)}, u32[]{:S(2)}) %collective-permute-start.25) | collective-permute-done | bytes 196640 | tf_op jit(solution)/shard_map/ppermute | solution.py:356
  63.7 1.1 %collective-permute-done.19 = bf16[32,4096]{1,0:T(8,128)(2,1)S(1)} collective-permute-done((bf16[32,4096]{1,0:T(8,128)(2,1)S(1)}, bf16[32,4096]{1,0:T(8,128)(2,1)S(1)}, u32[]{:S(2)}, u32[]{:S(2)}) %collective-permute-start.19) | collective-permute-done | bytes 262176 | tf_op jit(solution)/shard_map/ppermute | solution.py:356
  65.7 3.1 %collective-permute-start.28 = (bf16[8,4096]{1,0:T(8,128)(2,1)S(1)}, bf16[8,4096]{1,0:T(8,128)(2,1)S(1)}, u32[]{:S(2)}, u32[]{:S(2)}) collective-permute-start(bf16[8,4096]{1,0:T(8,128)(2,1)S(1)} %get-tuple-element.24), channel_id=1, source_target_pairs={{0,24},{1,25},{2,26},{3,27},{4,28},{5,29},{6,30},{7,31},{8,16},{9,... | collective-permute-start | bytes 196616 | tf_op jit(solution)/shard_map/ppermute | solution.py:356
  69.0 1.5 %collective-permute-start.20 = (bf16[8,4096]{1,0:T(8,128)(2,1)S(1)}, bf16[8,4096]{1,0:T(8,128)(2,1)S(1)}, u32[]{:S(2)}, u32[]{:S(2)}) collective-permute-start(bf16[8,4096]{1,0:T(8,128)(2,1)S(1)} %get-tuple-element.21), channel_id=1, source_target_pairs={{0,4},{1,5},{2,6},{3,7},{4,0},{5,1},{6,2},{7,3},{8,12},{9,13},{10,... | collective-permute-start | bytes 196616 | tf_op jit(solution)/shard_map/ppermute | solution.py:356
  71.2 1.0 %collective-permute-done.28 = bf16[8,4096]{1,0:T(8,128)(2,1)S(1)} collective-permute-done((bf16[8,4096]{1,0:T(8,128)(2,1)S(1)}, bf16[8,4096]{1,0:T(8,128)(2,1)S(1)}, u32[]{:S(2)}, u32[]{:S(2)}) %collective-permute-start.28) | collective-permute-done | bytes 65568 | tf_op jit(solution)/shard_map/ppermute | solution.py:356
  72.3 2.1 %collective-permute-done.27 = bf16[8,4096]{1,0:T(8,128)(2,1)S(1)} collective-permute-done((bf16[8,4096]{1,0:T(8,128)(2,1)S(1)}, bf16[8,4096]{1,0:T(8,128)(2,1)S(1)}, u32[]{:S(2)}, u32[]{:S(2)}) %collective-permute-start.27) | collective-permute-done | bytes 65568 | tf_op jit(solution)/shard_map/ppermute | solution.py:356
  (82 shorter events, 13.8 us)
Async XLA Ops:
  2.4 7.0 %collective-permute-start = (bf16[2,32,1152]{2,1,0:T(8,128)(2,1)S(1)}, bf16[2,32,1152]{2,1,0:T(8,128)(2,1)S(1)}, u32[]{:S(2)}, u32[]{:S(2)}) collective-permute-start(bf16[2,32,1152]{2,1,0:T(8,128)(2,1)S(1)} %attention.2.refs_11_), channel_id=1, source_target_pairs={{0,2},{1,3},{2,0},{3,1},{4,6},{5,7},{6,4},{7,5},{8,10},{9,11},{10,... | collective-permute-start | bytes 442376 | tf_op jit(solution)/shard_map/ppermute | solution.py:356
  15.4 4.4 %collective-permute-start.4 = (bf16[8,4096]{1,0:T(8,128)(2,1)S(1)}, bf16[8,4096]{1,0:T(8,128)(2,1)S(1)}, u32[]{:S(2)}, u32[]{:S(2)}) collective-permute-start(bf16[8,4096]{1,0:T(8,128)(2,1)S(1)} %fusion.11), channel_id=1, source_target_pairs={{0,2},{1,3},{2,0},{3,1},{4,6},{5,7},{6,4},{7,5},{8,10},{9,11},{10,... | collective-permute-start | bytes 196616 | tf_op jit(solution)/shard_map/ppermute | solution.py:356
  20.1 4.5 %collective-permute-start.5 = (bf16[8,4224]{1,0:T(8,128)(2,1)S(1)}, bf16[8,4224]{1,0:T(8,128)(2,1)S(1)}, u32[]{:S(2)}, u32[]{:S(2)}) collective-permute-start(bf16[8,4224]{1,0:T(8,128)(2,1)S(1)} %pad_maximum_fusion.1), channel_id=1, source_target_pairs={{0,8},{1,9},{2,10},{3,11},{4,12},{5,13},{6,14},{7,15},{8,0},{9,1},... | collective-permute-start | bytes 202760 | tf_op jit(solution)/shard_map/ppermute | solution.py:356
  21.7 7.1 %collective-permute-start.6 = (bf16[8,4224]{1,0:T(8,128)(2,1)S(1)}, bf16[8,4224]{1,0:T(8,128)(2,1)S(1)}, u32[]{:S(2)}, u32[]{:S(2)}) collective-permute-start(bf16[8,4224]{1,0:T(8,128)(2,1)S(1)} %pad_maximum_fusion.1), channel_id=1, source_target_pairs={{0,16},{1,17},{2,18},{3,19},{4,20},{5,21},{6,22},{7,23},{8,24},{9,... | collective-permute-start | bytes 202760 | tf_op jit(solution)/shard_map/ppermute | solution.py:356
  24.3 6.1 %collective-permute-start.7 = (bf16[8,4224]{1,0:T(8,128)(2,1)S(1)}, bf16[8,4224]{1,0:T(8,128)(2,1)S(1)}, u32[]{:S(2)}, u32[]{:S(2)}) collective-permute-start(bf16[8,4224]{1,0:T(8,128)(2,1)S(1)} %pad_maximum_fusion.1), channel_id=1, source_target_pairs={{0,24},{1,25},{2,26},{3,27},{4,28},{5,29},{6,30},{7,31},{8,16},{9,... | collective-permute-start | bytes 202760 | tf_op jit(solution)/shard_map/ppermute | solution.py:356
  24.8 8.7 %collective-permute-start.9 = (bf16[8,4224]{1,0:T(8,128)(2,1)S(1)}, bf16[8,4224]{1,0:T(8,128)(2,1)S(1)}, u32[]{:S(2)}, u32[]{:S(2)}) collective-permute-start(bf16[8,4224]{1,0:T(8,128)(2,1)S(1)} %get-tuple-element.45), channel_id=1, source_target_pairs={{0,2},{1,3},{2,0},{3,1},{4,6},{5,7},{6,4},{7,5},{8,10},{9,11},{10,... | collective-permute-start | bytes 202760 | tf_op jit(solution)/shard_map/ppermute | solution.py:356
  26.7 7.4 %collective-permute-start.8 = (bf16[8,4224]{1,0:T(8,128)(2,1)S(1)}, bf16[8,4224]{1,0:T(8,128)(2,1)S(1)}, u32[]{:S(2)}, u32[]{:S(2)}) collective-permute-start(bf16[8,4224]{1,0:T(8,128)(2,1)S(1)} %get-tuple-element.45), channel_id=1, source_target_pairs={{0,4},{1,5},{2,6},{3,7},{4,0},{5,1},{6,2},{7,3},{8,12},{9,13},{10,... | collective-permute-start | bytes 202760 | tf_op jit(solution)/shard_map/ppermute | solution.py:356
  30.4 8.7 %collective-permute-start.12 = (bf16[24,4224]{1,0:T(8,128)(2,1)S(1)}, bf16[24,4224]{1,0:T(8,128)(2,1)S(1)}, u32[]{:S(2)}, u32[]{:S(2)}) collective-permute-start(bf16[24,4224]{1,0:T(8,128)(2,1)S(1)} %get-tuple-element.36), channel_id=1, source_target_pairs={{0,6},{1,7},{2,4},{3,5},{4,2},{5,3},{6,0},{7,1},{8,14},{9,15},{10,... | collective-permute-start | bytes 608264 | tf_op jit(solution)/shard_map/ppermute | solution.py:356
  32.8 7.7 %collective-permute-start.10 = (bf16[24,4224]{1,0:T(8,128)(2,1)S(1)}, bf16[24,4224]{1,0:T(8,128)(2,1)S(1)}, u32[]{:S(2)}, u32[]{:S(2)}) collective-permute-start(bf16[24,4224]{1,0:T(8,128)(2,1)S(1)} %get-tuple-element.36), channel_id=1, source_target_pairs={{0,2},{1,3},{2,0},{3,1},{4,6},{5,7},{6,4},{7,5},{8,10},{9,11},{10,... | collective-permute-start | bytes 608264 | tf_op jit(solution)/shard_map/ppermute | solution.py:356
  33.5 8.0 %collective-permute-start.11 = (bf16[32,4224]{1,0:T(8,128)(2,1)S(1)}, bf16[32,4224]{1,0:T(8,128)(2,1)S(1)}, u32[]{:S(2)}, u32[]{:S(2)}) collective-permute-start(bf16[32,4224]{1,0:T(8,128)(2,1)S(1)} %pad_maximum_fusion), channel_id=1, source_target_pairs={{0,4},{1,5},{2,6},{3,7},{4,0},{5,1},{6,2},{7,3},{8,12},{9,13},{10,... | collective-permute-start | bytes 811016 | tf_op jit(solution)/shard_map/ppermute | solution.py:356
  34.1 7.4 %collective-permute-start.13 = (bf16[48,4224]{1,0:T(8,128)(2,1)S(1)}, bf16[48,4224]{1,0:T(8,128)(2,1)S(1)}, u32[]{:S(2)}, u32[]{:S(2)}) collective-permute-start(bf16[48,4224]{1,0:T(8,128)(2,1)S(1)} %get-tuple-element.30), channel_id=1, source_target_pairs={{0,1},{1,0},{2,3},{3,2},{4,5},{5,4},{6,7},{7,6},{8,9},{9,8},{10,11... | collective-permute-start | bytes 1216520 | tf_op jit(solution)/shard_map/ppermute | solution.py:356
  39.2 3.8 %collective-permute-start.16 = (bf16[24,4224]{1,0:T(8,128)(2,1)S(1)}, bf16[24,4224]{1,0:T(8,128)(2,1)S(1)}, u32[]{:S(2)}, u32[]{:S(2)}) collective-permute-start(bf16[24,4224]{1,0:T(8,128)(2,1)S(1)} %collective-permute-done.12), channel_id=1, source_target_pairs={{0,1},{1,0},{2,3},{3,2},{4,5},{5,4},{6,7},{7,6},{8,9},{9,8},{10,11... | collective-permute-start | bytes 608264 | tf_op jit(solution)/shard_map/ppermute | solution.py:356
  41.5 1.5 %collective-permute-start.15 = (bf16[32,4224]{1,0:T(8,128)(2,1)S(1)}, bf16[32,4224]{1,0:T(8,128)(2,1)S(1)}, u32[]{:S(2)}, u32[]{:S(2)}) collective-permute-start(bf16[32,4224]{1,0:T(8,128)(2,1)S(1)} %collective-permute-done.11), channel_id=1, source_target_pairs={{0,1},{1,0},{2,3},{3,2},{4,5},{5,4},{6,7},{7,6},{8,9},{9,8},{10,11... | collective-permute-start | bytes 811016 | tf_op jit(solution)/shard_map/ppermute | solution.py:356
  49.8 1.6 %collective-permute-start.24 = (bf16[24,4096]{1,0:T(8,128)(2,1)S(1)}, bf16[24,4096]{1,0:T(8,128)(2,1)S(1)}, u32[]{:S(2)}, u32[]{:S(2)}) collective-permute-start(bf16[24,4096]{1,0:T(8,128)(2,1)S(1)} %get-tuple-element.20), channel_id=1, source_target_pairs={{0,1},{1,0},{2,3},{3,2},{4,5},{5,4},{6,7},{7,6},{8,9},{9,8},{10,11... | collective-permute-start | bytes 589832 | tf_op jit(solution)/shard_map/ppermute | solution.py:356
  50.3 4.3 %collective-permute-start.18 = (bf16[32,4096]{1,0:T(8,128)(2,1)S(1)}, bf16[32,4096]{1,0:T(8,128)(2,1)S(1)}, u32[]{:S(2)}, u32[]{:S(2)}) collective-permute-start(bf16[32,4096]{1,0:T(8,128)(2,1)S(1)} %slice.121), channel_id=1, source_target_pairs={{0,1},{1,0},{2,3},{3,2},{4,5},{5,4},{6,7},{7,6},{8,9},{9,8},{10,11... | collective-permute-start | bytes 786440 | tf_op jit(solution)/shard_map/ppermute | solution.py:356
  50.5 4.8 %collective-permute-start.17 = (bf16[48,4096]{1,0:T(8,128)(2,1)S(1)}, bf16[48,4096]{1,0:T(8,128)(2,1)S(1)}, u32[]{:S(2)}, u32[]{:S(2)}) collective-permute-start(bf16[48,4096]{1,0:T(8,128)(2,1)S(1)} %slice.117), channel_id=1, source_target_pairs={{0,1},{1,0},{2,3},{3,2},{4,5},{5,4},{6,7},{7,6},{8,9},{9,8},{10,11... | collective-permute-start | bytes 1179656 | tf_op jit(solution)/shard_map/ppermute | solution.py:356
  51.5 8.7 %collective-permute-start.23 = (bf16[24,4096]{1,0:T(8,128)(2,1)S(1)}, bf16[24,4096]{1,0:T(8,128)(2,1)S(1)}, u32[]{:S(2)}, u32[]{:S(2)}) collective-permute-start(bf16[24,4096]{1,0:T(8,128)(2,1)S(1)} %get-tuple-element.17), channel_id=1, source_target_pairs={{0,6},{1,7},{2,4},{3,5},{4,2},{5,3},{6,0},{7,1},{8,14},{9,15},{10,... | collective-permute-start | bytes 589832 | tf_op jit(solution)/shard_map/ppermute | solution.py:356
  53.6 10.1 %collective-permute-start.25 = (bf16[24,4096]{1,0:T(8,128)(2,1)S(1)}, bf16[24,4096]{1,0:T(8,128)(2,1)S(1)}, u32[]{:S(2)}, u32[]{:S(2)}) collective-permute-start(bf16[24,4096]{1,0:T(8,128)(2,1)S(1)} %get-tuple-element.18), channel_id=1, source_target_pairs={{0,2},{1,3},{2,0},{3,1},{4,6},{5,7},{6,4},{7,5},{8,10},{9,11},{10,... | collective-permute-start | bytes 589832 | tf_op jit(solution)/shard_map/ppermute | solution.py:356
  54.7 10.1 %collective-permute-start.19 = (bf16[32,4096]{1,0:T(8,128)(2,1)S(1)}, bf16[32,4096]{1,0:T(8,128)(2,1)S(1)}, u32[]{:S(2)}, u32[]{:S(2)}) collective-permute-start(bf16[32,4096]{1,0:T(8,128)(2,1)S(1)} %add_convert_fusion), channel_id=1, source_target_pairs={{0,4},{1,5},{2,6},{3,7},{4,0},{5,1},{6,2},{7,3},{8,12},{9,13},{10,... | collective-permute-start | bytes 786440 | tf_op jit(solution)/shard_map/ppermute | solution.py:356
  64.9 6.3 %collective-permute-start.26 = (bf16[8,4096]{1,0:T(8,128)(2,1)S(1)}, bf16[8,4096]{1,0:T(8,128)(2,1)S(1)}, u32[]{:S(2)}, u32[]{:S(2)}) collective-permute-start(bf16[8,4096]{1,0:T(8,128)(2,1)S(1)} %get-tuple-element.23), channel_id=1, source_target_pairs={{0,8},{1,9},{2,10},{3,11},{4,12},{5,13},{6,14},{7,15},{8,0},{9,1},... | collective-permute-start | bytes 196616 | tf_op jit(solution)/shard_map/ppermute | solution.py:356
  65.7 6.6 %collective-permute-start.28 = (bf16[8,4096]{1,0:T(8,128)(2,1)S(1)}, bf16[8,4096]{1,0:T(8,128)(2,1)S(1)}, u32[]{:S(2)}, u32[]{:S(2)}) collective-permute-start(bf16[8,4096]{1,0:T(8,128)(2,1)S(1)} %get-tuple-element.24), channel_id=1, source_target_pairs={{0,24},{1,25},{2,26},{3,27},{4,28},{5,29},{6,30},{7,31},{8,16},{9,... | collective-permute-start | bytes 196616 | tf_op jit(solution)/shard_map/ppermute | solution.py:356
  68.8 5.6 %collective-permute-start.27 = (bf16[8,4096]{1,0:T(8,128)(2,1)S(1)}, bf16[8,4096]{1,0:T(8,128)(2,1)S(1)}, u32[]{:S(2)}, u32[]{:S(2)}) collective-permute-start(bf16[8,4096]{1,0:T(8,128)(2,1)S(1)} %get-tuple-element.25), channel_id=1, source_target_pairs={{0,16},{1,17},{2,18},{3,19},{4,20},{5,21},{6,22},{7,23},{8,24},{9,... | collective-permute-start | bytes 196616 | tf_op jit(solution)/shard_map/ppermute | solution.py:356
  69.0 5.4 %collective-permute-start.20 = (bf16[8,4096]{1,0:T(8,128)(2,1)S(1)}, bf16[8,4096]{1,0:T(8,128)(2,1)S(1)}, u32[]{:S(2)}, u32[]{:S(2)}) collective-permute-start(bf16[8,4096]{1,0:T(8,128)(2,1)S(1)} %get-tuple-element.21), channel_id=1, source_target_pairs={{0,4},{1,5},{2,6},{3,7},{4,0},{5,1},{6,2},{7,3},{8,12},{9,13},{10,... | collective-permute-start | bytes 196616 | tf_op jit(solution)/shard_map/ppermute | solution.py:356
  70.5 4.3 %collective-permute-start.21 = (bf16[8,4096]{1,0:T(8,128)(2,1)S(1)}, bf16[8,4096]{1,0:T(8,128)(2,1)S(1)}, u32[]{:S(2)}, u32[]{:S(2)}) collective-permute-start(bf16[8,4096]{1,0:T(8,128)(2,1)S(1)} %get-tuple-element.22), channel_id=1, source_target_pairs={{0,2},{1,3},{2,0},{3,1},{4,6},{5,7},{6,4},{7,5},{8,10},{9,11},{10,... | collective-permute-start | bytes 196616 | tf_op jit(solution)/shard_map/ppermute | solution.py:356
  (9 other events, 90.9 us)

commit v14 on v13

--- a/solution.py
+++ b/solution.py
@@ -211,9 +211,7 @@
 def projection_kernel(parts, cuts, *refs):
     got = refs[:parts]
     w_refs, refs = refs[parts : parts + cuts], refs[parts + cuts :]
-    ahead_hbm, out_ref, ahead_ref, attn, sem = refs
-    ahead = pltpu.make_async_copy(ahead_hbm, ahead_ref, sem)
-    ahead.start()
+    out_ref, attn = refs
     tensor_pos = lax.axis_index("tensor")
     width = w_refs[0].shape[1]
     depth = attn.shape[1]
@@ -249,10 +247,9 @@
             slot = tensor_pos ^ t
             block = result[t * share : (t + 1) * share].astype(BF)
             out_ref[slot & 1, slot >> 1, :, cols] = block
-    ahead.wait()
-
-
-def projection(got, weights, share, later):
+
+
+def projection(got, weights, share):
     parts = len(got)
     rows = got[0].shape[0]
     depth = sum(w.shape[0] for w in weights)
@@ -260,19 +257,19 @@
     vmem = pl.BlockSpec(memory_space=pltpu.VMEM)
     return pl.pallas_call(
         functools.partial(projection_kernel, parts, len(weights)),
-        out_shape=(
-            jax.ShapeDtypeStruct((2, parts // 2, share, width), BF),
-            pltpu.VMEM(later.shape, later.dtype),
-        ),
-        in_specs=[vmem] * (parts + len(weights)) + [pl.BlockSpec(memory_space=pltpu.HBM)],
-        out_specs=(vmem, vmem),
-        scratch_shapes=[pltpu.VMEM((rows, depth), BF), pltpu.SemaphoreType.DMA],
+        out_shape=jax.ShapeDtypeStruct((2, parts // 2, share, width), BF),
+        in_specs=[vmem] * (parts + len(weights)),
+        out_specs=vmem,
+        scratch_shapes=[pltpu.VMEM((rows, depth), BF)],
         compiler_params=pltpu.CompilerParams(vmem_limit_bytes=12 * MIB),
         name="projection",
-    )(*got, *weights, in_hbm(later))
-
-
-def expert_kernel(slots, x_ref, gate, up, down_hbm, out_ref, down, xc, act, res, sem):
+    )(*got, *weights)
+
+
+def expert_kernel(slots, sizes, *refs):
+    x_ref, gate, up, down_hbm = refs[:4]
+    outs = refs[4 : 4 + len(sizes)]
+    down, xc, act, res, sem = refs[4 + len(sizes) :]
     own = lax.axis_index("dp") * lax.axis_size("tensor") + lax.axis_index("tensor")
     rows = x_ref.shape[0]
     _, width, hidden = gate.shape
@@ -316,19 +313,22 @@
         down_copy(i).wait()
         cols = slice(i * dsize, (i + 1) * dsize)
         res[:slots, :] = matmul(act[...], down[:, cols]).astype(BF)
-        out_ref[:, cols] = matmul(spread, res[...]).astype(BF)
-
-
-def experts(x, expert_gate, expert_up, expert_down, share):
+        result, start = matmul(spread, res[...]), 0
+        for size, out in zip(sizes, outs):
+            out[:, cols] = result[start : start + size].astype(BF)
+            start += size
+
+
+def experts(x, expert_gate, expert_up, expert_down, share, sizes):
     rows = x.shape[0]
     _, width, hidden = expert_gate.shape
     slots = rows // share * CAP
     vmem = pl.BlockSpec(memory_space=pltpu.VMEM)
     return pl.pallas_call(
-        functools.partial(expert_kernel, slots),
-        out_shape=jax.ShapeDtypeStruct((rows, width), BF),
+        functools.partial(expert_kernel, slots, sizes),
+        out_shape=tuple(jax.ShapeDtypeStruct((size, width), BF) for size in sizes),
         in_specs=[vmem] * 3 + [pl.BlockSpec(memory_space=pltpu.HBM)],
-        out_specs=vmem,
+        out_specs=(vmem,) * len(sizes),
         scratch_shapes=[
             pltpu.VMEM((hidden, width), BF),
             pltpu.VMEM((slots, width), BF),
@@ -405,7 +405,7 @@
                 pair = plan.swap(pair, far)
             got += [pair[0], plan.swap(pair[1], plan.core)]
     _, table, *weights = results
-    partial, expert_gate = projection(got, weights, share, expert_gate)
+    partial = projection(got, weights, share)
     pair = total_of([partial[0], plan.swap(partial[1], plan.core)])
     projected = total_of([pair[0]] + plan.swaps(list(pair[1:]), plan.y))
     hidden = residual_in.astype(F32) + projected
@@ -423,19 +423,13 @@
     pieces = [jnp.concatenate([mine] + others + near_x + near_y)] + far_y + far_x + far_diagonal
     x = jnp.concatenate(pieces + [plan.swap(piece, plan.core) for piece in pieces])
 
-    result = experts(x, expert_gate, expert_up, expert_down, share)
-
-    sizes = [piece.shape[0] for piece in pieces]
-    starts = [sum(sizes[:i]) for i in range(len(sizes) + 1)]
-    every = starts[-1]
+    sizes = [piece.shape[0] for piece in pieces] * 2
+    results = experts(x, expert_gate, expert_up, expert_down, share, sizes)
+
+    half = len(pieces)
     sums = [
-        total_of(
-            [
-                result[starts[i] : starts[i + 1]],
-                plan.swap(result[every + starts[i] : every + starts[i + 1]], plan.core),
-            ]
-        )
-        for i in reversed(range(len(sizes)))
+        total_of([results[i], plan.swap(results[half + i], plan.core)])
+        for i in reversed(range(half))
     ][::-1]
     back = plan.swaps(sums[1:], plan.y + plan.x + plan.diagonal)
     height, x_end = rest.shape[0], len(plan.y) + len(plan.x)

time: 75.7 us -> 74.2 us (0.980)
  Pallas kernels: 15.7 us -> 14.7 us
    pallas_call x1, Pallas kernels: 2.94 us -> 1.79 us  [projection(): pl.pallas_call(functools.partial(projection_kernel, parts, len(weights)),...]
  transfers between devices with their start and end apart: 29 -> 29, of which waited for: 19 -> 18; matrix products, arithmetic and copies ran while one was open for 1% -> 1% of each run, Pallas kernels for 5% -> 5%
where the time goes in v14:
time: 74.2 us; the launch traced here: 74 us
  waiting for transfers between devices  29.3 us (39%)
  starting transfers between devices  27.7 us (37%)
  Pallas kernels  14.7 us (20%)
  other arithmetic  1.77 us (2%)
    ppermute x29, waiting for transfers between devices, swap(): lax.ppermute(value, ('dp', 'tensor'), [(i, i ^ flip) for i in range(self....  29.3 us
    ppermute x29, starting transfers between devices, swap(): lax.ppermute(value, ('dp', 'tensor'), [(i, i ^ flip) for i in range(self....  27.7 us
    pallas_call x1, Pallas kernels, experts(): pl.pallas_call(functools.partial(expert_kernel, slots, sizes), out_shape=...  6.48 us
    pallas_call x2, Pallas kernels, attention(): pl.pallas_call(functools.partial(attention_kernel, flip), out_shape=tuple...  6.45 us
    pallas_call x1, Pallas kernels, projection(): pl.pallas_call(functools.partial(projection_kernel, parts, len(weights)),...  1.79 us
  transfers between devices with their start and end apart: 29, of which 18 were waited for; matrix products, arithmetic and copies ran while one was open for 1% of the time, Pallas kernels for 5%

profile of v14, /device:TPU:0, one launch (start us, length us, event | category | flops | bytes accessed | tf_op | source)
XLA Modules:
  0.0 74.0 jit_solution(17463908756947287835)
XLA Ops:
  0.0 2.4 %attention.2.refs_11_ = bf16[2,32,1152]{2,1,0:T(8,128)(2,1)S(1)} custom-call(s32[32]{0:T(128)} %refs_0_.3, bf16[32,32,128]{2,1,0:T(8,128)(2,1)} %refs_1_.4, bf16[32,2,128]{2,1,0:T(2,128)(2,1)} %refs_2_.4, bf16[32,2,128]{2,1,0:T(2,128)(2,1)} %refs_3_.4, bf16[32,2,32,128]{3,2,1,0:T(8,128)(2,1)} %refs_4_.3, bf16[32,2,32,128]{3,2,1,0:T(8,128)(2,1)} %refs_5_.3, ...), custom_call_target="tpu_custom_call" | custom-call | flops 1048576 | bytes 1048576 | tf_op jit(solution)/shard_map/attention/pallas_call | solution.py:199
  2.4 3.0 %collective-permute-start = (bf16[2,32,1152]{2,1,0:T(8,128)(2,1)S(1)}, bf16[2,32,1152]{2,1,0:T(8,128)(2,1)S(1)}, u32[]{:S(2)}, u32[]{:S(2)}) collective-permute-start(bf16[2,32,1152]{2,1,0:T(8,128)(2,1)S(1)} %attention.2.refs_11_), channel_id=1, source_target_pairs={{0,2},{1,3},{2,0},{3,1},{4,6},{5,7},{6,4},{7,5},{8,10},{9,11},{10,... | collective-permute-start | bytes 442376 | tf_op jit(solution)/shard_map/ppermute | solution.py:356
  5.5 4.0 %attention.3 = (bf16[2,32,1152]{2,1,0:T(8,128)(2,1)S(1)}, bf16[8,128]{1,0:T(8,128)(2,1)S(1)}, bf16[512,4096]{1,0:T(8,128)(2,1)S(1)}, bf16[512,4096]{1,0:T(8,128)(2,1)S(1)}) custom-call(s32[32]{0:T(128)} %refs_0_.3, bf16[32,32,128]{2,1,0:T(8,128)(2,1)} %refs_1_.4, bf16[32,2,128]{2,1,0:T(2,128)(2,1)} %refs_2_.4, bf16[32,2,128]{2,1,0:T(2,128)(2,1)} %refs_3_.4, ...), custom_call_target="tpu_custom_call" | custom-call | flops 9437184 | bytes 9437184 | tf_op jit(solution)/shard_map/attention/pallas_call | solution.py:199
  11.1 1.8 %projection.1 = bf16[2,2,8,4096]{3,2,1,0:T(8,128)(2,1)S(1)} custom-call(bf16[32,1152]{1,0:T(8,128)(2,1)S(1)} %get-tuple-element.37.refs_0_, bf16[32,1152]{1,0:T(8,128)(2,1)S(1)} %collective-permute-done.1.refs_1_, bf16[32,1152]{1,0:T(8,128)(2,1)S(1)} %get-tuple-element.35.refs_2_, bf16[32,1152]{1,0:T(8,128)(2,1)S(1)} %collective-permute-done.2.refs_3_, ...), custom_call_target="tpu_custom_call" | custom-call | tf_op jit(solution)/shard_map/projection/pallas_call | solution.py:258
  13.3 1.0 %collective-permute-done.3 = bf16[2,8,4096]{2,1,0:T(8,128)(2,1)S(1)} collective-permute-done((bf16[2,8,4096]{2,1,0:T(8,128)(2,1)S(1)}, bf16[2,8,4096]{2,1,0:T(8,128)(2,1)S(1)}, u32[]{:S(2)}, u32[]{:S(2)}) %collective-permute-start.3) | collective-permute-done | bytes 131104 | tf_op jit(solution)/shard_map/ppermute | solution.py:356
  14.4 1.4 %collective-permute-start.4 = (bf16[8,4096]{1,0:T(8,128)(2,1)S(1)}, bf16[8,4096]{1,0:T(8,128)(2,1)S(1)}, u32[]{:S(2)}, u32[]{:S(2)}) collective-permute-start(bf16[8,4096]{1,0:T(8,128)(2,1)S(1)} %fusion.11), channel_id=1, source_target_pairs={{0,2},{1,3},{2,0},{3,1},{4,6},{5,7},{6,4},{7,5},{8,10},{9,11},{10,... | collective-permute-start | bytes 196616 | tf_op jit(solution)/shard_map/ppermute | solution.py:356
  15.8 3.0 %collective-permute-done.4 = bf16[8,4096]{1,0:T(8,128)(2,1)S(1)} collective-permute-done((bf16[8,4096]{1,0:T(8,128)(2,1)S(1)}, bf16[8,4096]{1,0:T(8,128)(2,1)S(1)}, u32[]{:S(2)}, u32[]{:S(2)}) %collective-permute-start.4) | collective-permute-done | bytes 65568 | tf_op jit(solution)/shard_map/ppermute | solution.py:356
  19.1 1.6 %collective-permute-start.5 = (bf16[8,4224]{1,0:T(8,128)(2,1)S(1)}, bf16[8,4224]{1,0:T(8,128)(2,1)S(1)}, u32[]{:S(2)}, u32[]{:S(2)}) collective-permute-start(bf16[8,4224]{1,0:T(8,128)(2,1)S(1)} %pad_maximum_fusion.1), channel_id=1, source_target_pairs={{0,8},{1,9},{2,10},{3,11},{4,12},{5,13},{6,14},{7,15},{8,0},{9,1},... | collective-permute-start | bytes 202760 | tf_op jit(solution)/shard_map/ppermute | solution.py:356
  20.7 2.6 %collective-permute-start.6 = (bf16[8,4224]{1,0:T(8,128)(2,1)S(1)}, bf16[8,4224]{1,0:T(8,128)(2,1)S(1)}, u32[]{:S(2)}, u32[]{:S(2)}) collective-permute-start(bf16[8,4224]{1,0:T(8,128)(2,1)S(1)} %pad_maximum_fusion.1), channel_id=1, source_target_pairs={{0,16},{1,17},{2,18},{3,19},{4,20},{5,21},{6,22},{7,23},{8,24},{9,... | collective-permute-start | bytes 202760 | tf_op jit(solution)/shard_map/ppermute | solution.py:356
  23.7 1.8 %collective-permute-start.9 = (bf16[8,4224]{1,0:T(8,128)(2,1)S(1)}, bf16[8,4224]{1,0:T(8,128)(2,1)S(1)}, u32[]{:S(2)}, u32[]{:S(2)}) collective-permute-start(bf16[8,4224]{1,0:T(8,128)(2,1)S(1)} %get-tuple-element.53), channel_id=1, source_target_pairs={{0,2},{1,3},{2,0},{3,1},{4,6},{5,7},{6,4},{7,5},{8,10},{9,11},{10,... | collective-permute-start | bytes 202760 | tf_op jit(solution)/shard_map/ppermute | solution.py:356
  25.6 1.5 %collective-permute-start.8 = (bf16[8,4224]{1,0:T(8,128)(2,1)S(1)}, bf16[8,4224]{1,0:T(8,128)(2,1)S(1)}, u32[]{:S(2)}, u32[]{:S(2)}) collective-permute-start(bf16[8,4224]{1,0:T(8,128)(2,1)S(1)} %get-tuple-element.53), channel_id=1, source_target_pairs={{0,4},{1,5},{2,6},{3,7},{4,0},{5,1},{6,2},{7,3},{8,12},{9,13},{10,... | collective-permute-start | bytes 202760 | tf_op jit(solution)/shard_map/ppermute | solution.py:356
  27.8 1.6 %collective-permute-done.7 = bf16[8,4224]{1,0:T(8,128)(2,1)S(1)} collective-permute-done((bf16[8,4224]{1,0:T(8,128)(2,1)S(1)}, bf16[8,4224]{1,0:T(8,128)(2,1)S(1)}, u32[]{:S(2)}, u32[]{:S(2)}) %collective-permute-start.7) | collective-permute-done | bytes 67616 | tf_op jit(solution)/shard_map/ppermute | solution.py:356
  29.4 2.2 %collective-permute-start.12 = (bf16[24,4224]{1,0:T(8,128)(2,1)S(1)}, bf16[24,4224]{1,0:T(8,128)(2,1)S(1)}, u32[]{:S(2)}, u32[]{:S(2)}) collective-permute-start(bf16[24,4224]{1,0:T(8,128)(2,1)S(1)} %get-tuple-element.44), channel_id=1, source_target_pairs={{0,6},{1,7},{2,4},{3,5},{4,2},{5,3},{6,0},{7,1},{8,14},{9,15},{10,... | collective-permute-start | bytes 608264 | tf_op jit(solution)/shard_map/ppermute | solution.py:356
  33.2 5.0 %collective-permute-done.12 = bf16[24,4224]{1,0:T(8,128)(2,1)S(1)} collective-permute-done((bf16[24,4224]{1,0:T(8,128)(2,1)S(1)}, bf16[24,4224]{1,0:T(8,128)(2,1)S(1)}, u32[]{:S(2)}, u32[]{:S(2)}) %collective-permute-start.12) | collective-permute-done | bytes 202784 | tf_op jit(solution)/shard_map/ppermute | solution.py:356
  38.2 1.3 %collective-permute-done.10 = bf16[24,4224]{1,0:T(8,128)(2,1)S(1)} collective-permute-done((bf16[24,4224]{1,0:T(8,128)(2,1)S(1)}, bf16[24,4224]{1,0:T(8,128)(2,1)S(1)}, u32[]{:S(2)}, u32[]{:S(2)}) %collective-permute-start.10) | collective-permute-done | bytes 202784 | tf_op jit(solution)/shard_map/ppermute | solution.py:356
  42.0 6.5 %experts.1 = (bf16[48,4096]{1,0:T(8,128)(2,1)S(1)}, bf16[24,4096]{1,0:T(8,128)(2,1)S(1)}, bf16[32,4096]{1,0:T(8,128)(2,1)S(1)}, bf16[24,4096]{1,0:T(8,128)(2,1)S...) custom-call(bf16[256,4224]{1,0:T(8,128)(2,1)S(1)} %constant_dynamic-, ...), custom_call_target="tpu_custom_call" | custom-call | tf_op jit(solution)/shard_map/experts/pallas_call | solution.py:327
  50.1 2.2 %collective-permute-start.23 = (bf16[24,4096]{1,0:T(8,128)(2,1)S(1)}, bf16[24,4096]{1,0:T(8,128)(2,1)S(1)}, u32[]{:S(2)}, u32[]{:S(2)}) collective-permute-start(bf16[24,4096]{1,0:T(8,128)(2,1)S(1)} %add_convert_fusion.2), channel_id=1, source_target_pairs={{0,6},{1,7},{2,4},{3,5},{4,2},{5,3},{6,0},{7,1},{8,14},{9,15},{10,... | collective-permute-start | bytes 589832 | tf_op jit(solution)/shard_map/ppermute | solution.py:356
  54.0 4.8 %collective-permute-done.23 = bf16[24,4096]{1,0:T(8,128)(2,1)S(1)} collective-permute-done((bf16[24,4096]{1,0:T(8,128)(2,1)S(1)}, bf16[24,4096]{1,0:T(8,128)(2,1)S(1)}, u32[]{:S(2)}, u32[]{:S(2)}) %collective-permute-start.23) | collective-permute-done | bytes 196640 | tf_op jit(solution)/shard_map/ppermute | solution.py:356
  58.8 3.4 %collective-permute-done.25 = bf16[24,4096]{1,0:T(8,128)(2,1)S(1)} collective-permute-done((bf16[24,4096]{1,0:T(8,128)(2,1)S(1)}, bf16[24,4096]{1,0:T(8,128)(2,1)S(1)}, u32[]{:S(2)}, u32[]{:S(2)}) %collective-permute-start.25) | collective-permute-done | bytes 196640 | tf_op jit(solution)/shard_map/ppermute | solution.py:356
  62.2 1.1 %collective-permute-done.19 = bf16[32,4096]{1,0:T(8,128)(2,1)S(1)} collective-permute-done((bf16[32,4096]{1,0:T(8,128)(2,1)S(1)}, bf16[32,4096]{1,0:T(8,128)(2,1)S(1)}, u32[]{:S(2)}, u32[]{:S(2)}) %collective-permute-start.19) | collective-permute-done | bytes 262176 | tf_op jit(solution)/shard_map/ppermute | solution.py:356
  64.2 3.1 %collective-permute-start.28 = (bf16[8,4096]{1,0:T(8,128)(2,1)S(1)}, bf16[8,4096]{1,0:T(8,128)(2,1)S(1)}, u32[]{:S(2)}, u32[]{:S(2)}) collective-permute-start(bf16[8,4096]{1,0:T(8,128)(2,1)S(1)} %get-tuple-element.32), channel_id=1, source_target_pairs={{0,24},{1,25},{2,26},{3,27},{4,28},{5,29},{6,30},{7,31},{8,16},{9,... | collective-permute-start | bytes 196616 | tf_op jit(solution)/shard_map/ppermute | solution.py:356
  67.5 1.6 %collective-permute-start.20 = (bf16[8,4096]{1,0:T(8,128)(2,1)S(1)}, bf16[8,4096]{1,0:T(8,128)(2,1)S(1)}, u32[]{:S(2)}, u32[]{:S(2)}) collective-permute-start(bf16[8,4096]{1,0:T(8,128)(2,1)S(1)} %get-tuple-element.29), channel_id=1, source_target_pairs={{0,4},{1,5},{2,6},{3,7},{4,0},{5,1},{6,2},{7,3},{8,12},{9,13},{10,... | collective-permute-start | bytes 196616 | tf_op jit(solution)/shard_map/ppermute | solution.py:356
  69.6 1.0 %collective-permute-done.28 = bf16[8,4096]{1,0:T(8,128)(2,1)S(1)} collective-permute-done((bf16[8,4096]{1,0:T(8,128)(2,1)S(1)}, bf16[8,4096]{1,0:T(8,128)(2,1)S(1)}, u32[]{:S(2)}, u32[]{:S(2)}) %collective-permute-start.28) | collective-permute-done | bytes 65568 | tf_op jit(solution)/shard_map/ppermute | solution.py:356
  70.7 2.1 %collective-permute-done.27 = bf16[8,4096]{1,0:T(8,128)(2,1)S(1)} collective-permute-done((bf16[8,4096]{1,0:T(8,128)(2,1)S(1)}, bf16[8,4096]{1,0:T(8,128)(2,1)S(1)}, u32[]{:S(2)}, u32[]{:S(2)}) %collective-permute-start.27) | collective-permute-done | bytes 65568 | tf_op jit(solution)/shard_map/ppermute | solution.py:356
  (85 shorter events, 13.6 us)
Async XLA Ops:
  2.4 7.2 %collective-permute-start = (bf16[2,32,1152]{2,1,0:T(8,128)(2,1)S(1)}, bf16[2,32,1152]{2,1,0:T(8,128)(2,1)S(1)}, u32[]{:S(2)}, u32[]{:S(2)}) collective-permute-start(bf16[2,32,1152]{2,1,0:T(8,128)(2,1)S(1)} %attention.2.refs_11_), channel_id=1, source_target_pairs={{0,2},{1,3},{2,0},{3,1},{4,6},{5,7},{6,4},{7,5},{8,10},{9,11},{10,... | collective-permute-start | bytes 442376 | tf_op jit(solution)/shard_map/ppermute | solution.py:356
  14.4 4.4 %collective-permute-start.4 = (bf16[8,4096]{1,0:T(8,128)(2,1)S(1)}, bf16[8,4096]{1,0:T(8,128)(2,1)S(1)}, u32[]{:S(2)}, u32[]{:S(2)}) collective-permute-start(bf16[8,4096]{1,0:T(8,128)(2,1)S(1)} %fusion.11), channel_id=1, source_target_pairs={{0,2},{1,3},{2,0},{3,1},{4,6},{5,7},{6,4},{7,5},{8,10},{9,11},{10,... | collective-permute-start | bytes 196616 | tf_op jit(solution)/shard_map/ppermute | solution.py:356
  19.1 4.5 %collective-permute-start.5 = (bf16[8,4224]{1,0:T(8,128)(2,1)S(1)}, bf16[8,4224]{1,0:T(8,128)(2,1)S(1)}, u32[]{:S(2)}, u32[]{:S(2)}) collective-permute-start(bf16[8,4224]{1,0:T(8,128)(2,1)S(1)} %pad_maximum_fusion.1), channel_id=1, source_target_pairs={{0,8},{1,9},{2,10},{3,11},{4,12},{5,13},{6,14},{7,15},{8,0},{9,1},... | collective-permute-start | bytes 202760 | tf_op jit(solution)/shard_map/ppermute | solution.py:356
  20.7 7.1 %collective-permute-start.6 = (bf16[8,4224]{1,0:T(8,128)(2,1)S(1)}, bf16[8,4224]{1,0:T(8,128)(2,1)S(1)}, u32[]{:S(2)}, u32[]{:S(2)}) collective-permute-start(bf16[8,4224]{1,0:T(8,128)(2,1)S(1)} %pad_maximum_fusion.1), channel_id=1, source_target_pairs={{0,16},{1,17},{2,18},{3,19},{4,20},{5,21},{6,22},{7,23},{8,24},{9,... | collective-permute-start | bytes 202760 | tf_op jit(solution)/shard_map/ppermute | solution.py:356
  23.3 6.1 %collective-permute-start.7 = (bf16[8,4224]{1,0:T(8,128)(2,1)S(1)}, bf16[8,4224]{1,0:T(8,128)(2,1)S(1)}, u32[]{:S(2)}, u32[]{:S(2)}) collective-permute-start(bf16[8,4224]{1,0:T(8,128)(2,1)S(1)} %pad_maximum_fusion.1), channel_id=1, source_target_pairs={{0,24},{1,25},{2,26},{3,27},{4,28},{5,29},{6,30},{7,31},{8,16},{9,... | collective-permute-start | bytes 202760 | tf_op jit(solution)/shard_map/ppermute | solution.py:356
  23.7 8.7 %collective-permute-start.9 = (bf16[8,4224]{1,0:T(8,128)(2,1)S(1)}, bf16[8,4224]{1,0:T(8,128)(2,1)S(1)}, u32[]{:S(2)}, u32[]{:S(2)}) collective-permute-start(bf16[8,4224]{1,0:T(8,128)(2,1)S(1)} %get-tuple-element.53), channel_id=1, source_target_pairs={{0,2},{1,3},{2,0},{3,1},{4,6},{5,7},{6,4},{7,5},{8,10},{9,11},{10,... | collective-permute-start | bytes 202760 | tf_op jit(solution)/shard_map/ppermute | solution.py:356
  25.6 7.5 %collective-permute-start.8 = (bf16[8,4224]{1,0:T(8,128)(2,1)S(1)}, bf16[8,4224]{1,0:T(8,128)(2,1)S(1)}, u32[]{:S(2)}, u32[]{:S(2)}) collective-permute-start(bf16[8,4224]{1,0:T(8,128)(2,1)S(1)} %get-tuple-element.53), channel_id=1, source_target_pairs={{0,4},{1,5},{2,6},{3,7},{4,0},{5,1},{6,2},{7,3},{8,12},{9,13},{10,... | collective-permute-start | bytes 202760 | tf_op jit(solution)/shard_map/ppermute | solution.py:356
  29.4 8.7 %collective-permute-start.12 = (bf16[24,4224]{1,0:T(8,128)(2,1)S(1)}, bf16[24,4224]{1,0:T(8,128)(2,1)S(1)}, u32[]{:S(2)}, u32[]{:S(2)}) collective-permute-start(bf16[24,4224]{1,0:T(8,128)(2,1)S(1)} %get-tuple-element.44), channel_id=1, source_target_pairs={{0,6},{1,7},{2,4},{3,5},{4,2},{5,3},{6,0},{7,1},{8,14},{9,15},{10,... | collective-permute-start | bytes 608264 | tf_op jit(solution)/shard_map/ppermute | solution.py:356
  31.6 7.9 %collective-permute-start.10 = (bf16[24,4224]{1,0:T(8,128)(2,1)S(1)}, bf16[24,4224]{1,0:T(8,128)(2,1)S(1)}, u32[]{:S(2)}, u32[]{:S(2)}) collective-permute-start(bf16[24,4224]{1,0:T(8,128)(2,1)S(1)} %get-tuple-element.44), channel_id=1, source_target_pairs={{0,2},{1,3},{2,0},{3,1},{4,6},{5,7},{6,4},{7,5},{8,10},{9,11},{10,... | collective-permute-start | bytes 608264 | tf_op jit(solution)/shard_map/ppermute | solution.py:356
  32.5 7.9 %collective-permute-start.11 = (bf16[32,4224]{1,0:T(8,128)(2,1)S(1)}, bf16[32,4224]{1,0:T(8,128)(2,1)S(1)}, u32[]{:S(2)}, u32[]{:S(2)}) collective-permute-start(bf16[32,4224]{1,0:T(8,128)(2,1)S(1)} %pad_maximum_fusion), channel_id=1, source_target_pairs={{0,4},{1,5},{2,6},{3,7},{4,0},{5,1},{6,2},{7,3},{8,12},{9,13},{10,... | collective-permute-start | bytes 811016 | tf_op jit(solution)/shard_map/ppermute | solution.py:356
  33.1 7.3 %collective-permute-start.13 = (bf16[48,4224]{1,0:T(8,128)(2,1)S(1)}, bf16[48,4224]{1,0:T(8,128)(2,1)S(1)}, u32[]{:S(2)}, u32[]{:S(2)}) collective-permute-start(bf16[48,4224]{1,0:T(8,128)(2,1)S(1)} %get-tuple-element.38), channel_id=1, source_target_pairs={{0,1},{1,0},{2,3},{3,2},{4,5},{5,4},{6,7},{7,6},{8,9},{9,8},{10,11... | collective-permute-start | bytes 1216520 | tf_op jit(solution)/shard_map/ppermute | solution.py:356
  38.2 3.8 %collective-permute-start.16 = (bf16[24,4224]{1,0:T(8,128)(2,1)S(1)}, bf16[24,4224]{1,0:T(8,128)(2,1)S(1)}, u32[]{:S(2)}, u32[]{:S(2)}) collective-permute-start(bf16[24,4224]{1,0:T(8,128)(2,1)S(1)} %collective-permute-done.12), channel_id=1, source_target_pairs={{0,1},{1,0},{2,3},{3,2},{4,5},{5,4},{6,7},{7,6},{8,9},{9,8},{10,11... | collective-permute-start | bytes 608264 | tf_op jit(solution)/shard_map/ppermute | solution.py:356
  40.4 1.5 %collective-permute-start.15 = (bf16[32,4224]{1,0:T(8,128)(2,1)S(1)}, bf16[32,4224]{1,0:T(8,128)(2,1)S(1)}, u32[]{:S(2)}, u32[]{:S(2)}) collective-permute-start(bf16[32,4224]{1,0:T(8,128)(2,1)S(1)} %collective-permute-done.11), channel_id=1, source_target_pairs={{0,1},{1,0},{2,3},{3,2},{4,5},{5,4},{6,7},{7,6},{8,9},{9,8},{10,11... | collective-permute-start | bytes 811016 | tf_op jit(solution)/shard_map/ppermute | solution.py:356
  48.7 3.5 %collective-permute-start.24 = (bf16[24,4096]{1,0:T(8,128)(2,1)S(1)}, bf16[24,4096]{1,0:T(8,128)(2,1)S(1)}, u32[]{:S(2)}, u32[]{:S(2)}) collective-permute-start(bf16[24,4096]{1,0:T(8,128)(2,1)S(1)} %get-tuple-element.28), channel_id=1, source_target_pairs={{0,1},{1,0},{2,3},{3,2},{4,5},{5,4},{6,7},{7,6},{8,9},{9,8},{10,11... | collective-permute-start | bytes 589832 | tf_op jit(solution)/shard_map/ppermute | solution.py:356
  49.1 4.1 %collective-permute-start.18 = (bf16[32,4096]{1,0:T(8,128)(2,1)S(1)}, bf16[32,4096]{1,0:T(8,128)(2,1)S(1)}, u32[]{:S(2)}, u32[]{:S(2)}) collective-permute-start(bf16[32,4096]{1,0:T(8,128)(2,1)S(1)} %get-tuple-element.24), channel_id=1, source_target_pairs={{0,1},{1,0},{2,3},{3,2},{4,5},{5,4},{6,7},{7,6},{8,9},{9,8},{10,11... | collective-permute-start | bytes 786440 | tf_op jit(solution)/shard_map/ppermute | solution.py:356
  49.2 4.7 %collective-permute-start.17 = (bf16[48,4096]{1,0:T(8,128)(2,1)S(1)}, bf16[48,4096]{1,0:T(8,128)(2,1)S(1)}, u32[]{:S(2)}, u32[]{:S(2)}) collective-permute-start(bf16[48,4096]{1,0:T(8,128)(2,1)S(1)} %get-tuple-element.22), channel_id=1, source_target_pairs={{0,1},{1,0},{2,3},{3,2},{4,5},{5,4},{6,7},{7,6},{8,9},{9,8},{10,11... | collective-permute-start | bytes 1179656 | tf_op jit(solution)/shard_map/ppermute | solution.py:356
  50.1 8.8 %collective-permute-start.23 = (bf16[24,4096]{1,0:T(8,128)(2,1)S(1)}, bf16[24,4096]{1,0:T(8,128)(2,1)S(1)}, u32[]{:S(2)}, u32[]{:S(2)}) collective-permute-start(bf16[24,4096]{1,0:T(8,128)(2,1)S(1)} %add_convert_fusion.2), channel_id=1, source_target_pairs={{0,6},{1,7},{2,4},{3,5},{4,2},{5,3},{6,0},{7,1},{8,14},{9,15},{10,... | collective-permute-start | bytes 589832 | tf_op jit(solution)/shard_map/ppermute | solution.py:356
  52.3 9.9 %collective-permute-start.25 = (bf16[24,4096]{1,0:T(8,128)(2,1)S(1)}, bf16[24,4096]{1,0:T(8,128)(2,1)S(1)}, u32[]{:S(2)}, u32[]{:S(2)}) collective-permute-start(bf16[24,4096]{1,0:T(8,128)(2,1)S(1)} %add_convert_fusion.1), channel_id=1, source_target_pairs={{0,2},{1,3},{2,0},{3,1},{4,6},{5,7},{6,4},{7,5},{8,10},{9,11},{10,... | collective-permute-start | bytes 589832 | tf_op jit(solution)/shard_map/ppermute | solution.py:356
  53.3 10.1 %collective-permute-start.19 = (bf16[32,4096]{1,0:T(8,128)(2,1)S(1)}, bf16[32,4096]{1,0:T(8,128)(2,1)S(1)}, u32[]{:S(2)}, u32[]{:S(2)}) collective-permute-start(bf16[32,4096]{1,0:T(8,128)(2,1)S(1)} %add_convert_fusion), channel_id=1, source_target_pairs={{0,4},{1,5},{2,6},{3,7},{4,0},{5,1},{6,2},{7,3},{8,12},{9,13},{10,... | collective-permute-start | bytes 786440 | tf_op jit(solution)/shard_map/ppermute | solution.py:356
  63.5 6.2 %collective-permute-start.26 = (bf16[8,4096]{1,0:T(8,128)(2,1)S(1)}, bf16[8,4096]{1,0:T(8,128)(2,1)S(1)}, u32[]{:S(2)}, u32[]{:S(2)}) collective-permute-start(bf16[8,4096]{1,0:T(8,128)(2,1)S(1)} %get-tuple-element.31), channel_id=1, source_target_pairs={{0,8},{1,9},{2,10},{3,11},{4,12},{5,13},{6,14},{7,15},{8,0},{9,1},... | collective-permute-start | bytes 196616 | tf_op jit(solution)/shard_map/ppermute | solution.py:356
  64.2 6.5 %collective-permute-start.28 = (bf16[8,4096]{1,0:T(8,128)(2,1)S(1)}, bf16[8,4096]{1,0:T(8,128)(2,1)S(1)}, u32[]{:S(2)}, u32[]{:S(2)}) collective-permute-start(bf16[8,4096]{1,0:T(8,128)(2,1)S(1)} %get-tuple-element.32), channel_id=1, source_target_pairs={{0,24},{1,25},{2,26},{3,27},{4,28},{5,29},{6,30},{7,31},{8,16},{9,... | collective-permute-start | bytes 196616 | tf_op jit(solution)/shard_map/ppermute | solution.py:356
  67.3 5.5 %collective-permute-start.27 = (bf16[8,4096]{1,0:T(8,128)(2,1)S(1)}, bf16[8,4096]{1,0:T(8,128)(2,1)S(1)}, u32[]{:S(2)}, u32[]{:S(2)}) collective-permute-start(bf16[8,4096]{1,0:T(8,128)(2,1)S(1)} %get-tuple-element.33), channel_id=1, source_target_pairs={{0,16},{1,17},{2,18},{3,19},{4,20},{5,21},{6,22},{7,23},{8,24},{9,... | collective-permute-start | bytes 196616 | tf_op jit(solution)/shard_map/ppermute | solution.py:356
  67.5 5.3 %collective-permute-start.20 = (bf16[8,4096]{1,0:T(8,128)(2,1)S(1)}, bf16[8,4096]{1,0:T(8,128)(2,1)S(1)}, u32[]{:S(2)}, u32[]{:S(2)}) collective-permute-start(bf16[8,4096]{1,0:T(8,128)(2,1)S(1)} %get-tuple-element.29), channel_id=1, source_target_pairs={{0,4},{1,5},{2,6},{3,7},{4,0},{5,1},{6,2},{7,3},{8,12},{9,13},{10,... | collective-permute-start | bytes 196616 | tf_op jit(solution)/shard_map/ppermute | solution.py:356
  69.0 4.3 %collective-permute-start.21 = (bf16[8,4096]{1,0:T(8,128)(2,1)S(1)}, bf16[8,4096]{1,0:T(8,128)(2,1)S(1)}, u32[]{:S(2)}, u32[]{:S(2)}) collective-permute-start(bf16[8,4096]{1,0:T(8,128)(2,1)S(1)} %get-tuple-element.30), channel_id=1, source_target_pairs={{0,2},{1,3},{2,0},{3,1},{4,6},{5,7},{6,4},{7,5},{8,10},{9,11},{10,... | collective-permute-start | bytes 196616 | tf_op jit(solution)/shard_map/ppermute | solution.py:356
  (11 other events, 153.4 us)

commit v15 on v14

--- a/solution.py
+++ b/solution.py
@@ -413,17 +413,38 @@
 
     mine = jnp.concatenate([normed, table], axis=1)
     others = plan.spread(mine, plan.z)
-    first = mine + others[0][:, :1] * 0
+    cut = plan.zlen // 2
+    first = jnp.concatenate([mine + others[0][:, :1] * 0] + others[: cut - 1])
+    rest = jnp.concatenate(others[cut - 1 :])
     near_x = plan.spread(first, plan.x)
     near_y = plan.spread(first, plan.y)
-    rest = jnp.concatenate(others)
     far_diagonal = plan.spread(rest, plan.diagonal)
     far_y = plan.spread(rest, plan.y)
-    far_x = plan.spread(jnp.concatenate(others + near_y), plan.x)
-    pieces = [jnp.concatenate([mine] + others + near_x + near_y)] + far_y + far_x + far_diagonal
-    x = jnp.concatenate(pieces + [plan.swap(piece, plan.core) for piece in pieces])
-
-    sizes = [piece.shape[0] for piece in pieces] * 2
+    far_x = plan.spread(jnp.concatenate([rest] + near_y), plan.x)
+
+    def ordered(column, near_x, near_y, far_x, far_y, far_diagonal):
+        size, height = first.shape[0], rest.shape[0]
+        own = [column] + [v[:share] for v in near_x] + [v[:share] for v in near_y]
+        along_y = [[near[share:], far] for near, far in zip(near_y, far_y)]
+        through = [
+            [v[height + k * size : height + (k + 1) * size] for k in range(len(plan.y))]
+            for v in far_x
+        ]
+        along_x = [
+            [near[share:], far[:height]] + [v[:share] for v in more]
+            for near, far, more in zip(near_x, far_x, through)
+        ]
+        more = [v for row in through for v in row]
+        diagonal = [[near[share:], far] for near, far in zip(more, far_diagonal)]
+        return [own] + along_y + along_x + diagonal
+
+    lists = [[jnp.concatenate([mine] + others)], near_x, near_y, far_x, far_y, far_diagonal]
+    pieces = ordered(lists[0][0], *lists[1:])
+    lists = [[plan.swap(v, plan.core) for v in values] for values in lists]
+    there = ordered(lists[0][0], *lists[1:])
+    x = jnp.concatenate([v for piece in pieces + there for v in piece])
+
+    sizes = [sum(v.shape[0] for v in piece) for piece in pieces] * 2
     results = experts(x, expert_gate, expert_up, expert_down, share, sizes)
 
     half = len(pieces)
@@ -432,7 +453,7 @@
         for i in reversed(range(half))
     ][::-1]
     back = plan.swaps(sums[1:], plan.y + plan.x + plan.diagonal)
-    height, x_end = rest.shape[0], len(plan.y) + len(plan.x)
+    height, x_end = (plan.zlen - 1) * share, len(plan.y) + len(plan.x)
     column = sums[0][: share + height]
     near = sums[0][share + height :].reshape(-1, share, width)
     through = [v[height:] for v in back[len(plan.y) : x_end]]

time: 74.2 us -> 75.5 us (1.018)
  starting transfers between devices: 27.7 us -> 28.7 us
    ppermute x29 -> x31, starting transfers between devices: 27.7 us -> 28.7 us  [swap(): lax.ppermute(value, ('dp', 'tensor'), [(i, i ^ flip) for i in range(self....]
    ppermute x29 -> x31, waiting for transfers between devices: 29.3 us -> 29.5 us  [swap(): lax.ppermute(value, ('dp', 'tensor'), [(i, i ^ flip) for i in range(self....]
  transfers between devices with their start and end apart: 29 -> 31, of which waited for: 18 -> 15; matrix products, arithmetic and copies ran while one was open for 1% -> 1% of each run, Pallas kernels for 5% -> 5%
where the time goes in v15:
time: 75.5 us; the launch traced here: 75.4 us
  waiting for transfers between devices  29.5 us (39%)
  starting transfers between devices  28.7 us (38%)
  Pallas kernels  14.7 us (19%)
  other arithmetic  1.78 us (2%)
    ppermute x31, waiting for transfers between devices, swap(): lax.ppermute(value, ('dp', 'tensor'), [(i, i ^ flip) for i in range(self....  29.5 us
    ppermute x31, starting transfers between devices, swap(): lax.ppermute(value, ('dp', 'tensor'), [(i, i ^ flip) for i in range(self....  28.7 us
    pallas_call x1, Pallas kernels, experts(): pl.pallas_call(functools.partial(expert_kernel, slots, sizes), out_shape=...  6.49 us
    pallas_call x2, Pallas kernels, attention(): pl.pallas_call(functools.partial(attention_kernel, flip), out_shape=tuple...  6.45 us
    pallas_call x1, Pallas kernels, projection(): pl.pallas_call(functools.partial(projection_kernel, parts, len(weights)),...  1.79 us
  transfers between devices with their start and end apart: 31, of which 15 were waited for; matrix products, arithmetic and copies ran while one was open for 1% of the time, Pallas kernels for 5%

profile of v15, /device:TPU:0, one launch (start us, length us, event | category | flops | bytes accessed | tf_op | source)
XLA Modules:
  0.0 75.4 jit_solution(12413292274024998421)
XLA Ops:
  0.0 2.4 %attention.2.refs_11_ = bf16[2,32,1152]{2,1,0:T(8,128)(2,1)S(1)} custom-call(s32[32]{0:T(128)} %refs_0_.3, bf16[32,32,128]{2,1,0:T(8,128)(2,1)} %refs_1_.4, bf16[32,2,128]{2,1,0:T(2,128)(2,1)} %refs_2_.4, bf16[32,2,128]{2,1,0:T(2,128)(2,1)} %refs_3_.4, bf16[32,2,32,128]{3,2,1,0:T(8,128)(2,1)} %refs_4_.3, bf16[32,2,32,128]{3,2,1,0:T(8,128)(2,1)} %refs_5_.3, ...), custom_call_target="tpu_custom_call" | custom-call | flops 1048576 | bytes 1048576 | tf_op jit(solution)/shard_map/attention/pallas_call | solution.py:199
  2.4 3.0 %collective-permute-start = (bf16[2,32,1152]{2,1,0:T(8,128)(2,1)S(1)}, bf16[2,32,1152]{2,1,0:T(8,128)(2,1)S(1)}, u32[]{:S(2)}, u32[]{:S(2)}) collective-permute-start(bf16[2,32,1152]{2,1,0:T(8,128)(2,1)S(1)} %attention.2.refs_11_), channel_id=1, source_target_pairs={{0,2},{1,3},{2,0},{3,1},{4,6},{5,7},{6,4},{7,5},{8,10},{9,11},{10,... | collective-permute-start | bytes 442376 | tf_op jit(solution)/shard_map/ppermute | solution.py:356
  5.5 4.0 %attention.3 = (bf16[2,32,1152]{2,1,0:T(8,128)(2,1)S(1)}, bf16[8,128]{1,0:T(8,128)(2,1)S(1)}, bf16[512,4096]{1,0:T(8,128)(2,1)S(1)}, bf16[512,4096]{1,0:T(8,128)(2,1)S(1)}) custom-call(s32[32]{0:T(128)} %refs_0_.3, bf16[32,32,128]{2,1,0:T(8,128)(2,1)} %refs_1_.4, bf16[32,2,128]{2,1,0:T(2,128)(2,1)} %refs_2_.4, bf16[32,2,128]{2,1,0:T(2,128)(2,1)} %refs_3_.4, ...), custom_call_target="tpu_custom_call" | custom-call | flops 9437184 | bytes 9437184 | tf_op jit(solution)/shard_map/attention/pallas_call | solution.py:199
  11.1 1.8 %projection.1 = bf16[2,2,8,4096]{3,2,1,0:T(8,128)(2,1)S(1)} custom-call(bf16[32,1152]{1,0:T(8,128)(2,1)S(1)} %get-tuple-element.37.refs_0_, bf16[32,1152]{1,0:T(8,128)(2,1)S(1)} %collective-permute-done.1.refs_1_, bf16[32,1152]{1,0:T(8,128)(2,1)S(1)} %get-tuple-element.35.refs_2_, bf16[32,1152]{1,0:T(8,128)(2,1)S(1)} %collective-permute-done.2.refs_3_, ...), custom_call_target="tpu_custom_call" | custom-call | tf_op jit(solution)/shard_map/projection/pallas_call | solution.py:258
  14.4 1.4 %collective-permute-start.4 = (bf16[8,4096]{1,0:T(8,128)(2,1)S(1)}, bf16[8,4096]{1,0:T(8,128)(2,1)S(1)}, u32[]{:S(2)}, u32[]{:S(2)}) collective-permute-start(bf16[8,4096]{1,0:T(8,128)(2,1)S(1)} %fusion.11), channel_id=1, source_target_pairs={{0,2},{1,3},{2,0},{3,1},{4,6},{5,7},{6,4},{7,5},{8,10},{9,11},{10,... | collective-permute-start | bytes 196616 | tf_op jit(solution)/shard_map/ppermute | solution.py:356
  15.8 3.0 %collective-permute-done.4 = bf16[8,4096]{1,0:T(8,128)(2,1)S(1)} collective-permute-done((bf16[8,4096]{1,0:T(8,128)(2,1)S(1)}, bf16[8,4096]{1,0:T(8,128)(2,1)S(1)}, u32[]{:S(2)}, u32[]{:S(2)}) %collective-permute-start.4) | collective-permute-done | bytes 65568 | tf_op jit(solution)/shard_map/ppermute | solution.py:356
  19.1 1.6 %collective-permute-start.5 = (bf16[8,4224]{1,0:T(8,128)(2,1)S(1)}, bf16[8,4224]{1,0:T(8,128)(2,1)S(1)}, u32[]{:S(2)}, u32[]{:S(2)}) collective-permute-start(bf16[8,4224]{1,0:T(8,128)(2,1)S(1)} %pad_maximum_fusion.3), channel_id=1, source_target_pairs={{0,8},{1,9},{2,10},{3,11},{4,12},{5,13},{6,14},{7,15},{8,0},{9,1},... | collective-permute-start | bytes 202760 | tf_op jit(solution)/shard_map/ppermute | solution.py:356
  20.7 2.6 %collective-permute-start.6 = (bf16[8,4224]{1,0:T(8,128)(2,1)S(1)}, bf16[8,4224]{1,0:T(8,128)(2,1)S(1)}, u32[]{:S(2)}, u32[]{:S(2)}) collective-permute-start(bf16[8,4224]{1,0:T(8,128)(2,1)S(1)} %pad_maximum_fusion.3), channel_id=1, source_target_pairs={{0,16},{1,17},{2,18},{3,19},{4,20},{5,21},{6,22},{7,23},{8,24},{9,... | collective-permute-start | bytes 202760 | tf_op jit(solution)/shard_map/ppermute | solution.py:356
  23.8 1.9 %collective-permute-start.9 = (bf16[16,4224]{1,0:T(8,128)(2,1)S(1)}, bf16[16,4224]{1,0:T(8,128)(2,1)S(1)}, u32[]{:S(2)}, u32[]{:S(2)}) collective-permute-start(bf16[16,4224]{1,0:T(8,128)(2,1)S(1)} %pad_maximum_fusion.2), channel_id=1, source_target_pairs={{0,2},{1,3},{2,0},{3,1},{4,6},{5,7},{6,4},{7,5},{8,10},{9,11},{10,... | collective-permute-start | bytes 405512 | tf_op jit(solution)/shard_map/ppermute | solution.py:356
  25.6 1.5 %collective-permute-start.8 = (bf16[16,4224]{1,0:T(8,128)(2,1)S(1)}, bf16[16,4224]{1,0:T(8,128)(2,1)S(1)}, u32[]{:S(2)}, u32[]{:S(2)}) collective-permute-start(bf16[16,4224]{1,0:T(8,128)(2,1)S(1)} %pad_maximum_fusion.2), channel_id=1, source_target_pairs={{0,4},{1,5},{2,6},{3,7},{4,0},{5,1},{6,2},{7,3},{8,12},{9,13},{10,... | collective-permute-start | bytes 405512 | tf_op jit(solution)/shard_map/ppermute | solution.py:356
  27.9 1.6 %collective-permute-done.7 = bf16[8,4224]{1,0:T(8,128)(2,1)S(1)} collective-permute-done((bf16[8,4224]{1,0:T(8,128)(2,1)S(1)}, bf16[8,4224]{1,0:T(8,128)(2,1)S(1)}, u32[]{:S(2)}, u32[]{:S(2)}) %collective-permute-start.7) | collective-permute-done | bytes 67616 | tf_op jit(solution)/shard_map/ppermute | solution.py:356
  29.4 2.2 %collective-permute-start.12 = (bf16[16,4224]{1,0:T(8,128)(2,1)S(1)}, bf16[16,4224]{1,0:T(8,128)(2,1)S(1)}, u32[]{:S(2)}, u32[]{:S(2)}) collective-permute-start(bf16[16,4224]{1,0:T(8,128)(2,1)S(1)} %get-tuple-element.40), channel_id=1, source_target_pairs={{0,6},{1,7},{2,4},{3,5},{4,2},{5,3},{6,0},{7,1},{8,14},{9,15},{10,... | collective-permute-start | bytes 405512 | tf_op jit(solution)/shard_map/ppermute | solution.py:356
  33.4 3.5 %collective-permute-done.10 = bf16[16,4224]{1,0:T(8,128)(2,1)S(1)} collective-permute-done((bf16[16,4224]{1,0:T(8,128)(2,1)S(1)}, bf16[16,4224]{1,0:T(8,128)(2,1)S(1)}, u32[]{:S(2)}, u32[]{:S(2)}) %collective-permute-start.10) | collective-permute-done | bytes 135200 | tf_op jit(solution)/shard_map/ppermute | solution.py:356
  37.5 4.0 %collective-permute-done.11 = bf16[32,4224]{1,0:T(8,128)(2,1)S(1)} collective-permute-done((bf16[32,4224]{1,0:T(8,128)(2,1)S(1)}, bf16[32,4224]{1,0:T(8,128)(2,1)S(1)}, u32[]{:S(2)}, u32[]{:S(2)}) %collective-permute-start.11) | collective-permute-done | bytes 270368 | tf_op jit(solution)/shard_map/ppermute | solution.py:356
  43.4 6.5 %experts.1 = (bf16[48,4096]{1,0:T(8,128)(2,1)S(1)}, bf16[24,4096]{1,0:T(8,128)(2,1)S(1)}, bf16[32,4096]{1,0:T(8,128)(2,1)S(1)}, bf16[24,4096]{1,0:T(8,128)(2,1)S...) custom-call(bf16[256,4224]{1,0:T(8,128)(2,1)S(1)} %constant_dynamic-, ...), custom_call_target="tpu_custom_call" | custom-call | tf_op jit(solution)/shard_map/experts/pallas_call | solution.py:327
  51.4 1.3 %collective-permute-start.25 = (bf16[24,4096]{1,0:T(8,128)(2,1)S(1)}, bf16[24,4096]{1,0:T(8,128)(2,1)S(1)}, u32[]{:S(2)}, u32[]{:S(2)}) collective-permute-start(bf16[24,4096]{1,0:T(8,128)(2,1)S(1)} %add_convert_fusion.2), channel_id=1, source_target_pairs={{0,6},{1,7},{2,4},{3,5},{4,2},{5,3},{6,0},{7,1},{8,14},{9,15},{10,... | collective-permute-start | bytes 589832 | tf_op jit(solution)/shard_map/ppermute | solution.py:356
  52.8 1.3 %collective-permute-start.27 = (bf16[24,4096]{1,0:T(8,128)(2,1)S(1)}, bf16[24,4096]{1,0:T(8,128)(2,1)S(1)}, u32[]{:S(2)}, u32[]{:S(2)}) collective-permute-start(bf16[24,4096]{1,0:T(8,128)(2,1)S(1)} %add_convert_fusion.1), channel_id=1, source_target_pairs={{0,2},{1,3},{2,0},{3,1},{4,6},{5,7},{6,4},{7,5},{8,10},{9,11},{10,... | collective-permute-start | bytes 589832 | tf_op jit(solution)/shard_map/ppermute | solution.py:356
  55.4 4.8 %collective-permute-done.25 = bf16[24,4096]{1,0:T(8,128)(2,1)S(1)} collective-permute-done((bf16[24,4096]{1,0:T(8,128)(2,1)S(1)}, bf16[24,4096]{1,0:T(8,128)(2,1)S(1)}, u32[]{:S(2)}, u32[]{:S(2)}) %collective-permute-start.25) | collective-permute-done | bytes 196640 | tf_op jit(solution)/shard_map/ppermute | solution.py:356
  60.2 3.6 %collective-permute-done.27 = bf16[24,4096]{1,0:T(8,128)(2,1)S(1)} collective-permute-done((bf16[24,4096]{1,0:T(8,128)(2,1)S(1)}, bf16[24,4096]{1,0:T(8,128)(2,1)S(1)}, u32[]{:S(2)}, u32[]{:S(2)}) %collective-permute-start.27) | collective-permute-done | bytes 196640 | tf_op jit(solution)/shard_map/ppermute | solution.py:356
  63.8 1.2 %collective-permute-done.21 = bf16[32,4096]{1,0:T(8,128)(2,1)S(1)} collective-permute-done((bf16[32,4096]{1,0:T(8,128)(2,1)S(1)}, bf16[32,4096]{1,0:T(8,128)(2,1)S(1)}, u32[]{:S(2)}, u32[]{:S(2)}) %collective-permute-start.21) | collective-permute-done | bytes 262176 | tf_op jit(solution)/shard_map/ppermute | solution.py:356
  65.5 2.1 %collective-permute-start.30 = (bf16[8,4096]{1,0:T(8,128)(2,1)S(1)}, bf16[8,4096]{1,0:T(8,128)(2,1)S(1)}, u32[]{:S(2)}, u32[]{:S(2)}) collective-permute-start(bf16[8,4096]{1,0:T(8,128)(2,1)S(1)} %get-tuple-element.32), channel_id=1, source_target_pairs={{0,24},{1,25},{2,26},{3,27},{4,28},{5,29},{6,30},{7,31},{8,16},{9,... | collective-permute-start | bytes 196616 | tf_op jit(solution)/shard_map/ppermute | solution.py:356
  67.6 1.1 %collective-permute-start.29 = (bf16[8,4096]{1,0:T(8,128)(2,1)S(1)}, bf16[8,4096]{1,0:T(8,128)(2,1)S(1)}, u32[]{:S(2)}, u32[]{:S(2)}) collective-permute-start(bf16[8,4096]{1,0:T(8,128)(2,1)S(1)} %get-tuple-element.33), channel_id=1, source_target_pairs={{0,16},{1,17},{2,18},{3,19},{4,20},{5,21},{6,22},{7,23},{8,24},{9,... | collective-permute-start | bytes 196616 | tf_op jit(solution)/shard_map/ppermute | solution.py:356
  68.9 1.1 %collective-permute-start.22 = (bf16[8,4096]{1,0:T(8,128)(2,1)S(1)}, bf16[8,4096]{1,0:T(8,128)(2,1)S(1)}, u32[]{:S(2)}, u32[]{:S(2)}) collective-permute-start(bf16[8,4096]{1,0:T(8,128)(2,1)S(1)} %get-tuple-element.29), channel_id=1, source_target_pairs={{0,4},{1,5},{2,6},{3,7},{4,0},{5,1},{6,2},{7,3},{8,12},{9,13},{10,... | collective-permute-start | bytes 196616 | tf_op jit(solution)/shard_map/ppermute | solution.py:356
  72.0 2.6 %collective-permute-done.29 = bf16[8,4096]{1,0:T(8,128)(2,1)S(1)} collective-permute-done((bf16[8,4096]{1,0:T(8,128)(2,1)S(1)}, bf16[8,4096]{1,0:T(8,128)(2,1)S(1)}, u32[]{:S(2)}, u32[]{:S(2)}) %collective-permute-start.29) | collective-permute-done | bytes 65568 | tf_op jit(solution)/shard_map/ppermute | solution.py:356
  (94 shorter events, 14.8 us)
Async XLA Ops:
  2.4 7.2 %collective-permute-start = (bf16[2,32,1152]{2,1,0:T(8,128)(2,1)S(1)}, bf16[2,32,1152]{2,1,0:T(8,128)(2,1)S(1)}, u32[]{:S(2)}, u32[]{:S(2)}) collective-permute-start(bf16[2,32,1152]{2,1,0:T(8,128)(2,1)S(1)} %attention.2.refs_11_), channel_id=1, source_target_pairs={{0,2},{1,3},{2,0},{3,1},{4,6},{5,7},{6,4},{7,5},{8,10},{9,11},{10,... | collective-permute-start | bytes 442376 | tf_op jit(solution)/shard_map/ppermute | solution.py:356
  14.4 4.4 %collective-permute-start.4 = (bf16[8,4096]{1,0:T(8,128)(2,1)S(1)}, bf16[8,4096]{1,0:T(8,128)(2,1)S(1)}, u32[]{:S(2)}, u32[]{:S(2)}) collective-permute-start(bf16[8,4096]{1,0:T(8,128)(2,1)S(1)} %fusion.11), channel_id=1, source_target_pairs={{0,2},{1,3},{2,0},{3,1},{4,6},{5,7},{6,4},{7,5},{8,10},{9,11},{10,... | collective-permute-start | bytes 196616 | tf_op jit(solution)/shard_map/ppermute | solution.py:356
  19.1 4.5 %collective-permute-start.5 = (bf16[8,4224]{1,0:T(8,128)(2,1)S(1)}, bf16[8,4224]{1,0:T(8,128)(2,1)S(1)}, u32[]{:S(2)}, u32[]{:S(2)}) collective-permute-start(bf16[8,4224]{1,0:T(8,128)(2,1)S(1)} %pad_maximum_fusion.3), channel_id=1, source_target_pairs={{0,8},{1,9},{2,10},{3,11},{4,12},{5,13},{6,14},{7,15},{8,0},{9,1},... | collective-permute-start | bytes 202760 | tf_op jit(solution)/shard_map/ppermute | solution.py:356
  20.7 7.1 %collective-permute-start.6 = (bf16[8,4224]{1,0:T(8,128)(2,1)S(1)}, bf16[8,4224]{1,0:T(8,128)(2,1)S(1)}, u32[]{:S(2)}, u32[]{:S(2)}) collective-permute-start(bf16[8,4224]{1,0:T(8,128)(2,1)S(1)} %pad_maximum_fusion.3), channel_id=1, source_target_pairs={{0,16},{1,17},{2,18},{3,19},{4,20},{5,21},{6,22},{7,23},{8,24},{9,... | collective-permute-start | bytes 202760 | tf_op jit(solution)/shard_map/ppermute | solution.py:356
  23.3 6.1 %collective-permute-start.7 = (bf16[8,4224]{1,0:T(8,128)(2,1)S(1)}, bf16[8,4224]{1,0:T(8,128)(2,1)S(1)}, u32[]{:S(2)}, u32[]{:S(2)}) collective-permute-start(bf16[8,4224]{1,0:T(8,128)(2,1)S(1)} %pad_maximum_fusion.3), channel_id=1, source_target_pairs={{0,24},{1,25},{2,26},{3,27},{4,28},{5,29},{6,30},{7,31},{8,16},{9,... | collective-permute-start | bytes 202760 | tf_op jit(solution)/shard_map/ppermute | solution.py:356
  23.8 8.7 %collective-permute-start.9 = (bf16[16,4224]{1,0:T(8,128)(2,1)S(1)}, bf16[16,4224]{1,0:T(8,128)(2,1)S(1)}, u32[]{:S(2)}, u32[]{:S(2)}) collective-permute-start(bf16[16,4224]{1,0:T(8,128)(2,1)S(1)} %pad_maximum_fusion.2), channel_id=1, source_target_pairs={{0,2},{1,3},{2,0},{3,1},{4,6},{5,7},{6,4},{7,5},{8,10},{9,11},{10,... | collective-permute-start | bytes 405512 | tf_op jit(solution)/shard_map/ppermute | solution.py:356
  25.6 7.6 %collective-permute-start.8 = (bf16[16,4224]{1,0:T(8,128)(2,1)S(1)}, bf16[16,4224]{1,0:T(8,128)(2,1)S(1)}, u32[]{:S(2)}, u32[]{:S(2)}) collective-permute-start(bf16[16,4224]{1,0:T(8,128)(2,1)S(1)} %pad_maximum_fusion.2), channel_id=1, source_target_pairs={{0,4},{1,5},{2,6},{3,7},{4,0},{5,1},{6,2},{7,3},{8,12},{9,13},{10,... | collective-permute-start | bytes 405512 | tf_op jit(solution)/shard_map/ppermute | solution.py:356
  29.4 7.5 %collective-permute-start.12 = (bf16[16,4224]{1,0:T(8,128)(2,1)S(1)}, bf16[16,4224]{1,0:T(8,128)(2,1)S(1)}, u32[]{:S(2)}, u32[]{:S(2)}) collective-permute-start(bf16[16,4224]{1,0:T(8,128)(2,1)S(1)} %get-tuple-element.40), channel_id=1, source_target_pairs={{0,6},{1,7},{2,4},{3,5},{4,2},{5,3},{6,0},{7,1},{8,14},{9,15},{10,... | collective-permute-start | bytes 405512 | tf_op jit(solution)/shard_map/ppermute | solution.py:356
  31.6 5.2 %collective-permute-start.10 = (bf16[16,4224]{1,0:T(8,128)(2,1)S(1)}, bf16[16,4224]{1,0:T(8,128)(2,1)S(1)}, u32[]{:S(2)}, u32[]{:S(2)}) collective-permute-start(bf16[16,4224]{1,0:T(8,128)(2,1)S(1)} %get-tuple-element.40), channel_id=1, source_target_pairs={{0,2},{1,3},{2,0},{3,1},{4,6},{5,7},{6,4},{7,5},{8,10},{9,11},{10,... | collective-permute-start | bytes 405512 | tf_op jit(solution)/shard_map/ppermute | solution.py:356
  32.5 9.0 %collective-permute-start.13 = (bf16[32,4224]{1,0:T(8,128)(2,1)S(1)}, bf16[32,4224]{1,0:T(8,128)(2,1)S(1)}, u32[]{:S(2)}, u32[]{:S(2)}) collective-permute-start(bf16[32,4224]{1,0:T(8,128)(2,1)S(1)} %get-tuple-element.38), channel_id=1, source_target_pairs={{0,1},{1,0},{2,3},{3,2},{4,5},{5,4},{6,7},{7,6},{8,9},{9,8},{10,11... | collective-permute-start | bytes 811016 | tf_op jit(solution)/shard_map/ppermute | solution.py:356
  32.6 8.9 %collective-permute-start.11 = (bf16[32,4224]{1,0:T(8,128)(2,1)S(1)}, bf16[32,4224]{1,0:T(8,128)(2,1)S(1)}, u32[]{:S(2)}, u32[]{:S(2)}) collective-permute-start(bf16[32,4224]{1,0:T(8,128)(2,1)S(1)} %get-tuple-element.39), channel_id=1, source_target_pairs={{0,4},{1,5},{2,6},{3,7},{4,0},{5,1},{6,2},{7,3},{8,12},{9,13},{10,... | collective-permute-start | bytes 811016 | tf_op jit(solution)/shard_map/ppermute | solution.py:356
  33.2 9.0 %collective-permute-start.15 = (bf16[16,4224]{1,0:T(8,128)(2,1)S(1)}, bf16[16,4224]{1,0:T(8,128)(2,1)S(1)}, u32[]{:S(2)}, u32[]{:S(2)}) collective-permute-start(bf16[16,4224]{1,0:T(8,128)(2,1)S(1)} %collective-permute-done.9), channel_id=1, source_target_pairs={{0,1},{1,0},{2,3},{3,2},{4,5},{5,4},{6,7},{7,6},{8,9},{9,8},{10,11... | collective-permute-start | bytes 405512 | tf_op jit(solution)/shard_map/ppermute | solution.py:356
  36.9 5.3 %collective-permute-start.14 = (bf16[16,4224]{1,0:T(8,128)(2,1)S(1)}, bf16[16,4224]{1,0:T(8,128)(2,1)S(1)}, u32[]{:S(2)}, u32[]{:S(2)}) collective-permute-start(bf16[16,4224]{1,0:T(8,128)(2,1)S(1)} %collective-permute-done.8), channel_id=1, source_target_pairs={{0,1},{1,0},{2,3},{3,2},{4,5},{5,4},{6,7},{7,6},{8,9},{9,8},{10,11... | collective-permute-start | bytes 405512 | tf_op jit(solution)/shard_map/ppermute | solution.py:356
  36.9 5.3 %collective-permute-start.16 = (bf16[16,4224]{1,0:T(8,128)(2,1)S(1)}, bf16[16,4224]{1,0:T(8,128)(2,1)S(1)}, u32[]{:S(2)}, u32[]{:S(2)}) collective-permute-start(bf16[16,4224]{1,0:T(8,128)(2,1)S(1)} %collective-permute-done.10), channel_id=1, source_target_pairs={{0,1},{1,0},{2,3},{3,2},{4,5},{5,4},{6,7},{7,6},{8,9},{9,8},{10,11... | collective-permute-start | bytes 405512 | tf_op jit(solution)/shard_map/ppermute | solution.py:356
  50.5 3.7 %collective-permute-start.20 = (bf16[32,4096]{1,0:T(8,128)(2,1)S(1)}, bf16[32,4096]{1,0:T(8,128)(2,1)S(1)}, u32[]{:S(2)}, u32[]{:S(2)}) collective-permute-start(bf16[32,4096]{1,0:T(8,128)(2,1)S(1)} %get-tuple-element.24), channel_id=1, source_target_pairs={{0,1},{1,0},{2,3},{3,2},{4,5},{5,4},{6,7},{7,6},{8,9},{9,8},{10,11... | collective-permute-start | bytes 786440 | tf_op jit(solution)/shard_map/ppermute | solution.py:356
  50.8 4.4 %collective-permute-start.19 = (bf16[48,4096]{1,0:T(8,128)(2,1)S(1)}, bf16[48,4096]{1,0:T(8,128)(2,1)S(1)}, u32[]{:S(2)}, u32[]{:S(2)}) collective-permute-start(bf16[48,4096]{1,0:T(8,128)(2,1)S(1)} %get-tuple-element.22), channel_id=1, source_target_pairs={{0,1},{1,0},{2,3},{3,2},{4,5},{5,4},{6,7},{7,6},{8,9},{9,8},{10,11... | collective-permute-start | bytes 1179656 | tf_op jit(solution)/shard_map/ppermute | solution.py:356
  51.4 8.7 %collective-permute-start.25 = (bf16[24,4096]{1,0:T(8,128)(2,1)S(1)}, bf16[24,4096]{1,0:T(8,128)(2,1)S(1)}, u32[]{:S(2)}, u32[]{:S(2)}) collective-permute-start(bf16[24,4096]{1,0:T(8,128)(2,1)S(1)} %add_convert_fusion.2), channel_id=1, source_target_pairs={{0,6},{1,7},{2,4},{3,5},{4,2},{5,3},{6,0},{7,1},{8,14},{9,15},{10,... | collective-permute-start | bytes 589832 | tf_op jit(solution)/shard_map/ppermute | solution.py:356
  52.8 11.0 %collective-permute-start.27 = (bf16[24,4096]{1,0:T(8,128)(2,1)S(1)}, bf16[24,4096]{1,0:T(8,128)(2,1)S(1)}, u32[]{:S(2)}, u32[]{:S(2)}) collective-permute-start(bf16[24,4096]{1,0:T(8,128)(2,1)S(1)} %add_convert_fusion.1), channel_id=1, source_target_pairs={{0,2},{1,3},{2,0},{3,1},{4,6},{5,7},{6,4},{7,5},{8,10},{9,11},{10,... | collective-permute-start | bytes 589832 | tf_op jit(solution)/shard_map/ppermute | solution.py:356
  54.2 10.8 %collective-permute-start.21 = (bf16[32,4096]{1,0:T(8,128)(2,1)S(1)}, bf16[32,4096]{1,0:T(8,128)(2,1)S(1)}, u32[]{:S(2)}, u32[]{:S(2)}) collective-permute-start(bf16[32,4096]{1,0:T(8,128)(2,1)S(1)} %add_convert_fusion), channel_id=1, source_target_pairs={{0,4},{1,5},{2,6},{3,7},{4,0},{5,1},{6,2},{7,3},{8,12},{9,13},{10,... | collective-permute-start | bytes 786440 | tf_op jit(solution)/shard_map/ppermute | solution.py:356
  65.1 5.9 %collective-permute-start.28 = (bf16[8,4096]{1,0:T(8,128)(2,1)S(1)}, bf16[8,4096]{1,0:T(8,128)(2,1)S(1)}, u32[]{:S(2)}, u32[]{:S(2)}) collective-permute-start(bf16[8,4096]{1,0:T(8,128)(2,1)S(1)} %get-tuple-element.31), channel_id=1, source_target_pairs={{0,8},{1,9},{2,10},{3,11},{4,12},{5,13},{6,14},{7,15},{8,0},{9,1},... | collective-permute-start | bytes 196616 | tf_op jit(solution)/shard_map/ppermute | solution.py:356
  65.5 6.6 %collective-permute-start.30 = (bf16[8,4096]{1,0:T(8,128)(2,1)S(1)}, bf16[8,4096]{1,0:T(8,128)(2,1)S(1)}, u32[]{:S(2)}, u32[]{:S(2)}) collective-permute-start(bf16[8,4096]{1,0:T(8,128)(2,1)S(1)} %get-tuple-element.32), channel_id=1, source_target_pairs={{0,24},{1,25},{2,26},{3,27},{4,28},{5,29},{6,30},{7,31},{8,16},{9,... | collective-permute-start | bytes 196616 | tf_op jit(solution)/shard_map/ppermute | solution.py:356
  67.6 7.1 %collective-permute-start.29 = (bf16[8,4096]{1,0:T(8,128)(2,1)S(1)}, bf16[8,4096]{1,0:T(8,128)(2,1)S(1)}, u32[]{:S(2)}, u32[]{:S(2)}) collective-permute-start(bf16[8,4096]{1,0:T(8,128)(2,1)S(1)} %get-tuple-element.33), channel_id=1, source_target_pairs={{0,16},{1,17},{2,18},{3,19},{4,20},{5,21},{6,22},{7,23},{8,24},{9,... | collective-permute-start | bytes 196616 | tf_op jit(solution)/shard_map/ppermute | solution.py:356
  68.9 5.8 %collective-permute-start.22 = (bf16[8,4096]{1,0:T(8,128)(2,1)S(1)}, bf16[8,4096]{1,0:T(8,128)(2,1)S(1)}, u32[]{:S(2)}, u32[]{:S(2)}) collective-permute-start(bf16[8,4096]{1,0:T(8,128)(2,1)S(1)} %get-tuple-element.29), channel_id=1, source_target_pairs={{0,4},{1,5},{2,6},{3,7},{4,0},{5,1},{6,2},{7,3},{8,12},{9,13},{10,... | collective-permute-start | bytes 196616 | tf_op jit(solution)/shard_map/ppermute | solution.py:356
  70.0 4.7 %collective-permute-start.23 = (bf16[8,4096]{1,0:T(8,128)(2,1)S(1)}, bf16[8,4096]{1,0:T(8,128)(2,1)S(1)}, u32[]{:S(2)}, u32[]{:S(2)}) collective-permute-start(bf16[8,4096]{1,0:T(8,128)(2,1)S(1)} %get-tuple-element.30), channel_id=1, source_target_pairs={{0,2},{1,3},{2,0},{3,1},{4,6},{5,7},{6,4},{7,5},{8,10},{9,11},{10,... | collective-permute-start | bytes 196616 | tf_op jit(solution)/shard_map/ppermute | solution.py:356
  (13 other events, 161.9 us)

commit v16 on v14

--- a/solution.py
+++ b/solution.py
@@ -442,7 +442,7 @@
     wait = back[len(plan.y)][:share, :1] * 0
     near_x = plan.swaps([value + wait for value in near[: len(plan.x)]], plan.x)
     near_y = plan.swaps(list(through.reshape(-1, share, width)), plan.y)
-    moe_sum = total_of([column[:share]] + near_x + near_y + others)
+    moe_sum = total_of([column[:share]] + near_x + near_y + others[-1:] + others[:-1])
     return (hidden + moe_sum).astype(BF)
 
 

time: 74.2 us -> 74.8 us (level)
  starting transfers between devices: 27.7 us -> 28.6 us
    ppermute x29, starting transfers between devices: 27.7 us -> 28.6 us  [swap(): lax.ppermute(value, ('dp', 'tensor'), [(i, i ^ flip) for i in range(self....]
where the time goes in v16:
time: 74.8 us; the launch traced here: 74.7 us
  waiting for transfers between devices  29 us (39%)
  starting transfers between devices  28.6 us (38%)
  Pallas kernels  14.7 us (20%)
  other arithmetic  1.77 us (2%)
    ppermute x29, waiting for transfers between devices, swap(): lax.ppermute(value, ('dp', 'tensor'), [(i, i ^ flip) for i in range(self....  29 us
    ppermute x29, starting transfers between devices, swap(): lax.ppermute(value, ('dp', 'tensor'), [(i, i ^ flip) for i in range(self....  28.6 us
    pallas_call x1, Pallas kernels, experts(): pl.pallas_call(functools.partial(expert_kernel, slots, sizes), out_shape=...  6.48 us
    pallas_call x2, Pallas kernels, attention(): pl.pallas_call(functools.partial(attention_kernel, flip), out_shape=tuple...  6.45 us
    pallas_call x1, Pallas kernels, projection(): pl.pallas_call(functools.partial(projection_kernel, parts, len(weights)),...  1.79 us
  transfers between devices with their start and end apart: 29, of which 18 were waited for; matrix products, arithmetic and copies ran while one was open for 1% of the time, Pallas kernels for 5%

profile of v16, /device:TPU:0, one launch (start us, length us, event | category | flops | bytes accessed | tf_op | source)
XLA Modules:
  0.0 74.7 jit_solution(14719771173390490012)
XLA Ops:
  0.0 2.4 %attention.2.refs_11_ = bf16[2,32,1152]{2,1,0:T(8,128)(2,1)S(1)} custom-call(s32[32]{0:T(128)} %refs_0_.3, bf16[32,32,128]{2,1,0:T(8,128)(2,1)} %refs_1_.4, bf16[32,2,128]{2,1,0:T(2,128)(2,1)} %refs_2_.4, bf16[32,2,128]{2,1,0:T(2,128)(2,1)} %refs_3_.4, bf16[32,2,32,128]{3,2,1,0:T(8,128)(2,1)} %refs_4_.3, bf16[32,2,32,128]{3,2,1,0:T(8,128)(2,1)} %refs_5_.3, ...), custom_call_target="tpu_custom_call" | custom-call | flops 1048576 | bytes 1048576 | tf_op jit(solution)/shard_map/attention/pallas_call | solution.py:199
  2.4 3.0 %collective-permute-start = (bf16[2,32,1152]{2,1,0:T(8,128)(2,1)S(1)}, bf16[2,32,1152]{2,1,0:T(8,128)(2,1)S(1)}, u32[]{:S(2)}, u32[]{:S(2)}) collective-permute-start(bf16[2,32,1152]{2,1,0:T(8,128)(2,1)S(1)} %attention.2.refs_11_), channel_id=1, source_target_pairs={{0,2},{1,3},{2,0},{3,1},{4,6},{5,7},{6,4},{7,5},{8,10},{9,11},{10,... | collective-permute-start | bytes 442376 | tf_op jit(solution)/shard_map/ppermute | solution.py:356
  5.5 4.0 %attention.3 = (bf16[2,32,1152]{2,1,0:T(8,128)(2,1)S(1)}, bf16[8,128]{1,0:T(8,128)(2,1)S(1)}, bf16[512,4096]{1,0:T(8,128)(2,1)S(1)}, bf16[512,4096]{1,0:T(8,128)(2,1)S(1)}) custom-call(s32[32]{0:T(128)} %refs_0_.3, bf16[32,32,128]{2,1,0:T(8,128)(2,1)} %refs_1_.4, bf16[32,2,128]{2,1,0:T(2,128)(2,1)} %refs_2_.4, bf16[32,2,128]{2,1,0:T(2,128)(2,1)} %refs_3_.4, ...), custom_call_target="tpu_custom_call" | custom-call | flops 9437184 | bytes 9437184 | tf_op jit(solution)/shard_map/attention/pallas_call | solution.py:199
  11.1 1.8 %projection.1 = bf16[2,2,8,4096]{3,2,1,0:T(8,128)(2,1)S(1)} custom-call(bf16[32,1152]{1,0:T(8,128)(2,1)S(1)} %get-tuple-element.37.refs_0_, bf16[32,1152]{1,0:T(8,128)(2,1)S(1)} %collective-permute-done.1.refs_1_, bf16[32,1152]{1,0:T(8,128)(2,1)S(1)} %get-tuple-element.35.refs_2_, bf16[32,1152]{1,0:T(8,128)(2,1)S(1)} %collective-permute-done.2.refs_3_, ...), custom_call_target="tpu_custom_call" | custom-call | tf_op jit(solution)/shard_map/projection/pallas_call | solution.py:258
  14.4 1.4 %collective-permute-start.4 = (bf16[8,4096]{1,0:T(8,128)(2,1)S(1)}, bf16[8,4096]{1,0:T(8,128)(2,1)S(1)}, u32[]{:S(2)}, u32[]{:S(2)}) collective-permute-start(bf16[8,4096]{1,0:T(8,128)(2,1)S(1)} %fusion.11), channel_id=1, source_target_pairs={{0,2},{1,3},{2,0},{3,1},{4,6},{5,7},{6,4},{7,5},{8,10},{9,11},{10,... | collective-permute-start | bytes 196616 | tf_op jit(solution)/shard_map/ppermute | solution.py:356
  15.8 3.0 %collective-permute-done.4 = bf16[8,4096]{1,0:T(8,128)(2,1)S(1)} collective-permute-done((bf16[8,4096]{1,0:T(8,128)(2,1)S(1)}, bf16[8,4096]{1,0:T(8,128)(2,1)S(1)}, u32[]{:S(2)}, u32[]{:S(2)}) %collective-permute-start.4) | collective-permute-done | bytes 65568 | tf_op jit(solution)/shard_map/ppermute | solution.py:356
  19.1 1.6 %collective-permute-start.5 = (bf16[8,4224]{1,0:T(8,128)(2,1)S(1)}, bf16[8,4224]{1,0:T(8,128)(2,1)S(1)}, u32[]{:S(2)}, u32[]{:S(2)}) collective-permute-start(bf16[8,4224]{1,0:T(8,128)(2,1)S(1)} %pad_maximum_fusion.1), channel_id=1, source_target_pairs={{0,8},{1,9},{2,10},{3,11},{4,12},{5,13},{6,14},{7,15},{8,0},{9,1},... | collective-permute-start | bytes 202760 | tf_op jit(solution)/shard_map/ppermute | solution.py:356
  20.7 2.6 %collective-permute-start.6 = (bf16[8,4224]{1,0:T(8,128)(2,1)S(1)}, bf16[8,4224]{1,0:T(8,128)(2,1)S(1)}, u32[]{:S(2)}, u32[]{:S(2)}) collective-permute-start(bf16[8,4224]{1,0:T(8,128)(2,1)S(1)} %pad_maximum_fusion.1), channel_id=1, source_target_pairs={{0,16},{1,17},{2,18},{3,19},{4,20},{5,21},{6,22},{7,23},{8,24},{9,... | collective-permute-start | bytes 202760 | tf_op jit(solution)/shard_map/ppermute | solution.py:356
  23.7 1.8 %collective-permute-start.9 = (bf16[8,4224]{1,0:T(8,128)(2,1)S(1)}, bf16[8,4224]{1,0:T(8,128)(2,1)S(1)}, u32[]{:S(2)}, u32[]{:S(2)}) collective-permute-start(bf16[8,4224]{1,0:T(8,128)(2,1)S(1)} %get-tuple-element.53), channel_id=1, source_target_pairs={{0,2},{1,3},{2,0},{3,1},{4,6},{5,7},{6,4},{7,5},{8,10},{9,11},{10,... | collective-permute-start | bytes 202760 | tf_op jit(solution)/shard_map/ppermute | solution.py:356
  25.6 1.5 %collective-permute-start.8 = (bf16[8,4224]{1,0:T(8,128)(2,1)S(1)}, bf16[8,4224]{1,0:T(8,128)(2,1)S(1)}, u32[]{:S(2)}, u32[]{:S(2)}) collective-permute-start(bf16[8,4224]{1,0:T(8,128)(2,1)S(1)} %get-tuple-element.53), channel_id=1, source_target_pairs={{0,4},{1,5},{2,6},{3,7},{4,0},{5,1},{6,2},{7,3},{8,12},{9,13},{10,... | collective-permute-start | bytes 202760 | tf_op jit(solution)/shard_map/ppermute | solution.py:356
  27.8 1.6 %collective-permute-done.7 = bf16[8,4224]{1,0:T(8,128)(2,1)S(1)} collective-permute-done((bf16[8,4224]{1,0:T(8,128)(2,1)S(1)}, bf16[8,4224]{1,0:T(8,128)(2,1)S(1)}, u32[]{:S(2)}, u32[]{:S(2)}) %collective-permute-start.7) | collective-permute-done | bytes 67616 | tf_op jit(solution)/shard_map/ppermute | solution.py:356
  29.4 2.2 %collective-permute-start.12 = (bf16[24,4224]{1,0:T(8,128)(2,1)S(1)}, bf16[24,4224]{1,0:T(8,128)(2,1)S(1)}, u32[]{:S(2)}, u32[]{:S(2)}) collective-permute-start(bf16[24,4224]{1,0:T(8,128)(2,1)S(1)} %get-tuple-element.44), channel_id=1, source_target_pairs={{0,6},{1,7},{2,4},{3,5},{4,2},{5,3},{6,0},{7,1},{8,14},{9,15},{10,... | collective-permute-start | bytes 608264 | tf_op jit(solution)/shard_map/ppermute | solution.py:356
  33.2 5.0 %collective-permute-done.12 = bf16[24,4224]{1,0:T(8,128)(2,1)S(1)} collective-permute-done((bf16[24,4224]{1,0:T(8,128)(2,1)S(1)}, bf16[24,4224]{1,0:T(8,128)(2,1)S(1)}, u32[]{:S(2)}, u32[]{:S(2)}) %collective-permute-start.12) | collective-permute-done | bytes 202784 | tf_op jit(solution)/shard_map/ppermute | solution.py:356
  38.2 1.3 %collective-permute-done.10 = bf16[24,4224]{1,0:T(8,128)(2,1)S(1)} collective-permute-done((bf16[24,4224]{1,0:T(8,128)(2,1)S(1)}, bf16[24,4224]{1,0:T(8,128)(2,1)S(1)}, u32[]{:S(2)}, u32[]{:S(2)}) %collective-permute-start.10) | collective-permute-done | bytes 202784 | tf_op jit(solution)/shard_map/ppermute | solution.py:356
  42.0 6.5 %experts.1 = (bf16[48,4096]{1,0:T(8,128)(2,1)S(1)}, bf16[24,4096]{1,0:T(8,128)(2,1)S(1)}, bf16[32,4096]{1,0:T(8,128)(2,1)S(1)}, bf16[24,4096]{1,0:T(8,128)(2,1)S...) custom-call(bf16[256,4224]{1,0:T(8,128)(2,1)S(1)} %constant_dynamic-, ...), custom_call_target="tpu_custom_call" | custom-call | tf_op jit(solution)/shard_map/experts/pallas_call | solution.py:327
  50.1 2.2 %collective-permute-start.23 = (bf16[24,4096]{1,0:T(8,128)(2,1)S(1)}, bf16[24,4096]{1,0:T(8,128)(2,1)S(1)}, u32[]{:S(2)}, u32[]{:S(2)}) collective-permute-start(bf16[24,4096]{1,0:T(8,128)(2,1)S(1)} %add_convert_fusion.2), channel_id=1, source_target_pairs={{0,6},{1,7},{2,4},{3,5},{4,2},{5,3},{6,0},{7,1},{8,14},{9,15},{10,... | collective-permute-start | bytes 589832 | tf_op jit(solution)/shard_map/ppermute | solution.py:356
  54.0 4.8 %collective-permute-done.23 = bf16[24,4096]{1,0:T(8,128)(2,1)S(1)} collective-permute-done((bf16[24,4096]{1,0:T(8,128)(2,1)S(1)}, bf16[24,4096]{1,0:T(8,128)(2,1)S(1)}, u32[]{:S(2)}, u32[]{:S(2)}) %collective-permute-start.23) | collective-permute-done | bytes 196640 | tf_op jit(solution)/shard_map/ppermute | solution.py:356
  58.8 3.4 %collective-permute-done.25 = bf16[24,4096]{1,0:T(8,128)(2,1)S(1)} collective-permute-done((bf16[24,4096]{1,0:T(8,128)(2,1)S(1)}, bf16[24,4096]{1,0:T(8,128)(2,1)S(1)}, u32[]{:S(2)}, u32[]{:S(2)}) %collective-permute-start.25) | collective-permute-done | bytes 196640 | tf_op jit(solution)/shard_map/ppermute | solution.py:356
  62.2 1.1 %collective-permute-done.19 = bf16[32,4096]{1,0:T(8,128)(2,1)S(1)} collective-permute-done((bf16[32,4096]{1,0:T(8,128)(2,1)S(1)}, bf16[32,4096]{1,0:T(8,128)(2,1)S(1)}, u32[]{:S(2)}, u32[]{:S(2)}) %collective-permute-start.19) | collective-permute-done | bytes 262176 | tf_op jit(solution)/shard_map/ppermute | solution.py:356
  63.5 1.9 %collective-permute-start.26 = (bf16[8,4096]{1,0:T(8,128)(2,1)S(1)}, bf16[8,4096]{1,0:T(8,128)(2,1)S(1)}, u32[]{:S(2)}, u32[]{:S(2)}) collective-permute-start(bf16[8,4096]{1,0:T(8,128)(2,1)S(1)} %get-tuple-element.31), channel_id=1, source_target_pairs={{0,24},{1,25},{2,26},{3,27},{4,28},{5,29},{6,30},{7,31},{8,16},{9,... | collective-permute-start | bytes 196616 | tf_op jit(solution)/shard_map/ppermute | solution.py:356
  65.9 2.0 %collective-permute-start.27 = (bf16[8,4096]{1,0:T(8,128)(2,1)S(1)}, bf16[8,4096]{1,0:T(8,128)(2,1)S(1)}, u32[]{:S(2)}, u32[]{:S(2)}) collective-permute-start(bf16[8,4096]{1,0:T(8,128)(2,1)S(1)} %get-tuple-element.33), channel_id=1, source_target_pairs={{0,8},{1,9},{2,10},{3,11},{4,12},{5,13},{6,14},{7,15},{8,0},{9,1},... | collective-permute-start | bytes 196616 | tf_op jit(solution)/shard_map/ppermute | solution.py:356
  68.1 1.6 %collective-permute-start.20 = (bf16[8,4096]{1,0:T(8,128)(2,1)S(1)}, bf16[8,4096]{1,0:T(8,128)(2,1)S(1)}, u32[]{:S(2)}, u32[]{:S(2)}) collective-permute-start(bf16[8,4096]{1,0:T(8,128)(2,1)S(1)} %get-tuple-element.29), channel_id=1, source_target_pairs={{0,4},{1,5},{2,6},{3,7},{4,0},{5,1},{6,2},{7,3},{8,12},{9,13},{10,... | collective-permute-start | bytes 196616 | tf_op jit(solution)/shard_map/ppermute | solution.py:356
  70.5 1.6 %collective-permute-done.28 = bf16[8,4096]{1,0:T(8,128)(2,1)S(1)} collective-permute-done((bf16[8,4096]{1,0:T(8,128)(2,1)S(1)}, bf16[8,4096]{1,0:T(8,128)(2,1)S(1)}, u32[]{:S(2)}, u32[]{:S(2)}) %collective-permute-start.28) | collective-permute-done | bytes 65568 | tf_op jit(solution)/shard_map/ppermute | solution.py:356
  72.5 1.5 %collective-permute-done.21 = bf16[8,4096]{1,0:T(8,128)(2,1)S(1)} collective-permute-done((bf16[8,4096]{1,0:T(8,128)(2,1)S(1)}, bf16[8,4096]{1,0:T(8,128)(2,1)S(1)}, u32[]{:S(2)}, u32[]{:S(2)}) %collective-permute-start.21) | collective-permute-done | bytes 65568 | tf_op jit(solution)/shard_map/ppermute | solution.py:356
  (85 shorter events, 14.4 us)
Async XLA Ops:
  2.4 7.2 %collective-permute-start = (bf16[2,32,1152]{2,1,0:T(8,128)(2,1)S(1)}, bf16[2,32,1152]{2,1,0:T(8,128)(2,1)S(1)}, u32[]{:S(2)}, u32[]{:S(2)}) collective-permute-start(bf16[2,32,1152]{2,1,0:T(8,128)(2,1)S(1)} %attention.2.refs_11_), channel_id=1, source_target_pairs={{0,2},{1,3},{2,0},{3,1},{4,6},{5,7},{6,4},{7,5},{8,10},{9,11},{10,... | collective-permute-start | bytes 442376 | tf_op jit(solution)/shard_map/ppermute | solution.py:356
  14.4 4.4 %collective-permute-start.4 = (bf16[8,4096]{1,0:T(8,128)(2,1)S(1)}, bf16[8,4096]{1,0:T(8,128)(2,1)S(1)}, u32[]{:S(2)}, u32[]{:S(2)}) collective-permute-start(bf16[8,4096]{1,0:T(8,128)(2,1)S(1)} %fusion.11), channel_id=1, source_target_pairs={{0,2},{1,3},{2,0},{3,1},{4,6},{5,7},{6,4},{7,5},{8,10},{9,11},{10,... | collective-permute-start | bytes 196616 | tf_op jit(solution)/shard_map/ppermute | solution.py:356
  19.1 4.5 %collective-permute-start.5 = (bf16[8,4224]{1,0:T(8,128)(2,1)S(1)}, bf16[8,4224]{1,0:T(8,128)(2,1)S(1)}, u32[]{:S(2)}, u32[]{:S(2)}) collective-permute-start(bf16[8,4224]{1,0:T(8,128)(2,1)S(1)} %pad_maximum_fusion.1), channel_id=1, source_target_pairs={{0,8},{1,9},{2,10},{3,11},{4,12},{5,13},{6,14},{7,15},{8,0},{9,1},... | collective-permute-start | bytes 202760 | tf_op jit(solution)/shard_map/ppermute | solution.py:356
  20.7 7.1 %collective-permute-start.6 = (bf16[8,4224]{1,0:T(8,128)(2,1)S(1)}, bf16[8,4224]{1,0:T(8,128)(2,1)S(1)}, u32[]{:S(2)}, u32[]{:S(2)}) collective-permute-start(bf16[8,4224]{1,0:T(8,128)(2,1)S(1)} %pad_maximum_fusion.1), channel_id=1, source_target_pairs={{0,16},{1,17},{2,18},{3,19},{4,20},{5,21},{6,22},{7,23},{8,24},{9,... | collective-permute-start | bytes 202760 | tf_op jit(solution)/shard_map/ppermute | solution.py:356
  23.3 6.1 %collective-permute-start.7 = (bf16[8,4224]{1,0:T(8,128)(2,1)S(1)}, bf16[8,4224]{1,0:T(8,128)(2,1)S(1)}, u32[]{:S(2)}, u32[]{:S(2)}) collective-permute-start(bf16[8,4224]{1,0:T(8,128)(2,1)S(1)} %pad_maximum_fusion.1), channel_id=1, source_target_pairs={{0,24},{1,25},{2,26},{3,27},{4,28},{5,29},{6,30},{7,31},{8,16},{9,... | collective-permute-start | bytes 202760 | tf_op jit(solution)/shard_map/ppermute | solution.py:356
  23.7 8.7 %collective-permute-start.9 = (bf16[8,4224]{1,0:T(8,128)(2,1)S(1)}, bf16[8,4224]{1,0:T(8,128)(2,1)S(1)}, u32[]{:S(2)}, u32[]{:S(2)}) collective-permute-start(bf16[8,4224]{1,0:T(8,128)(2,1)S(1)} %get-tuple-element.53), channel_id=1, source_target_pairs={{0,2},{1,3},{2,0},{3,1},{4,6},{5,7},{6,4},{7,5},{8,10},{9,11},{10,... | collective-permute-start | bytes 202760 | tf_op jit(solution)/shard_map/ppermute | solution.py:356
  25.6 7.5 %collective-permute-start.8 = (bf16[8,4224]{1,0:T(8,128)(2,1)S(1)}, bf16[8,4224]{1,0:T(8,128)(2,1)S(1)}, u32[]{:S(2)}, u32[]{:S(2)}) collective-permute-start(bf16[8,4224]{1,0:T(8,128)(2,1)S(1)} %get-tuple-element.53), channel_id=1, source_target_pairs={{0,4},{1,5},{2,6},{3,7},{4,0},{5,1},{6,2},{7,3},{8,12},{9,13},{10,... | collective-permute-start | bytes 202760 | tf_op jit(solution)/shard_map/ppermute | solution.py:356
  29.4 8.7 %collective-permute-start.12 = (bf16[24,4224]{1,0:T(8,128)(2,1)S(1)}, bf16[24,4224]{1,0:T(8,128)(2,1)S(1)}, u32[]{:S(2)}, u32[]{:S(2)}) collective-permute-start(bf16[24,4224]{1,0:T(8,128)(2,1)S(1)} %get-tuple-element.44), channel_id=1, source_target_pairs={{0,6},{1,7},{2,4},{3,5},{4,2},{5,3},{6,0},{7,1},{8,14},{9,15},{10,... | collective-permute-start | bytes 608264 | tf_op jit(solution)/shard_map/ppermute | solution.py:356
  31.6 7.9 %collective-permute-start.10 = (bf16[24,4224]{1,0:T(8,128)(2,1)S(1)}, bf16[24,4224]{1,0:T(8,128)(2,1)S(1)}, u32[]{:S(2)}, u32[]{:S(2)}) collective-permute-start(bf16[24,4224]{1,0:T(8,128)(2,1)S(1)} %get-tuple-element.44), channel_id=1, source_target_pairs={{0,2},{1,3},{2,0},{3,1},{4,6},{5,7},{6,4},{7,5},{8,10},{9,11},{10,... | collective-permute-start | bytes 608264 | tf_op jit(solution)/shard_map/ppermute | solution.py:356
  32.5 7.9 %collective-permute-start.11 = (bf16[32,4224]{1,0:T(8,128)(2,1)S(1)}, bf16[32,4224]{1,0:T(8,128)(2,1)S(1)}, u32[]{:S(2)}, u32[]{:S(2)}) collective-permute-start(bf16[32,4224]{1,0:T(8,128)(2,1)S(1)} %pad_maximum_fusion), channel_id=1, source_target_pairs={{0,4},{1,5},{2,6},{3,7},{4,0},{5,1},{6,2},{7,3},{8,12},{9,13},{10,... | collective-permute-start | bytes 811016 | tf_op jit(solution)/shard_map/ppermute | solution.py:356
  33.1 7.3 %collective-permute-start.13 = (bf16[48,4224]{1,0:T(8,128)(2,1)S(1)}, bf16[48,4224]{1,0:T(8,128)(2,1)S(1)}, u32[]{:S(2)}, u32[]{:S(2)}) collective-permute-start(bf16[48,4224]{1,0:T(8,128)(2,1)S(1)} %get-tuple-element.38), channel_id=1, source_target_pairs={{0,1},{1,0},{2,3},{3,2},{4,5},{5,4},{6,7},{7,6},{8,9},{9,8},{10,11... | collective-permute-start | bytes 1216520 | tf_op jit(solution)/shard_map/ppermute | solution.py:356
  38.2 3.8 %collective-permute-start.16 = (bf16[24,4224]{1,0:T(8,128)(2,1)S(1)}, bf16[24,4224]{1,0:T(8,128)(2,1)S(1)}, u32[]{:S(2)}, u32[]{:S(2)}) collective-permute-start(bf16[24,4224]{1,0:T(8,128)(2,1)S(1)} %collective-permute-done.12), channel_id=1, source_target_pairs={{0,1},{1,0},{2,3},{3,2},{4,5},{5,4},{6,7},{7,6},{8,9},{9,8},{10,11... | collective-permute-start | bytes 608264 | tf_op jit(solution)/shard_map/ppermute | solution.py:356
  40.4 1.5 %collective-permute-start.15 = (bf16[32,4224]{1,0:T(8,128)(2,1)S(1)}, bf16[32,4224]{1,0:T(8,128)(2,1)S(1)}, u32[]{:S(2)}, u32[]{:S(2)}) collective-permute-start(bf16[32,4224]{1,0:T(8,128)(2,1)S(1)} %collective-permute-done.11), channel_id=1, source_target_pairs={{0,1},{1,0},{2,3},{3,2},{4,5},{5,4},{6,7},{7,6},{8,9},{9,8},{10,11... | collective-permute-start | bytes 811016 | tf_op jit(solution)/shard_map/ppermute | solution.py:356
  48.7 3.5 %collective-permute-start.24 = (bf16[24,4096]{1,0:T(8,128)(2,1)S(1)}, bf16[24,4096]{1,0:T(8,128)(2,1)S(1)}, u32[]{:S(2)}, u32[]{:S(2)}) collective-permute-start(bf16[24,4096]{1,0:T(8,128)(2,1)S(1)} %get-tuple-element.28), channel_id=1, source_target_pairs={{0,1},{1,0},{2,3},{3,2},{4,5},{5,4},{6,7},{7,6},{8,9},{9,8},{10,11... | collective-permute-start | bytes 589832 | tf_op jit(solution)/shard_map/ppermute | solution.py:356
  49.1 4.1 %collective-permute-start.18 = (bf16[32,4096]{1,0:T(8,128)(2,1)S(1)}, bf16[32,4096]{1,0:T(8,128)(2,1)S(1)}, u32[]{:S(2)}, u32[]{:S(2)}) collective-permute-start(bf16[32,4096]{1,0:T(8,128)(2,1)S(1)} %get-tuple-element.24), channel_id=1, source_target_pairs={{0,1},{1,0},{2,3},{3,2},{4,5},{5,4},{6,7},{7,6},{8,9},{9,8},{10,11... | collective-permute-start | bytes 786440 | tf_op jit(solution)/shard_map/ppermute | solution.py:356
  49.2 4.7 %collective-permute-start.17 = (bf16[48,4096]{1,0:T(8,128)(2,1)S(1)}, bf16[48,4096]{1,0:T(8,128)(2,1)S(1)}, u32[]{:S(2)}, u32[]{:S(2)}) collective-permute-start(bf16[48,4096]{1,0:T(8,128)(2,1)S(1)} %get-tuple-element.22), channel_id=1, source_target_pairs={{0,1},{1,0},{2,3},{3,2},{4,5},{5,4},{6,7},{7,6},{8,9},{9,8},{10,11... | collective-permute-start | bytes 1179656 | tf_op jit(solution)/shard_map/ppermute | solution.py:356
  50.1 8.8 %collective-permute-start.23 = (bf16[24,4096]{1,0:T(8,128)(2,1)S(1)}, bf16[24,4096]{1,0:T(8,128)(2,1)S(1)}, u32[]{:S(2)}, u32[]{:S(2)}) collective-permute-start(bf16[24,4096]{1,0:T(8,128)(2,1)S(1)} %add_convert_fusion.2), channel_id=1, source_target_pairs={{0,6},{1,7},{2,4},{3,5},{4,2},{5,3},{6,0},{7,1},{8,14},{9,15},{10,... | collective-permute-start | bytes 589832 | tf_op jit(solution)/shard_map/ppermute | solution.py:356
  52.3 9.9 %collective-permute-start.25 = (bf16[24,4096]{1,0:T(8,128)(2,1)S(1)}, bf16[24,4096]{1,0:T(8,128)(2,1)S(1)}, u32[]{:S(2)}, u32[]{:S(2)}) collective-permute-start(bf16[24,4096]{1,0:T(8,128)(2,1)S(1)} %add_convert_fusion.1), channel_id=1, source_target_pairs={{0,2},{1,3},{2,0},{3,1},{4,6},{5,7},{6,4},{7,5},{8,10},{9,11},{10,... | collective-permute-start | bytes 589832 | tf_op jit(solution)/shard_map/ppermute | solution.py:356
  53.3 10.1 %collective-permute-start.19 = (bf16[32,4096]{1,0:T(8,128)(2,1)S(1)}, bf16[32,4096]{1,0:T(8,128)(2,1)S(1)}, u32[]{:S(2)}, u32[]{:S(2)}) collective-permute-start(bf16[32,4096]{1,0:T(8,128)(2,1)S(1)} %add_convert_fusion), channel_id=1, source_target_pairs={{0,4},{1,5},{2,6},{3,7},{4,0},{5,1},{6,2},{7,3},{8,12},{9,13},{10,... | collective-permute-start | bytes 786440 | tf_op jit(solution)/shard_map/ppermute | solution.py:356
  63.5 7.1 %collective-permute-start.26 = (bf16[8,4096]{1,0:T(8,128)(2,1)S(1)}, bf16[8,4096]{1,0:T(8,128)(2,1)S(1)}, u32[]{:S(2)}, u32[]{:S(2)}) collective-permute-start(bf16[8,4096]{1,0:T(8,128)(2,1)S(1)} %get-tuple-element.31), channel_id=1, source_target_pairs={{0,24},{1,25},{2,26},{3,27},{4,28},{5,29},{6,30},{7,31},{8,16},{9,... | collective-permute-start | bytes 196616 | tf_op jit(solution)/shard_map/ppermute | solution.py:356
  65.4 6.8 %collective-permute-start.28 = (bf16[8,4096]{1,0:T(8,128)(2,1)S(1)}, bf16[8,4096]{1,0:T(8,128)(2,1)S(1)}, u32[]{:S(2)}, u32[]{:S(2)}) collective-permute-start(bf16[8,4096]{1,0:T(8,128)(2,1)S(1)} %get-tuple-element.32), channel_id=1, source_target_pairs={{0,16},{1,17},{2,18},{3,19},{4,20},{5,21},{6,22},{7,23},{8,24},{9,... | collective-permute-start | bytes 196616 | tf_op jit(solution)/shard_map/ppermute | solution.py:356
  65.9 6.3 %collective-permute-start.27 = (bf16[8,4096]{1,0:T(8,128)(2,1)S(1)}, bf16[8,4096]{1,0:T(8,128)(2,1)S(1)}, u32[]{:S(2)}, u32[]{:S(2)}) collective-permute-start(bf16[8,4096]{1,0:T(8,128)(2,1)S(1)} %get-tuple-element.33), channel_id=1, source_target_pairs={{0,8},{1,9},{2,10},{3,11},{4,12},{5,13},{6,14},{7,15},{8,0},{9,1},... | collective-permute-start | bytes 196616 | tf_op jit(solution)/shard_map/ppermute | solution.py:356
  68.1 4.3 %collective-permute-start.20 = (bf16[8,4096]{1,0:T(8,128)(2,1)S(1)}, bf16[8,4096]{1,0:T(8,128)(2,1)S(1)}, u32[]{:S(2)}, u32[]{:S(2)}) collective-permute-start(bf16[8,4096]{1,0:T(8,128)(2,1)S(1)} %get-tuple-element.29), channel_id=1, source_target_pairs={{0,4},{1,5},{2,6},{3,7},{4,0},{5,1},{6,2},{7,3},{8,12},{9,13},{10,... | collective-permute-start | bytes 196616 | tf_op jit(solution)/shard_map/ppermute | solution.py:356
  69.7 4.3 %collective-permute-start.21 = (bf16[8,4096]{1,0:T(8,128)(2,1)S(1)}, bf16[8,4096]{1,0:T(8,128)(2,1)S(1)}, u32[]{:S(2)}, u32[]{:S(2)}) collective-permute-start(bf16[8,4096]{1,0:T(8,128)(2,1)S(1)} %get-tuple-element.30), channel_id=1, source_target_pairs={{0,2},{1,3},{2,0},{3,1},{4,6},{5,7},{6,4},{7,5},{8,10},{9,11},{10,... | collective-permute-start | bytes 196616 | tf_op jit(solution)/shard_map/ppermute | solution.py:356
  (11 other events, 153.4 us)

commit v17 on v16

--- a/solution.py
+++ b/solution.py
@@ -442,7 +442,7 @@
     wait = back[len(plan.y)][:share, :1] * 0
     near_x = plan.swaps([value + wait for value in near[: len(plan.x)]], plan.x)
     near_y = plan.swaps(list(through.reshape(-1, share, width)), plan.y)
-    moe_sum = total_of([column[:share]] + near_x + near_y + others[-1:] + others[:-1])
+    moe_sum = total_of([column[:share]] + near_x + near_y + others[::-1])
     return (hidden + moe_sum).astype(BF)
 
 

time: 74.8 us -> 74.8 us (level)
  no operation moved by 1% of the time
where the time goes in v17:
time: 74.8 us; the launch traced here: 74.7 us
  waiting for transfers between devices  29 us (39%)
  starting transfers between devices  28.6 us (38%)
  Pallas kernels  14.7 us (20%)
  other arithmetic  1.77 us (2%)
    ppermute x29, waiting for transfers between devices, swap(): lax.ppermute(value, ('dp', 'tensor'), [(i, i ^ flip) for i in range(self....  29 us
    ppermute x29, starting transfers between devices, swap(): lax.ppermute(value, ('dp', 'tensor'), [(i, i ^ flip) for i in range(self....  28.6 us
    pallas_call x1, Pallas kernels, experts(): pl.pallas_call(functools.partial(expert_kernel, slots, sizes), out_shape=...  6.48 us
    pallas_call x2, Pallas kernels, attention(): pl.pallas_call(functools.partial(attention_kernel, flip), out_shape=tuple...  6.45 us
    pallas_call x1, Pallas kernels, projection(): pl.pallas_call(functools.partial(projection_kernel, parts, len(weights)),...  1.79 us
  transfers between devices with their start and end apart: 29, of which 18 were waited for; matrix products, arithmetic and copies ran while one was open for 1% of the time, Pallas kernels for 5%

profile of v17, /device:TPU:0, one launch (start us, length us, event | category | flops | bytes accessed | tf_op | source)
XLA Modules:
  0.0 74.7 jit_solution(17854932196624902283)
XLA Ops:
  0.0 2.4 %attention.2.refs_11_ = bf16[2,32,1152]{2,1,0:T(8,128)(2,1)S(1)} custom-call(s32[32]{0:T(128)} %refs_0_.3, bf16[32,32,128]{2,1,0:T(8,128)(2,1)} %refs_1_.4, bf16[32,2,128]{2,1,0:T(2,128)(2,1)} %refs_2_.4, bf16[32,2,128]{2,1,0:T(2,128)(2,1)} %refs_3_.4, bf16[32,2,32,128]{3,2,1,0:T(8,128)(2,1)} %refs_4_.3, bf16[32,2,32,128]{3,2,1,0:T(8,128)(2,1)} %refs_5_.3, ...), custom_call_target="tpu_custom_call" | custom-call | flops 1048576 | bytes 1048576 | tf_op jit(solution)/shard_map/attention/pallas_call | solution.py:199
  2.4 3.0 %collective-permute-start = (bf16[2,32,1152]{2,1,0:T(8,128)(2,1)S(1)}, bf16[2,32,1152]{2,1,0:T(8,128)(2,1)S(1)}, u32[]{:S(2)}, u32[]{:S(2)}) collective-permute-start(bf16[2,32,1152]{2,1,0:T(8,128)(2,1)S(1)} %attention.2.refs_11_), channel_id=1, source_target_pairs={{0,2},{1,3},{2,0},{3,1},{4,6},{5,7},{6,4},{7,5},{8,10},{9,11},{10,... | collective-permute-start | bytes 442376 | tf_op jit(solution)/shard_map/ppermute | solution.py:356
  5.5 4.0 %attention.3 = (bf16[2,32,1152]{2,1,0:T(8,128)(2,1)S(1)}, bf16[8,128]{1,0:T(8,128)(2,1)S(1)}, bf16[512,4096]{1,0:T(8,128)(2,1)S(1)}, bf16[512,4096]{1,0:T(8,128)(2,1)S(1)}) custom-call(s32[32]{0:T(128)} %refs_0_.3, bf16[32,32,128]{2,1,0:T(8,128)(2,1)} %refs_1_.4, bf16[32,2,128]{2,1,0:T(2,128)(2,1)} %refs_2_.4, bf16[32,2,128]{2,1,0:T(2,128)(2,1)} %refs_3_.4, ...), custom_call_target="tpu_custom_call" | custom-call | flops 9437184 | bytes 9437184 | tf_op jit(solution)/shard_map/attention/pallas_call | solution.py:199
  11.1 1.8 %projection.1 = bf16[2,2,8,4096]{3,2,1,0:T(8,128)(2,1)S(1)} custom-call(bf16[32,1152]{1,0:T(8,128)(2,1)S(1)} %get-tuple-element.37.refs_0_, bf16[32,1152]{1,0:T(8,128)(2,1)S(1)} %collective-permute-done.1.refs_1_, bf16[32,1152]{1,0:T(8,128)(2,1)S(1)} %get-tuple-element.35.refs_2_, bf16[32,1152]{1,0:T(8,128)(2,1)S(1)} %collective-permute-done.2.refs_3_, ...), custom_call_target="tpu_custom_call" | custom-call | tf_op jit(solution)/shard_map/projection/pallas_call | solution.py:258
  14.4 1.4 %collective-permute-start.4 = (bf16[8,4096]{1,0:T(8,128)(2,1)S(1)}, bf16[8,4096]{1,0:T(8,128)(2,1)S(1)}, u32[]{:S(2)}, u32[]{:S(2)}) collective-permute-start(bf16[8,4096]{1,0:T(8,128)(2,1)S(1)} %fusion.11), channel_id=1, source_target_pairs={{0,2},{1,3},{2,0},{3,1},{4,6},{5,7},{6,4},{7,5},{8,10},{9,11},{10,... | collective-permute-start | bytes 196616 | tf_op jit(solution)/shard_map/ppermute | solution.py:356
  15.8 3.0 %collective-permute-done.4 = bf16[8,4096]{1,0:T(8,128)(2,1)S(1)} collective-permute-done((bf16[8,4096]{1,0:T(8,128)(2,1)S(1)}, bf16[8,4096]{1,0:T(8,128)(2,1)S(1)}, u32[]{:S(2)}, u32[]{:S(2)}) %collective-permute-start.4) | collective-permute-done | bytes 65568 | tf_op jit(solution)/shard_map/ppermute | solution.py:356
  19.1 1.6 %collective-permute-start.5 = (bf16[8,4224]{1,0:T(8,128)(2,1)S(1)}, bf16[8,4224]{1,0:T(8,128)(2,1)S(1)}, u32[]{:S(2)}, u32[]{:S(2)}) collective-permute-start(bf16[8,4224]{1,0:T(8,128)(2,1)S(1)} %pad_maximum_fusion.1), channel_id=1, source_target_pairs={{0,8},{1,9},{2,10},{3,11},{4,12},{5,13},{6,14},{7,15},{8,0},{9,1},... | collective-permute-start | bytes 202760 | tf_op jit(solution)/shard_map/ppermute | solution.py:356
  20.7 2.6 %collective-permute-start.6 = (bf16[8,4224]{1,0:T(8,128)(2,1)S(1)}, bf16[8,4224]{1,0:T(8,128)(2,1)S(1)}, u32[]{:S(2)}, u32[]{:S(2)}) collective-permute-start(bf16[8,4224]{1,0:T(8,128)(2,1)S(1)} %pad_maximum_fusion.1), channel_id=1, source_target_pairs={{0,16},{1,17},{2,18},{3,19},{4,20},{5,21},{6,22},{7,23},{8,24},{9,... | collective-permute-start | bytes 202760 | tf_op jit(solution)/shard_map/ppermute | solution.py:356
  23.7 1.8 %collective-permute-start.9 = (bf16[8,4224]{1,0:T(8,128)(2,1)S(1)}, bf16[8,4224]{1,0:T(8,128)(2,1)S(1)}, u32[]{:S(2)}, u32[]{:S(2)}) collective-permute-start(bf16[8,4224]{1,0:T(8,128)(2,1)S(1)} %get-tuple-element.53), channel_id=1, source_target_pairs={{0,2},{1,3},{2,0},{3,1},{4,6},{5,7},{6,4},{7,5},{8,10},{9,11},{10,... | collective-permute-start | bytes 202760 | tf_op jit(solution)/shard_map/ppermute | solution.py:356
  25.6 1.5 %collective-permute-start.8 = (bf16[8,4224]{1,0:T(8,128)(2,1)S(1)}, bf16[8,4224]{1,0:T(8,128)(2,1)S(1)}, u32[]{:S(2)}, u32[]{:S(2)}) collective-permute-start(bf16[8,4224]{1,0:T(8,128)(2,1)S(1)} %get-tuple-element.53), channel_id=1, source_target_pairs={{0,4},{1,5},{2,6},{3,7},{4,0},{5,1},{6,2},{7,3},{8,12},{9,13},{10,... | collective-permute-start | bytes 202760 | tf_op jit(solution)/shard_map/ppermute | solution.py:356
  27.8 1.6 %collective-permute-done.7 = bf16[8,4224]{1,0:T(8,128)(2,1)S(1)} collective-permute-done((bf16[8,4224]{1,0:T(8,128)(2,1)S(1)}, bf16[8,4224]{1,0:T(8,128)(2,1)S(1)}, u32[]{:S(2)}, u32[]{:S(2)}) %collective-permute-start.7) | collective-permute-done | bytes 67616 | tf_op jit(solution)/shard_map/ppermute | solution.py:356
  29.4 2.2 %collective-permute-start.12 = (bf16[24,4224]{1,0:T(8,128)(2,1)S(1)}, bf16[24,4224]{1,0:T(8,128)(2,1)S(1)}, u32[]{:S(2)}, u32[]{:S(2)}) collective-permute-start(bf16[24,4224]{1,0:T(8,128)(2,1)S(1)} %get-tuple-element.44), channel_id=1, source_target_pairs={{0,6},{1,7},{2,4},{3,5},{4,2},{5,3},{6,0},{7,1},{8,14},{9,15},{10,... | collective-permute-start | bytes 608264 | tf_op jit(solution)/shard_map/ppermute | solution.py:356
  33.2 5.0 %collective-permute-done.12 = bf16[24,4224]{1,0:T(8,128)(2,1)S(1)} collective-permute-done((bf16[24,4224]{1,0:T(8,128)(2,1)S(1)}, bf16[24,4224]{1,0:T(8,128)(2,1)S(1)}, u32[]{:S(2)}, u32[]{:S(2)}) %collective-permute-start.12) | collective-permute-done | bytes 202784 | tf_op jit(solution)/shard_map/ppermute | solution.py:356
  38.2 1.3 %collective-permute-done.10 = bf16[24,4224]{1,0:T(8,128)(2,1)S(1)} collective-permute-done((bf16[24,4224]{1,0:T(8,128)(2,1)S(1)}, bf16[24,4224]{1,0:T(8,128)(2,1)S(1)}, u32[]{:S(2)}, u32[]{:S(2)}) %collective-permute-start.10) | collective-permute-done | bytes 202784 | tf_op jit(solution)/shard_map/ppermute | solution.py:356
  42.0 6.5 %experts.1 = (bf16[48,4096]{1,0:T(8,128)(2,1)S(1)}, bf16[24,4096]{1,0:T(8,128)(2,1)S(1)}, bf16[32,4096]{1,0:T(8,128)(2,1)S(1)}, bf16[24,4096]{1,0:T(8,128)(2,1)S...) custom-call(bf16[256,4224]{1,0:T(8,128)(2,1)S(1)} %constant_dynamic-, ...), custom_call_target="tpu_custom_call" | custom-call | tf_op jit(solution)/shard_map/experts/pallas_call | solution.py:327
  50.1 2.2 %collective-permute-start.23 = (bf16[24,4096]{1,0:T(8,128)(2,1)S(1)}, bf16[24,4096]{1,0:T(8,128)(2,1)S(1)}, u32[]{:S(2)}, u32[]{:S(2)}) collective-permute-start(bf16[24,4096]{1,0:T(8,128)(2,1)S(1)} %add_convert_fusion.2), channel_id=1, source_target_pairs={{0,6},{1,7},{2,4},{3,5},{4,2},{5,3},{6,0},{7,1},{8,14},{9,15},{10,... | collective-permute-start | bytes 589832 | tf_op jit(solution)/shard_map/ppermute | solution.py:356
  54.0 4.8 %collective-permute-done.23 = bf16[24,4096]{1,0:T(8,128)(2,1)S(1)} collective-permute-done((bf16[24,4096]{1,0:T(8,128)(2,1)S(1)}, bf16[24,4096]{1,0:T(8,128)(2,1)S(1)}, u32[]{:S(2)}, u32[]{:S(2)}) %collective-permute-start.23) | collective-permute-done | bytes 196640 | tf_op jit(solution)/shard_map/ppermute | solution.py:356
  58.8 3.4 %collective-permute-done.25 = bf16[24,4096]{1,0:T(8,128)(2,1)S(1)} collective-permute-done((bf16[24,4096]{1,0:T(8,128)(2,1)S(1)}, bf16[24,4096]{1,0:T(8,128)(2,1)S(1)}, u32[]{:S(2)}, u32[]{:S(2)}) %collective-permute-start.25) | collective-permute-done | bytes 196640 | tf_op jit(solution)/shard_map/ppermute | solution.py:356
  62.2 1.1 %collective-permute-done.19 = bf16[32,4096]{1,0:T(8,128)(2,1)S(1)} collective-permute-done((bf16[32,4096]{1,0:T(8,128)(2,1)S(1)}, bf16[32,4096]{1,0:T(8,128)(2,1)S(1)}, u32[]{:S(2)}, u32[]{:S(2)}) %collective-permute-start.19) | collective-permute-done | bytes 262176 | tf_op jit(solution)/shard_map/ppermute | solution.py:356
  63.5 1.9 %collective-permute-start.26 = (bf16[8,4096]{1,0:T(8,128)(2,1)S(1)}, bf16[8,4096]{1,0:T(8,128)(2,1)S(1)}, u32[]{:S(2)}, u32[]{:S(2)}) collective-permute-start(bf16[8,4096]{1,0:T(8,128)(2,1)S(1)} %get-tuple-element.31), channel_id=1, source_target_pairs={{0,24},{1,25},{2,26},{3,27},{4,28},{5,29},{6,30},{7,31},{8,16},{9,... | collective-permute-start | bytes 196616 | tf_op jit(solution)/shard_map/ppermute | solution.py:356
  66.4 1.5 %collective-permute-start.27 = (bf16[8,4096]{1,0:T(8,128)(2,1)S(1)}, bf16[8,4096]{1,0:T(8,128)(2,1)S(1)}, u32[]{:S(2)}, u32[]{:S(2)}) collective-permute-start(bf16[8,4096]{1,0:T(8,128)(2,1)S(1)} %get-tuple-element.33), channel_id=1, source_target_pairs={{0,16},{1,17},{2,18},{3,19},{4,20},{5,21},{6,22},{7,23},{8,24},{9,... | collective-permute-start | bytes 196616 | tf_op jit(solution)/shard_map/ppermute | solution.py:356
  68.1 1.6 %collective-permute-start.20 = (bf16[8,4096]{1,0:T(8,128)(2,1)S(1)}, bf16[8,4096]{1,0:T(8,128)(2,1)S(1)}, u32[]{:S(2)}, u32[]{:S(2)}) collective-permute-start(bf16[8,4096]{1,0:T(8,128)(2,1)S(1)} %get-tuple-element.29), channel_id=1, source_target_pairs={{0,4},{1,5},{2,6},{3,7},{4,0},{5,1},{6,2},{7,3},{8,12},{9,13},{10,... | collective-permute-start | bytes 196616 | tf_op jit(solution)/shard_map/ppermute | solution.py:356
  70.5 1.7 %collective-permute-done.27 = bf16[8,4096]{1,0:T(8,128)(2,1)S(1)} collective-permute-done((bf16[8,4096]{1,0:T(8,128)(2,1)S(1)}, bf16[8,4096]{1,0:T(8,128)(2,1)S(1)}, u32[]{:S(2)}, u32[]{:S(2)}) %collective-permute-start.27) | collective-permute-done | bytes 65568 | tf_op jit(solution)/shard_map/ppermute | solution.py:356
  72.5 1.5 %collective-permute-done.21 = bf16[8,4096]{1,0:T(8,128)(2,1)S(1)} collective-permute-done((bf16[8,4096]{1,0:T(8,128)(2,1)S(1)}, bf16[8,4096]{1,0:T(8,128)(2,1)S(1)}, u32[]{:S(2)}, u32[]{:S(2)}) %collective-permute-start.21) | collective-permute-done | bytes 65568 | tf_op jit(solution)/shard_map/ppermute | solution.py:356
  (85 shorter events, 14.8 us)
Async XLA Ops:
  2.4 7.2 %collective-permute-start = (bf16[2,32,1152]{2,1,0:T(8,128)(2,1)S(1)}, bf16[2,32,1152]{2,1,0:T(8,128)(2,1)S(1)}, u32[]{:S(2)}, u32[]{:S(2)}) collective-permute-start(bf16[2,32,1152]{2,1,0:T(8,128)(2,1)S(1)} %attention.2.refs_11_), channel_id=1, source_target_pairs={{0,2},{1,3},{2,0},{3,1},{4,6},{5,7},{6,4},{7,5},{8,10},{9,11},{10,... | collective-permute-start | bytes 442376 | tf_op jit(solution)/shard_map/ppermute | solution.py:356
  14.4 4.4 %collective-permute-start.4 = (bf16[8,4096]{1,0:T(8,128)(2,1)S(1)}, bf16[8,4096]{1,0:T(8,128)(2,1)S(1)}, u32[]{:S(2)}, u32[]{:S(2)}) collective-permute-start(bf16[8,4096]{1,0:T(8,128)(2,1)S(1)} %fusion.11), channel_id=1, source_target_pairs={{0,2},{1,3},{2,0},{3,1},{4,6},{5,7},{6,4},{7,5},{8,10},{9,11},{10,... | collective-permute-start | bytes 196616 | tf_op jit(solution)/shard_map/ppermute | solution.py:356
  19.1 4.5 %collective-permute-start.5 = (bf16[8,4224]{1,0:T(8,128)(2,1)S(1)}, bf16[8,4224]{1,0:T(8,128)(2,1)S(1)}, u32[]{:S(2)}, u32[]{:S(2)}) collective-permute-start(bf16[8,4224]{1,0:T(8,128)(2,1)S(1)} %pad_maximum_fusion.1), channel_id=1, source_target_pairs={{0,8},{1,9},{2,10},{3,11},{4,12},{5,13},{6,14},{7,15},{8,0},{9,1},... | collective-permute-start | bytes 202760 | tf_op jit(solution)/shard_map/ppermute | solution.py:356
  20.7 7.1 %collective-permute-start.6 = (bf16[8,4224]{1,0:T(8,128)(2,1)S(1)}, bf16[8,4224]{1,0:T(8,128)(2,1)S(1)}, u32[]{:S(2)}, u32[]{:S(2)}) collective-permute-start(bf16[8,4224]{1,0:T(8,128)(2,1)S(1)} %pad_maximum_fusion.1), channel_id=1, source_target_pairs={{0,16},{1,17},{2,18},{3,19},{4,20},{5,21},{6,22},{7,23},{8,24},{9,... | collective-permute-start | bytes 202760 | tf_op jit(solution)/shard_map/ppermute | solution.py:356
  23.3 6.1 %collective-permute-start.7 = (bf16[8,4224]{1,0:T(8,128)(2,1)S(1)}, bf16[8,4224]{1,0:T(8,128)(2,1)S(1)}, u32[]{:S(2)}, u32[]{:S(2)}) collective-permute-start(bf16[8,4224]{1,0:T(8,128)(2,1)S(1)} %pad_maximum_fusion.1), channel_id=1, source_target_pairs={{0,24},{1,25},{2,26},{3,27},{4,28},{5,29},{6,30},{7,31},{8,16},{9,... | collective-permute-start | bytes 202760 | tf_op jit(solution)/shard_map/ppermute | solution.py:356
  23.7 8.7 %collective-permute-start.9 = (bf16[8,4224]{1,0:T(8,128)(2,1)S(1)}, bf16[8,4224]{1,0:T(8,128)(2,1)S(1)}, u32[]{:S(2)}, u32[]{:S(2)}) collective-permute-start(bf16[8,4224]{1,0:T(8,128)(2,1)S(1)} %get-tuple-element.53), channel_id=1, source_target_pairs={{0,2},{1,3},{2,0},{3,1},{4,6},{5,7},{6,4},{7,5},{8,10},{9,11},{10,... | collective-permute-start | bytes 202760 | tf_op jit(solution)/shard_map/ppermute | solution.py:356
  25.6 7.5 %collective-permute-start.8 = (bf16[8,4224]{1,0:T(8,128)(2,1)S(1)}, bf16[8,4224]{1,0:T(8,128)(2,1)S(1)}, u32[]{:S(2)}, u32[]{:S(2)}) collective-permute-start(bf16[8,4224]{1,0:T(8,128)(2,1)S(1)} %get-tuple-element.53), channel_id=1, source_target_pairs={{0,4},{1,5},{2,6},{3,7},{4,0},{5,1},{6,2},{7,3},{8,12},{9,13},{10,... | collective-permute-start | bytes 202760 | tf_op jit(solution)/shard_map/ppermute | solution.py:356
  29.4 8.7 %collective-permute-start.12 = (bf16[24,4224]{1,0:T(8,128)(2,1)S(1)}, bf16[24,4224]{1,0:T(8,128)(2,1)S(1)}, u32[]{:S(2)}, u32[]{:S(2)}) collective-permute-start(bf16[24,4224]{1,0:T(8,128)(2,1)S(1)} %get-tuple-element.44), channel_id=1, source_target_pairs={{0,6},{1,7},{2,4},{3,5},{4,2},{5,3},{6,0},{7,1},{8,14},{9,15},{10,... | collective-permute-start | bytes 608264 | tf_op jit(solution)/shard_map/ppermute | solution.py:356
  31.6 7.9 %collective-permute-start.10 = (bf16[24,4224]{1,0:T(8,128)(2,1)S(1)}, bf16[24,4224]{1,0:T(8,128)(2,1)S(1)}, u32[]{:S(2)}, u32[]{:S(2)}) collective-permute-start(bf16[24,4224]{1,0:T(8,128)(2,1)S(1)} %get-tuple-element.44), channel_id=1, source_target_pairs={{0,2},{1,3},{2,0},{3,1},{4,6},{5,7},{6,4},{7,5},{8,10},{9,11},{10,... | collective-permute-start | bytes 608264 | tf_op jit(solution)/shard_map/ppermute | solution.py:356
  32.5 7.9 %collective-permute-start.11 = (bf16[32,4224]{1,0:T(8,128)(2,1)S(1)}, bf16[32,4224]{1,0:T(8,128)(2,1)S(1)}, u32[]{:S(2)}, u32[]{:S(2)}) collective-permute-start(bf16[32,4224]{1,0:T(8,128)(2,1)S(1)} %pad_maximum_fusion), channel_id=1, source_target_pairs={{0,4},{1,5},{2,6},{3,7},{4,0},{5,1},{6,2},{7,3},{8,12},{9,13},{10,... | collective-permute-start | bytes 811016 | tf_op jit(solution)/shard_map/ppermute | solution.py:356
  33.1 7.3 %collective-permute-start.13 = (bf16[48,4224]{1,0:T(8,128)(2,1)S(1)}, bf16[48,4224]{1,0:T(8,128)(2,1)S(1)}, u32[]{:S(2)}, u32[]{:S(2)}) collective-permute-start(bf16[48,4224]{1,0:T(8,128)(2,1)S(1)} %get-tuple-element.38), channel_id=1, source_target_pairs={{0,1},{1,0},{2,3},{3,2},{4,5},{5,4},{6,7},{7,6},{8,9},{9,8},{10,11... | collective-permute-start | bytes 1216520 | tf_op jit(solution)/shard_map/ppermute | solution.py:356
  38.2 3.8 %collective-permute-start.16 = (bf16[24,4224]{1,0:T(8,128)(2,1)S(1)}, bf16[24,4224]{1,0:T(8,128)(2,1)S(1)}, u32[]{:S(2)}, u32[]{:S(2)}) collective-permute-start(bf16[24,4224]{1,0:T(8,128)(2,1)S(1)} %collective-permute-done.12), channel_id=1, source_target_pairs={{0,1},{1,0},{2,3},{3,2},{4,5},{5,4},{6,7},{7,6},{8,9},{9,8},{10,11... | collective-permute-start | bytes 608264 | tf_op jit(solution)/shard_map/ppermute | solution.py:356
  40.4 1.5 %collective-permute-start.15 = (bf16[32,4224]{1,0:T(8,128)(2,1)S(1)}, bf16[32,4224]{1,0:T(8,128)(2,1)S(1)}, u32[]{:S(2)}, u32[]{:S(2)}) collective-permute-start(bf16[32,4224]{1,0:T(8,128)(2,1)S(1)} %collective-permute-done.11), channel_id=1, source_target_pairs={{0,1},{1,0},{2,3},{3,2},{4,5},{5,4},{6,7},{7,6},{8,9},{9,8},{10,11... | collective-permute-start | bytes 811016 | tf_op jit(solution)/shard_map/ppermute | solution.py:356
  48.7 3.5 %collective-permute-start.24 = (bf16[24,4096]{1,0:T(8,128)(2,1)S(1)}, bf16[24,4096]{1,0:T(8,128)(2,1)S(1)}, u32[]{:S(2)}, u32[]{:S(2)}) collective-permute-start(bf16[24,4096]{1,0:T(8,128)(2,1)S(1)} %get-tuple-element.28), channel_id=1, source_target_pairs={{0,1},{1,0},{2,3},{3,2},{4,5},{5,4},{6,7},{7,6},{8,9},{9,8},{10,11... | collective-permute-start | bytes 589832 | tf_op jit(solution)/shard_map/ppermute | solution.py:356
  49.1 4.1 %collective-permute-start.18 = (bf16[32,4096]{1,0:T(8,128)(2,1)S(1)}, bf16[32,4096]{1,0:T(8,128)(2,1)S(1)}, u32[]{:S(2)}, u32[]{:S(2)}) collective-permute-start(bf16[32,4096]{1,0:T(8,128)(2,1)S(1)} %get-tuple-element.24), channel_id=1, source_target_pairs={{0,1},{1,0},{2,3},{3,2},{4,5},{5,4},{6,7},{7,6},{8,9},{9,8},{10,11... | collective-permute-start | bytes 786440 | tf_op jit(solution)/shard_map/ppermute | solution.py:356
  49.2 4.7 %collective-permute-start.17 = (bf16[48,4096]{1,0:T(8,128)(2,1)S(1)}, bf16[48,4096]{1,0:T(8,128)(2,1)S(1)}, u32[]{:S(2)}, u32[]{:S(2)}) collective-permute-start(bf16[48,4096]{1,0:T(8,128)(2,1)S(1)} %get-tuple-element.22), channel_id=1, source_target_pairs={{0,1},{1,0},{2,3},{3,2},{4,5},{5,4},{6,7},{7,6},{8,9},{9,8},{10,11... | collective-permute-start | bytes 1179656 | tf_op jit(solution)/shard_map/ppermute | solution.py:356
  50.1 8.8 %collective-permute-start.23 = (bf16[24,4096]{1,0:T(8,128)(2,1)S(1)}, bf16[24,4096]{1,0:T(8,128)(2,1)S(1)}, u32[]{:S(2)}, u32[]{:S(2)}) collective-permute-start(bf16[24,4096]{1,0:T(8,128)(2,1)S(1)} %add_convert_fusion.2), channel_id=1, source_target_pairs={{0,6},{1,7},{2,4},{3,5},{4,2},{5,3},{6,0},{7,1},{8,14},{9,15},{10,... | collective-permute-start | bytes 589832 | tf_op jit(solution)/shard_map/ppermute | solution.py:356
  52.3 9.9 %collective-permute-start.25 = (bf16[24,4096]{1,0:T(8,128)(2,1)S(1)}, bf16[24,4096]{1,0:T(8,128)(2,1)S(1)}, u32[]{:S(2)}, u32[]{:S(2)}) collective-permute-start(bf16[24,4096]{1,0:T(8,128)(2,1)S(1)} %add_convert_fusion.1), channel_id=1, source_target_pairs={{0,2},{1,3},{2,0},{3,1},{4,6},{5,7},{6,4},{7,5},{8,10},{9,11},{10,... | collective-permute-start | bytes 589832 | tf_op jit(solution)/shard_map/ppermute | solution.py:356
  53.3 10.1 %collective-permute-start.19 = (bf16[32,4096]{1,0:T(8,128)(2,1)S(1)}, bf16[32,4096]{1,0:T(8,128)(2,1)S(1)}, u32[]{:S(2)}, u32[]{:S(2)}) collective-permute-start(bf16[32,4096]{1,0:T(8,128)(2,1)S(1)} %add_convert_fusion), channel_id=1, source_target_pairs={{0,4},{1,5},{2,6},{3,7},{4,0},{5,1},{6,2},{7,3},{8,12},{9,13},{10,... | collective-permute-start | bytes 786440 | tf_op jit(solution)/shard_map/ppermute | solution.py:356
  63.5 7.1 %collective-permute-start.26 = (bf16[8,4096]{1,0:T(8,128)(2,1)S(1)}, bf16[8,4096]{1,0:T(8,128)(2,1)S(1)}, u32[]{:S(2)}, u32[]{:S(2)}) collective-permute-start(bf16[8,4096]{1,0:T(8,128)(2,1)S(1)} %get-tuple-element.31), channel_id=1, source_target_pairs={{0,24},{1,25},{2,26},{3,27},{4,28},{5,29},{6,30},{7,31},{8,16},{9,... | collective-permute-start | bytes 196616 | tf_op jit(solution)/shard_map/ppermute | solution.py:356
  65.4 5.2 %collective-permute-start.28 = (bf16[8,4096]{1,0:T(8,128)(2,1)S(1)}, bf16[8,4096]{1,0:T(8,128)(2,1)S(1)}, u32[]{:S(2)}, u32[]{:S(2)}) collective-permute-start(bf16[8,4096]{1,0:T(8,128)(2,1)S(1)} %get-tuple-element.32), channel_id=1, source_target_pairs={{0,8},{1,9},{2,10},{3,11},{4,12},{5,13},{6,14},{7,15},{8,0},{9,1},... | collective-permute-start | bytes 196616 | tf_op jit(solution)/shard_map/ppermute | solution.py:356
  66.4 5.9 %collective-permute-start.27 = (bf16[8,4096]{1,0:T(8,128)(2,1)S(1)}, bf16[8,4096]{1,0:T(8,128)(2,1)S(1)}, u32[]{:S(2)}, u32[]{:S(2)}) collective-permute-start(bf16[8,4096]{1,0:T(8,128)(2,1)S(1)} %get-tuple-element.33), channel_id=1, source_target_pairs={{0,16},{1,17},{2,18},{3,19},{4,20},{5,21},{6,22},{7,23},{8,24},{9,... | collective-permute-start | bytes 196616 | tf_op jit(solution)/shard_map/ppermute | solution.py:356
  68.1 4.3 %collective-permute-start.20 = (bf16[8,4096]{1,0:T(8,128)(2,1)S(1)}, bf16[8,4096]{1,0:T(8,128)(2,1)S(1)}, u32[]{:S(2)}, u32[]{:S(2)}) collective-permute-start(bf16[8,4096]{1,0:T(8,128)(2,1)S(1)} %get-tuple-element.29), channel_id=1, source_target_pairs={{0,4},{1,5},{2,6},{3,7},{4,0},{5,1},{6,2},{7,3},{8,12},{9,13},{10,... | collective-permute-start | bytes 196616 | tf_op jit(solution)/shard_map/ppermute | solution.py:356
  69.7 4.3 %collective-permute-start.21 = (bf16[8,4096]{1,0:T(8,128)(2,1)S(1)}, bf16[8,4096]{1,0:T(8,128)(2,1)S(1)}, u32[]{:S(2)}, u32[]{:S(2)}) collective-permute-start(bf16[8,4096]{1,0:T(8,128)(2,1)S(1)} %get-tuple-element.30), channel_id=1, source_target_pairs={{0,2},{1,3},{2,0},{3,1},{4,6},{5,7},{6,4},{7,5},{8,10},{9,11},{10,... | collective-permute-start | bytes 196616 | tf_op jit(solution)/shard_map/ppermute | solution.py:356
  (11 other events, 153.4 us)

commit v18 on v14

--- a/solution.py
+++ b/solution.py
@@ -39,10 +39,11 @@
 def attention_kernel(flip, *refs):
     sources, refs = refs[:8], refs[8:]
     if flip == 0:
-        ids_hbm, gates_hbm, w_hbm, _, out_ref, table_ref, *w_refs = refs[:8]
-        refs = refs[8:]
+        w_hbm, ids_hbm, gates_hbm, _, out_ref, w_ref, table_ref = refs[:7]
+        refs = refs[7:]
     else:
-        out_ref, refs = refs[0], refs[1:]
+        w_hbm, out_ref, w_ref = refs[:3]
+        refs = refs[3:]
     len_hbm, q_hbm, nk_hbm, nv_hbm, k_hbm, v_hbm, qg_hbm, kg_hbm = sources
     lengths, q_ref, nk_ref, nv_ref, k_ref, v_ref, qg_ref, kg_ref = refs[:8]
     nk_scr, nv_scr, num, tops, totals, score, weight, sem = refs[8:16]
@@ -66,16 +67,16 @@
     if flip == 0:
         ids_ref, gates_ref = refs[16:]
         pairs = [(ids_hbm, ids_ref), (gates_hbm, gates_ref)] + pairs
-        size = w_refs[0].shape[0]
-        pairs += [(w_hbm.at[pl.ds(i * size, size)], ref) for i, ref in enumerate(w_refs)]
+    start = 0 if flip else w_hbm.shape[0] - w_ref.shape[0]
+    pairs.append((w_hbm.at[pl.ds(start, w_ref.shape[0])], w_ref))
     copies = [pltpu.make_async_copy(src, dst, sem.at[i]) for i, (src, dst) in enumerate(pairs)]
     for c in copies:
         c.start()
+    ahead, copies = copies[-1], copies[:-1]
     if flip == 0:
         for c in copies[:2]:
             c.wait()
-        ahead = copies[-2:]
-        copies = copies[2:-2]
+        copies = copies[2:]
         gates = gates_ref[...]
         route = (gates / jnp.sum(gates, axis=1, keepdims=True)).astype(BF).astype(F32)
         expert = iota(table_ref.shape, 1)
@@ -153,9 +154,7 @@
             side = jnp.where(lane == heads_own + h, high, side)
             side = jnp.where(lane == 2 * heads_own + h, total - high, side)
         out_ref[slot, :, heads_own * hd :] = side.astype(BF)
-    if flip == 0:
-        for c in ahead:
-            c.wait()
+    ahead.wait()
 
 
 def attention(
@@ -166,8 +165,13 @@
     group = heads // kvh
     blocks = rows // 8
     args = [lengths, queries, new_keys, new_values, key_cache, value_cache]
-    args = [in_hbm(a) for a in (*args, qg.reshape(1, -1), kg.reshape(1, -1))]
-    outs = [jax.ShapeDtypeStruct((parts // kvh, rows, heads // parts * hd + LANES), BF)]
+    later, *more = more
+    share = later.shape[0] // 4
+    args = [in_hbm(a) for a in (*args, qg.reshape(1, -1), kg.reshape(1, -1), later)]
+    outs = [
+        jax.ShapeDtypeStruct((parts // kvh, rows, heads // parts * hd + LANES), BF),
+        pltpu.VMEM((share if flip else 3 * share, later.shape[1]), later.dtype),
+    ]
     scratch = [
         pltpu.SMEM((rows,), I32),
         pltpu.VMEM((rows, group, hd), BF),
@@ -189,11 +193,10 @@
     specs = [pl.BlockSpec(memory_space=pltpu.HBM)] * len(args)
     size = 2 * rows * group * hd * 8
     if flip == 0:
-        expert_ids, gate_weights, lanes, later, earlier = more
-        args += [in_hbm(a) for a in (expert_ids, gate_weights, later)] + [earlier]
-        specs += [pl.BlockSpec(memory_space=pltpu.HBM)] * 3 + [pl.BlockSpec(memory_space=pl.ANY)]
+        expert_ids, gate_weights, lanes, earlier = more
+        args += [in_hbm(expert_ids), in_hbm(gate_weights), earlier]
+        specs += [pl.BlockSpec(memory_space=pltpu.HBM)] * 2 + [pl.BlockSpec(memory_space=pl.ANY)]
         outs.append(jax.ShapeDtypeStruct((expert_ids.shape[0], lanes), BF))
-        outs += [pltpu.VMEM((later.shape[0] // 2, later.shape[1]), later.dtype)] * 2
         scratch += [pltpu.VMEM(expert_ids.shape, I32), pltpu.VMEM(gate_weights.shape, F32)]
         size = size + 2 * later.size
     return pl.pallas_call(
@@ -233,13 +236,15 @@
         cols = slice(h * hd, (h + 1) * hd)
         terms = [g[:, cols].astype(F32) * f[:, h : h + 1] for g, f in zip(got, factors)]
         attn[:, cols] = functools.reduce(jnp.add, terms).astype(BF)
-    part = depth // cuts
+    ends = [0]
+    for w_ref in w_refs:
+        ends.append(ends[-1] + w_ref.shape[0])
     for start in range(0, width, size):
         cols = slice(start, start + size)
         result = functools.reduce(
             jnp.add,
             [
-                matmul(attn[:, k * part : (k + 1) * part], w_ref[:, cols])
+                matmul(attn[:, ends[k] : ends[k + 1]], w_ref[:, cols])
                 for k, w_ref in enumerate(w_refs)
             ],
         )
@@ -393,18 +398,19 @@
 
     inputs = (lengths, queries, new_keys, new_values, key_cache, value_cache, query_gain, key_gain)
     groups = key_cache.shape[1]
-    got, local = [], None
+    got, local, weights = [], None, []
     for flip in reversed(range(groups)):
-        more = (expert_ids, gate_weights, lanes, out_proj, local)
+        more = (out_proj, expert_ids, gate_weights, lanes, local)
         results = attention(flip, *inputs, tensor, more)
         local = results[0]
+        weights.append(results[1])
         for j in range(0, tensor // groups, 2):
             far = flip * (tensor // groups) + j
             pair = local[j : j + 2]
             if far:
                 pair = plan.swap(pair, far)
             got += [pair[0], plan.swap(pair[1], plan.core)]
-    _, table, *weights = results
+    table = results[2]
     partial = projection(got, weights, share)
     pair = total_of([partial[0], plan.swap(partial[1], plan.core)])
     projected = total_of([pair[0]] + plan.swaps(list(pair[1:]), plan.y))

time: 74.2 us -> 73.3 us (0.988)
  transfers between devices with their start and end apart: 29 -> 29, of which waited for: 18 -> 17; matrix products, arithmetic and copies ran while one was open for 1% -> 1% of each run, Pallas kernels for 5% -> 5%
where the time goes in v18:
time: 73.3 us; the launch traced here: 73.1 us
  waiting for transfers between devices  28.8 us (39%)
  starting transfers between devices  27.8 us (38%)
  Pallas kernels  14.1 us (19%)
  other arithmetic  1.75 us (2%)
    ppermute x29, waiting for transfers between devices, swap(): lax.ppermute(value, ('dp', 'tensor'), [(i, i ^ flip) for i in range(self....  28.8 us
    ppermute x29, starting transfers between devices, swap(): lax.ppermute(value, ('dp', 'tensor'), [(i, i ^ flip) for i in range(self....  27.8 us
    pallas_call x1, Pallas kernels, experts(): pl.pallas_call(functools.partial(expert_kernel, slots, sizes), out_shape=...  6.5 us
    pallas_call x2, Pallas kernels, attention(): pl.pallas_call(functools.partial(attention_kernel, flip), out_shape=tuple...  5.79 us
    pallas_call x1, Pallas kernels, projection(): pl.pallas_call(functools.partial(projection_kernel, parts, len(weights)),...  1.8 us
  transfers between devices with their start and end apart: 29, of which 17 were waited for; matrix products, arithmetic and copies ran while one was open for 1% of the time, Pallas kernels for 5%

profile of v18, /device:TPU:0, one launch (start us, length us, event | category | flops | bytes accessed | tf_op | source)
XLA Modules:
  0.0 73.1 jit_solution(8656178333432549046)
XLA Ops:
  0.0 2.4 %attention.2 = (bf16[2,32,1152]{2,1,0:T(8,128)(2,1)S(1)}, bf16[256,4096]{1,0:T(8,128)(2,1)S(1)}) custom-call(s32[32]{0:T(128)} %refs_0_.3, bf16[32,32,128]{2,1,0:T(8,128)(2,1)} %refs_1_.4, bf16[32,2,128]{2,1,0:T(2,128)(2,1)} %refs_2_.4, bf16[32,2,128]{2,1,0:T(2,128)(2,1)} %refs_3_.4, bf16[32,2,32,128]{3,2,1,0:T(8,128)(2,1)} %refs_4_.3, ...), custom_call_target="tpu_custom_call" | custom-call | flops 1048576 | bytes 1048576 | tf_op jit(solution)/shard_map/attention/pallas_call | solution.py:202
  2.4 3.0 %collective-permute-start = (bf16[2,32,1152]{2,1,0:T(8,128)(2,1)S(1)}, bf16[2,32,1152]{2,1,0:T(8,128)(2,1)S(1)}, u32[]{:S(2)}, u32[]{:S(2)}) collective-permute-start(bf16[2,32,1152]{2,1,0:T(8,128)(2,1)S(1)} %get-tuple-element.18.refs_11_), channel_id=1, source_target_pairs={{0,2},{1,3},{2,0},{3,1},{4,6},{5,7},{6,4},{7,5},{8,10},{9,11},{10,... | collective-permute-start | bytes 442376 | tf_op jit(solution)/shard_map/ppermute | solution.py:361
  5.5 3.4 %attention.3 = (bf16[2,32,1152]{2,1,0:T(8,128)(2,1)S(1)}, bf16[768,4096]{1,0:T(8,128)(2,1)S(1)}, bf16[8,128]{1,0:T(8,128)(2,1)S(1)}) custom-call(s32[32]{0:T(128)} %refs_0_.3, bf16[32,32,128]{2,1,0:T(8,128)(2,1)} %refs_1_.4, bf16[32,2,128]{2,1,0:T(2,128)(2,1)} %refs_2_.4, bf16[32,2,128]{2,1,0:T(2,128)(2,1)} %refs_3_.4, bf16[32,2,32,128]{3,2,1,0:T(8,128)(2,1)} %refs_4_.3, ...), custom_call_target="tpu_custom_call" | custom-call | flops 9437184 | bytes 9437184 | tf_op jit(solution)/shard_map/attention/pallas_call | solution.py:202
  10.7 1.8 %projection.1 = bf16[2,2,8,4096]{3,2,1,0:T(8,128)(2,1)S(1)} custom-call(bf16[32,1152]{1,0:T(8,128)(2,1)S(1)} %get-tuple-element.39.refs_0_, bf16[32,1152]{1,0:T(8,128)(2,1)S(1)} %collective-permute-done.1.refs_1_, bf16[32,1152]{1,0:T(8,128)(2,1)S(1)} %get-tuple-element.37.refs_2_, bf16[32,1152]{1,0:T(8,128)(2,1)S(1)} %collective-permute-done.2.refs_3_, ...), custom_call_target="tpu_custom_call" | custom-call | tf_op jit(solution)/shard_map/projection/pallas_call | solution.py:263
  14.0 1.8 %collective-permute-start.4 = (bf16[8,4096]{1,0:T(8,128)(2,1)S(1)}, bf16[8,4096]{1,0:T(8,128)(2,1)S(1)}, u32[]{:S(2)}, u32[]{:S(2)}) collective-permute-start(bf16[8,4096]{1,0:T(8,128)(2,1)S(1)} %fusion.11), channel_id=1, source_target_pairs={{0,2},{1,3},{2,0},{3,1},{4,6},{5,7},{6,4},{7,5},{8,10},{9,11},{10,... | collective-permute-start | bytes 196616 | tf_op jit(solution)/shard_map/ppermute | solution.py:361
  15.8 2.5 %collective-permute-done.4 = bf16[8,4096]{1,0:T(8,128)(2,1)S(1)} collective-permute-done((bf16[8,4096]{1,0:T(8,128)(2,1)S(1)}, bf16[8,4096]{1,0:T(8,128)(2,1)S(1)}, u32[]{:S(2)}, u32[]{:S(2)}) %collective-permute-start.4) | collective-permute-done | bytes 65568 | tf_op jit(solution)/shard_map/ppermute | solution.py:361
  18.6 1.9 %collective-permute-start.5 = (bf16[8,4224]{1,0:T(8,128)(2,1)S(1)}, bf16[8,4224]{1,0:T(8,128)(2,1)S(1)}, u32[]{:S(2)}, u32[]{:S(2)}) collective-permute-start(bf16[8,4224]{1,0:T(8,128)(2,1)S(1)} %pad_maximum_fusion.1), channel_id=1, source_target_pairs={{0,8},{1,9},{2,10},{3,11},{4,12},{5,13},{6,14},{7,15},{8,0},{9,1},... | collective-permute-start | bytes 202760 | tf_op jit(solution)/shard_map/ppermute | solution.py:361
  20.4 2.6 %collective-permute-start.6 = (bf16[8,4224]{1,0:T(8,128)(2,1)S(1)}, bf16[8,4224]{1,0:T(8,128)(2,1)S(1)}, u32[]{:S(2)}, u32[]{:S(2)}) collective-permute-start(bf16[8,4224]{1,0:T(8,128)(2,1)S(1)} %pad_maximum_fusion.1), channel_id=1, source_target_pairs={{0,16},{1,17},{2,18},{3,19},{4,20},{5,21},{6,22},{7,23},{8,24},{9,... | collective-permute-start | bytes 202760 | tf_op jit(solution)/shard_map/ppermute | solution.py:361
  23.8 1.8 %collective-permute-start.9 = (bf16[8,4224]{1,0:T(8,128)(2,1)S(1)}, bf16[8,4224]{1,0:T(8,128)(2,1)S(1)}, u32[]{:S(2)}, u32[]{:S(2)}) collective-permute-start(bf16[8,4224]{1,0:T(8,128)(2,1)S(1)} %get-tuple-element.55), channel_id=1, source_target_pairs={{0,2},{1,3},{2,0},{3,1},{4,6},{5,7},{6,4},{7,5},{8,10},{9,11},{10,... | collective-permute-start | bytes 202760 | tf_op jit(solution)/shard_map/ppermute | solution.py:361
  25.6 1.5 %collective-permute-start.8 = (bf16[8,4224]{1,0:T(8,128)(2,1)S(1)}, bf16[8,4224]{1,0:T(8,128)(2,1)S(1)}, u32[]{:S(2)}, u32[]{:S(2)}) collective-permute-start(bf16[8,4224]{1,0:T(8,128)(2,1)S(1)} %get-tuple-element.55), channel_id=1, source_target_pairs={{0,4},{1,5},{2,6},{3,7},{4,0},{5,1},{6,2},{7,3},{8,12},{9,13},{10,... | collective-permute-start | bytes 202760 | tf_op jit(solution)/shard_map/ppermute | solution.py:361
  27.1 2.0 %collective-permute-done.7 = bf16[8,4224]{1,0:T(8,128)(2,1)S(1)} collective-permute-done((bf16[8,4224]{1,0:T(8,128)(2,1)S(1)}, bf16[8,4224]{1,0:T(8,128)(2,1)S(1)}, u32[]{:S(2)}, u32[]{:S(2)}) %collective-permute-start.7) | collective-permute-done | bytes 67616 | tf_op jit(solution)/shard_map/ppermute | solution.py:361
  29.1 2.5 %collective-permute-start.12 = (bf16[24,4224]{1,0:T(8,128)(2,1)S(1)}, bf16[24,4224]{1,0:T(8,128)(2,1)S(1)}, u32[]{:S(2)}, u32[]{:S(2)}) collective-permute-start(bf16[24,4224]{1,0:T(8,128)(2,1)S(1)} %get-tuple-element.46), channel_id=1, source_target_pairs={{0,6},{1,7},{2,4},{3,5},{4,2},{5,3},{6,0},{7,1},{8,14},{9,15},{10,... | collective-permute-start | bytes 608264 | tf_op jit(solution)/shard_map/ppermute | solution.py:361
  32.9 4.9 %collective-permute-done.12 = bf16[24,4224]{1,0:T(8,128)(2,1)S(1)} collective-permute-done((bf16[24,4224]{1,0:T(8,128)(2,1)S(1)}, bf16[24,4224]{1,0:T(8,128)(2,1)S(1)}, u32[]{:S(2)}, u32[]{:S(2)}) %collective-permute-start.12) | collective-permute-done | bytes 202784 | tf_op jit(solution)/shard_map/ppermute | solution.py:361
  38.8 1.5 %collective-permute-done.11 = bf16[32,4224]{1,0:T(8,128)(2,1)S(1)} collective-permute-done((bf16[32,4224]{1,0:T(8,128)(2,1)S(1)}, bf16[32,4224]{1,0:T(8,128)(2,1)S(1)}, u32[]{:S(2)}, u32[]{:S(2)}) %collective-permute-start.11) | collective-permute-done | bytes 270368 | tf_op jit(solution)/shard_map/ppermute | solution.py:361
  40.5 1.4 %collective-permute-done.15 = bf16[32,4224]{1,0:T(8,128)(2,1)S(1)} collective-permute-done((bf16[32,4224]{1,0:T(8,128)(2,1)S(1)}, bf16[32,4224]{1,0:T(8,128)(2,1)S(1)}, u32[]{:S(2)}, u32[]{:S(2)}) %collective-permute-start.15) | collective-permute-done | bytes 270368 | tf_op jit(solution)/shard_map/ppermute | solution.py:361
  42.0 6.5 %experts.1 = (bf16[48,4096]{1,0:T(8,128)(2,1)S(1)}, bf16[24,4096]{1,0:T(8,128)(2,1)S(1)}, bf16[32,4096]{1,0:T(8,128)(2,1)S(1)}, bf16[24,4096]{1,0:T(8,128)(2,1)S...) custom-call(bf16[256,4224]{1,0:T(8,128)(2,1)S(1)} %constant_dynamic-, ...), custom_call_target="tpu_custom_call" | custom-call | tf_op jit(solution)/shard_map/experts/pallas_call | solution.py:332
  50.1 1.5 %collective-permute-start.23 = (bf16[24,4096]{1,0:T(8,128)(2,1)S(1)}, bf16[24,4096]{1,0:T(8,128)(2,1)S(1)}, u32[]{:S(2)}, u32[]{:S(2)}) collective-permute-start(bf16[24,4096]{1,0:T(8,128)(2,1)S(1)} %add_convert_fusion.2), channel_id=1, source_target_pairs={{0,6},{1,7},{2,4},{3,5},{4,2},{5,3},{6,0},{7,1},{8,14},{9,15},{10,... | collective-permute-start | bytes 589832 | tf_op jit(solution)/shard_map/ppermute | solution.py:361
  51.7 1.6 %collective-permute-start.25 = (bf16[24,4096]{1,0:T(8,128)(2,1)S(1)}, bf16[24,4096]{1,0:T(8,128)(2,1)S(1)}, u32[]{:S(2)}, u32[]{:S(2)}) collective-permute-start(bf16[24,4096]{1,0:T(8,128)(2,1)S(1)} %add_convert_fusion.1), channel_id=1, source_target_pairs={{0,2},{1,3},{2,0},{3,1},{4,6},{5,7},{6,4},{7,5},{8,10},{9,11},{10,... | collective-permute-start | bytes 589832 | tf_op jit(solution)/shard_map/ppermute | solution.py:361
  54.0 4.9 %collective-permute-done.23 = bf16[24,4096]{1,0:T(8,128)(2,1)S(1)} collective-permute-done((bf16[24,4096]{1,0:T(8,128)(2,1)S(1)}, bf16[24,4096]{1,0:T(8,128)(2,1)S(1)}, u32[]{:S(2)}, u32[]{:S(2)}) %collective-permute-start.23) | collective-permute-done | bytes 196640 | tf_op jit(solution)/shard_map/ppermute | solution.py:361
  58.9 3.4 %collective-permute-done.25 = bf16[24,4096]{1,0:T(8,128)(2,1)S(1)} collective-permute-done((bf16[24,4096]{1,0:T(8,128)(2,1)S(1)}, bf16[24,4096]{1,0:T(8,128)(2,1)S(1)}, u32[]{:S(2)}, u32[]{:S(2)}) %collective-permute-start.25) | collective-permute-done | bytes 196640 | tf_op jit(solution)/shard_map/ppermute | solution.py:361
  63.3 1.8 %collective-permute-start.28 = (bf16[8,4096]{1,0:T(8,128)(2,1)S(1)}, bf16[8,4096]{1,0:T(8,128)(2,1)S(1)}, u32[]{:S(2)}, u32[]{:S(2)}) collective-permute-start(bf16[8,4096]{1,0:T(8,128)(2,1)S(1)} %get-tuple-element.34), channel_id=1, source_target_pairs={{0,24},{1,25},{2,26},{3,27},{4,28},{5,29},{6,30},{7,31},{8,16},{9,... | collective-permute-start | bytes 196616 | tf_op jit(solution)/shard_map/ppermute | solution.py:361
  65.0 1.7 %collective-permute-start.27 = (bf16[8,4096]{1,0:T(8,128)(2,1)S(1)}, bf16[8,4096]{1,0:T(8,128)(2,1)S(1)}, u32[]{:S(2)}, u32[]{:S(2)}) collective-permute-start(bf16[8,4096]{1,0:T(8,128)(2,1)S(1)} %get-tuple-element.35), channel_id=1, source_target_pairs={{0,16},{1,17},{2,18},{3,19},{4,20},{5,21},{6,22},{7,23},{8,24},{9,... | collective-permute-start | bytes 196616 | tf_op jit(solution)/shard_map/ppermute | solution.py:361
  68.1 1.5 %collective-permute-start.21 = (bf16[8,4096]{1,0:T(8,128)(2,1)S(1)}, bf16[8,4096]{1,0:T(8,128)(2,1)S(1)}, u32[]{:S(2)}, u32[]{:S(2)}) collective-permute-start(bf16[8,4096]{1,0:T(8,128)(2,1)S(1)} %get-tuple-element.32), channel_id=1, source_target_pairs={{0,2},{1,3},{2,0},{3,1},{4,6},{5,7},{6,4},{7,5},{8,10},{9,11},{10,... | collective-permute-start | bytes 196616 | tf_op jit(solution)/shard_map/ppermute | solution.py:361
  69.7 2.5 %collective-permute-done.27 = bf16[8,4096]{1,0:T(8,128)(2,1)S(1)} collective-permute-done((bf16[8,4096]{1,0:T(8,128)(2,1)S(1)}, bf16[8,4096]{1,0:T(8,128)(2,1)S(1)}, u32[]{:S(2)}, u32[]{:S(2)}) %collective-permute-start.27) | collective-permute-done | bytes 65568 | tf_op jit(solution)/shard_map/ppermute | solution.py:361
  (85 shorter events, 12.6 us)
Async XLA Ops:
  2.4 6.9 %collective-permute-start = (bf16[2,32,1152]{2,1,0:T(8,128)(2,1)S(1)}, bf16[2,32,1152]{2,1,0:T(8,128)(2,1)S(1)}, u32[]{:S(2)}, u32[]{:S(2)}) collective-permute-start(bf16[2,32,1152]{2,1,0:T(8,128)(2,1)S(1)} %get-tuple-element.18.refs_11_), channel_id=1, source_target_pairs={{0,2},{1,3},{2,0},{3,1},{4,6},{5,7},{6,4},{7,5},{8,10},{9,11},{10,... | collective-permute-start | bytes 442376 | tf_op jit(solution)/shard_map/ppermute | solution.py:361
  14.0 4.3 %collective-permute-start.4 = (bf16[8,4096]{1,0:T(8,128)(2,1)S(1)}, bf16[8,4096]{1,0:T(8,128)(2,1)S(1)}, u32[]{:S(2)}, u32[]{:S(2)}) collective-permute-start(bf16[8,4096]{1,0:T(8,128)(2,1)S(1)} %fusion.11), channel_id=1, source_target_pairs={{0,2},{1,3},{2,0},{3,1},{4,6},{5,7},{6,4},{7,5},{8,10},{9,11},{10,... | collective-permute-start | bytes 196616 | tf_op jit(solution)/shard_map/ppermute | solution.py:361
  18.6 5.0 %collective-permute-start.5 = (bf16[8,4224]{1,0:T(8,128)(2,1)S(1)}, bf16[8,4224]{1,0:T(8,128)(2,1)S(1)}, u32[]{:S(2)}, u32[]{:S(2)}) collective-permute-start(bf16[8,4224]{1,0:T(8,128)(2,1)S(1)} %pad_maximum_fusion.1), channel_id=1, source_target_pairs={{0,8},{1,9},{2,10},{3,11},{4,12},{5,13},{6,14},{7,15},{8,0},{9,1},... | collective-permute-start | bytes 202760 | tf_op jit(solution)/shard_map/ppermute | solution.py:361
  20.4 6.7 %collective-permute-start.6 = (bf16[8,4224]{1,0:T(8,128)(2,1)S(1)}, bf16[8,4224]{1,0:T(8,128)(2,1)S(1)}, u32[]{:S(2)}, u32[]{:S(2)}) collective-permute-start(bf16[8,4224]{1,0:T(8,128)(2,1)S(1)} %pad_maximum_fusion.1), channel_id=1, source_target_pairs={{0,16},{1,17},{2,18},{3,19},{4,20},{5,21},{6,22},{7,23},{8,24},{9,... | collective-permute-start | bytes 202760 | tf_op jit(solution)/shard_map/ppermute | solution.py:361
  23.0 6.1 %collective-permute-start.7 = (bf16[8,4224]{1,0:T(8,128)(2,1)S(1)}, bf16[8,4224]{1,0:T(8,128)(2,1)S(1)}, u32[]{:S(2)}, u32[]{:S(2)}) collective-permute-start(bf16[8,4224]{1,0:T(8,128)(2,1)S(1)} %pad_maximum_fusion.1), channel_id=1, source_target_pairs={{0,24},{1,25},{2,26},{3,27},{4,28},{5,29},{6,30},{7,31},{8,16},{9,... | collective-permute-start | bytes 202760 | tf_op jit(solution)/shard_map/ppermute | solution.py:361
  23.8 8.4 %collective-permute-start.9 = (bf16[8,4224]{1,0:T(8,128)(2,1)S(1)}, bf16[8,4224]{1,0:T(8,128)(2,1)S(1)}, u32[]{:S(2)}, u32[]{:S(2)}) collective-permute-start(bf16[8,4224]{1,0:T(8,128)(2,1)S(1)} %get-tuple-element.55), channel_id=1, source_target_pairs={{0,2},{1,3},{2,0},{3,1},{4,6},{5,7},{6,4},{7,5},{8,10},{9,11},{10,... | collective-permute-start | bytes 202760 | tf_op jit(solution)/shard_map/ppermute | solution.py:361
  25.6 7.2 %collective-permute-start.8 = (bf16[8,4224]{1,0:T(8,128)(2,1)S(1)}, bf16[8,4224]{1,0:T(8,128)(2,1)S(1)}, u32[]{:S(2)}, u32[]{:S(2)}) collective-permute-start(bf16[8,4224]{1,0:T(8,128)(2,1)S(1)} %get-tuple-element.55), channel_id=1, source_target_pairs={{0,4},{1,5},{2,6},{3,7},{4,0},{5,1},{6,2},{7,3},{8,12},{9,13},{10,... | collective-permute-start | bytes 202760 | tf_op jit(solution)/shard_map/ppermute | solution.py:361
  29.1 8.6 %collective-permute-start.12 = (bf16[24,4224]{1,0:T(8,128)(2,1)S(1)}, bf16[24,4224]{1,0:T(8,128)(2,1)S(1)}, u32[]{:S(2)}, u32[]{:S(2)}) collective-permute-start(bf16[24,4224]{1,0:T(8,128)(2,1)S(1)} %get-tuple-element.46), channel_id=1, source_target_pairs={{0,6},{1,7},{2,4},{3,5},{4,2},{5,3},{6,0},{7,1},{8,14},{9,15},{10,... | collective-permute-start | bytes 608264 | tf_op jit(solution)/shard_map/ppermute | solution.py:361
  31.7 7.2 %collective-permute-start.10 = (bf16[24,4224]{1,0:T(8,128)(2,1)S(1)}, bf16[24,4224]{1,0:T(8,128)(2,1)S(1)}, u32[]{:S(2)}, u32[]{:S(2)}) collective-permute-start(bf16[24,4224]{1,0:T(8,128)(2,1)S(1)} %get-tuple-element.46), channel_id=1, source_target_pairs={{0,2},{1,3},{2,0},{3,1},{4,6},{5,7},{6,4},{7,5},{8,10},{9,11},{10,... | collective-permute-start | bytes 608264 | tf_op jit(solution)/shard_map/ppermute | solution.py:361
  32.2 8.2 %collective-permute-start.11 = (bf16[32,4224]{1,0:T(8,128)(2,1)S(1)}, bf16[32,4224]{1,0:T(8,128)(2,1)S(1)}, u32[]{:S(2)}, u32[]{:S(2)}) collective-permute-start(bf16[32,4224]{1,0:T(8,128)(2,1)S(1)} %pad_maximum_fusion), channel_id=1, source_target_pairs={{0,4},{1,5},{2,6},{3,7},{4,0},{5,1},{6,2},{7,3},{8,12},{9,13},{10,... | collective-permute-start | bytes 811016 | tf_op jit(solution)/shard_map/ppermute | solution.py:361
  32.8 7.6 %collective-permute-start.13 = (bf16[48,4224]{1,0:T(8,128)(2,1)S(1)}, bf16[48,4224]{1,0:T(8,128)(2,1)S(1)}, u32[]{:S(2)}, u32[]{:S(2)}) collective-permute-start(bf16[48,4224]{1,0:T(8,128)(2,1)S(1)} %get-tuple-element.40), channel_id=1, source_target_pairs={{0,1},{1,0},{2,3},{3,2},{4,5},{5,4},{6,7},{7,6},{8,9},{9,8},{10,11... | collective-permute-start | bytes 1216520 | tf_op jit(solution)/shard_map/ppermute | solution.py:361
  37.8 4.2 %collective-permute-start.16 = (bf16[24,4224]{1,0:T(8,128)(2,1)S(1)}, bf16[24,4224]{1,0:T(8,128)(2,1)S(1)}, u32[]{:S(2)}, u32[]{:S(2)}) collective-permute-start(bf16[24,4224]{1,0:T(8,128)(2,1)S(1)} %collective-permute-done.12), channel_id=1, source_target_pairs={{0,1},{1,0},{2,3},{3,2},{4,5},{5,4},{6,7},{7,6},{8,9},{9,8},{10,11... | collective-permute-start | bytes 608264 | tf_op jit(solution)/shard_map/ppermute | solution.py:361
  38.8 1.7 %collective-permute-start.14 = (bf16[24,4224]{1,0:T(8,128)(2,1)S(1)}, bf16[24,4224]{1,0:T(8,128)(2,1)S(1)}, u32[]{:S(2)}, u32[]{:S(2)}) collective-permute-start(bf16[24,4224]{1,0:T(8,128)(2,1)S(1)} %collective-permute-done.10), channel_id=1, source_target_pairs={{0,1},{1,0},{2,3},{3,2},{4,5},{5,4},{6,7},{7,6},{8,9},{9,8},{10,11... | collective-permute-start | bytes 608264 | tf_op jit(solution)/shard_map/ppermute | solution.py:361
  48.8 2.8 %collective-permute-start.24 = (bf16[24,4096]{1,0:T(8,128)(2,1)S(1)}, bf16[24,4096]{1,0:T(8,128)(2,1)S(1)}, u32[]{:S(2)}, u32[]{:S(2)}) collective-permute-start(bf16[24,4096]{1,0:T(8,128)(2,1)S(1)} %get-tuple-element.30), channel_id=1, source_target_pairs={{0,1},{1,0},{2,3},{3,2},{4,5},{5,4},{6,7},{7,6},{8,9},{9,8},{10,11... | collective-permute-start | bytes 589832 | tf_op jit(solution)/shard_map/ppermute | solution.py:361
  49.1 4.1 %collective-permute-start.18 = (bf16[32,4096]{1,0:T(8,128)(2,1)S(1)}, bf16[32,4096]{1,0:T(8,128)(2,1)S(1)}, u32[]{:S(2)}, u32[]{:S(2)}) collective-permute-start(bf16[32,4096]{1,0:T(8,128)(2,1)S(1)} %get-tuple-element.26), channel_id=1, source_target_pairs={{0,1},{1,0},{2,3},{3,2},{4,5},{5,4},{6,7},{7,6},{8,9},{9,8},{10,11... | collective-permute-start | bytes 786440 | tf_op jit(solution)/shard_map/ppermute | solution.py:361
  49.3 4.7 %collective-permute-start.17 = (bf16[48,4096]{1,0:T(8,128)(2,1)S(1)}, bf16[48,4096]{1,0:T(8,128)(2,1)S(1)}, u32[]{:S(2)}, u32[]{:S(2)}) collective-permute-start(bf16[48,4096]{1,0:T(8,128)(2,1)S(1)} %get-tuple-element.24), channel_id=1, source_target_pairs={{0,1},{1,0},{2,3},{3,2},{4,5},{5,4},{6,7},{7,6},{8,9},{9,8},{10,11... | collective-permute-start | bytes 1179656 | tf_op jit(solution)/shard_map/ppermute | solution.py:361
  50.1 8.8 %collective-permute-start.23 = (bf16[24,4096]{1,0:T(8,128)(2,1)S(1)}, bf16[24,4096]{1,0:T(8,128)(2,1)S(1)}, u32[]{:S(2)}, u32[]{:S(2)}) collective-permute-start(bf16[24,4096]{1,0:T(8,128)(2,1)S(1)} %add_convert_fusion.2), channel_id=1, source_target_pairs={{0,6},{1,7},{2,4},{3,5},{4,2},{5,3},{6,0},{7,1},{8,14},{9,15},{10,... | collective-permute-start | bytes 589832 | tf_op jit(solution)/shard_map/ppermute | solution.py:361
  51.7 10.6 %collective-permute-start.25 = (bf16[24,4096]{1,0:T(8,128)(2,1)S(1)}, bf16[24,4096]{1,0:T(8,128)(2,1)S(1)}, u32[]{:S(2)}, u32[]{:S(2)}) collective-permute-start(bf16[24,4096]{1,0:T(8,128)(2,1)S(1)} %add_convert_fusion.1), channel_id=1, source_target_pairs={{0,2},{1,3},{2,0},{3,1},{4,6},{5,7},{6,4},{7,5},{8,10},{9,11},{10,... | collective-permute-start | bytes 589832 | tf_op jit(solution)/shard_map/ppermute | solution.py:361
  53.3 9.7 %collective-permute-start.19 = (bf16[32,4096]{1,0:T(8,128)(2,1)S(1)}, bf16[32,4096]{1,0:T(8,128)(2,1)S(1)}, u32[]{:S(2)}, u32[]{:S(2)}) collective-permute-start(bf16[32,4096]{1,0:T(8,128)(2,1)S(1)} %add_convert_fusion), channel_id=1, source_target_pairs={{0,4},{1,5},{2,6},{3,7},{4,0},{5,1},{6,2},{7,3},{8,12},{9,13},{10,... | collective-permute-start | bytes 786440 | tf_op jit(solution)/shard_map/ppermute | solution.py:361
  63.2 6.5 %collective-permute-start.26 = (bf16[8,4096]{1,0:T(8,128)(2,1)S(1)}, bf16[8,4096]{1,0:T(8,128)(2,1)S(1)}, u32[]{:S(2)}, u32[]{:S(2)}) collective-permute-start(bf16[8,4096]{1,0:T(8,128)(2,1)S(1)} %get-tuple-element.33), channel_id=1, source_target_pairs={{0,8},{1,9},{2,10},{3,11},{4,12},{5,13},{6,14},{7,15},{8,0},{9,1},... | collective-permute-start | bytes 196616 | tf_op jit(solution)/shard_map/ppermute | solution.py:361
  63.3 6.4 %collective-permute-start.28 = (bf16[8,4096]{1,0:T(8,128)(2,1)S(1)}, bf16[8,4096]{1,0:T(8,128)(2,1)S(1)}, u32[]{:S(2)}, u32[]{:S(2)}) collective-permute-start(bf16[8,4096]{1,0:T(8,128)(2,1)S(1)} %get-tuple-element.34), channel_id=1, source_target_pairs={{0,24},{1,25},{2,26},{3,27},{4,28},{5,29},{6,30},{7,31},{8,16},{9,... | collective-permute-start | bytes 196616 | tf_op jit(solution)/shard_map/ppermute | solution.py:361
  65.0 7.1 %collective-permute-start.27 = (bf16[8,4096]{1,0:T(8,128)(2,1)S(1)}, bf16[8,4096]{1,0:T(8,128)(2,1)S(1)}, u32[]{:S(2)}, u32[]{:S(2)}) collective-permute-start(bf16[8,4096]{1,0:T(8,128)(2,1)S(1)} %get-tuple-element.35), channel_id=1, source_target_pairs={{0,16},{1,17},{2,18},{3,19},{4,20},{5,21},{6,22},{7,23},{8,24},{9,... | collective-permute-start | bytes 196616 | tf_op jit(solution)/shard_map/ppermute | solution.py:361
  66.9 5.2 %collective-permute-start.20 = (bf16[8,4096]{1,0:T(8,128)(2,1)S(1)}, bf16[8,4096]{1,0:T(8,128)(2,1)S(1)}, u32[]{:S(2)}, u32[]{:S(2)}) collective-permute-start(bf16[8,4096]{1,0:T(8,128)(2,1)S(1)} %get-tuple-element.31), channel_id=1, source_target_pairs={{0,4},{1,5},{2,6},{3,7},{4,0},{5,1},{6,2},{7,3},{8,12},{9,13},{10,... | collective-permute-start | bytes 196616 | tf_op jit(solution)/shard_map/ppermute | solution.py:361
  68.1 4.3 %collective-permute-start.21 = (bf16[8,4096]{1,0:T(8,128)(2,1)S(1)}, bf16[8,4096]{1,0:T(8,128)(2,1)S(1)}, u32[]{:S(2)}, u32[]{:S(2)}) collective-permute-start(bf16[8,4096]{1,0:T(8,128)(2,1)S(1)} %get-tuple-element.32), channel_id=1, source_target_pairs={{0,2},{1,3},{2,0},{3,1},{4,6},{5,7},{6,4},{7,5},{8,10},{9,11},{10,... | collective-permute-start | bytes 196616 | tf_op jit(solution)/shard_map/ppermute | solution.py:361
  (11 other events, 154.9 us)
